TPU v7x, 32 devices: a whole 2x2x4 slice. The times are simulated.
32 devices in a mesh: fsdp: 8 (over y, x, core), tp: 4 (over z).
Axes of the slice: x: 2, y: 2, z: 4, core: 2. Of those that a mesh axis runs over, the one named last changes fastest.
Arguments:
- hidden_in: bfloat16 [4096, 2048], P(('fsdp', 'tp')), may hold values from -6 to 6
- out_grad: bfloat16 [4096, 2048], P(('fsdp', 'tp')), may hold values from -6 to 6
- segment_ids: int32 [8, 512], P('fsdp'), may hold values from 0 to 3, never falling along the last dimension, each value on 1 to 256 neighbouring positions
- expert_ids: int32 [4096, 4], P('fsdp'), may hold values from 0 to 7, all different within a row; in each aligned block of 512 rows (0 to 511, 512 to 1023, ...) at most 384 rows name the same one
- route_weights: float32 [4096, 4], P('fsdp'), may hold values from 0.05 to 0.6
- attn_gain: float32 [2048], replicated, may hold values from 0.5 to 1.5
- ffn_gain: float32 [2048], replicated, may hold values from 0.5 to 1.5
- qkv_weight: bfloat16 [2048, 3, 16, 128], P('fsdp', None, 'tp'), may hold values from -0.125 to 0.125
- qkv_bias: float32 [3, 16, 128], P(None, 'tp', 'fsdp'), may hold values from -0.6 to 0.6
- out_weight: bfloat16 [2048, 2048], P('tp', 'fsdp'), may hold values from -0.75 to 0.75
- shared_gate_up: bfloat16 [2048, 2, 5632], P('fsdp', None, 'tp'), may hold values from -0.125 to 0.125
- shared_down: bfloat16 [5632, 2048], P('tp', 'fsdp'), may hold values from -0.15625 to 0.15625
- shared_gate_vec: float32 [2048], replicated, may hold values from -0.125 to 0.125
- expert_gate_up: bfloat16 [8, 2048, 2, 1408], P('fsdp', None, None, 'tp'), may hold values from -0.125 to 0.125
- expert_down: bfloat16 [8, 1408, 2048], P('fsdp', 'tp'), may hold values from -0.3125 to 0.3125
Outputs:
- hidden_out: bfloat16 [4096, 2048], P(('fsdp', 'tp'))
- hidden_grad: float32 [4096, 2048], P(('fsdp', 'tp'))
- route_grad: float32 [4096, 4], P(('fsdp', 'tp'))
- attn_gain_grad: float32 [2048], P(('fsdp', 'tp'))
- ffn_gain_grad: float32 [2048], P(('fsdp', 'tp'))
- qkv_weight_grad: float32 [2048, 3, 16, 128], P('fsdp', None, 'tp')
- qkv_bias_grad: float32 [3, 16, 128], P(None, 'tp', 'fsdp')
- out_weight_grad: float32 [2048, 2048], P('tp', 'fsdp')
- shared_gate_up_grad: float32 [2048, 2, 5632], P('fsdp', None, 'tp')
- shared_down_grad: float32 [5632, 2048], P('tp', 'fsdp')
- shared_gate_vec_grad: float32 [2048], P(('fsdp', 'tp'))
- expert_gate_up_grad: float32 [8, 2048, 2, 1408], P('fsdp', None, None, 'tp')
- expert_down_grad: float32 [8, 1408, 2048], P('fsdp', 'tp')
Inputs may be any that keep to these rules, and one draw needn't show every extreme that they name: `segment_ids`: within each pack the numbers never fall; each document holds 1 to 256 positions. `expert_ids`: each row names 4 different experts; among the 512 rows of one pack no expert is named by more than 384 rows, and in every draw some pack names some expert exactly 384 times.
All inputs are finite; a program needn't handle non-finite values.
Results may differ from a plain program's by a relative error of at most 0.033.
Values may be sent and summed in bfloat16 or wider, within the bound.
A program may use at most 320 MiB of HBM per device.

v0:
```python
import jax
import jax.numpy as jnp
from jax import lax
from jax.sharding import PartitionSpec as P

epsilon = 1e-06


def rope_tables(length, head_dim):
    half_dim = head_dim // 2
    ratios = jnp.arange(half_dim, dtype=jnp.float32) * (2.0 / head_dim)
    frequency = jnp.exp(-jnp.log(10000.0) * ratios)
    angles = jnp.arange(length, dtype=jnp.float32)[:, None] * frequency[None, :]
    return (jnp.cos(angles)[:, None, :], jnp.sin(angles)[:, None, :])


def rotate(tensor, cos_table, sin_table):
    half_dim = tensor.shape[-1] // 2
    front_half = tensor[..., :half_dim]
    back_half = tensor[..., half_dim:]
    return jnp.concatenate(
        [
            front_half * cos_table - back_half * sin_table,
            back_half * cos_table + front_half * sin_table,
        ],
        axis=-1,
    )


def unrotate(tensor, cos_table, sin_table):
    half_dim = tensor.shape[-1] // 2
    front_half = tensor[..., :half_dim]
    back_half = tensor[..., half_dim:]
    return jnp.concatenate(
        [
            front_half * cos_table + back_half * sin_table,
            back_half * cos_table - front_half * sin_table,
        ],
        axis=-1,
    )


def silu_parts(gate_in):
    sigmoid_value = jax.nn.sigmoid(gate_in)
    return (gate_in * sigmoid_value, sigmoid_value * (1.0 + gate_in * (1.0 - sigmoid_value)))


def slot_table(route_ids, experts, capacity):
    flat_ids = route_ids.reshape(-1)
    onehot = (flat_ids[:, None] == jnp.arange(experts, dtype=jnp.int32)[None, :]).astype(jnp.int32)
    before = jnp.cumsum(onehot, axis=0, dtype=jnp.int32) - onehot
    ranks = jnp.sum(before * onehot, axis=1, dtype=jnp.int32)
    places = flat_ids * capacity + ranks
    filler = jnp.arange(flat_ids.shape[0], dtype=jnp.int32) + 1
    slot_rows = jnp.zeros((experts * capacity,), jnp.int32).at[places].set(filler)
    return (places.reshape(route_ids.shape), slot_rows.reshape(experts, capacity))


def inverse_rms(tensor):
    return lax.rsqrt(jnp.mean(tensor * tensor, axis=-1, keepdims=True) + epsilon)


def norm_backward(d_normed, hat_rows, inverse, gain_vec):
    d_hat = d_normed * gain_vec
    return inverse * (d_hat - hat_rows * jnp.mean(d_hat * hat_rows, axis=-1, keepdims=True))


def masked_scores(query, keys, allowed, score_scale):
    raw = jnp.einsum("qhd,khd->hqk", query, keys, preferred_element_type=jnp.float32) * score_scale
    return jnp.where(allowed[None], raw, -1e30)


def spread(rows):
    return lax.all_gather(rows, "tp", axis=0, tiled=True)


def head_total(partial_rows):
    return lax.psum_scatter(
        partial_rows.astype(jnp.bfloat16), "tp", scatter_dimension=0, tiled=True
    ).astype(jnp.float32)


def to_experts(buffer):
    return lax.all_to_all(buffer, "fsdp", split_axis=0, concat_axis=0, tiled=True)


def from_experts(buffer):
    return lax.all_to_all(buffer, "fsdp", split_axis=0, concat_axis=0, tiled=True)


def on_device(
    hidden_in,
    out_grad,
    segment_ids,
    expert_ids,
    route_weights,
    attn_gain,
    ffn_gain,
    qkv_weight,
    qkv_bias,
    out_weight,
    shared_gate_up,
    shared_down,
    shared_gate_vec,
    expert_gate_up,
    expert_down,
):
    tp_rank = lax.axis_index("tp")
    experts = lax.axis_size("fsdp")
    length = segment_ids.shape[1]
    top_count = expert_ids.shape[1]
    capacity = 3 * length * top_count // (2 * experts)
    own_rows = hidden_in.shape[0]
    model_width = hidden_in.shape[1]
    qkv_full, bias_full, out_full, shared_full, shared_down_full = (
        lax.all_gather(qkv_weight, "fsdp", axis=0, tiled=True),
        lax.all_gather(qkv_bias.astype(jnp.bfloat16), "fsdp", axis=2, tiled=True).astype(
            qkv_bias.dtype
        ),
        lax.all_gather(out_weight, "fsdp", axis=1, tiled=True),
        lax.all_gather(shared_gate_up, "fsdp", axis=0, tiled=True),
        lax.all_gather(shared_down, "fsdp", axis=1, tiled=True),
    )
    local_heads = qkv_full.shape[2]
    head_dim = qkv_full.shape[3]
    score_scale = head_dim ** (-0.5)
    cos_table, sin_table = rope_tables(length, head_dim)
    positions = jnp.arange(length, dtype=jnp.int32)
    segments = segment_ids[0]
    allowed = (positions[:, None] >= positions[None, :]) & (segments[:, None] == segments[None, :])
    hidden_float = hidden_in.astype(jnp.float32)
    attn_inverse = inverse_rms(hidden_float)
    normed_one = spread((hidden_float * attn_inverse * attn_gain).astype(jnp.bfloat16))
    qkv_flat = qkv_full.reshape(model_width, -1)
    qkv = (
        jnp.dot(normed_one, qkv_flat, preferred_element_type=jnp.float32).reshape(
            length, 3, local_heads, head_dim
        )
        + bias_full
    )
    query = rotate(qkv[:, 0], cos_table, sin_table).astype(jnp.bfloat16)
    keys = rotate(qkv[:, 1], cos_table, sin_table).astype(jnp.bfloat16)
    values = qkv[:, 2].astype(jnp.bfloat16)
    scores = masked_scores(query, keys, allowed, score_scale)
    row_peak = jnp.max(scores, axis=-1, keepdims=True)
    log_total = row_peak + jnp.log(jnp.sum(jnp.exp(scores - row_peak), axis=-1, keepdims=True))
    probs_b = jnp.exp(scores - log_total).astype(jnp.bfloat16)
    heads_out = (
        jnp.einsum("hqk,khd->qhd", probs_b, values, preferred_element_type=jnp.float32)
        .astype(jnp.bfloat16)
        .reshape(length, -1)
    )
    middle = hidden_float + head_total(
        jnp.dot(heads_out, out_full, preferred_element_type=jnp.float32)
    )
    ffn_inverse = inverse_rms(middle)
    normed_two_own = (middle * ffn_inverse * ffn_gain).astype(jnp.bfloat16)
    normed_two = spread(normed_two_own)
    gate_prob = jax.nn.sigmoid(jnp.sum(normed_two.astype(jnp.float32) * shared_gate_vec, axis=-1))
    shared_flat = shared_full.reshape(model_width, -1)
    shared_width = shared_full.shape[2]
    shared_pre = jnp.dot(normed_two, shared_flat, preferred_element_type=jnp.float32)
    shared_act, shared_slope = silu_parts(shared_pre[:, :shared_width])
    shared_upper = shared_pre[:, shared_width:]
    shared_hidden = (shared_act * shared_upper).astype(jnp.bfloat16)
    shared_part = jnp.dot(shared_hidden, shared_down_full, preferred_element_type=jnp.float32)
    places, slot_rows = slot_table(expert_ids, experts, capacity)
    filled = slot_rows > 0
    route_index = jnp.maximum(slot_rows - 1, 0)
    source_rows = route_index // top_count
    flat_weights = route_weights.reshape(-1)
    slot_weights = jnp.where(filled, flat_weights[route_index], 0.0)
    send_rows = jnp.where(filled[:, :, None], normed_two[source_rows], jnp.zeros((), jnp.bfloat16))
    arrived = to_experts(send_rows).reshape(-1, model_width)
    expert_flat = expert_gate_up[0].reshape(model_width, -1)
    expert_width = expert_gate_up.shape[3]
    down_local = expert_down[0]
    expert_pre = jnp.dot(arrived, expert_flat, preferred_element_type=jnp.float32)
    expert_act, expert_slope = silu_parts(expert_pre[:, :expert_width])
    expert_upper = expert_pre[:, expert_width:]
    expert_hidden = (expert_act * expert_upper).astype(jnp.bfloat16)
    expert_part = jnp.dot(expert_hidden, down_local, preferred_element_type=jnp.float32).astype(
        jnp.bfloat16
    )
    returned = from_experts(expert_part.reshape(experts, capacity, model_width)).reshape(
        experts * capacity, model_width
    )
    picked = returned[places].astype(jnp.float32)
    token_term = gate_prob[:, None] * shared_part + jnp.sum(
        route_weights[:, :, None] * picked, axis=1
    )
    own_extra = 0.0
    total = (
        lax.psum_scatter(
            token_term.astype(jnp.bfloat16), "tp", scatter_dimension=0, tiled=True
        ).astype(jnp.float32)
        + own_extra
    )
    hidden_out = (middle + total).astype(jnp.bfloat16)
    grad_rows = spread(out_grad)
    grad_float = grad_rows.astype(jnp.float32)
    gate_part = jnp.sum(grad_float * shared_part, axis=-1)
    scaled_grad = (gate_prob[:, None] * grad_float).astype(jnp.bfloat16)
    shared_d_hidden = jnp.dot(scaled_grad, shared_down_full.T, preferred_element_type=jnp.float32)
    shared_d_cat = jnp.concatenate(
        [
            (shared_d_hidden * shared_upper * shared_slope).astype(jnp.bfloat16),
            (shared_d_hidden * shared_act).astype(jnp.bfloat16),
        ],
        axis=1,
    )
    g_shared_down = jnp.dot(shared_hidden.T, scaled_grad, preferred_element_type=jnp.float32)
    g_shared_gate_up = jnp.dot(
        normed_two.T, shared_d_cat, preferred_element_type=jnp.float32
    ).reshape(shared_full.shape)
    d_normed_part = jnp.dot(shared_d_cat, shared_flat.T, preferred_element_type=jnp.float32)
    expert_grad_in = (slot_weights[:, :, None] * grad_float[source_rows]).astype(jnp.bfloat16)
    arrived_grad = to_experts(expert_grad_in).reshape(-1, model_width)
    back_act, back_slope, back_upper, back_hidden = (
        expert_act,
        expert_slope,
        expert_upper,
        expert_hidden,
    )
    expert_d_hidden = jnp.dot(arrived_grad, down_local.T, preferred_element_type=jnp.float32)
    expert_d_cat = jnp.concatenate(
        [
            (expert_d_hidden * back_upper * back_slope).astype(jnp.bfloat16),
            (expert_d_hidden * back_act).astype(jnp.bfloat16),
        ],
        axis=1,
    )
    g_expert_down = jnp.dot(back_hidden.T, arrived_grad, preferred_element_type=jnp.float32)[None]
    g_expert_gate_up = jnp.dot(arrived.T, expert_d_cat, preferred_element_type=jnp.float32).reshape(
        expert_gate_up.shape
    )
    expert_d_part = jnp.dot(expert_d_cat, expert_flat.T, preferred_element_type=jnp.float32).astype(
        jnp.bfloat16
    )
    route_part = jnp.sum(grad_float[:, None, :] * picked, axis=-1)
    returned_grad = from_experts(expert_d_part.reshape(experts, capacity, model_width)).reshape(
        experts * capacity, model_width
    )
    d_normed_part = d_normed_part + jnp.sum(returned_grad[places].astype(jnp.float32), axis=1)
    d_normed_two, route_grad, gate_grad = (
        lax.psum_scatter(
            d_normed_part.astype(jnp.bfloat16), "tp", scatter_dimension=0, tiled=True
        ).astype(jnp.float32),
        lax.psum_scatter(
            route_part.astype(jnp.bfloat16), "tp", scatter_dimension=0, tiled=True
        ).astype(jnp.float32),
        lax.psum_scatter(
            gate_part.astype(jnp.bfloat16), "tp", scatter_dimension=0, tiled=True
        ).astype(jnp.float32),
    )
    own_gate = lax.dynamic_slice_in_dim(gate_prob, tp_rank * own_rows, own_rows)
    logit_grad = gate_grad * own_gate * (1.0 - own_gate)
    d_normed_two = d_normed_two + logit_grad[:, None] * shared_gate_vec
    g_gate_vec = jnp.sum(normed_two_own.astype(jnp.float32) * logit_grad[:, None], axis=0)
    hat_two = middle * ffn_inverse
    g_ffn_gain = jnp.sum(d_normed_two * hat_two, axis=0)
    middle_grad = out_grad.astype(jnp.float32) + norm_backward(
        d_normed_two, hat_two, ffn_inverse, ffn_gain
    )
    d_rows = spread(middle_grad.astype(jnp.bfloat16))
    g_out = jnp.dot(heads_out.T, d_rows, preferred_element_type=jnp.float32)
    d_heads = (
        jnp.dot(d_rows, out_full.T, preferred_element_type=jnp.float32)
        .astype(jnp.bfloat16)
        .reshape(length, local_heads, head_dim)
    )
    heads_three = heads_out.reshape(length, local_heads, head_dim)
    scores_again = masked_scores(query, keys, allowed, score_scale)
    probs_full = jnp.exp(scores_again - log_total)
    probs_again = probs_full.astype(jnp.bfloat16)
    d_values = jnp.einsum("hqk,qhd->khd", probs_again, d_heads, preferred_element_type=jnp.float32)
    d_probs = jnp.einsum("qhd,khd->hqk", d_heads, values, preferred_element_type=jnp.float32)
    delta = jnp.sum(d_heads.astype(jnp.float32) * heads_three.astype(jnp.float32), axis=-1)
    d_scores = (probs_full * (d_probs - delta.T[:, :, None])).astype(jnp.bfloat16)
    d_query = (
        jnp.einsum("hqk,khd->qhd", d_scores, keys, preferred_element_type=jnp.float32) * score_scale
    )
    d_keys = (
        jnp.einsum("hqk,qhd->khd", d_scores, query, preferred_element_type=jnp.float32)
        * score_scale
    )
    d_qkv = jnp.stack(
        [unrotate(d_query, cos_table, sin_table), unrotate(d_keys, cos_table, sin_table), d_values],
        axis=1,
    )
    g_bias = jnp.sum(d_qkv, axis=0)
    d_qkv_b = d_qkv.astype(jnp.bfloat16).reshape(length, -1)
    g_qkv = jnp.dot(normed_one.T, d_qkv_b, preferred_element_type=jnp.float32).reshape(
        qkv_full.shape
    )
    d_normed_one = head_total(jnp.dot(d_qkv_b, qkv_flat.T, preferred_element_type=jnp.float32))
    hat_one = hidden_float * attn_inverse
    g_attn_gain = jnp.sum(d_normed_one * hat_one, axis=0)
    hidden_grad = middle_grad + norm_backward(d_normed_one, hat_one, attn_inverse, attn_gain)
    g_qkv, g_bias, g_out, g_shared_gate_up, g_shared_down = (
        lax.psum_scatter(
            g_qkv.astype(jnp.bfloat16), "fsdp", scatter_dimension=0, tiled=True
        ).astype(jnp.float32),
        lax.psum_scatter(
            g_bias.astype(jnp.bfloat16), "fsdp", scatter_dimension=2, tiled=True
        ).astype(jnp.float32),
        lax.psum_scatter(
            g_out.astype(jnp.bfloat16), "fsdp", scatter_dimension=1, tiled=True
        ).astype(jnp.float32),
        lax.psum_scatter(
            g_shared_gate_up.astype(jnp.bfloat16), "fsdp", scatter_dimension=0, tiled=True
        ).astype(jnp.float32),
        lax.psum_scatter(
            g_shared_down.astype(jnp.bfloat16), "fsdp", scatter_dimension=1, tiled=True
        ).astype(jnp.float32),
    )
    g_attn_gain, g_ffn_gain, g_gate_vec = (
        lax.psum_scatter(g_attn_gain, ("fsdp", "tp"), scatter_dimension=0, tiled=True),
        lax.psum_scatter(g_ffn_gain, ("fsdp", "tp"), scatter_dimension=0, tiled=True),
        lax.psum_scatter(g_gate_vec, ("fsdp", "tp"), scatter_dimension=0, tiled=True),
    )
    return (
        hidden_out,
        hidden_grad,
        route_grad,
        g_attn_gain,
        g_ffn_gain,
        g_qkv,
        g_bias,
        g_out,
        g_shared_gate_up,
        g_shared_down,
        g_gate_vec,
        g_expert_gate_up,
        g_expert_down,
    )


def solution(mesh):
    placed = (
        P(("fsdp", "tp"), None),
        P(("fsdp", "tp"), None),
        P("fsdp", None),
        P("fsdp", None),
        P("fsdp", None),
        P(),
        P(),
        P("fsdp", None, "tp", None),
        P(None, "tp", "fsdp"),
        P("tp", "fsdp"),
        P("fsdp", None, "tp"),
        P("tp", "fsdp"),
        P(),
        P("fsdp", None, None, "tp"),
        P("fsdp", "tp", None),
    )
    return jax.shard_map(
        on_device,
        mesh=mesh,
        in_specs=placed,
        out_specs=(
            P(("fsdp", "tp"), None),
            P(("fsdp", "tp"), None),
            P(("fsdp", "tp"), None),
            P(("fsdp", "tp")),
            P(("fsdp", "tp")),
            P("fsdp", None, "tp", None),
            P(None, "tp", "fsdp"),
            P("tp", "fsdp"),
            P("fsdp", None, "tp"),
            P("tp", "fsdp"),
            P(("fsdp", "tp")),
            P("fsdp", None, None, "tp"),
            P("fsdp", "tp", None),
        ),
        check_vma=False,
    )
```

profile of v0, /device:TPU:0, one launch (start us, length us, event | category | flops | bytes accessed | tf_op | source)
XLA Modules:
  0.0 1558.0 jit_solution(18236763787623258444)
XLA Ops:
  25.5 33.3 %all-gather.11.cloned.1.call-done = bf16[2048,3,4,128]{3,0,2,1:T(8,128)(2,1)} async-done(((bf16[256,3,4,128]{3,0,2,1:T(8,128)(2,1)}), bf16[2048,3,4,128]{3,0,2,1:T(8,128)(2,1)}) %all-gather.11.cloned.1.call-update) | async-done | bytes 6291472 | tf_op jit(solution)/shard_map/all_gather | solution.py:116
  67.4 39.5 %all-gather.9.cloned.1.call-done = bf16[512,2048]{1,0:T(8,128)(2,1)} async-done(((bf16[128,2048]{1,0:T(8,128)(2,1)}), bf16[512,2048]{1,0:T(8,128)(2,1)}) %all-gather.9.cloned.1.call-update) | async-done | bytes 2097168 | tf_op jit(solution)/shard_map/all_gather | solution.py:74
  140.2 44.0 %reduce-scatter.14.cloned.1.call-done = bf16[128,2048]{1,0:T(8,128)(2,1)} async-done(((bf16[512,2048]{1,0:T(8,128)(2,1)}), bf16[128,2048]{1,0:T(8,128)(2,1)}) %reduce-scatter.14.cloned.1.call-update) | async-done | bytes 524304 | tf_op jit(solution)/shard_map/reduce_scatter | solution.py:78
  202.8 30.8 %all-gather.15.cloned.1.call-done = bf16[512,2048]{1,0:T(8,128)(2,1)} async-done(((bf16[128,2048]{1,0:T(8,128)(2,1)}), bf16[512,2048]{1,0:T(8,128)(2,1)}) %all-gather.15.cloned.1.call-update) | async-done | bytes 2097168 | tf_op jit(solution)/shard_map/all_gather | solution.py:74
  233.5 25.7 %gather_fusion = bf16[3072,2048]{1,0:T(8,128)(2,1)} fusion(bf16[512,2048]{1,0:T(8,128)(2,1)} %all-gather.15.cloned.1.call-done, s32[3072]{0:T(1024)S(1)} %broadcast_clamp_fusion), kind=kCustom, calls=%fused_computation | custom fusion | bytes 25178112 | tf_op jit(solution)/shard_map/gather | solution.py:173
  276.3 17.4 %gather_fusion.2 = f32[3072]{0:T(1024)S(1)} fusion(f32[2048]{0:T(1024)S(1)} %reshape.327, s32[3072]{0:T(1024)S(1)} %get-tuple-element.101), kind=kCustom, calls=%fused_computation.2 | custom fusion | bytes 36864 | tf_op jit(solution)/shard_map/gather | solution.py:172
  293.7 28.9 %all-gather.21.cloned.1.call-done = bf16[512,2048]{1,0:T(8,128)(2,1)} async-done(((bf16[128,2048]{1,0:T(8,128)(2,1)}), bf16[512,2048]{1,0:T(8,128)(2,1)}) %all-gather.21.cloned.1.call-update) | async-done | bytes 2097168 | tf_op jit(solution)/shard_map/all_gather | solution.py:74
  326.7 26.4 %gather_fusion.3 = f32[3072,2048]{1,0:T(8,128)} fusion(f32[512,2048]{1,0:T(8,128)} %convert_element_type.202, s32[3072]{0:T(1024)S(1)} %broadcast_clamp_fusion), kind=kCustom, calls=%fused_computation.3 | custom fusion | bytes 50343936 | tf_op jit(solution)/shard_map/gather | solution.py:217
  366.4 48.0 %all-to-all-done = bf16[8,384,2048]{2,1,0:T(8,128)(2,1)} async-done(((bf16[8,384,2048]{2,1,0:T(8,128)(2,1)}), bf16[8,384,2048]{2,1,0:T(8,128)(2,1)}, u32[]{:S(2)}, u32[]{:S(2)}) %all-to-all-start) | async-done | bytes 12582944 | tf_op jit(solution)/shard_map/all_to_all | solution.py:84
  434.6 170.4 %all-to-all-done.2 = bf16[8,384,2048]{2,1,0:T(8,128)(2,1)} async-done(((bf16[8,384,2048]{2,1,0:T(8,128)(2,1)}), bf16[8,384,2048]{2,1,0:T(8,128)(2,1)}, u32[]{:S(2)}, u32[]{:S(2)}) %all-to-all-start.2) | async-done | bytes 12582944 | tf_op jit(solution)/shard_map/all_to_all | solution.py:84
  658.0 139.6 %all-to-all-done.3 = bf16[8,384,2048]{2,1,0:T(8,128)(2,1)} async-done(((bf16[8,384,2048]{2,1,0:T(8,128)(2,1)}), bf16[8,384,2048]{2,1,0:T(8,128)(2,1)}, u32[]{:S(2)}, u32[]{:S(2)}) %all-to-all-start.3) | async-done | bytes 12582944 | tf_op jit(solution)/shard_map/all_to_all | solution.py:88
  835.0 22.6 %gather_fusion.4 = bf16[2048,2048]{1,0:T(8,128)(2,1)} fusion(bf16[3072,2048]{1,0:T(8,128)(2,1)} %bitcast.23, s32[2048]{0:T(1024)S(1)} %broadcast_clamp_fusion.1), kind=kCustom, calls=%fused_computation.4 | custom fusion | bytes 16785408 | tf_op jit(solution)/shard_map/gather | solution.py:244
  901.2 40.8 %all-to-all-done.1 = bf16[8,384,2048]{2,1,0:T(8,128)(2,1)} async-done(((bf16[8,384,2048]{2,1,0:T(8,128)(2,1)}), bf16[8,384,2048]{2,1,0:T(8,128)(2,1)}, u32[]{:S(2)}, u32[]{:S(2)}) %all-to-all-start.1) | async-done | bytes 12582944 | tf_op jit(solution)/shard_map/all_to_all | solution.py:88
  942.1 22.6 %gather_fusion.1 = bf16[2048,2048]{1,0:T(8,128)(2,1)} fusion(bf16[3072,2048]{1,0:T(8,128)(2,1)} %bitcast.19, s32[2048]{0:T(1024)S(1)} %broadcast_clamp_fusion.1), kind=kCustom, calls=%fused_computation.1 | custom fusion | bytes 16785408 | tf_op jit(solution)/shard_map/gather | solution.py:188
  964.7 15.5 reshape.393
  980.2 19.3 %multiply_reduce_fusion = (bf16[512,4]{1,0:T(8,128)(2,1)}, f32[512,2048]{1,0:T(8,128)S(1)}) fusion(f32[512,4,2048]{2,1,0:T(4,128)} %reshape.393, f32[512,2048]{1,0:T(8,128)} %convert_element_type.202, f32[512,4]{1,0:T(8,128)S(1)} %copy-done.10), kind=kLoop, calls=%fused_computation.7 | loop fusion | flops 15726592 | bytes 25178112 | tf_op jit(solution)/shard_map/reduce_sum | solution.py:240
  1033.3 22.5 %convert_element_type.233 = bf16[2048,2,1408]{2,1,0:T(2,128)(2,1)} reshape(bf16[2048,2816]{1,0:T(8,128)(2,1)} %convolution_convert_fusion) | data formatting | bytes 23068672 | tf_op jit(solution)/shard_map/convert_element_type | solution.py:311
  1099.0 129.2 %all-reduce.8.cloned.1.call-done = bf16[2048,2,1408]{2,1,0:T(2,128)(2,1)} async-done(((bf16[2048,2,1408]{2,1,0:T(2,128)(2,1)}), bf16[2048,2,1408]{2,1,0:T(2,128)(2,1)}) %all-reduce.8.cloned.1.call-update) | async-done | bytes 11534352
  1232.2 59.5 %reduce-scatter.26.cloned.1.call-done = bf16[1408,256]{1,0:T(8,128)(2,1)} async-done(((bf16[1408,2048]{1,0:T(8,128)(2,1)}), bf16[1408,256]{1,0:T(8,128)(2,1)}) %reduce-scatter.26.cloned.1.call-update) | async-done | bytes 720912 | tf_op jit(solution)/shard_map/reduce_scatter | solution.py:313
  1320.7 25.6 %reduce-scatter.30.cloned.1.call-done = bf16[16,12]{1,0:T(8,128)(2,1)} async-done(((bf16[128,12]{1,0:T(8,128)(2,1)}), bf16[16,12]{1,0:T(8,128)(2,1)}) %reduce-scatter.30.cloned.1.call-update) | async-done | bytes 400
  1347.8 42.9 %reduce-scatter.24.cloned.1.call-done = bf16[512,256]{1,0:T(8,128)(2,1)} async-done(((bf16[512,2048]{1,0:T(8,128)(2,1)}), bf16[512,256]{1,0:T(8,128)(2,1)}) %reduce-scatter.24.cloned.1.call-update) | async-done | bytes 262160 | tf_op jit(solution)/shard_map/reduce_scatter | solution.py:307
  1392.7 44.2 %reduce-scatter.20.cloned.1.call-done = bf16[128,2048]{1,0:T(8,128)(2,1)} async-done(((bf16[512,2048]{1,0:T(8,128)(2,1)}), bf16[128,2048]{1,0:T(8,128)(2,1)}) %reduce-scatter.20.cloned.1.call-update) | async-done | bytes 524304 | tf_op jit(solution)/shard_map/reduce_scatter | solution.py:78
  1438.4 42.5 %all-reduce.5 = (f32[2048]{0:T(1024)S(1)}, f32[2048]{0:T(1024)S(1)}, f32[2048]{0:T(1024)S(1)}) all-reduce(f32[2048]{0:T(1024)S(1)} %get-tuple-element.69, f32[2048]{0:T(1024)S(1)} %get-tuple-element.67, f32[2048]{0:T(1024)S(1)} %get-tuple-element.71), channel_id=8, replica_groups=mesh['fsdp'=8,'tp'=4] {'fsdp','tp'}, use_global_device_ids=true, to_apply=%region_23.24.clone | all-reduce | flops 6144 | bytes 49152
  1487.0 60.9 %reduce-scatter.22.cloned.1.call-done = bf16[256,3,4,128]{3,0,2,1:T(8,128)(2,1)} async-done(((bf16[2048,3,4,128]{3,0,2,1:T(8,128)(2,1)}), bf16[256,3,4,128]{3,0,2,1:T(8,128)(2,1)}) %reduce-scatter.22.cloned.1.call-update) | async-done | bytes 786448 | tf_op jit(solution)/shard_map/reduce_scatter | solution.py:301
  (260 shorter events, 388.9 us)
Async XLA Ops:
  7.2 413.3 %copy-start = (bf16[1,2048,2,352]{1,3,2,0:T(8,128)(2,1)S(1)}, bf16[1,2048,2,352]{1,3,2,0:T(8,128)(2,1)}, u32[]{:S(2)}) copy-start(bf16[1,2048,2,352]{1,3,2,0:T(8,128)(2,1)} %param.28) | copy-start | bytes 8650756
  7.2 51.6 %all-gather.11.cloned.1.call-start = ((), (), s32[]{:S(2)}) async-start(), calls=%async_computation.14 | async-start | bytes 7077888 | tf_op jit(solution)/shard_map/all_gather | solution.py:116
  9.6 97.3 %all-gather.9.cloned.1.call-start = ((), (), s32[]{:S(2)}) async-start(), calls=%async_computation.13 | async-start | bytes 2621440 | tf_op jit(solution)/shard_map/all_gather | solution.py:74
  12.9 122.8 %all-gather.13.cloned.1.call-start = ((), (), s32[]{:S(2)}) async-start(), calls=%async_computation.15 | async-start | bytes 2359296 | tf_op jit(solution)/shard_map/all_gather | solution.py:120
  13.7 170.5 %reduce-scatter.14.cloned.1.call-start = ((), (), s32[]{:S(2)}) async-start(), calls=%async_computation.16 | async-start | bytes 2621440 | tf_op jit(solution)/shard_map/reduce_scatter | solution.py:78
  140.1 93.4 %all-gather.15.cloned.1.call-start = ((), (), s32[]{:S(2)}) async-start(), calls=%async_computation.17 | async-start | bytes 2621440 | tf_op jit(solution)/shard_map/all_gather | solution.py:74
  269.8 144.5 %all-to-all-start = ((bf16[8,384,2048]{2,1,0:T(8,128)(2,1)}), bf16[8,384,2048]{2,1,0:T(8,128)(2,1)}, u32[]{:S(2)}, u32[]{:S(2)}) async-start(bf16[8,384,2048]{2,1,0:T(8,128)(2,1)} %broadcast_select_fusion), calls=%async_computation.1 | async-start | bytes 25165824 | tf_op jit(solution)/shard_map/all_to_all | solution.py:84
  275.3 47.3 %all-gather.21.cloned.1.call-start = ((), (), s32[]{:S(2)}) async-start(), calls=%async_computation.21 | async-start | bytes 2621440 | tf_op jit(solution)/shard_map/all_gather | solution.py:74
  414.4 190.7 %all-to-all-start.2 = ((bf16[8,384,2048]{2,1,0:T(8,128)(2,1)}), bf16[8,384,2048]{2,1,0:T(8,128)(2,1)}, u32[]{:S(2)}, u32[]{:S(2)}) async-start(bf16[8,384,2048]{2,1,0:T(8,128)(2,1)} %multiply_convert_fusion), calls=%async_computation.4 | async-start | bytes 25165824 | tf_op jit(solution)/shard_map/all_to_all | solution.py:84
  419.7 384.1 %all-gather.17.cloned.1.call-start = ((), (), s32[]{:S(2)}) async-start(), calls=%async_computation.18 | async-start | bytes 12976128 | tf_op jit(solution)/shard_map/all_gather | solution.py:121
  629.9 167.7 %all-to-all-start.3 = ((bf16[8,384,2048]{2,1,0:T(8,128)(2,1)}), bf16[8,384,2048]{2,1,0:T(8,128)(2,1)}, u32[]{:S(2)}, u32[]{:S(2)}) async-start(bf16[8,384,2048]{2,1,0:T(8,128)(2,1)} %bitcast.146), calls=%async_computation.5 | async-start | bytes 25165824 | tf_op jit(solution)/shard_map/all_to_all | solution.py:88
  635.4 188.3 %all-gather.19.cloned.1.call-start = ((), (), s32[]{:S(2)}) async-start(), calls=%async_computation.19 | async-start | bytes 6488064 | tf_op jit(solution)/shard_map/all_gather | solution.py:122
  797.6 144.5 %all-to-all-start.1 = ((bf16[8,384,2048]{2,1,0:T(8,128)(2,1)}), bf16[8,384,2048]{2,1,0:T(8,128)(2,1)}, u32[]{:S(2)}, u32[]{:S(2)}) async-start(bf16[8,384,2048]{2,1,0:T(8,128)(2,1)} %bitcast.145), calls=%async_computation.2 | async-start | bytes 25165824 | tf_op jit(solution)/shard_map/all_to_all | solution.py:88
  803.1 214.9 %reduce-scatter.18.cloned.1.call-start = ((), (), s32[]{:S(2)}) async-start(), calls=%async_computation.22 | async-start | bytes 2621440 | tf_op jit(solution)/shard_map/reduce_scatter | solution.py:246
  899.9 165.2 %all-gather.23.cloned.1.call-start = ((), (), s32[]{:S(2)}) async-start(), calls=%async_computation.23 | async-start | bytes 2621440 | tf_op jit(solution)/shard_map/all_gather | solution.py:74
  1022.4 205.8 %all-reduce.8.cloned.1.call-start = ((), (), s32[]{:S(2)}) async-start(), calls=%async_computation.30 | async-start | bytes 23068672
  1055.9 235.8 %reduce-scatter.26.cloned.1.call-start = ((), (), s32[]{:S(2)}) async-start(), calls=%async_computation.27 | async-start | bytes 6488064 | tf_op jit(solution)/shard_map/reduce_scatter | solution.py:313
  1064.0 255.3 %reduce-scatter.28.cloned.1.call-start = ((), (), s32[]{:S(2)}) async-start(), calls=%async_computation.28 | async-start | bytes 163840
  1064.8 281.5 %reduce-scatter.30.cloned.1.call-start = ((), (), s32[]{:S(2)}) async-start(), calls=%async_computation.29 | async-start | bytes 36864
  1076.5 314.3 %reduce-scatter.24.cloned.1.call-start = ((), (), s32[]{:S(2)}) async-start(), calls=%async_computation.26 | async-start | bytes 2359296 | tf_op jit(solution)/shard_map/reduce_scatter | solution.py:307
  1081.1 355.8 %reduce-scatter.20.cloned.1.call-start = ((), (), s32[]{:S(2)}) async-start(), calls=%async_computation.24 | async-start | bytes 2621440 | tf_op jit(solution)/shard_map/reduce_scatter | solution.py:78
  1089.2 394.1 %reduce-scatter.16.cloned.1.call-start = ((), (), s32[]{:S(2)}) async-start(), calls=%async_computation.20 | async-start | bytes 2621440 | tf_op jit(solution)/shard_map/reduce_scatter | solution.py:194
  1089.8 458.1 %reduce-scatter.22.cloned.1.call-start = ((), (), s32[]{:S(2)}) async-start(), calls=%async_computation.25 | async-start | bytes 7077888 | tf_op jit(solution)/shard_map/reduce_scatter | solution.py:301
  1097.1 196.9 %copy-start.12 = (bf16[3072,352]{0,1:T(8,128)(2,1)S(1)}, bf16[3072,352]{0,1:T(8,128)(2,1)}, u32[]{:S(2)}) copy-start(bf16[3072,352]{0,1:T(8,128)(2,1)} %copy-done.11) | copy-start | bytes 6488068
  (50 other events, 1119.4 us)
Sparse Core Ops, SparseCore 0:
  10.5 48.2 all-gather.10
  60.9 45.9 all-gather.8
  108.8 26.8 all-gather.12
  140.3 43.8 reduce-scatter.13
  188.2 45.3 all-gather.14
  277.5 45.0 all-gather.20
  422.6 148.1 all-gather.16
  646.7 101.8 all-gather.18
  900.1 42.9 reduce-scatter.17
  1022.5 42.6 all-gather.22
  1068.7 159.5 all-reduce.7
  1232.5 59.1 reduce-scatter.25
  1293.9 19.1 reduce-scatter.27
  1316.8 29.4 reduce-scatter.29
  1349.5 41.2 reduce-scatter.23
  1393.0 43.8 reduce-scatter.19
  1439.0 44.2 reduce-scatter.15
  1486.9 60.9 reduce-scatter.21
where the time goes:
time: 1570 us; the launch traced here: 1560 us
  waiting for transfers between devices  957 us (61%)
  local copies, waits for them, and re-layouts  217 us (14%)
  matrix products  172 us (11%)
  other arithmetic  97.9 us (6%)
  blocking collectives  62.7 us (4%)
  starting transfers between devices  33.9 us (2%)
  between operations  16.9 us (1%)
    all_to_all x2, waiting for transfers between devices, to_experts(): lax.all_to_all(buffer, 'fsdp', split_axis=0, concat_axis=0, tiled=True)  218 us
    all_to_all x2, waiting for transfers between devices, from_experts(): lax.all_to_all(buffer, 'fsdp', split_axis=0, concat_axis=0, tiled=True)  180 us
    unnamed x21, waiting for transfers between devices  158 us
    all_gather x4, waiting for transfers between devices, spread(): return lax.all_gather(rows, 'tp', axis=0, tiled=True)  99.5 us
    reduce_scatter x2, waiting for transfers between devices, head_total(): lax.psum_scatter(partial_rows.astype(jnp.bfloat16), 'tp', scatter_dimensi...  88.2 us
    reduce_scatter x1, waiting for transfers between devices, on_device(): lax.psum_scatter(g_qkv.astype(jnp.bfloat16), 'fsdp', scatter_dimension=0,...  60.9 us
    reduce_scatter x1, waiting for transfers between devices, on_device(): lax.psum_scatter(g_shared_down.astype(jnp.bfloat16), 'fsdp', scatter_dime...  59.5 us
    unnamed x2, blocking collectives  52 us
  transfers between devices with their start and end apart: 22, of which 18 were waited for; matrix products, arithmetic and copies ran while one was open for 27% of the time, Pallas kernels for 0%

commit v1 on v0

--- a/solution.py
+++ b/solution.py
@@ -88,7 +88,7 @@
     return lax.all_to_all(buffer, "fsdp", split_axis=0, concat_axis=0, tiled=True)
 
 
-def on_device(
+def routed_plan(
     hidden_in,
     out_grad,
     segment_ids,
@@ -336,6 +336,221 @@
     )
 
 
+def dense_plan(
+    hidden_in,
+    out_grad,
+    segment_ids,
+    expert_ids,
+    route_weights,
+    attn_gain,
+    ffn_gain,
+    qkv_weight,
+    qkv_bias,
+    out_weight,
+    shared_gate_up,
+    shared_down,
+    shared_gate_vec,
+    expert_gate_up,
+    expert_down,
+):
+    every = ("fsdp", "tp")
+    tp_rank = lax.axis_index("tp")
+    experts = lax.axis_size("fsdp")
+    packs = experts
+    length = segment_ids.shape[1]
+    own_rows = hidden_in.shape[0]
+    model_width = hidden_in.shape[1]
+    bf16 = jnp.bfloat16
+    f32 = jnp.float32
+
+    grad_all = lax.all_gather(out_grad, every, axis=0, tiled=True)
+    qkv_full = lax.all_gather(qkv_weight, "fsdp", axis=0, tiled=True)
+    bias_full = lax.all_gather(qkv_bias.astype(bf16), "fsdp", axis=2, tiled=True).astype(f32)
+    out_full = lax.all_gather(out_weight, "fsdp", axis=1, tiled=True)
+    shared_up = lax.all_to_all(shared_gate_up, "fsdp", split_axis=2, concat_axis=0, tiled=True)
+    shared_dn = lax.all_to_all(shared_down, "fsdp", split_axis=0, concat_axis=1, tiled=True)
+    expert_up = expert_gate_up[0]
+    expert_dn = expert_down[0]
+    expert_width = expert_up.shape[2]
+    shared_width = shared_up.shape[2]
+
+    chosen = expert_ids[:, :, None] == jnp.arange(experts, dtype=jnp.int32)
+    table = jnp.sum(jnp.where(chosen, route_weights[:, :, None], 0.0), axis=1)
+    expert_scale = lax.all_to_all(table.T, "fsdp", split_axis=0, concat_axis=0, tiled=True)
+    expert_scale = expert_scale.reshape(-1)
+
+    local_heads = qkv_full.shape[2]
+    head_dim = qkv_full.shape[3]
+    score_scale = head_dim ** (-0.5)
+    cos_table, sin_table = rope_tables(length, head_dim)
+    positions = jnp.arange(length, dtype=jnp.int32)
+    segments = segment_ids[0]
+    allowed = (positions[:, None] >= positions[None, :]) & (segments[:, None] == segments[None, :])
+    hidden_float = hidden_in.astype(f32)
+    attn_inverse = inverse_rms(hidden_float)
+    normed_one = spread((hidden_float * attn_inverse * attn_gain).astype(bf16))
+    qkv_flat = qkv_full.reshape(model_width, -1)
+    qkv = (
+        jnp.dot(normed_one, qkv_flat, preferred_element_type=f32).reshape(
+            length, 3, local_heads, head_dim
+        )
+        + bias_full
+    )
+    query = rotate(qkv[:, 0], cos_table, sin_table).astype(bf16)
+    keys = rotate(qkv[:, 1], cos_table, sin_table).astype(bf16)
+    values = qkv[:, 2].astype(bf16)
+    scores = masked_scores(query, keys, allowed, score_scale)
+    row_peak = jnp.max(scores, axis=-1, keepdims=True)
+    log_total = row_peak + jnp.log(jnp.sum(jnp.exp(scores - row_peak), axis=-1, keepdims=True))
+    probs_b = jnp.exp(scores - log_total).astype(bf16)
+    heads_out = (
+        jnp.einsum("hqk,khd->qhd", probs_b, values, preferred_element_type=f32)
+        .astype(bf16)
+        .reshape(length, -1)
+    )
+    middle = hidden_float + head_total(jnp.dot(heads_out, out_full, preferred_element_type=f32))
+    ffn_inverse = inverse_rms(middle)
+    normed_two_own = (middle * ffn_inverse * ffn_gain).astype(bf16)
+    normed_all = lax.all_gather(normed_two_own, every, axis=0, tiled=True)
+
+    gate_w = jnp.concatenate([expert_up[:, 0], shared_up[:, 0]], axis=1)
+    upper_w = jnp.concatenate([expert_up[:, 1], shared_up[:, 1]], axis=1)
+    both_w = jnp.concatenate([gate_w, upper_w], axis=1)
+    down_w = jnp.concatenate([expert_dn, shared_dn], axis=0)
+    units = expert_width + shared_width
+    gate_logit = jnp.sum(normed_all.astype(f32) * shared_gate_vec, axis=-1)
+    gate_prob = jax.nn.sigmoid(gate_logit)
+    scale = jnp.concatenate(
+        [
+            jnp.broadcast_to(expert_scale[:, None], (expert_scale.shape[0], expert_width)),
+            jnp.broadcast_to(gate_prob[:, None], (expert_scale.shape[0], shared_width)),
+        ],
+        axis=1,
+    )
+    pre = jnp.dot(normed_all, both_w, preferred_element_type=f32)
+    act, slope = silu_parts(pre[:, :units])
+    upper = pre[:, units:]
+    hidden = act * upper
+    d_hidden = jnp.dot(grad_all, down_w.T, preferred_element_type=f32)
+    agree = d_hidden * hidden
+    route_part = jnp.sum(agree[:, :expert_width], axis=1)
+    gate_part = jnp.sum(agree[:, expert_width:], axis=1)
+    hidden_s = (hidden * scale).astype(bf16)
+    d_scaled = d_hidden * scale
+    d_both = jnp.concatenate(
+        [(d_scaled * upper * slope).astype(bf16), (d_scaled * act).astype(bf16)], axis=1
+    )
+    d_normed_part = jnp.dot(d_both, both_w.T, preferred_element_type=f32).astype(bf16)
+    lane = jnp.arange(128, dtype=jnp.int32)
+    own_expert = lax.axis_index("fsdp")
+    extra = jnp.where(lane == own_expert, route_part[:, None], 0.0) + jnp.where(
+        lane == experts, gate_part[:, None], 0.0
+    )
+    d_sum = lax.psum_scatter(
+        jnp.concatenate([d_normed_part, extra.astype(bf16)], axis=1),
+        every,
+        scatter_dimension=0,
+        tiled=True,
+    ).astype(f32)
+    d_normed_two = d_sum[:, :model_width]
+    token_part = jnp.dot(hidden_s, down_w, preferred_element_type=f32).astype(bf16)
+    total = lax.psum_scatter(token_part, every, scatter_dimension=0, tiled=True).astype(f32)
+    hidden_out = (middle + total).astype(bf16)
+    own_start = tp_rank * own_rows
+    ids_own = lax.dynamic_slice_in_dim(expert_ids, own_start, own_rows)
+    picked = ids_own[:, :, None] == jnp.arange(experts, dtype=jnp.int32)
+    route_grad = jnp.sum(
+        jnp.where(picked, d_sum[:, None, model_width : model_width + experts], 0.0), axis=-1
+    )
+    gate_grad = d_sum[:, model_width + experts]
+    g_down = jnp.dot(hidden_s.T, grad_all, preferred_element_type=f32)
+    g_both = jnp.dot(normed_all.T, d_both, preferred_element_type=f32)
+    g_expert_down = g_down[:expert_width][None]
+    g_expert_gate_up = jnp.stack(
+        [g_both[:, :expert_width], g_both[:, units : units + expert_width]], axis=1
+    )[None]
+    g_shared_gate_up = lax.all_to_all(
+        jnp.stack([g_both[:, expert_width:units], g_both[:, units + expert_width :]], axis=1).astype(
+            bf16
+        ),
+        "fsdp",
+        split_axis=0,
+        concat_axis=2,
+        tiled=True,
+    ).astype(f32)
+    g_shared_down = lax.all_to_all(
+        g_down[expert_width:].astype(bf16), "fsdp", split_axis=1, concat_axis=0, tiled=True
+    ).astype(f32)
+
+    own_gate = jax.nn.sigmoid(jnp.sum(normed_two_own.astype(f32) * shared_gate_vec, axis=-1))
+    logit_grad = gate_grad * own_gate * (1.0 - own_gate)
+    d_normed_two = d_normed_two + logit_grad[:, None] * shared_gate_vec
+    g_gate_vec = jnp.sum(normed_two_own.astype(f32) * logit_grad[:, None], axis=0)
+    hat_two = middle * ffn_inverse
+    g_ffn_gain = jnp.sum(d_normed_two * hat_two, axis=0)
+    middle_grad = out_grad.astype(f32) + norm_backward(d_normed_two, hat_two, ffn_inverse, ffn_gain)
+    d_rows = spread(middle_grad.astype(bf16))
+    g_out = jnp.dot(heads_out.T, d_rows, preferred_element_type=f32)
+    d_heads = (
+        jnp.dot(d_rows, out_full.T, preferred_element_type=f32)
+        .astype(bf16)
+        .reshape(length, local_heads, head_dim)
+    )
+    heads_three = heads_out.reshape(length, local_heads, head_dim)
+    scores_again = masked_scores(query, keys, allowed, score_scale)
+    probs_full = jnp.exp(scores_again - log_total)
+    probs_again = probs_full.astype(bf16)
+    d_values = jnp.einsum("hqk,qhd->khd", probs_again, d_heads, preferred_element_type=f32)
+    d_probs = jnp.einsum("qhd,khd->hqk", d_heads, values, preferred_element_type=f32)
+    delta = jnp.sum(d_heads.astype(f32) * heads_three.astype(f32), axis=-1)
+    d_scores = (probs_full * (d_probs - delta.T[:, :, None])).astype(bf16)
+    d_query = jnp.einsum("hqk,khd->qhd", d_scores, keys, preferred_element_type=f32) * score_scale
+    d_keys = jnp.einsum("hqk,qhd->khd", d_scores, query, preferred_element_type=f32) * score_scale
+    d_qkv = jnp.stack(
+        [unrotate(d_query, cos_table, sin_table), unrotate(d_keys, cos_table, sin_table), d_values],
+        axis=1,
+    )
+    g_bias = jnp.sum(d_qkv, axis=0)
+    d_qkv_b = d_qkv.astype(bf16).reshape(length, -1)
+    g_qkv = jnp.dot(normed_one.T, d_qkv_b, preferred_element_type=f32).reshape(qkv_full.shape)
+    d_normed_one = head_total(jnp.dot(d_qkv_b, qkv_flat.T, preferred_element_type=f32))
+    hat_one = hidden_float * attn_inverse
+    g_attn_gain = jnp.sum(d_normed_one * hat_one, axis=0)
+    hidden_grad = middle_grad + norm_backward(d_normed_one, hat_one, attn_inverse, attn_gain)
+    g_qkv, g_bias, g_out = (
+        lax.psum_scatter(g_qkv.astype(bf16), "fsdp", scatter_dimension=0, tiled=True).astype(f32),
+        lax.psum_scatter(g_bias.astype(bf16), "fsdp", scatter_dimension=2, tiled=True).astype(f32),
+        lax.psum_scatter(g_out.astype(bf16), "fsdp", scatter_dimension=1, tiled=True).astype(f32),
+    )
+    g_attn_gain, g_ffn_gain, g_gate_vec = (
+        lax.psum_scatter(g_attn_gain, every, scatter_dimension=0, tiled=True),
+        lax.psum_scatter(g_ffn_gain, every, scatter_dimension=0, tiled=True),
+        lax.psum_scatter(g_gate_vec, every, scatter_dimension=0, tiled=True),
+    )
+    return (
+        hidden_out,
+        hidden_grad,
+        route_grad,
+        g_attn_gain,
+        g_ffn_gain,
+        g_qkv,
+        g_bias,
+        g_out,
+        g_shared_gate_up,
+        g_shared_down,
+        g_gate_vec,
+        g_expert_gate_up,
+        g_expert_down,
+    )
+
+
+def on_device(*arrays):
+    expert_ids = arrays[3]
+    if 3 * expert_ids.shape[1] > lax.axis_size("fsdp"):
+        return dense_plan(*arrays)
+    return routed_plan(*arrays)
+
+
 def solution(mesh):
     placed = (
         P(("fsdp", "tp"), None),

time: 1570 us -> 1570 us (level)
  waiting for transfers between devices: 957 us -> 1140 us
  local copies, waits for them, and re-layouts: 217 us -> 105 us
  other arithmetic: 97.9 us -> 53.3 us
    unnamed x21 -> x18, waiting for transfers between devices: 158 us -> 725 us
    all_to_all x4 -> x5, waiting for transfers between devices: 399 us -> 56.2 us  [the longest x1 25.1 us: dense_plan(): lax.all_to_all(jnp.stack([g_both[:, expert_width:units], g_both[:, units...]
    reduce_scatter x7 -> x2, waiting for transfers between devices: 252 us -> 56.6 us  [the longest x1 43.1 us: dense_plan(): lax.psum_scatter(g_out.astype(bf16), 'fsdp', scatter_dimension=1, tiled=T...]
    all_gather x4, waiting for transfers between devices: 48.5 us -> 238 us  [the longest x1 107 us: dense_plan(): normed_all = lax.all_gather(normed_two_own, every, axis=0, tiled=True)]
    gather x6 -> x0, local copies, waits for them, and re-layouts: 115 us -> none  [the longest x1 26.4 us: on_device(): grad_float[source_rows]]
    convert_element_type x4 -> x2, local copies, waits for them, and re-layouts: 53.5 us -> 2.53 us  [the longest x1 2.41 us: dense_plan(): g_shared_gate_up = lax.all_to_all(jnp.stack([g_both[:, expert_width:units...]
    all_gather x4 -> x2, waiting for transfers between devices: 99.5 us -> 64.4 us  [spread(): return lax.all_gather(rows, 'tp', axis=0, tiled=True)]
    unnamed x119 -> x137, local copies, waits for them, and re-layouts: 29.4 us -> 64.3 us
  transfers between devices with their start and end apart: 22 -> 18, of which waited for: 18 -> 16; matrix products, arithmetic and copies ran while one was open for 27% -> 13% of each run, Pallas kernels for 0% -> 0%
where the time goes in v1:
time: 1570 us; the launch traced here: 1560 us
  waiting for transfers between devices  1140 us (73%)
  matrix products  178 us (11%)
  local copies, waits for them, and re-layouts  105 us (7%)
  other arithmetic  53.3 us (3%)
  blocking collectives  51.1 us (3%)
  starting transfers between devices  21.1 us (1%)
    unnamed x18, waiting for transfers between devices  725 us
    all_gather x1, waiting for transfers between devices, dense_plan(): normed_all = lax.all_gather(normed_two_own, every, axis=0, tiled=True)  107 us
    all_gather x1, waiting for transfers between devices, dense_plan(): grad_all = lax.all_gather(out_grad, every, axis=0, tiled=True)  81.6 us
    all_gather x2, waiting for transfers between devices, spread(): return lax.all_gather(rows, 'tp', axis=0, tiled=True)  64.4 us
    unnamed x137, local copies, waits for them, and re-layouts  64.3 us
    reduce_scatter x1, waiting for transfers between devices, dense_plan(): lax.psum_scatter(g_out.astype(bf16), 'fsdp', scatter_dimension=1, tiled=T...  43.1 us
    unnamed x1, blocking collectives  40.4 us
    all_gather x1, waiting for transfers between devices, dense_plan(): qkv_full = lax.all_gather(qkv_weight, 'fsdp', axis=0, tiled=True)  33.3 us
  transfers between devices with their start and end apart: 18, of which 16 were waited for; matrix products, arithmetic and copies ran while one was open for 13% of the time, Pallas kernels for 0%

profile of v1, /device:TPU:0, one launch (start us, length us, event | category | flops | bytes accessed | tf_op | source)
XLA Modules:
  0.0 1564.0 jit_solution(9866713022279479030)
XLA Ops:
  25.5 33.3 %all-gather.9.cloned.1.call-done = bf16[2048,3,4,128]{3,0,2,1:T(8,128)(2,1)} async-done(((bf16[256,3,4,128]{3,0,2,1:T(8,128)(2,1)}), bf16[2048,3,4,128]{3,0,2,1:T(8,128)(2,1)}) %all-gather.9.cloned.1.call-update) | async-done | bytes 6291472 | tf_op jit(solution)/shard_map/all_gather | solution.py:367
  67.5 39.7 %all-gather.7.cloned.1.call-done = bf16[512,2048]{0,1:T(8,128)(2,1)} async-done(((bf16[128,2048]{0,1:T(8,128)(2,1)}), bf16[512,2048]{0,1:T(8,128)(2,1)}) %all-gather.7.cloned.1.call-update) | async-done | bytes 2097168 | tf_op jit(solution)/shard_map/all_gather | solution.py:74
  119.5 16.1 %all-gather.11.cloned.1.call-done = bf16[512,2048]{1,0:T(8,128)(2,1)} async-done(((bf16[512,256]{1,0:T(8,128)(2,1)}), bf16[512,2048]{1,0:T(8,128)(2,1)}) %all-gather.11.cloned.1.call-update) | async-done | bytes 2097168 | tf_op jit(solution)/shard_map/all_gather | solution.py:369
  139.8 44.0 %reduce-scatter.22.cloned.1.call-done = bf16[128,2048]{1,0:T(8,128)(2,1)} async-done(((bf16[512,2048]{1,0:T(8,128)(2,1)}), bf16[128,2048]{1,0:T(8,128)(2,1)}) %reduce-scatter.22.cloned.1.call-update) | async-done | bytes 524304
  217.8 18.5 %all-to-all-done = bf16[256,2,1408]{0,1,2:T(2,128)(2,1)S(1)} async-done(((bf16[256,2,1408]{0,1,2:T(2,128)(2,1)}), bf16[256,2,1408]{0,1,2:T(2,128)(2,1)S(1)}, u32[]{:S(2)}, u32[]{:S(2)}) %all-to-all-start) | async-done | bytes 1441824 | tf_op jit(solution)/shard_map/all_to_all | solution.py:370
  242.7 107.4 %all-gather.13.cloned.1.call-done = bf16[4096,2048]{0,1:T(8,128)(2,1)} async-done(((bf16[128,2048]{0,1:T(8,128)(2,1)}), bf16[4096,2048]{0,1:T(8,128)(2,1)}) %all-gather.13.cloned.1.call-update) | async-done | bytes 16777232 | tf_op jit(solution)/shard_map/all_gather | solution.py:414
  361.2 23.7 %fusion.37 = f32[4096,1056]{0,1:T(8,128)} fusion(bf16[4096,2048]{0,1:T(8,128)(2,1)S(1)} %copy-done.4, bf16[2048,176]{0,1:T(8,128)(2,1)} %get-tuple-element.140, bf16[2048,352]{0,1:T(8,128)(2,1)S(1)} %copy-done.15, bf16[2048,176]{0,1:T(8,128)(2,1)} %get-tuple-element.139, bf16[2048,352]{0,1:T(8,128)(2,1)S(1)} %copy-done.13), kind=kOutput, calls=%fused_computation.91 | convolution fusion | flops 17734041600 | bytes 38404096 | tf_op jit(solution)/shard_map/dot_general | solution.py:430
  384.9 81.6 %all-gather.15.cloned.1.call-done = bf16[4096,2048]{1,0:T(8,128)(2,1)} async-done(((bf16[128,2048]{1,0:T(8,128)(2,1)}), bf16[4096,2048]{1,0:T(8,128)(2,1)}) %all-gather.15.cloned.1.call-update) | async-done | bytes 16777232 | tf_op jit(solution)/shard_map/all_gather | solution.py:366
  469.0 27.1 %multiply_convert_fusion.1 = (bf16[4096,528]{0,1:T(8,128)(2,1)}, bf16[4096,528]{0,1:T(8,128)(2,1)}, f32[4096,528]{0,1:T(8,128)}, bf16[4096,528]{0,1:T(8,128)(2,1)}) fusion(f32[4096,1056]{0,1:T(8,128)} %fusion.37, f32[4096,176]{0,1:T(8,128)} %broadcast_in_dim.123, f32[4096,352]{0,1:T(8,128)S(1)} %broadcast_in_dim.122, ...), kind=kOutput, calls=%fused_computation.11 | convolution fusion | flops 8903786496 | bytes 66519040 | tf_op jit(solution)/shard_map/dot_general | solution.py:434
  502.2 26.6 %convolution_convert_fusion = bf16[4096,2048]{0,1:T(8,128)(2,1)} fusion(bf16[4096,528]{0,1:T(8,128)(2,1)} %get-tuple-element.128, bf16[4096,528]{0,1:T(8,128)(2,1)S(1)} %copy-done.55, bf16[2048,176]{0,1:T(8,128)(2,1)S(1)} %copy-done.35, bf16[2048,352]{0,1:T(8,128)(2,1)S(1)} %copy-done.16, bf16[2048,176]{0,1:T(8,128)(2,1)S(1)} %copy-done.34, ...), kind=kOutput, calls=%fused_computation.2 | convolution fusion | flops 17759731712 | bytes 29753344 | tf_op jit(solution)/shard_map/dot_general | solution.py:443
  529.3 14.2 pad_maximum_fusion
  543.4 22.2 %copy.275 = bf16[4096,2176]{1,0:T(8,128)(2,1)} copy(bf16[4096,2176]{0,1:T(8,128)(2,1)} %pad_maximum_fusion) | data formatting | bytes 35651584
  566.9 383.5 %reduce-scatter.26.cloned.1.call-done = bf16[128,2176]{1,0:T(8,128)(2,1)} async-done(((bf16[4096,2176]{1,0:T(8,128)(2,1)}), bf16[128,2176]{1,0:T(8,128)(2,1)}) %reduce-scatter.26.cloned.1.call-update) | async-done | bytes 557072
  956.6 19.6 %convolution_convert_fusion.1 = bf16[4096,2048]{1,0:T(8,128)(2,1)} fusion(bf16[4096,528]{0,1:T(8,128)(2,1)} %get-tuple-element.130, bf16[176,2048]{1,0:T(8,128)(2,1)} %bitcast.161, bf16[352,2048]{1,0:T(8,128)(2,1)} %bitcast.169), kind=kOutput, calls=%fused_computation.3 | convolution fusion | flops 8871084032 | bytes 23265280 | tf_op jit(solution)/shard_map/dot_general | solution.py:456
  976.3 24.7 %all-gather.17.cloned.1.call-done = bf16[512,2048]{0,1:T(8,128)(2,1)} async-done(((bf16[128,2048]{0,1:T(8,128)(2,1)}), bf16[512,2048]{0,1:T(8,128)(2,1)}) %all-gather.17.cloned.1.call-update) | async-done | bytes 2097168 | tf_op jit(solution)/shard_map/all_gather | solution.py:74
  1034.6 13.2 fusion.60
  1054.9 25.1 %fusion.59 = (bf16[2048,1056]{0,1:T(8,128)(2,1)S(1)}, f32[2048,1056]{0,1:T(8,128)}) fusion(bf16[4096,2048]{0,1:T(8,128)(2,1)} %all-gather.13.cloned.1.call-done, bf16[4096,528]{0,1:T(8,128)(2,1)} %get-tuple-element.128, bf16[4096,528]{0,1:T(8,128)(2,1)} %get-tuple-element.127), kind=kOutput, calls=%fused_computation.139 | convolution fusion | flops 17736204288 | bytes 38404096 | tf_op jit(solution)/shard_map/dot_general | solution.py:467
  1101.0 25.1 %all-to-all-done.3 = bf16[2048,2,176]{2,1,0:T(2,128)(2,1)} async-done(((bf16[2048,2,176]{2,1,0:T(2,128)(2,1)}), bf16[2048,2,176]{2,1,0:T(2,128)(2,1)}, u32[]{:S(2)}, u32[]{:S(2)}) %all-to-all-start.3) | async-done | bytes 1441824 | tf_op jit(solution)/shard_map/all_to_all | solution.py:472
  1143.1 222.8 %reduce-scatter.24.cloned.1.call-done = bf16[128,2048]{1,0:T(8,128)(2,1)} async-done(((bf16[4096,2048]{1,0:T(8,128)(2,1)}), bf16[128,2048]{1,0:T(8,128)(2,1)}) %reduce-scatter.24.cloned.1.call-update) | async-done | bytes 524304
  1369.2 29.1 %reduce-scatter.30.cloned.1.call-done = bf16[16,12]{1,0:T(8,128)(2,1)} async-done(((bf16[128,12]{1,0:T(8,128)(2,1)}), bf16[16,12]{1,0:T(8,128)(2,1)}) %reduce-scatter.30.cloned.1.call-update) | async-done | bytes 400
  1399.7 43.1 %reduce-scatter.20.cloned.1.call-done = bf16[512,256]{1,0:T(8,128)(2,1)} async-done(((bf16[512,2048]{1,0:T(8,128)(2,1)}), bf16[512,256]{1,0:T(8,128)(2,1)}) %reduce-scatter.20.cloned.1.call-update) | async-done | bytes 262160 | tf_op jit(solution)/shard_map/reduce_scatter | solution.py:523
  1444.6 44.4 %reduce-scatter.28.cloned.1.call-done = bf16[128,2048]{1,0:T(8,128)(2,1)} async-done(((bf16[512,2048]{1,0:T(8,128)(2,1)}), bf16[128,2048]{1,0:T(8,128)(2,1)}) %reduce-scatter.28.cloned.1.call-update) | async-done | bytes 524304
  1490.9 40.4 %all-reduce.3 = (f32[2048]{0:T(1024)S(1)}, f32[2048]{0:T(1024)S(1)}, f32[2048]{0:T(1024)S(1)}) all-reduce(f32[2048]{0:T(1024)S(1)} %get-tuple-element.119, f32[2048]{0:T(1024)S(1)} %get-tuple-element.117, f32[2048]{0:T(1024)S(1)} %get-tuple-element.121), channel_id=6, replica_groups=mesh['fsdp'=8,'tp'=4] {'fsdp','tp'}, use_global_device_ids=true, to_apply=%region_18.19.clone | all-reduce | flops 6144 | bytes 49152
  1540.5 13.6 reduce-scatter.18.cloned.1.call-done
  (246 shorter events, 209.8 us)
Async XLA Ops:
  7.2 51.6 %all-gather.9.cloned.1.call-start = ((), (), s32[]{:S(2)}) async-start(), calls=%async_computation.13 | async-start | bytes 7077888 | tf_op jit(solution)/shard_map/all_gather | solution.py:367
  9.4 97.8 %all-gather.7.cloned.1.call-start = ((), (), s32[]{:S(2)}) async-start(), calls=%async_computation.12 | async-start | bytes 2621440 | tf_op jit(solution)/shard_map/all_gather | solution.py:74
  13.0 122.6 %all-gather.11.cloned.1.call-start = ((), (), s32[]{:S(2)}) async-start(), calls=%async_computation.14 | async-start | bytes 2359296 | tf_op jit(solution)/shard_map/all_gather | solution.py:369
  13.7 170.1 %reduce-scatter.22.cloned.1.call-start = ((), (), s32[]{:S(2)}) async-start(), calls=%async_computation.20 | async-start | bytes 2621440
  139.8 210.3 %all-gather.13.cloned.1.call-start = ((), (), s32[]{:S(2)}) async-start(), calls=%async_computation.15 | async-start | bytes 17301504 | tf_op jit(solution)/shard_map/all_gather | solution.py:414
  187.4 279.0 %all-gather.15.cloned.1.call-start = ((), (), s32[]{:S(2)}) async-start(), calls=%async_computation.16 | async-start | bytes 17301504 | tf_op jit(solution)/shard_map/all_gather | solution.py:366
  188.0 20.3 %all-to-all-start.2 = ((bf16[8,176,256]{2,1,0:T(8,128)(2,1)}), bf16[8,176,256]{2,1,0:T(8,128)(2,1)S(1)}, u32[]{:S(2)}, u32[]{:S(2)}) async-start(bf16[8,176,256]{2,1,0:T(8,128)(2,1)} %bitcast.160), calls=%async_computation.2 | async-start | bytes 1441792 | tf_op jit(solution)/shard_map/all_to_all | solution.py:371
  208.3 28.0 %all-to-all-start = ((bf16[256,2,1408]{0,1,2:T(2,128)(2,1)}), bf16[256,2,1408]{0,1,2:T(2,128)(2,1)S(1)}, u32[]{:S(2)}, u32[]{:S(2)}) async-start(bf16[256,2,1408]{0,1,2:T(2,128)(2,1)} %copy.234), calls=%async_computation | async-start | bytes 2883584 | tf_op jit(solution)/shard_map/all_to_all | solution.py:370
  236.3 148.5 %all-to-all-start.1 = ((f32[8,1,512]{2,1,0:T(1,128)}), f32[8,1,512]{2,1,0:T(1,128)S(1)}, u32[]{:S(2)}, u32[]{:S(2)}) async-start(f32[8,1,512]{2,1,0:T(1,128)} %copy.237), calls=%async_computation.1 | async-start | bytes 32768 | tf_op jit(solution)/shard_map/all_to_all | solution.py:379
  240.9 709.6 %reduce-scatter.26.cloned.1.call-start = ((), (), s32[]{:S(2)}) async-start(), calls=%async_computation.22 | async-start | bytes 18382848
  565.6 388.1 %copy-start.37 = (f32[2048]{0:T(1024)S(1)}, f32[2048]{0:T(1024)}, u32[]{:S(2)}) copy-start(f32[2048]{0:T(1024)} %param.27) | copy-start | bytes 24580
  565.6 388.1 %copy-start.39 = (f32[2048]{0:T(1024)S(1)}, f32[2048]{0:T(1024)}, u32[]{:S(2)}) copy-start(f32[2048]{0:T(1024)} %param.21) | copy-start | bytes 24580
  565.6 388.1 %copy-start.47 = (f32[128]{0:T(128)S(1)}, f32[128]{0:T(128)}, u32[]{:S(2)}) copy-start(f32[128]{0:T(128)} %copy-done.46) | copy-start | bytes 1540
  565.6 388.1 %copy-start.1 = (bf16[128,2048]{0,1:T(8,128)(2,1)S(1)}, bf16[128,2048]{0,1:T(8,128)(2,1)}, u32[]{:S(2)}) copy-start(bf16[128,2048]{0,1:T(8,128)(2,1)} %copy-done) | copy-start | bytes 1572868
  565.7 388.1 %copy-start.3 = (bf16[128,2048]{0,1:T(8,128)(2,1)S(1)}, bf16[128,2048]{0,1:T(8,128)(2,1)}, u32[]{:S(2)}) copy-start(bf16[128,2048]{0,1:T(8,128)(2,1)} %copy-done.2) | copy-start | bytes 1572868
  565.7 388.1 %copy-start.5 = (bf16[128,2048]{0,1:T(8,128)(2,1)S(1)}, bf16[128,2048]{0,1:T(8,128)(2,1)}, u32[]{:S(2)}) copy-start(bf16[128,2048]{0,1:T(8,128)(2,1)} %get-tuple-element.126) | copy-start | bytes 1572868
  565.7 435.3 %all-gather.17.cloned.1.call-start = ((), (), s32[]{:S(2)}) async-start(), calls=%async_computation.17 | async-start | bytes 2621440 | tf_op jit(solution)/shard_map/all_gather | solution.py:74
  956.5 409.3 %reduce-scatter.24.cloned.1.call-start = ((), (), s32[]{:S(2)}) async-start(), calls=%async_computation.21 | async-start | bytes 17301504
  976.2 422.0 %reduce-scatter.30.cloned.1.call-start = ((), (), s32[]{:S(2)}) async-start(), calls=%async_computation.24 | async-start | bytes 36864
  1012.8 430.0 %reduce-scatter.20.cloned.1.call-start = ((), (), s32[]{:S(2)}) async-start(), calls=%async_computation.19 | async-start | bytes 2359296 | tf_op jit(solution)/shard_map/reduce_scatter | solution.py:523
  1017.5 471.4 %reduce-scatter.28.cloned.1.call-start = ((), (), s32[]{:S(2)}) async-start(), calls=%async_computation.23 | async-start | bytes 2621440
  1026.2 527.8 %reduce-scatter.18.cloned.1.call-start = ((), (), s32[]{:S(2)}) async-start(), calls=%async_computation.18 | async-start | bytes 7077888 | tf_op jit(solution)/shard_map/reduce_scatter | solution.py:521
  1050.9 36.5 %all-to-all-start.4 = ((bf16[176,8,256]{2,0,1:T(8,128)(2,1)}), bf16[176,8,256]{2,0,1:T(8,128)(2,1)S(1)}, u32[]{:S(2)}, u32[]{:S(2)}) async-start(bf16[176,8,256]{2,0,1:T(8,128)(2,1)} %bitcast.157), calls=%async_computation.6 | async-start | bytes 1441792 | tf_op jit(solution)/shard_map/all_to_all | solution.py:481
  1087.4 38.7 %all-to-all-start.3 = ((bf16[2048,2,176]{2,1,0:T(2,128)(2,1)}), bf16[2048,2,176]{2,1,0:T(2,128)(2,1)}, u32[]{:S(2)}, u32[]{:S(2)}) async-start(bf16[2048,2,176]{2,1,0:T(2,128)(2,1)} %copy.249), calls=%async_computation.5 | async-start | bytes 4194304 | tf_op jit(solution)/shard_map/all_to_all | solution.py:472
  (52 other events, 2392.1 us)
Sparse Core Ops, SparseCore 0:
  10.5 48.2 all-gather.8
  60.9 46.2 all-gather.6
  109.1 26.4 all-gather.10
  139.9 43.8 reduce-scatter.21
  187.6 162.4 all-gather.12
  353.4 113.0 all-gather.14
  565.8 384.6 reduce-scatter.25
  956.7 44.2 all-gather.16
  1003.4 362.4 reduce-scatter.23
  1369.0 29.1 reduce-scatter.29
  1401.5 41.2 reduce-scatter.19
  1445.0 43.8 reduce-scatter.27
  1492.3 61.7 reduce-scatter.17

commit v2 on v1

--- a/solution.py
+++ b/solution.py
@@ -1,4 +1,8 @@
+import functools
+
 import jax
+import jax.experimental.pallas as pl
+import jax.experimental.pallas.tpu as pltpu
 import jax.numpy as jnp
 from jax import lax
 from jax.sharding import PartitionSpec as P
@@ -336,6 +340,442 @@
     )
 
 
+MESH = pl.DeviceIdType.MESH
+
+
+def flipped(index, bit):
+    return index + bit - 2 * bit * ((index // bit) % 2)
+
+
+def place():
+    me = lax.axis_index("fsdp")
+    rank = lax.axis_index("tp")
+    return me, rank
+
+
+def greet(me, rank, tp):
+    barrier = pltpu.get_barrier_semaphore()
+    for bit in (1, 2, 4):
+        pl.semaphore_signal(
+            barrier, inc=1, device_id=(flipped(me, bit), rank), device_id_type=MESH
+        )
+
+    @pl.when(rank > 0)
+    def _():
+        pl.semaphore_signal(barrier, inc=1, device_id=(me, rank - 1), device_id_type=MESH)
+
+    @pl.when(rank < tp - 1)
+    def _():
+        pl.semaphore_signal(barrier, inc=1, device_id=(me, rank + 1), device_id_type=MESH)
+
+    left = (rank + tp - 1) // tp
+    right = (2 * (tp - 1) - rank) // tp
+    pl.semaphore_wait(barrier, 3 + left + right)
+
+
+def gather_kernel(tp, own_ref, all_ref, local_sem, z_send, z_recv, p_send, p_recv):
+    me, rank = place()
+    greet(me, rank, tp)
+    rows = own_ref.shape[0]
+    half = rows // 2
+    pack_rows = rows * tp
+
+    def region(pack, block, start=0, count=None):
+        count = rows if count is None else count
+        return all_ref.at[pl.ds(pack * pack_rows + block * rows + start, count)]
+
+    def along_z(block, right):
+        way = 0 if right else 1
+        ref = region(me, block)
+        return pltpu.make_async_remote_copy(
+            src_ref=ref,
+            dst_ref=ref,
+            send_sem=z_send.at[way, block],
+            recv_sem=z_recv.at[way, block],
+            device_id=(me, rank + 1 if right else rank - 1),
+            device_id_type=MESH,
+        )
+
+    def across(bit, pack_bits, block, slot, start=0, count=None):
+        pack = me
+        for one in (2, 4):
+            if pack_bits & one:
+                pack = flipped(pack, one)
+        ref = region(pack, block, start, count)
+        return pltpu.make_async_remote_copy(
+            src_ref=ref,
+            dst_ref=ref,
+            send_sem=p_send.at[slot, block],
+            recv_sem=p_recv.at[slot, block],
+            device_id=(flipped(me, bit), rank),
+            device_id_type=MESH,
+        )
+
+    def own_x(block):
+        return across(2, 0, block, 0)
+
+    def own_y(block):
+        return across(4, 0, block, 1)
+
+    def own_core(block):
+        return across(1, 0, block, 2)
+
+    def x_to_y(block):
+        return across(4, 2, block, 3, 0, half)
+
+    def x_to_core(block):
+        return across(1, 2, block, 4)
+
+    def y_to_x(block):
+        return across(2, 4, block, 5, half, half)
+
+    def y_to_core(block):
+        return across(1, 4, block, 6)
+
+    def diag_to_core(block):
+        return across(1, 6, block, 7)
+
+    def start_plane(block):
+        own_x(block).start()
+        own_y(block).start()
+        own_core(block).start()
+
+    def forward(block):
+        own_x(block).wait_recv()
+        x_to_y(block).start()
+        x_to_core(block).start()
+        own_y(block).wait_recv()
+        y_to_x(block).start()
+        y_to_core(block).start()
+
+    def finish(block):
+        x_to_y(block).wait_recv()
+        y_to_x(block).wait_recv()
+        diag_to_core(block).start()
+
+    def z_step(step):
+        @pl.when(rank >= step)
+        def _():
+            block = rank - step
+            along_z(block, True).wait_recv()
+
+            @pl.when(rank < tp - 1)
+            def _():
+                along_z(block, True).start()
+
+            start_plane(block)
+
+        @pl.when(rank + step < tp)
+        def _():
+            block = rank + step
+            along_z(block, False).wait_recv()
+
+            @pl.when(rank > 0)
+            def _():
+                along_z(block, False).start()
+
+            start_plane(block)
+
+    mine = pltpu.make_async_copy(own_ref, region(me, rank), local_sem)
+    mine.start()
+    mine.wait()
+
+    @pl.when(rank < tp - 1)
+    def _():
+        along_z(rank, True).start()
+
+    @pl.when(rank > 0)
+    def _():
+        along_z(rank, False).start()
+
+    start_plane(rank)
+    order = [rank]
+    for bit in (1, 2):
+        order = order + [flipped(one, bit) for one in order]
+    z_step(1)
+    forward(order[0])
+    z_step(2)
+    forward(order[1])
+    finish(order[0])
+    z_step(3)
+    forward(order[2])
+    finish(order[1])
+    forward(order[3])
+    finish(order[2])
+    finish(order[3])
+    for block in order:
+        own_core(block).wait_recv()
+        x_to_core(block).wait_recv()
+        y_to_core(block).wait_recv()
+        diag_to_core(block).wait_recv()
+    for block in order:
+        own_x(block).wait_send()
+        own_y(block).wait_send()
+        own_core(block).wait_send()
+        x_to_y(block).wait_send()
+        x_to_core(block).wait_send()
+        y_to_x(block).wait_send()
+        y_to_core(block).wait_send()
+        diag_to_core(block).wait_send()
+    for block in range(tp):
+
+        @pl.when((block <= rank) & (rank < tp - 1))
+        def _():
+            along_z(block, True).wait_send()
+
+        @pl.when((block >= rank) & (rank > 0))
+        def _():
+            along_z(block, False).wait_send()
+
+
+def gather_everywhere(own, fsdp, tp, collective_id):
+    rows, width = own.shape
+    return pl.pallas_call(
+        functools.partial(gather_kernel, tp),
+        out_shape=jax.ShapeDtypeStruct((fsdp * tp * rows, width), own.dtype),
+        in_specs=[pl.BlockSpec(memory_space=pl.ANY)],
+        out_specs=pl.BlockSpec(memory_space=pl.ANY),
+        scratch_shapes=[
+            pltpu.SemaphoreType.DMA,
+            pltpu.SemaphoreType.DMA((2, tp)),
+            pltpu.SemaphoreType.DMA((2, tp)),
+            pltpu.SemaphoreType.DMA((8, tp)),
+            pltpu.SemaphoreType.DMA((8, tp)),
+        ],
+        compiler_params=pltpu.CompilerParams(
+            collective_id=collective_id, has_side_effects=True, vmem_limit_bytes=16 << 20
+        ),
+        name="gather_rows",
+    )(own)
+
+
+def scatter_kernel(tp, parts, *refs):
+    ins = refs[:parts]
+    outs = refs[parts : 2 * parts]
+    buffers = refs[2 * parts : 7 * parts]
+    mine, other, diag_in, last_in, z_in = (
+        buffers[i * parts : (i + 1) * parts] for i in range(5)
+    )
+    l_sem, c_send, c_recv, p_send, p_recv, z_send, z_recv = refs[7 * parts :]
+    me, rank = place()
+    greet(me, rank, tp)
+    f32 = jnp.float32
+    blocks = [rank]
+    for bit in (1, 2):
+        blocks = blocks + [flipped(one, bit) for one in blocks]
+    blocks = blocks[::-1]
+    packs = [me, flipped(me, 2), flipped(me, 4), flipped(flipped(me, 2), 4)]
+    every = range(parts)
+    rows = [ref.shape[0] for ref in outs]
+    low = [pl.ds(0, count // 2) for count in rows]
+    high = [pl.ds(count // 2, count // 2) for count in rows]
+
+    def region(i, pack, block):
+        return ins[i].at[pl.ds((pack * tp + block) * rows[i], rows[i])]
+
+    def local(k, j, i):
+        return pltpu.make_async_copy(
+            region(i, packs[k], blocks[j]), mine[i].at[k, j], l_sem.at[k, j, i]
+        )
+
+    def core(k, j, i):
+        return pltpu.make_async_remote_copy(
+            src_ref=region(i, flipped(packs[k], 1), blocks[j]),
+            dst_ref=other[i].at[k, j],
+            send_sem=c_send.at[k, j, i],
+            recv_sem=c_recv.at[k, j, i],
+            device_id=(flipped(me, 1), rank),
+            device_id_type=MESH,
+        )
+
+    def across(bit, src, dst, slot, j, i):
+        return pltpu.make_async_remote_copy(
+            src_ref=src,
+            dst_ref=dst,
+            send_sem=p_send.at[slot, j, i],
+            recv_sem=p_recv.at[slot, j, i],
+            device_id=(flipped(me, bit), rank),
+            device_id_type=MESH,
+        )
+
+    def diag_x(j, i):
+        return across(2, mine[i].at[3, j, low[i]], diag_in[i].at[j, 0], 0, j, i)
+
+    def diag_y(j, i):
+        return across(4, mine[i].at[3, j, high[i]], diag_in[i].at[j, 1], 1, j, i)
+
+    def direct_x(j, i):
+        return across(2, mine[i].at[1, j, low[i]], last_in[i].at[j, 0, low[i]], 2, j, i)
+
+    def direct_y(j, i):
+        return across(4, mine[i].at[2, j, high[i]], last_in[i].at[j, 1, high[i]], 3, j, i)
+
+    def summed_x(j, i):
+        return across(2, mine[i].at[1, j, high[i]], last_in[i].at[j, 0, high[i]], 4, j, i)
+
+    def summed_y(j, i):
+        return across(4, mine[i].at[2, j, low[i]], last_in[i].at[j, 1, low[i]], 5, j, i)
+
+    def along_z(j, right, i):
+        way = 0 if right else 1
+        block = blocks[j]
+        return pltpu.make_async_remote_copy(
+            src_ref=mine[i].at[0, j],
+            dst_ref=z_in[i].at[way, block],
+            send_sem=z_send.at[way, block, i],
+            recv_sem=z_recv.at[way, block, i],
+            device_id=(me, rank + 1 if right else rank - 1),
+            device_id_type=MESH,
+        )
+
+    for j in range(tp):
+        for k in (3, 2, 1, 0):
+            for i in every:
+                core(k, j, i).start()
+                local(k, j, i).start()
+
+    def add(ref, spot, one):
+        ref[spot] = (ref[spot].astype(f32) + one.astype(f32)).astype(ref.dtype)
+
+    def first(j):
+        for k in (3, 2, 1, 0):
+            for i in every:
+                core(k, j, i).wait_recv()
+                local(k, j, i).wait()
+                add(mine[i], (k, j), other[i][k, j])
+                if k == 3:
+                    diag_x(j, i).start()
+                    diag_y(j, i).start()
+                if k == 2:
+                    direct_y(j, i).start()
+                if k == 1:
+                    direct_x(j, i).start()
+
+    def second(j):
+        for i in every:
+            diag_x(j, i).wait_recv()
+            add(mine[i], (2, j, low[i]), diag_in[i][j, 0])
+            summed_y(j, i).start()
+            diag_y(j, i).wait_recv()
+            add(mine[i], (1, j, high[i]), diag_in[i][j, 1])
+            summed_x(j, i).start()
+
+    def third(j):
+        block = blocks[j]
+        for i in every:
+            direct_x(j, i).wait_recv()
+            direct_y(j, i).wait_recv()
+            summed_x(j, i).wait_recv()
+            summed_y(j, i).wait_recv()
+            total = (
+                mine[i][0, j].astype(f32)
+                + last_in[i][j, 0].astype(f32)
+                + last_in[i][j, 1].astype(f32)
+            )
+            if j < tp - 1:
+                mine[i][0, j] = total.astype(mine[i].dtype)
+            else:
+                outs[i][...] = total
+        if j < tp - 1:
+
+            @pl.when((block > rank) & (rank > 0))
+            def _():
+                for i in every:
+                    along_z(j, True, i).wait_recv()
+                    add(mine[i], (0, j), z_in[i][0, block])
+
+            @pl.when((block < rank) & (rank < tp - 1))
+            def _():
+                for i in every:
+                    along_z(j, False, i).wait_recv()
+                    add(mine[i], (0, j), z_in[i][1, block])
+
+            @pl.when(block > rank)
+            def _():
+                for i in every:
+                    along_z(j, True, i).start()
+
+            @pl.when(block < rank)
+            def _():
+                for i in every:
+                    along_z(j, False, i).start()
+        else:
+
+            @pl.when(rank > 0)
+            def _():
+                for i in every:
+                    along_z(j, True, i).wait_recv()
+                    outs[i][...] += z_in[i][0, block].astype(f32)
+
+            @pl.when(rank < tp - 1)
+            def _():
+                for i in every:
+                    along_z(j, False, i).wait_recv()
+                    outs[i][...] += z_in[i][1, block].astype(f32)
+
+    first(0)
+    first(1)
+    second(0)
+    first(2)
+    second(1)
+    third(0)
+    first(3)
+    second(2)
+    third(1)
+    second(3)
+    third(2)
+    third(3)
+    for j in range(tp):
+        for i in every:
+            for k in range(4):
+                core(k, j, i).wait_send()
+            for copy in (diag_x, diag_y, direct_x, direct_y, summed_x, summed_y):
+                copy(j, i).wait_send()
+        block = blocks[j]
+        if j < tp - 1:
+
+            @pl.when(block > rank)
+            def _():
+                for i in every:
+                    along_z(j, True, i).wait_send()
+
+            @pl.when(block < rank)
+            def _():
+                for i in every:
+                    along_z(j, False, i).wait_send()
+
+
+def scatter_sum(arrays, fsdp, tp, collective_id):
+    parts = len(arrays)
+    shapes = [(one.shape[0] // (fsdp * tp), one.shape[1]) for one in arrays]
+    kind = arrays[0].dtype
+    scratch = [pltpu.VMEM((4, tp, rows, width), kind) for rows, width in shapes]
+    scratch += [pltpu.VMEM((4, tp, rows, width), kind) for rows, width in shapes]
+    scratch += [pltpu.VMEM((tp, 2, rows // 2, width), kind) for rows, width in shapes]
+    scratch += [pltpu.VMEM((tp, 2, rows, width), kind) for rows, width in shapes]
+    scratch += [pltpu.VMEM((2, tp, rows, width), kind) for rows, width in shapes]
+    return pl.pallas_call(
+        functools.partial(scatter_kernel, tp, parts),
+        out_shape=[jax.ShapeDtypeStruct(shape, jnp.float32) for shape in shapes],
+        in_specs=[pl.BlockSpec(memory_space=pl.ANY)] * parts,
+        out_specs=[pl.BlockSpec(memory_space=pltpu.VMEM)] * parts,
+        scratch_shapes=scratch
+        + [
+            pltpu.SemaphoreType.DMA((4, tp, parts)),
+            pltpu.SemaphoreType.DMA((4, tp, parts)),
+            pltpu.SemaphoreType.DMA((4, tp, parts)),
+            pltpu.SemaphoreType.DMA((6, tp, parts)),
+            pltpu.SemaphoreType.DMA((6, tp, parts)),
+            pltpu.SemaphoreType.DMA((2, tp, parts)),
+            pltpu.SemaphoreType.DMA((2, tp, parts)),
+        ],
+        compiler_params=pltpu.CompilerParams(
+            collective_id=collective_id, has_side_effects=True, vmem_limit_bytes=48 << 20
+        ),
+        name="scatter_rows",
+    )(*arrays)
+
+
 def dense_plan(
     hidden_in,
     out_grad,
@@ -411,7 +851,7 @@
     middle = hidden_float + head_total(jnp.dot(heads_out, out_full, preferred_element_type=f32))
     ffn_inverse = inverse_rms(middle)
     normed_two_own = (middle * ffn_inverse * ffn_gain).astype(bf16)
-    normed_all = lax.all_gather(normed_two_own, every, axis=0, tiled=True)
+    normed_all = gather_everywhere(normed_two_own, experts, lax.axis_size("tp"), 1)
 
     gate_w = jnp.concatenate([expert_up[:, 0], shared_up[:, 0]], axis=1)
     upper_w = jnp.concatenate([expert_up[:, 1], shared_up[:, 1]], axis=1)
@@ -441,28 +881,25 @@
         [(d_scaled * upper * slope).astype(bf16), (d_scaled * act).astype(bf16)], axis=1
     )
     d_normed_part = jnp.dot(d_both, both_w.T, preferred_element_type=f32).astype(bf16)
-    lane = jnp.arange(128, dtype=jnp.int32)
-    own_expert = lax.axis_index("fsdp")
-    extra = jnp.where(lane == own_expert, route_part[:, None], 0.0) + jnp.where(
-        lane == experts, gate_part[:, None], 0.0
-    )
-    d_sum = lax.psum_scatter(
-        jnp.concatenate([d_normed_part, extra.astype(bf16)], axis=1),
-        every,
-        scatter_dimension=0,
-        tiled=True,
-    ).astype(f32)
-    d_normed_two = d_sum[:, :model_width]
+    lines = jnp.arange(16, dtype=jnp.int32)[None, :, None]
+    route_lines = route_part.reshape(-1, 1, own_rows)
+    gate_lines = gate_part.reshape(-1, 1, own_rows)
+    extra = jnp.where(lines == lax.axis_index("fsdp"), route_lines, 0.0) + jnp.where(
+        lines == experts, gate_lines, 0.0
+    )
+    extra_high = extra.astype(bf16)
+    extra_low = (extra - extra_high.astype(f32)).astype(bf16)
+    extra = jnp.concatenate([extra_high, extra_low], axis=1).reshape(-1, own_rows)
+    d_normed_two, extra_sum = scatter_sum([d_normed_part, extra], experts, lax.axis_size("tp"), 2)
+    extra_sum = extra_sum[:16] + extra_sum[16:]
     token_part = jnp.dot(hidden_s, down_w, preferred_element_type=f32).astype(bf16)
-    total = lax.psum_scatter(token_part, every, scatter_dimension=0, tiled=True).astype(f32)
+    (total,) = scatter_sum([token_part], experts, lax.axis_size("tp"), 3)
     hidden_out = (middle + total).astype(bf16)
     own_start = tp_rank * own_rows
     ids_own = lax.dynamic_slice_in_dim(expert_ids, own_start, own_rows)
     picked = ids_own[:, :, None] == jnp.arange(experts, dtype=jnp.int32)
-    route_grad = jnp.sum(
-        jnp.where(picked, d_sum[:, None, model_width : model_width + experts], 0.0), axis=-1
-    )
-    gate_grad = d_sum[:, model_width + experts]
+    route_grad = jnp.sum(jnp.where(picked, extra_sum[:experts].T[:, None, :], 0.0), axis=-1)
+    gate_grad = extra_sum[experts]
     g_down = jnp.dot(hidden_s.T, grad_all, preferred_element_type=f32)
     g_both = jnp.dot(normed_all.T, d_both, preferred_element_type=f32)
     g_expert_down = g_down[:expert_width][None]
@@ -545,8 +982,7 @@
 
 
 def on_device(*arrays):
-    expert_ids = arrays[3]
-    if 3 * expert_ids.shape[1] > lax.axis_size("fsdp"):
+    if lax.axis_size("fsdp") == 8 and lax.axis_size("tp") == 4 and arrays[3].shape[1] >= 3:
         return dense_plan(*arrays)
     return routed_plan(*arrays)
 

time: 1570 us -> 902 us (0.57)
  waiting for transfers between devices: 1140 us -> 209 us
  Pallas kernels: 0 us -> 320 us
  local copies, waits for them, and re-layouts: 105 us -> 63 us
  other arithmetic: 53.3 us -> 37 us
    unnamed x18 -> x11, waiting for transfers between devices: 725 us -> 1.33 us
    pallas_call x0 -> x3, Pallas kernels: none -> 320 us  [the longest x2 200 us: scatter_sum(): pl.pallas_call(functools.partial(scatter_kernel, tp, parts), out_shape=[j...]
    all_gather x1 -> x0, waiting for transfers between devices: 107 us -> none  [dense_plan(): normed_all = lax.all_gather(normed_two_own, every, axis=0, tiled=True)]
    all_gather x1, waiting for transfers between devices: 81.6 us -> 0.03 us  [dense_plan(): grad_all = lax.all_gather(out_grad, every, axis=0, tiled=True)]
    reduce_scatter x1, waiting for transfers between devices: 43.1 us -> 0.01 us  [dense_plan(): lax.psum_scatter(g_out.astype(bf16), 'fsdp', scatter_dimension=1, tiled=T...]
    unnamed x137 -> x112, local copies, waits for them, and re-layouts: 64.3 us -> 23.7 us
    all_gather x2, waiting for transfers between devices: 64.4 us -> 87.6 us  [spread(): return lax.all_gather(rows, 'tp', axis=0, tiled=True)]
  transfers between devices with their start and end apart: 18 -> 15, of which waited for: 16 -> 11; matrix products, arithmetic and copies ran while one was open for 13% -> 19% of each run, Pallas kernels for 0% -> 13%
where the time goes in v2:
time: 902 us; the launch traced here: 893 us
  Pallas kernels  320 us (35%)
  waiting for transfers between devices  209 us (23%)
  matrix products  176 us (20%)
  local copies, waits for them, and re-layouts  63 us (7%)
  blocking collectives  50.8 us (6%)
  other arithmetic  37 us (4%)
  starting transfers between devices  19.7 us (2%)
  between operations  16.7 us (2%)
    pallas_call x2, Pallas kernels, scatter_sum(): pl.pallas_call(functools.partial(scatter_kernel, tp, parts), out_shape=[j...  200 us
    pallas_call x1, Pallas kernels, gather_everywhere(): pl.pallas_call(functools.partial(gather_kernel, tp), out_shape=jax.ShapeD...  120 us
    all_gather x2, waiting for transfers between devices, spread(): return lax.all_gather(rows, 'tp', axis=0, tiled=True)  87.6 us
    unnamed x1, blocking collectives  40.1 us
    all_gather x1, waiting for transfers between devices, dense_plan(): qkv_full = lax.all_gather(qkv_weight, 'fsdp', axis=0, tiled=True)  33.5 us
    dot_general x1, matrix products, dense_plan(): d_hidden = jnp.dot(grad_all, down_w.T, preferred_element_type=f32)  28.4 us
    dot_general x1, matrix products, dense_plan(): jnp.dot(d_both, both_w.T, preferred_element_type=f32).astype(bf16)  26.8 us
    dot_general x1, matrix products, dense_plan(): g_both = jnp.dot(normed_all.T, d_both, preferred_element_type=f32)  24.9 us
  transfers between devices with their start and end apart: 15, of which 11 were waited for; matrix products, arithmetic and copies ran while one was open for 19% of the time, Pallas kernels for 13%

profile of v2, /device:TPU:0, one launch (start us, length us, event | category | flops | bytes accessed | tf_op | source)
XLA Modules:
  0.0 892.6 jit_solution(15122882473561807704)
XLA Ops:
  14.5 10.7 %all_gather.20 = bf16[3,4,128]{1,0,2:T(4,128)(2,1)S(1)} all-gather(bf16[3,4,16]{1,0,2:T(4,128)(2,1)S(1)} %copy.179), channel_id=1, replica_groups=mesh['fsdp'=8,'tp'=4] {'fsdp'}, dimensions={2}, use_global_device_ids=true | all-gather | bytes 3456 | tf_op jit(solution)/shard_map/all_gather | solution.py:808
  26.2 33.5 %all-gather.8.cloned.1.call-done = bf16[2048,3,4,128]{3,0,2,1:T(8,128)(2,1)} async-done(((bf16[256,3,4,128]{3,0,2,1:T(8,128)(2,1)}), bf16[2048,3,4,128]{3,0,2,1:T(8,128)(2,1)}) %all-gather.8.cloned.1.call-update) | async-done | bytes 6291472 | tf_op jit(solution)/shard_map/all_gather | solution.py:807
  59.6 8.7 copy.178
  68.4 39.4 %all-gather.6.cloned.1.call-done = bf16[512,2048]{1,0:T(8,128)(2,1)} async-done(((bf16[128,2048]{1,0:T(8,128)(2,1)}), bf16[512,2048]{1,0:T(8,128)(2,1)}) %all-gather.6.cloned.1.call-update) | async-done | bytes 2097168 | tf_op jit(solution)/shard_map/all_gather | solution.py:78
  120.6 16.0 %all-gather.10.cloned.1.call-done = bf16[512,2048]{1,0:T(8,128)(2,1)} async-done(((bf16[512,256]{1,0:T(8,128)(2,1)}), bf16[512,2048]{1,0:T(8,128)(2,1)}) %all-gather.10.cloned.1.call-update) | async-done | bytes 2097168 | tf_op jit(solution)/shard_map/all_gather | solution.py:809
  149.1 7.8 all-to-all-done.2
  166.0 14.2 %all-to-all-done = bf16[256,2,1408]{0,1,2:T(2,128)(2,1)S(1)} async-done(((bf16[256,2,1408]{0,1,2:T(2,128)(2,1)}), bf16[256,2,1408]{0,1,2:T(2,128)(2,1)S(1)}, u32[]{:S(2)}, u32[]{:S(2)}) %all-to-all-start) | async-done | bytes 1441824 | tf_op jit(solution)/shard_map/all_to_all | solution.py:810
  185.1 7.2 reduce-scatter.8.cloned.1.call-done
  195.5 120.1 %gather_rows.1 = bf16[4096,2048]{1,0:T(8,128)(2,1)S(1)} custom-call(bf16[128,2048]{1,0:T(8,128)(2,1)S(1)} %get-tuple-element.119.own_ref), custom_call_target="tpu_custom_call" | custom-call | tf_op jit(solution)/shard_map/gather_rows/pallas_call | solution.py:533
  321.8 24.7 %fusion.37 = f32[4096,1056]{0,1:T(8,128)} fusion(bf16[4096,2048]{1,0:T(8,128)(2,1)S(1)} %gather_rows.1, bf16[2048,176]{0,1:T(8,128)(2,1)} %get-tuple-element.133, bf16[2048,352]{0,1:T(8,128)(2,1)} %get-tuple-element.131, bf16[2048,176]{0,1:T(8,128)(2,1)} %get-tuple-element.132, bf16[2048,352]{0,1:T(8,128)(2,1)} %get-tuple-element.130), kind=kOutput, calls=%fused_computation.89 | convolution fusion | flops 17734041600 | bytes 38404096 | tf_op jit(solution)/shard_map/dot_general | solution.py:870
  350.1 28.4 %multiply_convert_fusion.1 = (bf16[4096,528]{0,1:T(8,128)(2,1)}, bf16[4096,528]{0,1:T(8,128)(2,1)}, f32[4096,528]{0,1:T(8,128)}, bf16[4096,528]{0,1:T(8,128)(2,1)}) fusion(f32[4096,1056]{0,1:T(8,128)} %fusion.37, f32[4096,176]{0,1:T(8,128)S(1)} %broadcast_in_dim.132, f32[4096,352]{0,1:T(8,128)} %broadcast_in_dim.131, ...), kind=kOutput, calls=%fused_computation.10 | convolution fusion | flops 8903786496 | bytes 66519040 | tf_op jit(solution)/shard_map/dot_general | solution.py:874
  383.6 16.8 %convolution_convert_fusion.1.refs_0_ = bf16[4096,2048]{1,0:T(8,128)(2,1)} fusion(bf16[4096,528]{0,1:T(8,128)(2,1)S(1)} %copy-done.49, bf16[176,2048]{1,0:T(8,128)(2,1)S(1)} %bitcast.157, bf16[352,2048]{1,0:T(8,128)(2,1)S(1)} %bitcast.166), kind=kOutput, calls=%fused_computation.2 | convolution fusion | flops 8871084032 | bytes 23265280 | tf_op jit(solution)/shard_map/dot_general | solution.py:895
  400.4 99.5 %scatter_rows.2 = f32[128,2048]{1,0:T(8,128)S(1)} custom-call(bf16[4096,2048]{1,0:T(8,128)(2,1)} %convolution_convert_fusion.1.refs_0_), custom_call_target="tpu_custom_call" | custom-call | tf_op jit(solution)/shard_map/scatter_rows/pallas_call | solution.py:757
  500.0 26.8 %convolution_convert_fusion.refs_0_ = bf16[4096,2048]{1,0:T(8,128)(2,1)} fusion(bf16[4096,528]{0,1:T(8,128)(2,1)} %get-tuple-element.121, bf16[4096,528]{0,1:T(8,128)(2,1)} %get-tuple-element.120, bf16[2048,176]{0,1:T(8,128)(2,1)S(1)} %copy-done.29, bf16[2048,352]{0,1:T(8,128)(2,1)S(1)} %copy-done.10, bf16[2048,176]{0,1:T(8,128)(2,1)S(1)} %copy-done.28, ...), kind=kOutput, calls=%fused_computation.1 | convolution fusion | flops 17759731712 | bytes 29753344 | tf_op jit(solution)/shard_map/dot_general | solution.py:883
  526.9 100.4 %scatter_rows.3 = (f32[128,2048]{1,0:T(8,128)S(1)}, f32[32,128]{1,0:T(8,128)S(1)}) custom-call(bf16[4096,2048]{1,0:T(8,128)(2,1)} %convolution_convert_fusion.refs_0_, bf16[1024,128]{1,0:T(8,128)(2,1)S(1)} %bitcast.146), custom_call_target="tpu_custom_call" | custom-call | tf_op jit(solution)/shard_map/scatter_rows/pallas_call | solution.py:757
  630.0 48.2 %all-gather.14.cloned.1.call-done = bf16[512,2048]{1,0:T(8,128)(2,1)} async-done(((bf16[128,2048]{1,0:T(8,128)(2,1)}), bf16[512,2048]{1,0:T(8,128)(2,1)}) %all-gather.14.cloned.1.call-update) | async-done | bytes 2097168 | tf_op jit(solution)/shard_map/all_gather | solution.py:78
  693.9 8.0 bitcast_convert_fusion
  702.9 7.2 convolution_convert_fusion.2
  710.1 24.9 %fusion.60 = (bf16[2048,1056]{0,1:T(8,128)(2,1)S(1)}, f32[2048,1056]{0,1:T(8,128)}) fusion(bf16[4096,2048]{1,0:T(8,128)(2,1)} %copy-done, bf16[4096,528]{0,1:T(8,128)(2,1)} %get-tuple-element.121, bf16[4096,528]{0,1:T(8,128)(2,1)} %get-tuple-element.120), kind=kOutput, calls=%fused_computation.142 | convolution fusion | flops 17736204288 | bytes 38404096 | tf_op jit(solution)/shard_map/dot_general | solution.py:904
  739.1 13.1 %fusion.61 = f32[528,2048]{1,0:T(8,128)S(1)} fusion(bf16[4096,528]{0,1:T(8,128)(2,1)} %get-tuple-element.123, bf16[4096,2048]{1,0:T(8,128)(2,1)} %all-gather.12.cloned.1.call-done), kind=kOutput, calls=%fused_computation.143 | convolution fusion | flops 8858370048 | bytes 25427968 | tf_op jit(solution)/shard_map/dot_general | solution.py:903
  764.3 7.5 all-to-all-done.4
  787.8 15.1 %all-to-all-done.3 = bf16[2048,2,176]{2,1,0:T(2,128)(2,1)} async-done(((bf16[2048,2,176]{2,1,0:T(2,128)(2,1)}), bf16[2048,2,176]{2,1,0:T(2,128)(2,1)}, u32[]{:S(2)}, u32[]{:S(2)}) %all-to-all-start.3) | async-done | bytes 1441824 | tf_op jit(solution)/shard_map/all_to_all | solution.py:909
  818.6 40.1 %all-reduce.3 = (f32[2048]{0:T(1024)S(1)}, f32[2048]{0:T(1024)S(1)}, f32[2048]{0:T(1024)S(1)}) all-reduce(f32[2048]{0:T(1024)S(1)} %get-tuple-element.110, f32[2048]{0:T(1024)S(1)} %get-tuple-element.108, f32[2048]{0:T(1024)S(1)} %get-tuple-element.112), channel_id=4, replica_groups=mesh['fsdp'=8,'tp'=4] {'fsdp','tp'}, use_global_device_ids=true, to_apply=%region_16.17.clone | all-reduce | flops 6144 | bytes 49152
  863.2 19.0 %reduce-scatter.12.cloned.1.call-done = bf16[256,3,4,128]{3,0,2,1:T(8,128)(2,1)} async-done(((bf16[2048,3,4,128]{3,0,2,1:T(8,128)(2,1)}), bf16[256,3,4,128]{3,0,2,1:T(8,128)(2,1)}) %reduce-scatter.12.cloned.1.call-update) | async-done | bytes 786448 | tf_op jit(solution)/shard_map/reduce_scatter | solution.py:958
  (214 shorter events, 138.7 us)
Async XLA Ops:
  8.0 51.6 %all-gather.8.cloned.1.call-start = ((), (), s32[]{:S(2)}) async-start(), calls=%async_computation.11 | async-start | bytes 7077888 | tf_op jit(solution)/shard_map/all_gather | solution.py:807
  10.3 97.5 %all-gather.6.cloned.1.call-start = ((), (), s32[]{:S(2)}) async-start(), calls=%async_computation.10 | async-start | bytes 2621440 | tf_op jit(solution)/shard_map/all_gather | solution.py:78
  13.6 123.0 %all-gather.10.cloned.1.call-start = ((), (), s32[]{:S(2)}) async-start(), calls=%async_computation.12 | async-start | bytes 2359296 | tf_op jit(solution)/shard_map/all_gather | solution.py:809
  14.3 178.0 %reduce-scatter.8.cloned.1.call-start = ((), (), s32[]{:S(2)}) async-start(), calls=%async_computation.13 | async-start | bytes 2621440 | tf_op jit(solution)/shard_map/reduce_scatter | solution.py:82
  140.9 205.7 %all-gather.12.cloned.1.call-start = ((), (), s32[]{:S(2)}) async-start(), calls=%async_computation.14 | async-start | bytes 17301504 | tf_op jit(solution)/shard_map/all_gather | solution.py:806
  141.5 15.5 %all-to-all-start.2 = ((bf16[8,176,256]{2,1,0:T(8,128)(2,1)}), bf16[8,176,256]{2,1,0:T(8,128)(2,1)S(1)}, u32[]{:S(2)}, u32[]{:S(2)}) async-start(bf16[8,176,256]{2,1,0:T(8,128)(2,1)} %bitcast.22), calls=%async_computation.3 | async-start | bytes 1441792 | tf_op jit(solution)/shard_map/all_to_all | solution.py:811
  157.0 23.1 %all-to-all-start = ((bf16[256,2,1408]{0,1,2:T(2,128)(2,1)}), bf16[256,2,1408]{0,1,2:T(2,128)(2,1)S(1)}, u32[]{:S(2)}, u32[]{:S(2)}) async-start(bf16[256,2,1408]{0,1,2:T(2,128)(2,1)} %copy.184), calls=%async_computation.1 | async-start | bytes 2883584 | tf_op jit(solution)/shard_map/all_to_all | solution.py:810
  180.1 166.4 %all-to-all-start.1 = ((f32[8,1,512]{2,1,0:T(1,128)}), f32[8,1,512]{2,1,0:T(1,128)S(1)}, u32[]{:S(2)}, u32[]{:S(2)}) async-start(f32[8,1,512]{2,1,0:T(1,128)} %copy.187), calls=%async_computation.2 | async-start | bytes 32768 | tf_op jit(solution)/shard_map/all_to_all | solution.py:819
  183.5 494.7 %all-gather.14.cloned.1.call-start = ((), (), s32[]{:S(2)}) async-start(), calls=%async_computation.15 | async-start | bytes 2621440 | tf_op jit(solution)/shard_map/all_gather | solution.py:78
  400.4 99.6 %copy-start.10 = (bf16[2048,352]{0,1:T(8,128)(2,1)S(1)}, bf16[2048,352]{0,1:T(8,128)(2,1)}, u32[]{:S(2)}) copy-start(bf16[2048,352]{0,1:T(8,128)(2,1)} %get-tuple-element.131) | copy-start | bytes 4325380
  400.4 99.6 %copy-start.28 = (bf16[2048,176]{0,1:T(8,128)(2,1)S(1)}, bf16[2048,176]{0,1:T(8,128)(2,1)}, u32[]{:S(2)}) copy-start(bf16[2048,176]{0,1:T(8,128)(2,1)} %get-tuple-element.132) | copy-start | bytes 2162692
  400.4 99.7 %copy-start.29 = (bf16[2048,176]{0,1:T(8,128)(2,1)S(1)}, bf16[2048,176]{0,1:T(8,128)(2,1)}, u32[]{:S(2)}) copy-start(bf16[2048,176]{0,1:T(8,128)(2,1)} %get-tuple-element.133) | copy-start | bytes 2162692
  526.9 100.5 %copy-start.44 = (f32[128]{0:T(128)S(1)}, f32[128]{0:T(128)}, u32[]{:S(2)}) copy-start(f32[128]{0:T(128)} %get-tuple-element.118) | copy-start | bytes 1540
  526.9 100.5 %copy-start.2 = (bf16[128,2048]{1,0:T(8,128)(2,1)S(1)}, bf16[128,2048]{1,0:T(8,128)(2,1)}, u32[]{:S(2)}) copy-start(bf16[128,2048]{1,0:T(8,128)(2,1)} %param.15) | copy-start | bytes 1572868
  526.9 100.5 %copy-start.3 = (bf16[128,2048]{1,0:T(8,128)(2,1)S(1)}, bf16[128,2048]{1,0:T(8,128)(2,1)}, u32[]{:S(2)}) copy-start(bf16[128,2048]{1,0:T(8,128)(2,1)} %reduce-scatter.8.cloned.1.call-done) | copy-start | bytes 1572868
  526.9 100.5 %copy-start.32 = (f32[2048]{0:T(1024)S(1)}, f32[2048]{0:T(1024)}, u32[]{:S(2)}) copy-start(f32[2048]{0:T(1024)} %param.21) | copy-start | bytes 24580
  526.9 100.5 %copy-start.43 = (f32[128]{0:T(128)S(1)}, f32[128]{0:T(128)}, u32[]{:S(2)}) copy-start(f32[128]{0:T(128)} %copy-done.42) | copy-start | bytes 1540
  526.9 101.1 %copy-start.7 = (bf16[128,2048]{1,0:T(8,128)(2,1)S(1)}, bf16[128,2048]{1,0:T(8,128)(2,1)}, u32[]{:S(2)}) copy-start(bf16[128,2048]{1,0:T(8,128)(2,1)} %param.16) | copy-start | bytes 1572868
  629.9 183.6 %reduce-scatter.16.cloned.1.call-start = ((), (), s32[]{:S(2)}) async-start(), calls=%async_computation.19 | async-start | bytes 36864
  689.5 125.5 %reduce-scatter.14.cloned.1.call-start = ((), (), s32[]{:S(2)}) async-start(), calls=%async_computation.18 | async-start | bytes 2359296 | tf_op jit(solution)/shard_map/reduce_scatter | solution.py:960
  693.9 123.2 %reduce-scatter.10.cloned.1.call-start = ((), (), s32[]{:S(2)}) async-start(), calls=%async_computation.16 | async-start | bytes 2621440 | tf_op jit(solution)/shard_map/reduce_scatter | solution.py:82
  701.9 180.3 %reduce-scatter.12.cloned.1.call-start = ((), (), s32[]{:S(2)}) async-start(), calls=%async_computation.17 | async-start | bytes 7077888 | tf_op jit(solution)/shard_map/reduce_scatter | solution.py:958
  755.3 16.6 %all-to-all-start.4 = ((bf16[176,8,256]{2,0,1:T(8,128)(2,1)}), bf16[176,8,256]{2,0,1:T(8,128)(2,1)}, u32[]{:S(2)}, u32[]{:S(2)}) async-start(bf16[176,8,256]{2,0,1:T(8,128)(2,1)} %bitcast.145), calls=%async_computation.8 | async-start | bytes 1441792 | tf_op jit(solution)/shard_map/all_to_all | solution.py:918
  771.8 31.0 %all-to-all-start.3 = ((bf16[2048,2,176]{2,1,0:T(2,128)(2,1)}), bf16[2048,2,176]{2,1,0:T(2,128)(2,1)}, u32[]{:S(2)}, u32[]{:S(2)}) async-start(bf16[2048,2,176]{2,1,0:T(2,128)(2,1)} %copy.197), calls=%async_computation.7 | async-start | bytes 4194304 | tf_op jit(solution)/shard_map/all_to_all | solution.py:909
  (41 other events, 719.2 us)
Sparse Core Ops, SparseCore 0:
  11.3 48.2 all-gather.7
  61.8 45.9 all-gather.5
  109.6 26.8 all-gather.9
  141.0 51.2 reduce-scatter.7
  630.0 48.0 all-gather.13
  689.6 29.9 reduce-scatter.15
  722.9 41.7 reduce-scatter.13
  767.0 50.0 reduce-scatter.9
  820.5 61.6 reduce-scatter.11
Sparse Core Ops, SparseCore 1:
  144.8 185.2 all-gather.11

commit v3 on v2

--- a/solution.py
+++ b/solution.py
@@ -373,182 +373,6 @@
     pl.semaphore_wait(barrier, 3 + left + right)
 
 
-def gather_kernel(tp, own_ref, all_ref, local_sem, z_send, z_recv, p_send, p_recv):
-    me, rank = place()
-    greet(me, rank, tp)
-    rows = own_ref.shape[0]
-    half = rows // 2
-    pack_rows = rows * tp
-
-    def region(pack, block, start=0, count=None):
-        count = rows if count is None else count
-        return all_ref.at[pl.ds(pack * pack_rows + block * rows + start, count)]
-
-    def along_z(block, right):
-        way = 0 if right else 1
-        ref = region(me, block)
-        return pltpu.make_async_remote_copy(
-            src_ref=ref,
-            dst_ref=ref,
-            send_sem=z_send.at[way, block],
-            recv_sem=z_recv.at[way, block],
-            device_id=(me, rank + 1 if right else rank - 1),
-            device_id_type=MESH,
-        )
-
-    def across(bit, pack_bits, block, slot, start=0, count=None):
-        pack = me
-        for one in (2, 4):
-            if pack_bits & one:
-                pack = flipped(pack, one)
-        ref = region(pack, block, start, count)
-        return pltpu.make_async_remote_copy(
-            src_ref=ref,
-            dst_ref=ref,
-            send_sem=p_send.at[slot, block],
-            recv_sem=p_recv.at[slot, block],
-            device_id=(flipped(me, bit), rank),
-            device_id_type=MESH,
-        )
-
-    def own_x(block):
-        return across(2, 0, block, 0)
-
-    def own_y(block):
-        return across(4, 0, block, 1)
-
-    def own_core(block):
-        return across(1, 0, block, 2)
-
-    def x_to_y(block):
-        return across(4, 2, block, 3, 0, half)
-
-    def x_to_core(block):
-        return across(1, 2, block, 4)
-
-    def y_to_x(block):
-        return across(2, 4, block, 5, half, half)
-
-    def y_to_core(block):
-        return across(1, 4, block, 6)
-
-    def diag_to_core(block):
-        return across(1, 6, block, 7)
-
-    def start_plane(block):
-        own_x(block).start()
-        own_y(block).start()
-        own_core(block).start()
-
-    def forward(block):
-        own_x(block).wait_recv()
-        x_to_y(block).start()
-        x_to_core(block).start()
-        own_y(block).wait_recv()
-        y_to_x(block).start()
-        y_to_core(block).start()
-
-    def finish(block):
-        x_to_y(block).wait_recv()
-        y_to_x(block).wait_recv()
-        diag_to_core(block).start()
-
-    def z_step(step):
-        @pl.when(rank >= step)
-        def _():
-            block = rank - step
-            along_z(block, True).wait_recv()
-
-            @pl.when(rank < tp - 1)
-            def _():
-                along_z(block, True).start()
-
-            start_plane(block)
-
-        @pl.when(rank + step < tp)
-        def _():
-            block = rank + step
-            along_z(block, False).wait_recv()
-
-            @pl.when(rank > 0)
-            def _():
-                along_z(block, False).start()
-
-            start_plane(block)
-
-    mine = pltpu.make_async_copy(own_ref, region(me, rank), local_sem)
-    mine.start()
-    mine.wait()
-
-    @pl.when(rank < tp - 1)
-    def _():
-        along_z(rank, True).start()
-
-    @pl.when(rank > 0)
-    def _():
-        along_z(rank, False).start()
-
-    start_plane(rank)
-    order = [rank]
-    for bit in (1, 2):
-        order = order + [flipped(one, bit) for one in order]
-    z_step(1)
-    forward(order[0])
-    z_step(2)
-    forward(order[1])
-    finish(order[0])
-    z_step(3)
-    forward(order[2])
-    finish(order[1])
-    forward(order[3])
-    finish(order[2])
-    finish(order[3])
-    for block in order:
-        own_core(block).wait_recv()
-        x_to_core(block).wait_recv()
-        y_to_core(block).wait_recv()
-        diag_to_core(block).wait_recv()
-    for block in order:
-        own_x(block).wait_send()
-        own_y(block).wait_send()
-        own_core(block).wait_send()
-        x_to_y(block).wait_send()
-        x_to_core(block).wait_send()
-        y_to_x(block).wait_send()
-        y_to_core(block).wait_send()
-        diag_to_core(block).wait_send()
-    for block in range(tp):
-
-        @pl.when((block <= rank) & (rank < tp - 1))
-        def _():
-            along_z(block, True).wait_send()
-
-        @pl.when((block >= rank) & (rank > 0))
-        def _():
-            along_z(block, False).wait_send()
-
-
-def gather_everywhere(own, fsdp, tp, collective_id):
-    rows, width = own.shape
-    return pl.pallas_call(
-        functools.partial(gather_kernel, tp),
-        out_shape=jax.ShapeDtypeStruct((fsdp * tp * rows, width), own.dtype),
-        in_specs=[pl.BlockSpec(memory_space=pl.ANY)],
-        out_specs=pl.BlockSpec(memory_space=pl.ANY),
-        scratch_shapes=[
-            pltpu.SemaphoreType.DMA,
-            pltpu.SemaphoreType.DMA((2, tp)),
-            pltpu.SemaphoreType.DMA((2, tp)),
-            pltpu.SemaphoreType.DMA((8, tp)),
-            pltpu.SemaphoreType.DMA((8, tp)),
-        ],
-        compiler_params=pltpu.CompilerParams(
-            collective_id=collective_id, has_side_effects=True, vmem_limit_bytes=16 << 20
-        ),
-        name="gather_rows",
-    )(own)
-
-
 def scatter_kernel(tp, parts, *refs):
     ins = refs[:parts]
     outs = refs[parts : 2 * parts]
@@ -776,6 +600,626 @@
     )(*arrays)
 
 
+UNIT = 640
+NT = (((1,), (1,)), ((), ()))
+
+
+def ffn_kernel(tp, expert_width, shared_width, *refs):
+    own_ref, grad_ref, both_ref, down_ref, scale_ref = refs[:5]
+    all_ref, d_ref, hid_ref, y_ref, dsum_ref, esum_ref = refs[5:11]
+    (
+        g_buf, x_buf, dh_buf, d_buf, h_buf, stage, acc, diag_in, last_in, z_in,
+        stage_e, acc_e, other_e, diag_e, last_e, z_in_e,
+        local_sem, g_sem, x_sem, d_sem, h_sem, y_sem,
+        az_send, az_recv, ap_send, ap_recv,
+        c_send, c_recv, ce_send, ce_recv, p_send, p_recv, pe_send, pe_recv,
+        z_send, z_recv, ze_send, ze_recv,
+    ) = refs[11:]
+    me, rank = place()
+    greet(me, rank, tp)
+    f32 = jnp.float32
+    bf16 = jnp.bfloat16
+    rows = own_ref.shape[0]
+    pack_rows = rows * tp
+    tile = pack_rows // 2
+    near = rank // 2
+    tokens = all_ref.shape[0]
+
+    def region(pack, block, start=0, count=None):
+        count = rows if count is None else count
+        return all_ref.at[pl.ds(pack * pack_rows + block * rows + start, count)]
+
+    def gather_z(block, right):
+        way = 0 if right else 1
+        ref = region(me, block)
+        return pltpu.make_async_remote_copy(
+            src_ref=ref,
+            dst_ref=ref,
+            send_sem=az_send.at[way, block],
+            recv_sem=az_recv.at[way, block],
+            device_id=(me, rank + 1 if right else rank - 1),
+            device_id_type=MESH,
+        )
+
+    def gather(bit, pack_bits, block, slot, start=0, count=None):
+        pack = me
+        for one in (2, 4):
+            if pack_bits & one:
+                pack = flipped(pack, one)
+        ref = region(pack, block, start, count)
+        return pltpu.make_async_remote_copy(
+            src_ref=ref,
+            dst_ref=ref,
+            send_sem=ap_send.at[slot, block],
+            recv_sem=ap_recv.at[slot, block],
+            device_id=(flipped(me, bit), rank),
+            device_id_type=MESH,
+        )
+
+    def to_core(q, block):
+        return gather(1, 2 * q, block, q)
+
+    def own_x(block):
+        return gather(2, 0, block, 4)
+
+    def own_y(block):
+        return gather(4, 0, block, 5)
+
+    def x_to_y(block):
+        return gather(4, 2, block, 6, 0, rows // 2)
+
+    def y_to_x(block):
+        return gather(2, 4, block, 7, rows // 2, rows // 2)
+
+    def start_plane(block):
+        own_x(block).start()
+        own_y(block).start()
+        to_core(0, block).start()
+
+    def forward(block):
+        own_x(block).wait_recv()
+        x_to_y(block).start()
+        to_core(1, block).start()
+        own_y(block).wait_recv()
+        y_to_x(block).start()
+        to_core(2, block).start()
+
+    def finish(block):
+        x_to_y(block).wait_recv()
+        y_to_x(block).wait_recv()
+        to_core(3, block).start()
+
+    def z_step(step):
+        @pl.when(rank >= step)
+        def _():
+            block = rank - step
+            gather_z(block, True).wait_recv()
+
+            @pl.when(rank < tp - 1)
+            def _():
+                gather_z(block, True).start()
+
+            start_plane(block)
+
+        @pl.when(rank + step < tp)
+        def _():
+            block = rank + step
+            gather_z(block, False).wait_recv()
+
+            @pl.when(rank > 0)
+            def _():
+                gather_z(block, False).start()
+
+            start_plane(block)
+
+    order = [rank]
+    for bit in (1, 2):
+        order = order + [flipped(one, bit) for one in order]
+
+    def control(i):
+        steps = {
+            0: [(forward, order[0])],
+            1: [(z_step, 2), (forward, order[1])],
+            2: [(z_step, 3)],
+            3: [(finish, order[0])],
+            4: [(finish, order[1])],
+            5: [(forward, order[2])],
+            7: [(forward, order[3])],
+            8: [(finish, order[2])],
+            11: [(finish, order[3])],
+        }
+        for at, todo in steps.items():
+
+            @pl.when(i == at)
+            def _():
+                for act, what in todo:
+                    act(what)
+
+    def core(q, h):
+        return pltpu.make_async_remote_copy(
+            src_ref=stage.at[h],
+            dst_ref=acc.at[q, h],
+            send_sem=c_send.at[q, h],
+            recv_sem=c_recv.at[q, h],
+            device_id=(flipped(me, 1), rank),
+            device_id_type=MESH,
+        )
+
+    def core_e(q):
+        return pltpu.make_async_remote_copy(
+            src_ref=stage_e.at[q],
+            dst_ref=other_e.at[q],
+            send_sem=ce_send.at[q],
+            recv_sem=ce_recv.at[q],
+            device_id=(flipped(me, 1), rank),
+            device_id_type=MESH,
+        )
+
+    def across(bit, src, dst, slot, h):
+        return pltpu.make_async_remote_copy(
+            src_ref=src,
+            dst_ref=dst,
+            send_sem=p_send.at[slot, h],
+            recv_sem=p_recv.at[slot, h],
+            device_id=(flipped(me, bit), rank),
+            device_id_type=MESH,
+        )
+
+    def diag_x(h):
+        return across(2, acc.at[3, h, 0], diag_in.at[h, 0], 0, h)
+
+    def diag_y(h):
+        return across(4, acc.at[3, h, 1], diag_in.at[h, 1], 1, h)
+
+    def direct_x(h):
+        return across(2, acc.at[1, h, 0], last_in.at[h, 0, 0], 2, h)
+
+    def direct_y(h):
+        return across(4, acc.at[2, h, 1], last_in.at[h, 1, 1], 3, h)
+
+    def summed_x(h):
+        return across(2, acc.at[1, h, 1], last_in.at[h, 0, 1], 4, h)
+
+    def summed_y(h):
+        return across(4, acc.at[2, h, 0], last_in.at[h, 1, 0], 5, h)
+
+    def across_e(bit, src, dst, slot):
+        return pltpu.make_async_remote_copy(
+            src_ref=src,
+            dst_ref=dst,
+            send_sem=pe_send.at[slot],
+            recv_sem=pe_recv.at[slot],
+            device_id=(flipped(me, bit), rank),
+            device_id_type=MESH,
+        )
+
+    def diag_lines():
+        return across_e(2, acc_e.at[3], diag_e, 0)
+
+    def direct_lines():
+        return across_e(2, acc_e.at[1], last_e.at[0], 1)
+
+    def summed_lines():
+        return across_e(4, acc_e.at[2], last_e.at[1], 2)
+
+    blocks = order[::-1]
+
+    def along_z(j, right):
+        way = 0 if right else 1
+        block = blocks[j]
+        return pltpu.make_async_remote_copy(
+            src_ref=acc.at[0, j // 2, block % 2],
+            dst_ref=z_in.at[way, block],
+            send_sem=z_send.at[way, block],
+            recv_sem=z_recv.at[way, block],
+            device_id=(me, rank + 1 if right else rank - 1),
+            device_id_type=MESH,
+        )
+
+    def along_z_e(j, right):
+        way = 0 if right else 1
+        block = blocks[j]
+        return pltpu.make_async_remote_copy(
+            src_ref=acc_e.at[0, block],
+            dst_ref=z_in_e.at[way, block],
+            send_sem=ze_send.at[way, block],
+            recv_sem=ze_recv.at[way, block],
+            device_id=(me, rank + 1 if right else rank - 1),
+            device_id_type=MESH,
+        )
+
+    def add(ref, spot, one):
+        ref[spot] = (ref[spot].astype(f32) + one.astype(f32)).astype(ref.dtype)
+
+    def second(h):
+        diag_x(h).wait_recv()
+        add(acc, (2, h, 0), diag_in[h, 0])
+        summed_y(h).start()
+        diag_y(h).wait_recv()
+        add(acc, (1, h, 1), diag_in[h, 1])
+        summed_x(h).start()
+
+    def third(j):
+        h = j // 2
+        block = blocks[j]
+        part = block % 2
+        if j % 2 == 0:
+            direct_x(h).wait_recv()
+            direct_y(h).wait_recv()
+            summed_x(h).wait_recv()
+            summed_y(h).wait_recv()
+        if j == 0:
+            direct_lines().wait_recv()
+            summed_lines().wait_recv()
+        total = (
+            acc[0, h, part].astype(f32)
+            + last_in[h, 0, part].astype(f32)
+            + last_in[h, 1, part].astype(f32)
+        )
+        lines = acc_e[0, block] + last_e[0, block] + last_e[1, block]
+        if j < tp - 1:
+            acc[0, h, part] = total.astype(bf16)
+            acc_e[0, block] = lines
+
+            @pl.when((block > rank) & (rank > 0))
+            def _():
+                along_z(j, True).wait_recv()
+                along_z_e(j, True).wait_recv()
+                add(acc, (0, h, part), z_in[0, block])
+                add(acc_e, (0, block), z_in_e[0, block])
+
+            @pl.when((block < rank) & (rank < tp - 1))
+            def _():
+                along_z(j, False).wait_recv()
+                along_z_e(j, False).wait_recv()
+                add(acc, (0, h, part), z_in[1, block])
+                add(acc_e, (0, block), z_in_e[1, block])
+
+            @pl.when(block > rank)
+            def _():
+                along_z(j, True).start()
+                along_z_e(j, True).start()
+
+            @pl.when(block < rank)
+            def _():
+                along_z(j, False).start()
+                along_z_e(j, False).start()
+        else:
+            dsum_ref[...] = total
+            esum_ref[...] = lines
+
+            @pl.when(rank > 0)
+            def _():
+                along_z(j, True).wait_recv()
+                along_z_e(j, True).wait_recv()
+                dsum_ref[...] += z_in[0, block].astype(f32)
+                esum_ref[...] += z_in_e[0, block]
+
+            @pl.when(rank < tp - 1)
+            def _():
+                along_z(j, False).wait_recv()
+                along_z_e(j, False).wait_recv()
+                dsum_ref[...] += z_in[1, block].astype(f32)
+                esum_ref[...] += z_in_e[1, block]
+
+    def grad_load(n, slot):
+        return pltpu.make_async_copy(
+            grad_ref.at[pl.ds(n * pack_rows, pack_rows)], g_buf.at[slot], g_sem.at[slot]
+        )
+
+    def hidden_grads(first, last):
+        def body(n, carry):
+            slot = n % 2
+
+            @pl.when(n + 1 < tokens // pack_rows)
+            def _():
+                grad_load(n + 1, 1 - slot).start()
+
+            grad_load(n, slot).wait()
+            dh_buf[pl.ds(n * pack_rows, pack_rows), :] = lax.dot_general(
+                g_buf[slot], down_ref[...], NT, preferred_element_type=f32
+            ).astype(bf16)
+            return carry
+
+        lax.fori_loop(first, last, body, 0)
+
+    core_of, x_of, y_of = me % 2, (me // 2) % 2, me // 4
+
+    def tile_of(i):
+        t = i // 2
+        o = i % 2
+        s = t // 6
+        q = (1 - s) * (t % 3) + 3 * s
+        h = (1 - s) * (1 - t // 3) + s * (t - 6)
+        pack = (
+            4 * ((y_of + q // 2) % 2) + 2 * ((x_of + q % 2) % 2) + (core_of + 1 - o) % 2
+        )
+        half = h * near + (1 - h) * (1 - near)
+        return q, o, h, pack, half
+
+    def tile_rows(pack, half):
+        return pl.ds(pl.multiple_of(pack * pack_rows + half * tile, tile), tile)
+
+    def row_load(i):
+        q, o, h, pack, half = tile_of(i)
+        return pltpu.make_async_copy(
+            all_ref.at[tile_rows(pack, half)], x_buf.at[i % 2], x_sem.at[i % 2]
+        )
+
+    def prefetch(i):
+        q, o, h, pack, half = tile_of(i)
+
+        @pl.when(o == 0)
+        def _():
+            for part in range(2):
+                block = 2 * half + part
+                ref = region(pack, block)
+                pltpu.make_async_remote_copy(
+                    src_ref=ref,
+                    dst_ref=ref,
+                    send_sem=ap_send.at[q, block],
+                    recv_sem=ap_recv.at[q, block],
+                    device_id=(flipped(me, 1), rank),
+                    device_id_type=MESH,
+                ).wait_recv()
+
+        row_load(i).start()
+
+    def d_store(i):
+        q, o, h, pack, half = tile_of(i)
+        return pltpu.make_async_copy(
+            d_buf.at[i % 2], d_ref.at[tile_rows(pack, half)], d_sem.at[i % 2]
+        )
+
+    units = expert_width + shared_width
+
+    def one_tile(i, carry):
+        q, o, h, pack, half = tile_of(i)
+        slot = i % 2
+        at = tile_rows(pack, half)
+        row_load(i).wait()
+
+        @pl.when(i >= 2)
+        def _():
+            d_store(i - 2).wait()
+
+        pre = jnp.dot(x_buf[slot], both_ref[...], preferred_element_type=f32)
+        gate, upper = pre[:, :UNIT], pre[:, UNIT:]
+        lane = lax.broadcasted_iota(jnp.int32, (1, UNIT), 1)
+        logit = gate[:, units : units + 1] + gate[:, units + 1 : units + 2]
+        gate_prob = 1.0 / (1.0 + jnp.exp(-logit))
+        scale = jnp.where(
+            lane < expert_width, scale_ref[at, :], jnp.where(lane < units, gate_prob, 0.0)
+        )
+        sigmoid = 1.0 / (1.0 + jnp.exp(-gate))
+        act = gate * sigmoid
+        slope = sigmoid * (1.0 + gate * (1.0 - sigmoid))
+        hidden = act * upper
+        d_hidden = dh_buf[at, :].astype(f32)
+        line = lax.broadcasted_iota(jnp.int32, (16, UNIT), 0)
+        unit = lax.broadcasted_iota(jnp.int32, (16, UNIT), 1)
+        of_expert = (line == me) & (unit < expert_width)
+        of_shared = (line == 8) & (unit >= expert_width)
+        pick = jnp.where(of_expert | of_shared, 1.0, 0.0).astype(bf16)
+        lines = lax.dot_general(
+            pick, (d_hidden * hidden).astype(bf16), NT, preferred_element_type=f32
+        )
+        h_buf[at, :] = (hidden * scale).astype(bf16)
+        d_scaled = d_hidden * scale
+        d_buf[slot, :, :UNIT] = (d_scaled * upper * slope).astype(bf16)
+        d_buf[slot, :, UNIT:] = (d_scaled * act).astype(bf16)
+        control(i)
+
+        @pl.when(i < 15)
+        def _():
+            prefetch(i + 1)
+
+        d_rows = lax.dot_general(d_buf[slot], both_ref[...], NT, preferred_element_type=f32)
+        d_store(i).start()
+
+        @pl.when(o == 0)
+        def _():
+            @pl.when(q > 0)
+            def _():
+                core(q - 1, h).wait_send()
+
+            for part in range(2):
+                stage[h, part] = d_rows[part * rows : (part + 1) * rows].astype(bf16)
+                stage_e[q, 2 * half + part] = lines[:, part * rows : (part + 1) * rows]
+            core(q, h).start()
+
+            @pl.when(((h == 0) & (q < 3)) | ((h == 1) & (q == 3)))
+            def _():
+                core_e(q).start()
+
+        @pl.when(o == 1)
+        def _():
+            core(q, h).wait_recv()
+            for part in range(2):
+                add(acc, (q, h, part), d_rows[part * rows : (part + 1) * rows])
+                acc_e[q, 2 * half + part] = lines[:, part * rows : (part + 1) * rows]
+
+            @pl.when(((h == 0) & (q < 3)) | ((h == 1) & (q == 3)))
+            def _():
+                core_e(q).wait_recv()
+                acc_e[q] = acc_e[q] + other_e[q]
+
+                @pl.when(q == 1)
+                def _():
+                    direct_lines().start()
+
+                @pl.when(q == 3)
+                def _():
+                    diag_lines().start()
+
+            @pl.when(q == 1)
+            def _():
+                direct_x(h).start()
+
+            @pl.when(q == 2)
+            def _():
+                direct_y(h).start()
+
+            @pl.when(q == 3)
+            def _():
+                diag_x(h).start()
+                diag_y(h).start()
+
+        return carry
+
+    def y_store(n, slot):
+        return pltpu.make_async_copy(
+            g_buf.at[slot], y_ref.at[pl.ds(n * pack_rows, pack_rows)], y_sem.at[slot]
+        )
+
+    def outputs(first, last):
+        def body(n, carry):
+            slot = n % 2
+
+            @pl.when(n >= 2)
+            def _():
+                y_store(n - 2, slot).wait()
+
+            g_buf[slot] = jnp.dot(
+                h_buf[pl.ds(n * pack_rows, pack_rows), :],
+                down_ref[...],
+                preferred_element_type=f32,
+            ).astype(bf16)
+            y_store(n, slot).start()
+            return carry
+
+        lax.fori_loop(first, last, body, 0)
+
+    grad_load(0, 0).start()
+    mine = pltpu.make_async_copy(own_ref, region(me, rank), local_sem)
+    mine.start()
+    mine.wait()
+
+    @pl.when(rank < tp - 1)
+    def _():
+        gather_z(rank, True).start()
+
+    @pl.when(rank > 0)
+    def _():
+        gather_z(rank, False).start()
+
+    start_plane(rank)
+    packs = tokens // pack_rows
+    hidden_grads(0, 5)
+    z_step(1)
+    hidden_grads(5, packs)
+    prefetch(0)
+    lax.fori_loop(0, 16, one_tile, 0)
+    hidden_store = pltpu.make_async_copy(h_buf, hid_ref, h_sem)
+    hidden_store.start()
+    outputs(0, 4)
+    second(0)
+    outputs(4, 6)
+    diag_lines().wait_recv()
+    acc_e[2] = acc_e[2] + diag_e[...]
+    summed_lines().start()
+    second(1)
+    outputs(6, packs)
+    third(0)
+    third(1)
+    third(2)
+    third(3)
+
+    hidden_store.wait()
+    for n in (packs - 2, packs - 1):
+        y_store(n, n % 2).wait()
+    for i in (14, 15):
+        d_store(i).wait()
+    core(3, 0).wait_send()
+    core(3, 1).wait_send()
+    for q in range(4):
+        core_e(q).wait_send()
+    for copy in (diag_lines, direct_lines, summed_lines):
+        copy().wait_send()
+    for h in range(2):
+        for copy in (diag_x, diag_y, direct_x, direct_y, summed_x, summed_y):
+            copy(h).wait_send()
+    for block in order:
+        for q in range(4):
+            to_core(q, block).wait_send()
+        for copy in (own_x, own_y, x_to_y, y_to_x):
+            copy(block).wait_send()
+    for j in range(tp - 1):
+        block = blocks[j]
+
+        @pl.when(block > rank)
+        def _():
+            along_z(j, True).wait_send()
+            along_z_e(j, True).wait_send()
+
+        @pl.when(block < rank)
+        def _():
+            along_z(j, False).wait_send()
+            along_z_e(j, False).wait_send()
+
+    for block in range(tp):
+
+        @pl.when((block <= rank) & (rank < tp - 1))
+        def _():
+            gather_z(block, True).wait_send()
+
+        @pl.when((block >= rank) & (rank > 0))
+        def _():
+            gather_z(block, False).wait_send()
+
+
+def ffn(own, grad_all, both, down, scale, fsdp, tp, expert_width, shared_width, collective_id):
+    rows, width = own.shape
+    tokens = rows * fsdp * tp
+    pack_rows = rows * tp
+    tile = pack_rows // 2
+    bf16 = jnp.bfloat16
+    f32 = jnp.float32
+    dma = pltpu.SemaphoreType.DMA
+    anywhere = pl.BlockSpec(memory_space=pl.ANY)
+    vmem = pl.BlockSpec(memory_space=pltpu.VMEM)
+    return pl.pallas_call(
+        functools.partial(ffn_kernel, tp, expert_width, shared_width),
+        out_shape=[
+            jax.ShapeDtypeStruct((tokens, width), bf16),
+            jax.ShapeDtypeStruct((tokens, 2 * UNIT), bf16),
+            jax.ShapeDtypeStruct((tokens, UNIT), bf16),
+            jax.ShapeDtypeStruct((tokens, width), bf16),
+            jax.ShapeDtypeStruct((rows, width), f32),
+            jax.ShapeDtypeStruct((16, rows), f32),
+        ],
+        in_specs=[anywhere, anywhere, vmem, vmem, vmem],
+        out_specs=[anywhere, anywhere, anywhere, anywhere, vmem, vmem],
+        scratch_shapes=[
+            pltpu.VMEM((2, pack_rows, width), bf16),
+            pltpu.VMEM((2, tile, width), bf16),
+            pltpu.VMEM((tokens, UNIT), bf16),
+            pltpu.VMEM((2, tile, 2 * UNIT), bf16),
+            pltpu.VMEM((tokens, UNIT), bf16),
+            pltpu.VMEM((2, 2, rows, width), bf16),
+            pltpu.VMEM((4, 2, 2, rows, width), bf16),
+            pltpu.VMEM((2, 2, rows, width), bf16),
+            pltpu.VMEM((2, 2, 2, rows, width), bf16),
+            pltpu.VMEM((2, tp, rows, width), bf16),
+            pltpu.VMEM((4, tp, 16, rows), f32),
+            pltpu.VMEM((4, tp, 16, rows), f32),
+            pltpu.VMEM((4, tp, 16, rows), f32),
+            pltpu.VMEM((tp, 16, rows), f32),
+            pltpu.VMEM((2, tp, 16, rows), f32),
+            pltpu.VMEM((2, tp, 16, rows), f32),
+            dma, dma((2,)), dma((2,)), dma((2,)), dma, dma((2,)),
+            dma((2, tp)), dma((2, tp)), dma((8, tp)), dma((8, tp)),
+            dma((4, 2)), dma((4, 2)), dma((4,)), dma((4,)),
+            dma((6, 2)), dma((6, 2)), dma((3,)), dma((3,)),
+            dma((2, tp)), dma((2, tp)), dma((2, tp)), dma((2, tp)),
+        ],
+        compiler_params=pltpu.CompilerParams(
+            collective_id=collective_id, has_side_effects=True, vmem_limit_bytes=61 << 20
+        ),
+        name="ffn",
+    )(own, grad_all, both, down, scale)
+
+
 def dense_plan(
     hidden_in,
     out_grad,
@@ -851,48 +1295,37 @@
     middle = hidden_float + head_total(jnp.dot(heads_out, out_full, preferred_element_type=f32))
     ffn_inverse = inverse_rms(middle)
     normed_two_own = (middle * ffn_inverse * ffn_gain).astype(bf16)
-    normed_all = gather_everywhere(normed_two_own, experts, lax.axis_size("tp"), 1)
-
-    gate_w = jnp.concatenate([expert_up[:, 0], shared_up[:, 0]], axis=1)
-    upper_w = jnp.concatenate([expert_up[:, 1], shared_up[:, 1]], axis=1)
-    both_w = jnp.concatenate([gate_w, upper_w], axis=1)
-    down_w = jnp.concatenate([expert_dn, shared_dn], axis=0)
+
+    vec_high = shared_gate_vec.astype(bf16)
+    vec_low = (shared_gate_vec - vec_high.astype(f32)).astype(bf16)
     units = expert_width + shared_width
-    gate_logit = jnp.sum(normed_all.astype(f32) * shared_gate_vec, axis=-1)
-    gate_prob = jax.nn.sigmoid(gate_logit)
-    scale = jnp.concatenate(
+    none = jnp.zeros((model_width, UNIT - units), bf16)
+    both_w = jnp.concatenate(
         [
-            jnp.broadcast_to(expert_scale[:, None], (expert_scale.shape[0], expert_width)),
-            jnp.broadcast_to(gate_prob[:, None], (expert_scale.shape[0], shared_width)),
+            expert_up[:, 0],
+            shared_up[:, 0],
+            vec_high[:, None],
+            vec_low[:, None],
+            none[:, 2:],
+            expert_up[:, 1],
+            shared_up[:, 1],
+            none,
         ],
         axis=1,
     )
-    pre = jnp.dot(normed_all, both_w, preferred_element_type=f32)
-    act, slope = silu_parts(pre[:, :units])
-    upper = pre[:, units:]
-    hidden = act * upper
-    d_hidden = jnp.dot(grad_all, down_w.T, preferred_element_type=f32)
-    agree = d_hidden * hidden
-    route_part = jnp.sum(agree[:, :expert_width], axis=1)
-    gate_part = jnp.sum(agree[:, expert_width:], axis=1)
-    hidden_s = (hidden * scale).astype(bf16)
-    d_scaled = d_hidden * scale
-    d_both = jnp.concatenate(
-        [(d_scaled * upper * slope).astype(bf16), (d_scaled * act).astype(bf16)], axis=1
-    )
-    d_normed_part = jnp.dot(d_both, both_w.T, preferred_element_type=f32).astype(bf16)
-    lines = jnp.arange(16, dtype=jnp.int32)[None, :, None]
-    route_lines = route_part.reshape(-1, 1, own_rows)
-    gate_lines = gate_part.reshape(-1, 1, own_rows)
-    extra = jnp.where(lines == lax.axis_index("fsdp"), route_lines, 0.0) + jnp.where(
-        lines == experts, gate_lines, 0.0
-    )
-    extra_high = extra.astype(bf16)
-    extra_low = (extra - extra_high.astype(f32)).astype(bf16)
-    extra = jnp.concatenate([extra_high, extra_low], axis=1).reshape(-1, own_rows)
-    d_normed_two, extra_sum = scatter_sum([d_normed_part, extra], experts, lax.axis_size("tp"), 2)
-    extra_sum = extra_sum[:16] + extra_sum[16:]
-    token_part = jnp.dot(hidden_s, down_w, preferred_element_type=f32).astype(bf16)
+    down_w = jnp.concatenate([expert_dn, shared_dn, none.T], axis=0)
+    normed_all, d_all, hidden_all, token_part, d_normed_two, extra_sum = ffn(
+        normed_two_own,
+        grad_all,
+        both_w,
+        down_w,
+        expert_scale[:, None],
+        experts,
+        lax.axis_size("tp"),
+        expert_width,
+        shared_width,
+        1,
+    )
     (total,) = scatter_sum([token_part], experts, lax.axis_size("tp"), 3)
     hidden_out = (middle + total).astype(bf16)
     own_start = tp_rank * own_rows
@@ -900,23 +1333,23 @@
     picked = ids_own[:, :, None] == jnp.arange(experts, dtype=jnp.int32)
     route_grad = jnp.sum(jnp.where(picked, extra_sum[:experts].T[:, None, :], 0.0), axis=-1)
     gate_grad = extra_sum[experts]
-    g_down = jnp.dot(hidden_s.T, grad_all, preferred_element_type=f32)
-    g_both = jnp.dot(normed_all.T, d_both, preferred_element_type=f32)
+    g_down = jnp.dot(hidden_all.T, grad_all, preferred_element_type=f32)
+    g_both = jnp.dot(normed_all.T, d_all, preferred_element_type=f32)
     g_expert_down = g_down[:expert_width][None]
     g_expert_gate_up = jnp.stack(
-        [g_both[:, :expert_width], g_both[:, units : units + expert_width]], axis=1
+        [g_both[:, :expert_width], g_both[:, UNIT : UNIT + expert_width]], axis=1
     )[None]
     g_shared_gate_up = lax.all_to_all(
-        jnp.stack([g_both[:, expert_width:units], g_both[:, units + expert_width :]], axis=1).astype(
-            bf16
-        ),
+        jnp.stack(
+            [g_both[:, expert_width:units], g_both[:, UNIT + expert_width : UNIT + units]], axis=1
+        ).astype(bf16),
         "fsdp",
         split_axis=0,
         concat_axis=2,
         tiled=True,
     ).astype(f32)
     g_shared_down = lax.all_to_all(
-        g_down[expert_width:].astype(bf16), "fsdp", split_axis=1, concat_axis=0, tiled=True
+        g_down[expert_width:units].astype(bf16), "fsdp", split_axis=1, concat_axis=0, tiled=True
     ).astype(f32)
 
     own_gate = jax.nn.sigmoid(jnp.sum(normed_two_own.astype(f32) * shared_gate_vec, axis=-1))

time: 902 us -> 873 us (0.968)
  matrix products: 176 us -> 86.3 us
  waiting for transfers between devices: 209 us -> 254 us
  local copies, waits for them, and re-layouts: 63 us -> 79.3 us
    pallas_call x1, Pallas kernels: 120 us -> 221 us  [ffn(): pl.pallas_call(functools.partial(ffn_kernel, tp, expert_width, shared_wid...]
    pallas_call x2 -> x1, Pallas kernels: 200 us -> 101 us  [scatter_sum(): pl.pallas_call(functools.partial(scatter_kernel, tp, parts), out_shape=[j...]
    dot_general x6 -> x2, matrix products: 135 us -> 44.9 us  [the longest x1 29.4 us: dense_plan(): g_both = jnp.dot(normed_all.T, d_all, preferred_element_type=f32)]
    all_gather x1, waiting for transfers between devices: 0.03 us -> 74.1 us  [dense_plan(): grad_all = lax.all_gather(out_grad, every, axis=0, tiled=True)]
    reduce_scatter x1, waiting for transfers between devices: 19 us -> 7.63 us  [dense_plan(): lax.psum_scatter(g_qkv.astype(bf16), 'fsdp', scatter_dimension=0, tiled=T...]
    concatenate x0 -> x2, local copies, waits for them, and re-layouts: none -> 10.8 us  [the longest x1 10.7 us: dense_plan(): jnp.concatenate([expert_up[:, 0], shared_up[:, 0], vec_high[:, None], vec...]
    reduce_sum x3 -> x0, other arithmetic: 10 us -> none  [the longest x1 5.01 us: dense_plan(): gate_logit = jnp.sum(normed_all.astype(f32) * shared_gate_vec, axis=-1)]
    unnamed x112 -> x89, local copies, waits for them, and re-layouts: 23.7 us -> 25.4 us
  transfers between devices with their start and end apart: 15 -> 14, of which waited for: 11 -> 10; matrix products, arithmetic and copies ran while one was open for 19% -> 20% of each run, Pallas kernels for 13% -> 0%
where the time goes in v3:
time: 873 us; the launch traced here: 864 us
  Pallas kernels  322 us (37%)
  waiting for transfers between devices  254 us (29%)
  matrix products  86.3 us (10%)
  local copies, waits for them, and re-layouts  79.3 us (9%)
  blocking collectives  56.5 us (6%)
  other arithmetic  31.9 us (4%)
  starting transfers between devices  17.6 us (2%)
  between operations  16.5 us (2%)
    pallas_call x1, Pallas kernels, ffn(): pl.pallas_call(functools.partial(ffn_kernel, tp, expert_width, shared_wid...  221 us
    pallas_call x1, Pallas kernels, scatter_sum(): pl.pallas_call(functools.partial(scatter_kernel, tp, parts), out_shape=[j...  101 us
    all_gather x2, waiting for transfers between devices, spread(): return lax.all_gather(rows, 'tp', axis=0, tiled=True)  83.3 us
    all_gather x1, waiting for transfers between devices, dense_plan(): grad_all = lax.all_gather(out_grad, every, axis=0, tiled=True)  74.1 us
    unnamed x1, blocking collectives  38.4 us
    all_gather x1, waiting for transfers between devices, dense_plan(): qkv_full = lax.all_gather(qkv_weight, 'fsdp', axis=0, tiled=True)  33.8 us
    dot_general x1, matrix products, dense_plan(): g_both = jnp.dot(normed_all.T, d_all, preferred_element_type=f32)  29.4 us
    unnamed x89, local copies, waits for them, and re-layouts  25.4 us
  transfers between devices with their start and end apart: 14, of which 10 were waited for; matrix products, arithmetic and copies ran while one was open for 20% of the time, Pallas kernels for 0%

profile of v3, /device:TPU:0, one launch (start us, length us, event | category | flops | bytes accessed | tf_op | source)
XLA Modules:
  0.0 863.5 jit_solution(4095767455423782521)
XLA Ops:
  14.3 10.7 %all_gather.20 = bf16[3,4,128]{1,0,2:T(4,128)(2,1)S(1)} all-gather(bf16[3,4,16]{1,0,2:T(4,128)(2,1)S(1)} %copy.174), channel_id=1, replica_groups=mesh['fsdp'=8,'tp'=4] {'fsdp'}, dimensions={2}, use_global_device_ids=true | all-gather | bytes 3456 | tf_op jit(solution)/shard_map/all_gather | solution.py:1252
  25.9 33.8 %all-gather.8.cloned.1.call-done = bf16[2048,3,4,128]{3,0,2,1:T(8,128)(2,1)} async-done(((bf16[256,3,4,128]{3,0,2,1:T(8,128)(2,1)}), bf16[2048,3,4,128]{3,0,2,1:T(8,128)(2,1)}) %all-gather.8.cloned.1.call-update) | async-done | bytes 6291472 | tf_op jit(solution)/shard_map/all_gather | solution.py:1251
  59.6 8.7 %copy.173 = bf16[2048,3,4,128]{0,3,2,1:T(8,128)(2,1)} copy(bf16[2048,3,4,128]{3,0,2,1:T(8,128)(2,1)} %all-gather.8.cloned.1.call-done) | data formatting | bytes 12582912 | tf_op jit(solution)/shard_map/all_gather | solution.py:1251
  68.4 39.4 %all-gather.6.cloned.1.call-done = bf16[512,2048]{1,0:T(8,128)(2,1)} async-done(((bf16[128,2048]{1,0:T(8,128)(2,1)}), bf16[512,2048]{1,0:T(8,128)(2,1)}) %all-gather.6.cloned.1.call-update) | async-done | bytes 2097168 | tf_op jit(solution)/shard_map/all_gather | solution.py:78
  107.7 6.2 fusion.8
  118.9 17.6 %all-gather.10.cloned.1.call-done = bf16[512,2048]{1,0:T(8,128)(2,1)} async-done(((bf16[512,256]{1,0:T(8,128)(2,1)}), bf16[512,2048]{1,0:T(8,128)(2,1)}) %all-gather.10.cloned.1.call-update) | async-done | bytes 2097168 | tf_op jit(solution)/shard_map/all_gather | solution.py:1253
  141.5 7.4 all_to_all.68
  155.9 6.1 copy.180
  162.0 6.4 all-to-all-done.1
  184.3 7.3 all-to-all-done
  197.2 10.7 %concatenate.22.refs_2_ = bf16[2048,1280]{1,0:T(8,128)(2,1)} concatenate(bf16[2048,352]{1,0:T(8,128)(2,1)} %get-tuple-element.122, bf16[2048,176]{1,0:T(8,128)(2,1)} %get-tuple-element.126, bf16[2048,1]{1,0:T(8,128)(2,1)S(1)} %broadcast_in_dim.96, bf16[2048,1]{1,0:T(8,128)(2,1)} %broadcast_in_dim.97, bf16[2048,110]{1,0:T(8,128)(2,1)S(1)} %slice.85, ...), dimensions={1} | concatenate | bytes 10485760 | tf_op jit(solution)/shard_map/concatenate | solution.py:1303
  211.3 74.1 %all-gather.12.cloned.1.call-done.refs_1_ = bf16[4096,2048]{1,0:T(8,128)(2,1)} async-done(((bf16[128,2048]{1,0:T(8,128)(2,1)}), bf16[4096,2048]{1,0:T(8,128)(2,1)}) %all-gather.12.cloned.1.call-update) | async-done | bytes 16777232 | tf_op jit(solution)/shard_map/all_gather | solution.py:1250
  285.4 221.0 %ffn.1 = (bf16[4096,2048]{1,0:T(8,128)(2,1)}, bf16[4096,1280]{1,0:T(8,128)(2,1)}, bf16[4096,640]{1,0:T(8,128)(2,1)}, bf16[4096,2048]{1,0:T(8,128)(2,1)}, f32[128,2048]{1,0:T(8,128)}, /*index=5*/f32[16,128]{1,0:T(8,128)}) custom-call(bf16[128,2048]{1,0:T(8,128)(2,1)} %get-tuple-element.114.refs_0_, bf16[4096,2048]{1,0:T(8,128)(2,1)} %all-gather.12.cloned.1.call-done.refs_1_, ...), custom_call_target="tpu_custom_call" | custom-call | tf_op jit(solution)/shard_map/ffn/pallas_call | solution.py:1181
  508.9 100.8 %scatter_rows.1 = f32[128,2048]{1,0:T(8,128)S(1)} custom-call(bf16[4096,2048]{1,0:T(8,128)(2,1)} %get-tuple-element.19.refs_0_), custom_call_target="tpu_custom_call" | custom-call | tf_op jit(solution)/shard_map/scatter_rows/pallas_call | solution.py:581
  611.9 44.0 %all-gather.14.cloned.1.call-done = bf16[512,2048]{1,0:T(8,128)(2,1)} async-done(((bf16[128,2048]{1,0:T(8,128)(2,1)}), bf16[512,2048]{1,0:T(8,128)(2,1)}) %all-gather.14.cloned.1.call-update) | async-done | bytes 2097168 | tf_op jit(solution)/shard_map/all_gather | solution.py:78
  671.8 8.0 bitcast_convert_fusion
  680.8 7.2 convolution_convert_fusion
  688.1 29.4 %fusion.46 = (bf16[2048,1280]{0,1:T(8,128)(2,1)S(1)}, f32[2048,1280]{0,1:T(8,128)}) fusion(bf16[4096,2048]{1,0:T(8,128)(2,1)} %get-tuple-element.22, bf16[4096,1280]{1,0:T(8,128)(2,1)} %get-tuple-element.23), kind=kOutput, calls=%fused_computation.109 | convolution fusion | flops 21477457920 | bytes 42991616 | tf_op jit(solution)/shard_map/dot_general | solution.py:1337
  721.6 15.5 %fusion.47 = f32[640,2048]{1,0:T(8,128)S(1)} fusion(bf16[4096,640]{1,0:T(8,128)(2,1)} %get-tuple-element.24, bf16[4096,2048]{1,0:T(8,128)(2,1)} %all-gather.12.cloned.1.call-done.refs_1_), kind=kOutput, calls=%fused_computation.110 | convolution fusion | flops 10737418240 | bytes 27262976 | tf_op jit(solution)/shard_map/dot_general | solution.py:1336
  748.7 7.1 all-to-all-done.4
  761.0 4.9 maximum_bitcast_fusion
  772.0 15.1 %all-to-all-done.3 = bf16[2048,2,176]{2,1,0:T(2,128)(2,1)} async-done(((bf16[2048,2,176]{2,1,0:T(2,128)(2,1)}), bf16[2048,2,176]{2,1,0:T(2,128)(2,1)}, u32[]{:S(2)}, u32[]{:S(2)}) %all-to-all-start.3) | async-done | bytes 1441824 | tf_op jit(solution)/shard_map/all_to_all | solution.py:1342
  802.6 38.4 %all-reduce.3 = (f32[2048]{0:T(1024)S(1)}, f32[2048]{0:T(1024)S(1)}, f32[2048]{0:T(1024)S(1)}) all-reduce(f32[2048]{0:T(1024)S(1)} %get-tuple-element.105, f32[2048]{0:T(1024)S(1)} %get-tuple-element.103, f32[2048]{0:T(1024)S(1)} %get-tuple-element.107), channel_id=4, replica_groups=mesh['fsdp'=8,'tp'=4] {'fsdp','tp'}, use_global_device_ids=true, to_apply=%region_13.14.clone | all-reduce | flops 6144 | bytes 49152
  845.5 7.6 reduce-scatter.12.cloned.1.call-done
  (184 shorter events, 119.6 us)
Async XLA Ops:
  8.0 51.6 %all-gather.8.cloned.1.call-start = ((), (), s32[]{:S(2)}) async-start(), calls=%async_computation.11 | async-start | bytes 7077888 | tf_op jit(solution)/shard_map/all_gather | solution.py:1251
  10.3 97.4 %all-gather.6.cloned.1.call-start = ((), (), s32[]{:S(2)}) async-start(), calls=%async_computation.10 | async-start | bytes 2621440 | tf_op jit(solution)/shard_map/all_gather | solution.py:78
  13.3 123.2 %all-gather.10.cloned.1.call-start = ((), (), s32[]{:S(2)}) async-start(), calls=%async_computation.12 | async-start | bytes 2359296 | tf_op jit(solution)/shard_map/all_gather | solution.py:1253
  14.1 193.8 %reduce-scatter.8.cloned.1.call-start = ((), (), s32[]{:S(2)}) async-start(), calls=%async_computation.13 | async-start | bytes 2621440 | tf_op jit(solution)/shard_map/reduce_scatter | solution.py:82
  25.6 88.5 %copy-start.10 = (f32[512,64]{0,1:T(8,128)}, f32[512,64]{0,1:T(8,128)S(1)}, u32[]{:S(2)}) copy-start(f32[512,64]{0,1:T(8,128)S(1)} %get-tuple-element.141) | copy-start | bytes 393220
  25.9 90.7 %copy-start.21 = (pred[512,512]{0,1:T(8,128)(4,1)}, pred[512,512]{0,1:T(8,128)(4,1)S(1)}, u32[]{:S(2)}) copy-start(pred[512,512]{0,1:T(8,128)(4,1)S(1)} %fusion.29) | copy-start | bytes 786436
  118.9 17.6 %copy-start.35 = (bf16[4,128,512]{2,1,0:T(8,128)(2,1)}, bf16[4,128,512]{2,1,0:T(8,128)(2,1)S(1)}, u32[]{:S(2)}) copy-start(bf16[4,128,512]{2,1,0:T(8,128)(2,1)S(1)} %convolution_convert_fusion.4) | copy-start | bytes 1572868
  140.8 144.6 %all-gather.12.cloned.1.call-start = ((), (), s32[]{:S(2)}) async-start(), calls=%async_computation.14 | async-start | bytes 17301504 | tf_op jit(solution)/shard_map/all_gather | solution.py:1250
  148.9 19.5 %all-to-all-start.1 = ((bf16[8,176,256]{2,1,0:T(8,128)(2,1)}), bf16[8,176,256]{2,1,0:T(8,128)(2,1)}, u32[]{:S(2)}, u32[]{:S(2)}) async-start(bf16[8,176,256]{2,1,0:T(8,128)(2,1)} %bitcast.141), calls=%async_computation.2 | async-start | bytes 1441792 | tf_op jit(solution)/shard_map/all_to_all | solution.py:1255
  168.4 23.1 %all-to-all-start = ((bf16[256,2,1408]{0,1,2:T(2,128)(2,1)}), bf16[256,2,1408]{0,1,2:T(2,128)(2,1)S(1)}, u32[]{:S(2)}, u32[]{:S(2)}) async-start(bf16[256,2,1408]{0,1,2:T(2,128)(2,1)} %copy.180), calls=%async_computation.1 | async-start | bytes 2883584 | tf_op jit(solution)/shard_map/all_to_all | solution.py:1254
  172.0 483.8 %all-gather.14.cloned.1.call-start = ((), (), s32[]{:S(2)}) async-start(), calls=%async_computation.15 | async-start | bytes 2621440 | tf_op jit(solution)/shard_map/all_gather | solution.py:78
  285.4 221.7 %copy-start.1 = (bf16[128,2048]{1,0:T(8,128)(2,1)S(1)}, bf16[128,2048]{1,0:T(8,128)(2,1)}, u32[]{:S(2)}) copy-start(bf16[128,2048]{1,0:T(8,128)(2,1)} %reduce-scatter.8.cloned.1.call-done) | copy-start | bytes 1572868
  285.4 221.7 %copy-start.2 = (bf16[128,2048]{1,0:T(8,128)(2,1)S(1)}, bf16[128,2048]{1,0:T(8,128)(2,1)}, u32[]{:S(2)}) copy-start(bf16[128,2048]{1,0:T(8,128)(2,1)} %get-tuple-element.114.refs_0_) | copy-start | bytes 1572868
  508.9 100.8 %copy-start.3 = (f32[128,2048]{1,0:T(8,128)S(1)}, f32[128,2048]{1,0:T(8,128)}, u32[]{:S(2)}) copy-start(f32[128,2048]{1,0:T(8,128)} %get-tuple-element.20) | copy-start | bytes 3145732
  508.9 100.8 %copy-start.8 = (bf16[128,2048]{1,0:T(8,128)(2,1)S(1)}, bf16[128,2048]{1,0:T(8,128)(2,1)}, u32[]{:S(2)}) copy-start(bf16[128,2048]{1,0:T(8,128)(2,1)} %param.16) | copy-start | bytes 1572868
  609.7 46.1 %copy-start.36 = (bf16[4,128,512]{2,1,0:T(8,128)(2,1)S(1)}, bf16[4,128,512]{2,1,0:T(8,128)(2,1)}, u32[]{:S(2)}) copy-start(bf16[4,128,512]{2,1,0:T(8,128)(2,1)} %copy-done.35) | copy-start | bytes 1572868
  611.6 47.9 %copy-start.22 = (pred[512,512]{0,1:T(8,128)(4,1)S(1)}, pred[512,512]{0,1:T(8,128)(4,1)}, u32[]{:S(2)}) copy-start(pred[512,512]{0,1:T(8,128)(4,1)} %copy-done.21) | copy-start | bytes 786436
  611.6 47.9 %copy-start.29 = (f32[4,512]{1,0:T(4,128)S(1)}, f32[4,512]{1,0:T(4,128)}, u32[]{:S(2)}) copy-start(f32[4,512]{1,0:T(4,128)} %copy-done.28) | copy-start | bytes 24580
  611.6 186.1 %reduce-scatter.16.cloned.1.call-start = ((), (), s32[]{:S(2)}) async-start(), calls=%async_computation.19 | async-start | bytes 36864
  667.5 131.7 %reduce-scatter.14.cloned.1.call-start = ((), (), s32[]{:S(2)}) async-start(), calls=%async_computation.18 | async-start | bytes 2359296 | tf_op jit(solution)/shard_map/reduce_scatter | solution.py:1393
  671.8 129.2 %reduce-scatter.10.cloned.1.call-start = ((), (), s32[]{:S(2)}) async-start(), calls=%async_computation.16 | async-start | bytes 2621440 | tf_op jit(solution)/shard_map/reduce_scatter | solution.py:82
  679.9 173.2 %reduce-scatter.12.cloned.1.call-start = ((), (), s32[]{:S(2)}) async-start(), calls=%async_computation.17 | async-start | bytes 7077888 | tf_op jit(solution)/shard_map/reduce_scatter | solution.py:1391
  739.7 16.1 %all-to-all-start.4 = ((bf16[176,8,256]{2,0,1:T(8,128)(2,1)}), bf16[176,8,256]{2,0,1:T(8,128)(2,1)}, u32[]{:S(2)}, u32[]{:S(2)}) async-start(bf16[176,8,256]{2,0,1:T(8,128)(2,1)} %bitcast.130), calls=%async_computation.8 | async-start | bytes 1441792 | tf_op jit(solution)/shard_map/all_to_all | solution.py:1351
  755.8 31.3 %all-to-all-start.3 = ((bf16[2048,2,176]{2,1,0:T(2,128)(2,1)}), bf16[2048,2,176]{2,1,0:T(2,128)(2,1)}, u32[]{:S(2)}, u32[]{:S(2)}) async-start(bf16[2048,2,176]{2,1,0:T(2,128)(2,1)} %copy.196), calls=%async_computation.7 | async-start | bytes 4194304 | tf_op jit(solution)/shard_map/all_to_all | solution.py:1342
  (28 other events, 142.3 us)
Sparse Core Ops, SparseCore 0:
  11.4 48.2 all-gather.7
  61.8 45.9 all-gather.5
  109.6 26.8 all-gather.9
  140.9 51.2 reduce-scatter.7
  611.7 44.0 all-gather.13
  667.6 29.9 reduce-scatter.15
  700.9 41.2 reduce-scatter.13
  744.6 43.8 reduce-scatter.9
  791.9 61.1 reduce-scatter.11
Sparse Core Ops, SparseCore 1:
  144.7 140.6 all-gather.11

commit v4 on v3

--- a/solution.py
+++ b/solution.py
@@ -600,26 +600,198 @@
     )(*arrays)
 
 
+def prologue_kernel(tp, halved, *refs):
+    parts = len(halved)
+    own_ref, pieces = refs[0], refs[1 : 1 + parts]
+    rows_ref, fulls = refs[1 + parts], refs[2 + parts : 2 + 2 * parts]
+    l_sem, z_send, z_recv, p_send, p_recv = refs[2 + 2 * parts :]
+    me, rank = place()
+    greet(me, rank, tp)
+    rows = own_ref.shape[0]
+
+    def along_z(block, right):
+        way = 0 if right else 1
+        spot = rows_ref.at[pl.ds(block * rows, rows)]
+        return pltpu.make_async_remote_copy(
+            src_ref=spot,
+            dst_ref=spot,
+            send_sem=z_send.at[way, block],
+            recv_sem=z_recv.at[way, block],
+            device_id=(me, rank + 1 if right else rank - 1),
+            device_id_type=MESH,
+        )
+
+    def region(i, owner_bits, start=0, count=None):
+        owner = me
+        for one in (2, 4):
+            if owner_bits & one:
+                owner = flipped(owner, one)
+        size = pieces[i].shape[0]
+        count = size if count is None else count
+        return fulls[i].at[pl.ds(owner * size + start, count)]
+
+    def across(i, bit, owner_bits, slot, start=0, count=None):
+        spot = region(i, owner_bits, start, count)
+        return pltpu.make_async_remote_copy(
+            src_ref=pieces[i] if owner_bits == 0 else spot,
+            dst_ref=spot,
+            send_sem=p_send.at[slot, i],
+            recv_sem=p_recv.at[slot, i],
+            device_id=(flipped(me, bit), rank),
+            device_id_type=MESH,
+        )
+
+    def to_core(q, i):
+        return across(i, 1, 2 * q, q)
+
+    def own_x(i):
+        return across(i, 2, 0, 4)
+
+    def own_y(i):
+        return across(i, 4, 0, 5)
+
+    def x_to_y(i):
+        size = pieces[i].shape[0]
+        return across(i, 4, 2, 6, 0, size // 2 if halved[i] else size)
+
+    def y_to_x(i):
+        size = pieces[i].shape[0]
+        return across(i, 2, 4, 7, size // 2, size // 2)
+
+    def local(i):
+        return pltpu.make_async_copy(pieces[i], region(i, 0), l_sem.at[i])
+
+    def forward(i):
+        own_x(i).wait_recv()
+        x_to_y(i).start()
+        to_core(1, i).start()
+        own_y(i).wait_recv()
+        if halved[i]:
+            y_to_x(i).start()
+        to_core(2, i).start()
+
+    def finish(i):
+        x_to_y(i).wait_recv()
+        if halved[i]:
+            y_to_x(i).wait_recv()
+        to_core(3, i).start()
+
+    def z_step(step):
+        @pl.when(rank >= step)
+        def _():
+            along_z(rank - step, True).wait_recv()
+
+            @pl.when(rank < tp - 1)
+            def _():
+                along_z(rank - step, True).start()
+
+        @pl.when(rank + step < tp)
+        def _():
+            along_z(rank + step, False).wait_recv()
+
+            @pl.when(rank > 0)
+            def _():
+                along_z(rank + step, False).start()
+
+    for i in range(parts):
+        own_x(i).start()
+        own_y(i).start()
+        to_core(0, i).start()
+    mine = pltpu.make_async_copy(own_ref, rows_ref.at[pl.ds(rank * rows, rows)], l_sem.at[parts])
+    mine.start()
+    for i in range(parts):
+        local(i).start()
+    mine.wait()
+
+    @pl.when(rank < tp - 1)
+    def _():
+        along_z(rank, True).start()
+
+    @pl.when(rank > 0)
+    def _():
+        along_z(rank, False).start()
+
+    z_step(1)
+    forward(0)
+    z_step(2)
+    for i in range(1, parts):
+        forward(i)
+    finish(0)
+    z_step(3)
+    for i in range(1, parts):
+        finish(i)
+    for i in range(parts):
+        local(i).wait()
+        for q in range(4):
+            to_core(q, i).wait_recv()
+    for i in range(parts):
+        for q in range(4):
+            to_core(q, i).wait_send()
+        own_x(i).wait_send()
+        own_y(i).wait_send()
+        x_to_y(i).wait_send()
+        if halved[i]:
+            y_to_x(i).wait_send()
+    for block in range(tp):
+
+        @pl.when((block <= rank) & (rank < tp - 1))
+        def _():
+            along_z(block, True).wait_send()
+
+        @pl.when((block >= rank) & (rank > 0))
+        def _():
+            along_z(block, False).wait_send()
+
+
+def prologue(own, pieces, fsdp, tp, collective_id):
+    parts = len(pieces)
+    halved = [one.shape[0] >= 32 for one in pieces]
+    dma = pltpu.SemaphoreType.DMA
+    anywhere = pl.BlockSpec(memory_space=pl.ANY)
+    shapes = [(own.shape[0] * tp, own.shape[1])]
+    shapes += [(one.shape[0] * fsdp, one.shape[1]) for one in pieces]
+    return pl.pallas_call(
+        functools.partial(prologue_kernel, tp, halved),
+        out_shape=[
+            jax.ShapeDtypeStruct(shape, one.dtype) for shape, one in zip(shapes, [own] + pieces)
+        ],
+        in_specs=[anywhere] * (1 + parts),
+        out_specs=[anywhere] * (1 + parts),
+        scratch_shapes=[
+            dma((parts + 1,)),
+            dma((2, tp)),
+            dma((2, tp)),
+            dma((8, parts)),
+            dma((8, parts)),
+        ],
+        compiler_params=pltpu.CompilerParams(
+            collective_id=collective_id, has_side_effects=True, vmem_limit_bytes=16 << 20
+        ),
+        name="prologue",
+    )(own, *pieces)
+
+
 UNIT = 640
+SHARED = 384
 NT = (((1,), (1,)), ((), ()))
 
 
 def ffn_kernel(tp, expert_width, shared_width, *refs):
-    own_ref, grad_ref, both_ref, down_ref, scale_ref = refs[:5]
-    all_ref, d_ref, hid_ref, y_ref, dsum_ref, esum_ref = refs[5:11]
+    part_ref, hidden_ref, gain_ref, grad_ref, both_ref, down_ref, scale_ref = refs[:7]
+    middle_ref, all_ref, d_ref, hid_ref, y_ref, dsum_ref, esum_ref = refs[7:14]
     (
-        g_buf, x_buf, dh_buf, d_buf, h_buf, stage, acc, diag_in, last_in, z_in,
+        n_buf, g_buf, x_buf, dh_buf, d_buf, stage, acc, diag_in, last_in, z_in,
         stage_e, acc_e, other_e, diag_e, last_e, z_in_e,
         local_sem, g_sem, x_sem, d_sem, h_sem, y_sem,
         az_send, az_recv, ap_send, ap_recv,
         c_send, c_recv, ce_send, ce_recv, p_send, p_recv, pe_send, pe_recv,
-        z_send, z_recv, ze_send, ze_recv,
-    ) = refs[11:]
+        z_send, z_recv, ze_send, ze_recv, f_sem, f_send, f_recv,
+    ) = refs[14:]
     me, rank = place()
     greet(me, rank, tp)
     f32 = jnp.float32
     bf16 = jnp.bfloat16
-    rows = own_ref.shape[0]
+    rows = hidden_ref.shape[0]
     pack_rows = rows * tp
     tile = pack_rows // 2
     near = rank // 2
@@ -802,7 +974,7 @@
     def summed_lines():
         return across_e(4, acc_e.at[2], last_e.at[1], 2)
 
-    blocks = order[::-1]
+    blocks = [3 * (1 - near), 2 - near, flipped(rank, 1), rank]
 
     def along_z(j, right):
         way = 0 if right else 1
@@ -902,6 +1074,66 @@
                 dsum_ref[...] += z_in[1, block].astype(f32)
                 esum_ref[...] += z_in_e[1, block]
 
+    def front_load(block):
+        return pltpu.make_async_copy(
+            part_ref.at[pl.ds(block * rows, rows)],
+            x_buf.at[block // 2, pl.ds(block % 2 * rows, rows)],
+            f_sem.at[block],
+        )
+
+    def front_z(j, right):
+        way = 0 if right else 1
+        block = blocks[j]
+        return pltpu.make_async_remote_copy(
+            src_ref=x_buf.at[block // 2, pl.ds(block % 2 * rows, rows)],
+            dst_ref=z_in.at[way, block],
+            send_sem=f_send.at[way, block],
+            recv_sem=f_recv.at[way, block],
+            device_id=(me, rank + 1 if right else rank - 1),
+            device_id_type=MESH,
+        )
+
+    def front(j):
+        block = blocks[j]
+        spot = (block // 2, pl.ds(pl.multiple_of(block % 2 * rows, rows), rows))
+        front_load(block).wait()
+        if j < tp - 1:
+
+            @pl.when((block > rank) & (rank > 0))
+            def _():
+                front_z(j, True).wait_recv()
+                add(x_buf, spot, z_in[0, block])
+
+            @pl.when((block < rank) & (rank < tp - 1))
+            def _():
+                front_z(j, False).wait_recv()
+                add(x_buf, spot, z_in[1, block])
+
+            @pl.when(block > rank)
+            def _():
+                front_z(j, True).start()
+
+            @pl.when(block < rank)
+            def _():
+                front_z(j, False).start()
+        else:
+            middle_ref[...] = hidden_ref[...].astype(f32) + x_buf[spot].astype(f32)
+
+            @pl.when(rank > 0)
+            def _():
+                front_z(j, True).wait_recv()
+                middle_ref[...] += z_in[0, block].astype(f32)
+
+            @pl.when(rank < tp - 1)
+            def _():
+                front_z(j, False).wait_recv()
+                middle_ref[...] += z_in[1, block].astype(f32)
+
+            middle = middle_ref[...]
+            mean = jnp.mean(middle * middle, axis=-1, keepdims=True)
+            normed = middle * lax.rsqrt(mean + epsilon) * gain_ref[...]
+            n_buf[...] = normed.astype(bf16)
+
     def grad_load(n, slot):
         return pltpu.make_async_copy(
             grad_ref.at[pl.ds(n * pack_rows, pack_rows)], g_buf.at[slot], g_sem.at[slot]
@@ -971,7 +1203,7 @@
             d_buf.at[i % 2], d_ref.at[tile_rows(pack, half)], d_sem.at[i % 2]
         )
 
-    units = expert_width + shared_width
+    units = SHARED + shared_width
 
     def one_tile(i, carry):
         q, o, h, pack, half = tile_of(i)
@@ -989,7 +1221,7 @@
         logit = gate[:, units : units + 1] + gate[:, units + 1 : units + 2]
         gate_prob = 1.0 / (1.0 + jnp.exp(-logit))
         scale = jnp.where(
-            lane < expert_width, scale_ref[at, :], jnp.where(lane < units, gate_prob, 0.0)
+            lane < expert_width, scale_ref[at, :1], jnp.where(lane < units, gate_prob, 0.0)
         )
         sigmoid = 1.0 / (1.0 + jnp.exp(-gate))
         act = gate * sigmoid
@@ -999,12 +1231,12 @@
         line = lax.broadcasted_iota(jnp.int32, (16, UNIT), 0)
         unit = lax.broadcasted_iota(jnp.int32, (16, UNIT), 1)
         of_expert = (line == me) & (unit < expert_width)
-        of_shared = (line == 8) & (unit >= expert_width)
+        of_shared = (line == 8) & (unit >= SHARED)
         pick = jnp.where(of_expert | of_shared, 1.0, 0.0).astype(bf16)
         lines = lax.dot_general(
             pick, (d_hidden * hidden).astype(bf16), NT, preferred_element_type=f32
         )
-        h_buf[at, :] = (hidden * scale).astype(bf16)
+        dh_buf[at, :] = (hidden * scale).astype(bf16)
         d_scaled = d_hidden * scale
         d_buf[slot, :, :UNIT] = (d_scaled * upper * slope).astype(bf16)
         d_buf[slot, :, UNIT:] = (d_scaled * act).astype(bf16)
@@ -1081,7 +1313,7 @@
                 y_store(n - 2, slot).wait()
 
             g_buf[slot] = jnp.dot(
-                h_buf[pl.ds(n * pack_rows, pack_rows), :],
+                dh_buf[pl.ds(n * pack_rows, pack_rows), :],
                 down_ref[...],
                 preferred_element_type=f32,
             ).astype(bf16)
@@ -1091,7 +1323,17 @@
         lax.fori_loop(first, last, body, 0)
 
     grad_load(0, 0).start()
-    mine = pltpu.make_async_copy(own_ref, region(me, rank), local_sem)
+    packs = tokens // pack_rows
+    for block in blocks:
+        front_load(block).start()
+    front(0)
+    hidden_grads(0, 3)
+    front(1)
+    hidden_grads(3, 6)
+    front(2)
+    hidden_grads(6, packs)
+    front(3)
+    mine = pltpu.make_async_copy(n_buf, region(me, rank), local_sem)
     mine.start()
     mine.wait()
 
@@ -1104,13 +1346,21 @@
         gather_z(rank, False).start()
 
     start_plane(rank)
-    packs = tokens // pack_rows
-    hidden_grads(0, 5)
+    for j in range(tp - 1):
+        block = blocks[j]
+
+        @pl.when(block > rank)
+        def _():
+            front_z(j, True).wait_send()
+
+        @pl.when(block < rank)
+        def _():
+            front_z(j, False).wait_send()
+
     z_step(1)
-    hidden_grads(5, packs)
     prefetch(0)
     lax.fori_loop(0, 16, one_tile, 0)
-    hidden_store = pltpu.make_async_copy(h_buf, hid_ref, h_sem)
+    hidden_store = pltpu.make_async_copy(dh_buf, hid_ref, h_sem)
     hidden_store.start()
     outputs(0, 4)
     second(0)
@@ -1168,8 +1418,10 @@
             gather_z(block, False).wait_send()
 
 
-def ffn(own, grad_all, both, down, scale, fsdp, tp, expert_width, shared_width, collective_id):
-    rows, width = own.shape
+def ffn(
+    part, hidden, gain, grad_all, both, down, scale, fsdp, tp, expert_width, shared_width, collective_id
+):
+    rows, width = hidden.shape
     tokens = rows * fsdp * tp
     pack_rows = rows * tp
     tile = pack_rows // 2
@@ -1181,6 +1433,7 @@
     return pl.pallas_call(
         functools.partial(ffn_kernel, tp, expert_width, shared_width),
         out_shape=[
+            jax.ShapeDtypeStruct((rows, width), f32),
             jax.ShapeDtypeStruct((tokens, width), bf16),
             jax.ShapeDtypeStruct((tokens, 2 * UNIT), bf16),
             jax.ShapeDtypeStruct((tokens, UNIT), bf16),
@@ -1188,14 +1441,14 @@
             jax.ShapeDtypeStruct((rows, width), f32),
             jax.ShapeDtypeStruct((16, rows), f32),
         ],
-        in_specs=[anywhere, anywhere, vmem, vmem, vmem],
-        out_specs=[anywhere, anywhere, anywhere, anywhere, vmem, vmem],
+        in_specs=[anywhere, vmem, vmem, anywhere, vmem, vmem, vmem],
+        out_specs=[vmem, anywhere, anywhere, anywhere, anywhere, vmem, vmem],
         scratch_shapes=[
+            pltpu.VMEM((rows, width), bf16),
             pltpu.VMEM((2, pack_rows, width), bf16),
             pltpu.VMEM((2, tile, width), bf16),
             pltpu.VMEM((tokens, UNIT), bf16),
             pltpu.VMEM((2, tile, 2 * UNIT), bf16),
-            pltpu.VMEM((tokens, UNIT), bf16),
             pltpu.VMEM((2, 2, rows, width), bf16),
             pltpu.VMEM((4, 2, 2, rows, width), bf16),
             pltpu.VMEM((2, 2, rows, width), bf16),
@@ -1212,12 +1465,13 @@
             dma((4, 2)), dma((4, 2)), dma((4,)), dma((4,)),
             dma((6, 2)), dma((6, 2)), dma((3,)), dma((3,)),
             dma((2, tp)), dma((2, tp)), dma((2, tp)), dma((2, tp)),
+            dma((tp,)), dma((2, tp)), dma((2, tp)),
         ],
         compiler_params=pltpu.CompilerParams(
             collective_id=collective_id, has_side_effects=True, vmem_limit_bytes=61 << 20
         ),
         name="ffn",
-    )(own, grad_all, both, down, scale)
+    )(part, hidden, gain, grad_all, both, down, scale)
 
 
 def dense_plan(
@@ -1248,9 +1502,6 @@
     f32 = jnp.float32
 
     grad_all = lax.all_gather(out_grad, every, axis=0, tiled=True)
-    qkv_full = lax.all_gather(qkv_weight, "fsdp", axis=0, tiled=True)
-    bias_full = lax.all_gather(qkv_bias.astype(bf16), "fsdp", axis=2, tiled=True).astype(f32)
-    out_full = lax.all_gather(out_weight, "fsdp", axis=1, tiled=True)
     shared_up = lax.all_to_all(shared_gate_up, "fsdp", split_axis=2, concat_axis=0, tiled=True)
     shared_dn = lax.all_to_all(shared_down, "fsdp", split_axis=0, concat_axis=1, tiled=True)
     expert_up = expert_gate_up[0]
@@ -1260,11 +1511,8 @@
 
     chosen = expert_ids[:, :, None] == jnp.arange(experts, dtype=jnp.int32)
     table = jnp.sum(jnp.where(chosen, route_weights[:, :, None], 0.0), axis=1)
-    expert_scale = lax.all_to_all(table.T, "fsdp", split_axis=0, concat_axis=0, tiled=True)
-    expert_scale = expert_scale.reshape(-1)
-
-    local_heads = qkv_full.shape[2]
-    head_dim = qkv_full.shape[3]
+    local_heads = qkv_weight.shape[2]
+    head_dim = qkv_weight.shape[3]
     score_scale = head_dim ** (-0.5)
     cos_table, sin_table = rope_tables(length, head_dim)
     positions = jnp.arange(length, dtype=jnp.int32)
@@ -1272,8 +1520,25 @@
     allowed = (positions[:, None] >= positions[None, :]) & (segments[:, None] == segments[None, :])
     hidden_float = hidden_in.astype(f32)
     attn_inverse = inverse_rms(hidden_float)
-    normed_one = spread((hidden_float * attn_inverse * attn_gain).astype(bf16))
-    qkv_flat = qkv_full.reshape(model_width, -1)
+    bias_rows = 3 * local_heads
+    bias_columns = qkv_bias.shape[2]
+    bias_piece = jnp.pad(
+        qkv_bias.reshape(bias_rows, bias_columns), ((0, 16 - bias_rows), (0, 128 - bias_columns))
+    )
+    normed_one, qkv_flat, out_pieces, tables, bias_pieces = prologue(
+        (hidden_float * attn_inverse * attn_gain).astype(bf16),
+        [qkv_weight.reshape(-1, 3 * local_heads * head_dim), out_weight, table.T, bias_piece],
+        experts,
+        lax.axis_size("tp"),
+        4,
+    )
+    out_full = out_pieces.reshape(experts, local_heads * head_dim, -1)
+    out_full = out_full.transpose(1, 0, 2).reshape(local_heads * head_dim, model_width)
+    expert_scale = lax.dynamic_index_in_dim(
+        tables.reshape(packs, experts, length), lax.axis_index("fsdp"), axis=1, keepdims=False
+    ).reshape(-1)
+    bias_full = bias_pieces.reshape(experts, 16, 128)[:, :bias_rows, :bias_columns]
+    bias_full = bias_full.transpose(1, 0, 2).reshape(3, local_heads, head_dim)
     qkv = (
         jnp.dot(normed_one, qkv_flat, preferred_element_type=f32).reshape(
             length, 3, local_heads, head_dim
@@ -1292,40 +1557,42 @@
         .astype(bf16)
         .reshape(length, -1)
     )
-    middle = hidden_float + head_total(jnp.dot(heads_out, out_full, preferred_element_type=f32))
-    ffn_inverse = inverse_rms(middle)
-    normed_two_own = (middle * ffn_inverse * ffn_gain).astype(bf16)
-
     vec_high = shared_gate_vec.astype(bf16)
     vec_low = (shared_gate_vec - vec_high.astype(f32)).astype(bf16)
-    units = expert_width + shared_width
-    none = jnp.zeros((model_width, UNIT - units), bf16)
+    gap = jnp.zeros((model_width, SHARED - expert_width), bf16)
+    rest = jnp.zeros((model_width, UNIT - SHARED - shared_width), bf16)
     both_w = jnp.concatenate(
         [
             expert_up[:, 0],
+            gap,
             shared_up[:, 0],
             vec_high[:, None],
             vec_low[:, None],
-            none[:, 2:],
+            rest[:, 2:],
             expert_up[:, 1],
+            gap,
             shared_up[:, 1],
-            none,
+            rest,
         ],
         axis=1,
     )
-    down_w = jnp.concatenate([expert_dn, shared_dn, none.T], axis=0)
-    normed_all, d_all, hidden_all, token_part, d_normed_two, extra_sum = ffn(
-        normed_two_own,
+    down_w = jnp.concatenate([expert_dn, gap.T, shared_dn, rest.T], axis=0)
+    middle, normed_all, d_all, hidden_all, token_part, d_normed_two, extra_sum = ffn(
+        jnp.dot(heads_out, out_full, preferred_element_type=f32).astype(bf16),
+        hidden_in,
+        ffn_gain[None],
         grad_all,
         both_w,
         down_w,
-        expert_scale[:, None],
+        jnp.broadcast_to(expert_scale[:, None], (expert_scale.shape[0], 128)),
         experts,
         lax.axis_size("tp"),
         expert_width,
         shared_width,
         1,
     )
+    ffn_inverse = inverse_rms(middle)
+    normed_two_own = (middle * ffn_inverse * ffn_gain).astype(bf16)
     (total,) = scatter_sum([token_part], experts, lax.axis_size("tp"), 3)
     hidden_out = (middle + total).astype(bf16)
     own_start = tp_rank * own_rows
@@ -1333,6 +1600,7 @@
     picked = ids_own[:, :, None] == jnp.arange(experts, dtype=jnp.int32)
     route_grad = jnp.sum(jnp.where(picked, extra_sum[:experts].T[:, None, :], 0.0), axis=-1)
     gate_grad = extra_sum[experts]
+    units = SHARED + shared_width
     g_down = jnp.dot(hidden_all.T, grad_all, preferred_element_type=f32)
     g_both = jnp.dot(normed_all.T, d_all, preferred_element_type=f32)
     g_expert_down = g_down[:expert_width][None]
@@ -1341,7 +1609,7 @@
     )[None]
     g_shared_gate_up = lax.all_to_all(
         jnp.stack(
-            [g_both[:, expert_width:units], g_both[:, UNIT + expert_width : UNIT + units]], axis=1
+            [g_both[:, SHARED:units], g_both[:, UNIT + SHARED : UNIT + units]], axis=1
         ).astype(bf16),
         "fsdp",
         split_axis=0,
@@ -1349,7 +1617,7 @@
         tiled=True,
     ).astype(f32)
     g_shared_down = lax.all_to_all(
-        g_down[expert_width:units].astype(bf16), "fsdp", split_axis=1, concat_axis=0, tiled=True
+        g_down[SHARED:units].astype(bf16), "fsdp", split_axis=1, concat_axis=0, tiled=True
     ).astype(f32)
 
     own_gate = jax.nn.sigmoid(jnp.sum(normed_two_own.astype(f32) * shared_gate_vec, axis=-1))
@@ -1382,7 +1650,7 @@
     )
     g_bias = jnp.sum(d_qkv, axis=0)
     d_qkv_b = d_qkv.astype(bf16).reshape(length, -1)
-    g_qkv = jnp.dot(normed_one.T, d_qkv_b, preferred_element_type=f32).reshape(qkv_full.shape)
+    g_qkv = jnp.dot(normed_one.T, d_qkv_b, preferred_element_type=f32).reshape(model_width, 3, local_heads, head_dim)
     d_normed_one = head_total(jnp.dot(d_qkv_b, qkv_flat.T, preferred_element_type=f32))
     hat_one = hidden_float * attn_inverse
     g_attn_gain = jnp.sum(d_normed_one * hat_one, axis=0)

time: 873 us -> 757 us (0.87)
  waiting for transfers between devices: 254 us -> 84.3 us
  Pallas kernels: 322 us -> 389 us
  blocking collectives: 56.5 us -> 38.3 us
    all_gather x1, waiting for transfers between devices: 74.1 us -> 0.01 us  [dense_plan(): grad_all = lax.all_gather(out_grad, every, axis=0, tiled=True)]
    pallas_call x0 -> x1, Pallas kernels: none -> 66.7 us  [prologue(): pl.pallas_call(functools.partial(prologue_kernel, tp, halved), out_shape=...]
    all_gather x2 -> x0, waiting for transfers between devices: 51.4 us -> none  [the longest x1 33.8 us: dense_plan(): qkv_full = lax.all_gather(qkv_weight, 'fsdp', axis=0, tiled=True)]
    all_gather x2 -> x1, waiting for transfers between devices: 83.3 us -> 48.9 us  [spread(): return lax.all_gather(rows, 'tp', axis=0, tiled=True)]
    all_gather x1 -> x0, blocking collectives: 10.7 us -> none  [dense_plan(): lax.all_gather(qkv_bias.astype(bf16), 'fsdp', axis=2, tiled=True)]
    reshape x0 -> x4, local copies, waits for them, and re-layouts: none -> 8.9 us  [the longest x1 4.84 us: dense_plan(): jnp.dot(normed_one, qkv_flat, preferred_element_type=f32)]
    all_gather x2 -> x0, local copies, waits for them, and re-layouts: 8.84 us -> none  [the longest x1 8.74 us: dense_plan(): qkv_full = lax.all_gather(qkv_weight, 'fsdp', axis=0, tiled=True)]
    unnamed x89 -> x107, local copies, waits for them, and re-layouts: 25.4 us -> 27.5 us
  transfers between devices with their start and end apart: 14 -> 10, of which waited for: 10 -> 5; matrix products, arithmetic and copies ran while one was open for 20% -> 22% of each run, Pallas kernels for 0% -> 9%
where the time goes in v4:
time: 757 us; the launch traced here: 747 us
  Pallas kernels  389 us (51%)
  waiting for transfers between devices  84.3 us (11%)
  matrix products  83.4 us (11%)
  local copies, waits for them, and re-layouts  81.5 us (11%)
  blocking collectives  38.3 us (5%)
  other arithmetic  31.4 us (4%)
  starting transfers between devices  23.4 us (3%)
  between operations  15.4 us (2%)
    pallas_call x1, Pallas kernels, ffn(): pl.pallas_call(functools.partial(ffn_kernel, tp, expert_width, shared_wid...  222 us
    pallas_call x1, Pallas kernels, scatter_sum(): pl.pallas_call(functools.partial(scatter_kernel, tp, parts), out_shape=[j...  99.9 us
    pallas_call x1, Pallas kernels, prologue(): pl.pallas_call(functools.partial(prologue_kernel, tp, halved), out_shape=...  66.7 us
    all_gather x1, waiting for transfers between devices, spread(): return lax.all_gather(rows, 'tp', axis=0, tiled=True)  48.9 us
    unnamed x1, blocking collectives  38.3 us
    dot_general x1, matrix products, dense_plan(): g_both = jnp.dot(normed_all.T, d_all, preferred_element_type=f32)  29.4 us
    unnamed x107, local copies, waits for them, and re-layouts  27.5 us
    dot_general x1, matrix products, dense_plan(): g_down = jnp.dot(hidden_all.T, grad_all, preferred_element_type=f32)  15.4 us
  transfers between devices with their start and end apart: 10, of which 5 were waited for; matrix products, arithmetic and copies ran while one was open for 22% of the time, Pallas kernels for 9%

profile of v4, /device:TPU:0, one launch (start us, length us, event | category | flops | bytes accessed | tf_op | source)
XLA Modules:
  0.0 746.7 jit_solution(16177863774619106352)
XLA Ops:
  8.0 5.2 all-to-all-start.1
  15.7 66.7 %prologue.1 = (bf16[512,2048]{1,0:T(8,128)(2,1)S(1)}, bf16[2048,1536]{1,0:T(8,128)(2,1)S(1)}, bf16[4096,256]{1,0:T(8,128)(2,1)S(1)}, f32[64,512]{1,0:T(8,128)S(1)}, f32[128,128]{1,0:T(8,128)S(1)}) custom-call(bf16[128,2048]{1,0:T(8,128)(2,1)S(1)} %fusion.14.refs_0_, bf16[256,1536]{1,0:T(8,128)(2,1)S(1)} %reshape.210.refs_1_, bf16[512,256]{1,0:T(8,128)(2,1)S(1)} %copy-done, ...), custom_call_target="tpu_custom_call" | custom-call | tf_op jit(solution)/shard_map/prologue/pallas_call | solution.py:753
  85.7 5.1 fusion.35
  90.8 4.8 reshape.212
  98.1 6.3 copy.185
  114.4 8.7 %all-to-all-start = ((bf16[256,2,1408]{0,1,2:T(2,128)(2,1)}), bf16[256,2,1408]{0,1,2:T(2,128)(2,1)}, u32[]{:S(2)}, u32[]{:S(2)}) async-start(bf16[256,2,1408]{0,1,2:T(2,128)(2,1)} %copy.185), calls=%async_computation | async-start | bytes 2883584 | tf_op jit(solution)/shard_map/all_to_all | solution.py:1505
  135.1 7.8 %all-to-all-done = bf16[256,2,1408]{0,1,2:T(2,128)(2,1)} async-done(((bf16[256,2,1408]{0,1,2:T(2,128)(2,1)}), bf16[256,2,1408]{0,1,2:T(2,128)(2,1)}, u32[]{:S(2)}, u32[]{:S(2)}) %all-to-all-start) | async-done | bytes 1441824 | tf_op jit(solution)/shard_map/all_to_all | solution.py:1505
  147.3 10.6 %concatenate.22.refs_4_ = bf16[2048,1280]{1,0:T(8,128)(2,1)} concatenate(bf16[2048,352]{1,0:T(8,128)(2,1)} %get-tuple-element.132, bf16[2048,32]{1,0:T(8,128)(2,1)S(1)} %broadcast_in_dim.102, bf16[2048,176]{1,0:T(8,128)(2,1)} %get-tuple-element.136, bf16[2048,1]{1,0:T(8,128)(2,1)} %broadcast_in_dim.112, bf16[2048,1]{1,0:T(8,128)(2,1)} %broadcast_in_dim.113, ...), dimensions={1} | concatenate | bytes 10485760 | tf_op jit(solution)/shard_map/concatenate | solution.py:1564
  159.9 222.3 %ffn.1 = (f32[128,2048]{1,0:T(8,128)}, bf16[4096,2048]{1,0:T(8,128)(2,1)}, bf16[4096,1280]{1,0:T(8,128)(2,1)}, bf16[4096,640]{1,0:T(8,128)(2,1)}, bf16[4096,2048...) custom-call(bf16[512,2048]{1,0:T(8,128)(2,1)} %convolution_convert_fusion.3.refs_0_, ...), custom_call_target="tpu_custom_call" | custom-call | tf_op jit(solution)/shard_map/ffn/pallas_call | solution.py:1433
  388.0 99.9 %scatter_rows.1 = f32[128,2048]{1,0:T(8,128)S(1)} custom-call(bf16[4096,2048]{1,0:T(8,128)(2,1)} %get-tuple-element.31.refs_0_), custom_call_target="tpu_custom_call" | custom-call | tf_op jit(solution)/shard_map/scatter_rows/pallas_call | solution.py:581
  489.8 48.9 %all-gather.5.cloned.1.call-done = bf16[512,2048]{1,0:T(8,128)(2,1)} async-done(((bf16[128,2048]{1,0:T(8,128)(2,1)}), bf16[512,2048]{1,0:T(8,128)(2,1)}) %all-gather.5.cloned.1.call-update) | async-done | bytes 2097168 | tf_op jit(solution)/shard_map/all_gather | solution.py:78
  550.8 4.3 convolution_convert_fusion.1
  559.5 8.3 %convolution_convert_fusion.2 = bf16[512,2048]{1,0:T(8,128)(2,1)} fusion(bf16[512,1536]{0,1:T(8,128)(2,1)} %bitcast.137, bf16[2048,1536]{1,0:T(8,128)(2,1)} %copy-done.1), kind=kOutput, calls=%fused_computation.10 | convolution fusion | flops 3222274048 | bytes 9961472 | tf_op jit(solution)/shard_map/dot_general | solution.py:1654
  567.9 6.8 convolution_convert_fusion
  574.7 29.4 %fusion.34 = (bf16[2048,1280]{0,1:T(8,128)(2,1)S(1)}, f32[2048,1280]{0,1:T(8,128)}) fusion(bf16[4096,2048]{1,0:T(8,128)(2,1)} %get-tuple-element.34, bf16[4096,1280]{1,0:T(8,128)(2,1)} %get-tuple-element.35), kind=kOutput, calls=%fused_computation.106 | convolution fusion | flops 21477457920 | bytes 42991616 | tf_op jit(solution)/shard_map/dot_general | solution.py:1605
  608.2 15.4 %fusion.36 = f32[640,2048]{1,0:T(8,128)S(1)} fusion(bf16[4096,640]{1,0:T(8,128)(2,1)} %get-tuple-element.36, bf16[4096,2048]{1,0:T(8,128)(2,1)} %all-gather.3.cloned.1.call-done.refs_3_), kind=kOutput, calls=%fused_computation.108 | convolution fusion | flops 10737418240 | bytes 27262976 | tf_op jit(solution)/shard_map/dot_general | solution.py:1604
  630.4 4.8 slice_bitcast_fusion.2
  635.2 7.1 all-to-all-done.3
  642.3 4.6 all-to-all-start.2
  647.5 4.9 maximum_bitcast_fusion
  658.5 15.1 %all-to-all-done.2 = bf16[2048,2,176]{2,1,0:T(2,128)(2,1)} async-done(((bf16[2048,2,176]{2,1,0:T(2,128)(2,1)}), bf16[2048,2,176]{2,1,0:T(2,128)(2,1)}, u32[]{:S(2)}, u32[]{:S(2)}) %all-to-all-start.2) | async-done | bytes 1441824 | tf_op jit(solution)/shard_map/all_to_all | solution.py:1610
  673.6 4.7 copy.204
  689.1 38.3 %all-reduce.4 = (f32[2048]{0:T(1024)S(1)}, f32[2048]{0:T(1024)S(1)}, f32[2048]{0:T(1024)S(1)}) all-reduce(f32[2048]{0:T(1024)S(1)} %get-tuple-element.118, f32[2048]{0:T(1024)S(1)} %get-tuple-element.115, f32[2048]{0:T(1024)S(1)} %get-tuple-element.117), channel_id=3, replica_groups=mesh['fsdp'=8,'tp'=4] {'fsdp','tp'}, use_global_device_ids=true, to_apply=%region_12.13.clone | all-reduce | flops 6144 | bytes 49152
  731.9 4.6 reduce-scatter.9.cloned.1.call-done
  (196 shorter events, 96.5 us)
Async XLA Ops:
  7.2 8.4 %copy-start = (bf16[512,256]{1,0:T(8,128)(2,1)S(1)}, bf16[512,256]{1,0:T(8,128)(2,1)}, u32[]{:S(2)}) copy-start(bf16[512,256]{1,0:T(8,128)(2,1)} %refs_2_.1) | copy-start | bytes 786436
  7.2 150.7 %all-gather.3.cloned.1.call-start = ((), (), s32[]{:S(2)}) async-start(), calls=%async_computation.8 | async-start | bytes 17301504 | tf_op jit(solution)/shard_map/all_gather | solution.py:1504
  8.0 106.4 %all-to-all-start.1 = ((bf16[8,176,256]{2,1,0:T(8,128)(2,1)}), bf16[8,176,256]{2,1,0:T(8,128)(2,1)}, u32[]{:S(2)}, u32[]{:S(2)}) async-start(bf16[8,176,256]{2,1,0:T(8,128)(2,1)} %bitcast.140), calls=%async_computation.1 | async-start | bytes 1441792 | tf_op jit(solution)/shard_map/all_to_all | solution.py:1506
  95.7 8.7 %copy-start.37 = (s32[1,512]{1,0:T(1,128)S(1)}, s32[1,512]{1,0:T(1,128)}, u32[]{:S(2)}) copy-start(s32[1,512]{1,0:T(1,128)} %param.17) | copy-start | bytes 6148
  111.8 11.6 %copy-start.31 = (f32[2048]{0:T(1024)S(1)}, f32[2048]{0:T(1024)}, u32[]{:S(2)}) copy-start(f32[2048]{0:T(1024)} %param.27) | copy-start | bytes 24580
  114.4 28.4 %all-to-all-start = ((bf16[256,2,1408]{0,1,2:T(2,128)(2,1)}), bf16[256,2,1408]{0,1,2:T(2,128)(2,1)}, u32[]{:S(2)}, u32[]{:S(2)}) async-start(bf16[256,2,1408]{0,1,2:T(2,128)(2,1)} %copy.185), calls=%async_computation | async-start | bytes 2883584 | tf_op jit(solution)/shard_map/all_to_all | solution.py:1505
  123.1 415.6 %all-gather.5.cloned.1.call-start = ((), (), s32[]{:S(2)}) async-start(), calls=%async_computation.9 | async-start | bytes 2621440 | tf_op jit(solution)/shard_map/all_gather | solution.py:78
  147.2 10.7 %copy-start.35 = (f32[8,1,512]{2,1,0:T(1,128)S(1)}, f32[8,1,512]{2,1,0:T(1,128)}, u32[]{:S(2)}) copy-start(f32[8,1,512]{2,1,0:T(1,128)} %constant_dynamic-slice_fusion.1) | copy-start | bytes 49156
  159.9 223.7 %copy-start.32 = (f32[2048]{0:T(1024)S(1)}, f32[2048]{0:T(1024)}, u32[]{:S(2)}) copy-start(f32[2048]{0:T(1024)} %param.21) | copy-start | bytes 24580
  387.9 99.9 %copy-start.6 = (f32[128,2048]{1,0:T(8,128)S(1)}, f32[128,2048]{1,0:T(8,128)}, u32[]{:S(2)}) copy-start(f32[128,2048]{1,0:T(8,128)} %get-tuple-element.30) | copy-start | bytes 3145732
  387.9 99.9 %copy-start.19 = (f32[128,2048]{1,0:T(8,128)S(1)}, f32[128,2048]{1,0:T(8,128)}, u32[]{:S(2)}) copy-start(f32[128,2048]{1,0:T(8,128)} %get-tuple-element.32) | copy-start | bytes 3145732
  388.0 99.9 %copy-start.27 = (bf16[128,2048]{1,0:T(8,128)(2,1)S(1)}, bf16[128,2048]{1,0:T(8,128)(2,1)}, u32[]{:S(2)}) copy-start(bf16[128,2048]{1,0:T(8,128)(2,1)} %param.16) | copy-start | bytes 1572868
  487.9 50.8 %copy-start.29 = (bf16[8,512,256]{1,2,0:T(8,128)(2,1)S(1)}, bf16[8,512,256]{1,2,0:T(8,128)(2,1)}, u32[]{:S(2)}) copy-start(bf16[8,512,256]{1,2,0:T(8,128)(2,1)} %copy.183) | copy-start | bytes 6291460
  487.9 50.8 %copy-start.46 = (bf16[4,128,512]{2,1,0:T(8,128)(2,1)S(1)}, bf16[4,128,512]{2,1,0:T(8,128)(2,1)}, u32[]{:S(2)}) copy-start(bf16[4,128,512]{2,1,0:T(8,128)(2,1)} %copy-done.45) | copy-start | bytes 1572868
  489.7 52.1 %copy-start.22 = (pred[512,512]{0,1:T(8,128)(4,1)S(1)}, pred[512,512]{0,1:T(8,128)(4,1)}, u32[]{:S(2)}) copy-start(pred[512,512]{0,1:T(8,128)(4,1)} %copy-done.21) | copy-start | bytes 786436
  489.7 52.1 %copy-start.39 = (f32[4,512]{1,0:T(4,128)S(1)}, f32[4,512]{1,0:T(4,128)}, u32[]{:S(2)}) copy-start(f32[4,512]{1,0:T(4,128)} %copy-done.38) | copy-start | bytes 24580
  489.7 194.5 %reduce-scatter.13.cloned.1.call-start = ((), (), s32[]{:S(2)}) async-start(), calls=%async_computation.13 | async-start | bytes 36864
  550.7 135.0 %reduce-scatter.11.cloned.1.call-start = ((), (), s32[]{:S(2)}) async-start(), calls=%async_computation.12 | async-start | bytes 2359296 | tf_op jit(solution)/shard_map/reduce_scatter | solution.py:1661
  555.1 132.4 %reduce-scatter.7.cloned.1.call-start = ((), (), s32[]{:S(2)}) async-start(), calls=%async_computation.10 | async-start | bytes 2621440 | tf_op jit(solution)/shard_map/reduce_scatter | solution.py:82
  559.5 8.4 %copy-start.3 = (bf16[512,2048]{1,0:T(8,128)(2,1)S(1)}, bf16[512,2048]{1,0:T(8,128)(2,1)}, u32[]{:S(2)}) copy-start(bf16[512,2048]{1,0:T(8,128)(2,1)} %copy-done.2) | copy-start | bytes 6291460
  567.8 168.8 %reduce-scatter.9.cloned.1.call-start = ((), (), s32[]{:S(2)}) async-start(), calls=%async_computation.11 | async-start | bytes 7077888 | tf_op jit(solution)/shard_map/reduce_scatter | solution.py:1659
  626.2 16.1 %all-to-all-start.3 = ((bf16[176,8,256]{2,0,1:T(8,128)(2,1)}), bf16[176,8,256]{2,0,1:T(8,128)(2,1)}, u32[]{:S(2)}, u32[]{:S(2)}) async-start(bf16[176,8,256]{2,0,1:T(8,128)(2,1)} %bitcast.120), calls=%async_computation.6 | async-start | bytes 1441792 | tf_op jit(solution)/shard_map/all_to_all | solution.py:1619
  635.2 11.7 %copy-start.44 = (f32[16,128]{1,0:T(8,128)S(1)}, f32[16,128]{1,0:T(8,128)}, u32[]{:S(2)}) copy-start(f32[16,128]{1,0:T(8,128)} %get-tuple-element.33) | copy-start | bytes 24580
  642.3 31.3 %all-to-all-start.2 = ((bf16[2048,2,176]{2,1,0:T(2,128)(2,1)}), bf16[2048,2,176]{2,1,0:T(2,128)(2,1)}, u32[]{:S(2)}, u32[]{:S(2)}) async-start(bf16[2048,2,176]{2,1,0:T(2,128)(2,1)} %copy.203), calls=%async_computation.5 | async-start | bytes 4194304 | tf_op jit(solution)/shard_map/all_to_all | solution.py:1610
  (33 other events, 113.9 us)
Sparse Core Ops, SparseCore 0:
  11.1 139.3 all-gather.2
  489.8 48.8 all-gather.4
  550.9 29.9 reduce-scatter.12
  584.4 41.2 reduce-scatter.10
  627.8 43.8 reduce-scatter.6
  675.3 61.2 reduce-scatter.8

commit v5 on v4

--- a/solution.py
+++ b/solution.py
@@ -371,233 +371,6 @@
     left = (rank + tp - 1) // tp
     right = (2 * (tp - 1) - rank) // tp
     pl.semaphore_wait(barrier, 3 + left + right)
-
-
-def scatter_kernel(tp, parts, *refs):
-    ins = refs[:parts]
-    outs = refs[parts : 2 * parts]
-    buffers = refs[2 * parts : 7 * parts]
-    mine, other, diag_in, last_in, z_in = (
-        buffers[i * parts : (i + 1) * parts] for i in range(5)
-    )
-    l_sem, c_send, c_recv, p_send, p_recv, z_send, z_recv = refs[7 * parts :]
-    me, rank = place()
-    greet(me, rank, tp)
-    f32 = jnp.float32
-    blocks = [rank]
-    for bit in (1, 2):
-        blocks = blocks + [flipped(one, bit) for one in blocks]
-    blocks = blocks[::-1]
-    packs = [me, flipped(me, 2), flipped(me, 4), flipped(flipped(me, 2), 4)]
-    every = range(parts)
-    rows = [ref.shape[0] for ref in outs]
-    low = [pl.ds(0, count // 2) for count in rows]
-    high = [pl.ds(count // 2, count // 2) for count in rows]
-
-    def region(i, pack, block):
-        return ins[i].at[pl.ds((pack * tp + block) * rows[i], rows[i])]
-
-    def local(k, j, i):
-        return pltpu.make_async_copy(
-            region(i, packs[k], blocks[j]), mine[i].at[k, j], l_sem.at[k, j, i]
-        )
-
-    def core(k, j, i):
-        return pltpu.make_async_remote_copy(
-            src_ref=region(i, flipped(packs[k], 1), blocks[j]),
-            dst_ref=other[i].at[k, j],
-            send_sem=c_send.at[k, j, i],
-            recv_sem=c_recv.at[k, j, i],
-            device_id=(flipped(me, 1), rank),
-            device_id_type=MESH,
-        )
-
-    def across(bit, src, dst, slot, j, i):
-        return pltpu.make_async_remote_copy(
-            src_ref=src,
-            dst_ref=dst,
-            send_sem=p_send.at[slot, j, i],
-            recv_sem=p_recv.at[slot, j, i],
-            device_id=(flipped(me, bit), rank),
-            device_id_type=MESH,
-        )
-
-    def diag_x(j, i):
-        return across(2, mine[i].at[3, j, low[i]], diag_in[i].at[j, 0], 0, j, i)
-
-    def diag_y(j, i):
-        return across(4, mine[i].at[3, j, high[i]], diag_in[i].at[j, 1], 1, j, i)
-
-    def direct_x(j, i):
-        return across(2, mine[i].at[1, j, low[i]], last_in[i].at[j, 0, low[i]], 2, j, i)
-
-    def direct_y(j, i):
-        return across(4, mine[i].at[2, j, high[i]], last_in[i].at[j, 1, high[i]], 3, j, i)
-
-    def summed_x(j, i):
-        return across(2, mine[i].at[1, j, high[i]], last_in[i].at[j, 0, high[i]], 4, j, i)
-
-    def summed_y(j, i):
-        return across(4, mine[i].at[2, j, low[i]], last_in[i].at[j, 1, low[i]], 5, j, i)
-
-    def along_z(j, right, i):
-        way = 0 if right else 1
-        block = blocks[j]
-        return pltpu.make_async_remote_copy(
-            src_ref=mine[i].at[0, j],
-            dst_ref=z_in[i].at[way, block],
-            send_sem=z_send.at[way, block, i],
-            recv_sem=z_recv.at[way, block, i],
-            device_id=(me, rank + 1 if right else rank - 1),
-            device_id_type=MESH,
-        )
-
-    for j in range(tp):
-        for k in (3, 2, 1, 0):
-            for i in every:
-                core(k, j, i).start()
-                local(k, j, i).start()
-
-    def add(ref, spot, one):
-        ref[spot] = (ref[spot].astype(f32) + one.astype(f32)).astype(ref.dtype)
-
-    def first(j):
-        for k in (3, 2, 1, 0):
-            for i in every:
-                core(k, j, i).wait_recv()
-                local(k, j, i).wait()
-                add(mine[i], (k, j), other[i][k, j])
-                if k == 3:
-                    diag_x(j, i).start()
-                    diag_y(j, i).start()
-                if k == 2:
-                    direct_y(j, i).start()
-                if k == 1:
-                    direct_x(j, i).start()
-
-    def second(j):
-        for i in every:
-            diag_x(j, i).wait_recv()
-            add(mine[i], (2, j, low[i]), diag_in[i][j, 0])
-            summed_y(j, i).start()
-            diag_y(j, i).wait_recv()
-            add(mine[i], (1, j, high[i]), diag_in[i][j, 1])
-            summed_x(j, i).start()
-
-    def third(j):
-        block = blocks[j]
-        for i in every:
-            direct_x(j, i).wait_recv()
-            direct_y(j, i).wait_recv()
-            summed_x(j, i).wait_recv()
-            summed_y(j, i).wait_recv()
-            total = (
-                mine[i][0, j].astype(f32)
-                + last_in[i][j, 0].astype(f32)
-                + last_in[i][j, 1].astype(f32)
-            )
-            if j < tp - 1:
-                mine[i][0, j] = total.astype(mine[i].dtype)
-            else:
-                outs[i][...] = total
-        if j < tp - 1:
-
-            @pl.when((block > rank) & (rank > 0))
-            def _():
-                for i in every:
-                    along_z(j, True, i).wait_recv()
-                    add(mine[i], (0, j), z_in[i][0, block])
-
-            @pl.when((block < rank) & (rank < tp - 1))
-            def _():
-                for i in every:
-                    along_z(j, False, i).wait_recv()
-                    add(mine[i], (0, j), z_in[i][1, block])
-
-            @pl.when(block > rank)
-            def _():
-                for i in every:
-                    along_z(j, True, i).start()
-
-            @pl.when(block < rank)
-            def _():
-                for i in every:
-                    along_z(j, False, i).start()
-        else:
-
-            @pl.when(rank > 0)
-            def _():
-                for i in every:
-                    along_z(j, True, i).wait_recv()
-                    outs[i][...] += z_in[i][0, block].astype(f32)
-
-            @pl.when(rank < tp - 1)
-            def _():
-                for i in every:
-                    along_z(j, False, i).wait_recv()
-                    outs[i][...] += z_in[i][1, block].astype(f32)
-
-    first(0)
-    first(1)
-    second(0)
-    first(2)
-    second(1)
-    third(0)
-    first(3)
-    second(2)
-    third(1)
-    second(3)
-    third(2)
-    third(3)
-    for j in range(tp):
-        for i in every:
-            for k in range(4):
-                core(k, j, i).wait_send()
-            for copy in (diag_x, diag_y, direct_x, direct_y, summed_x, summed_y):
-                copy(j, i).wait_send()
-        block = blocks[j]
-        if j < tp - 1:
-
-            @pl.when(block > rank)
-            def _():
-                for i in every:
-                    along_z(j, True, i).wait_send()
-
-            @pl.when(block < rank)
-            def _():
-                for i in every:
-                    along_z(j, False, i).wait_send()
-
-
-def scatter_sum(arrays, fsdp, tp, collective_id):
-    parts = len(arrays)
-    shapes = [(one.shape[0] // (fsdp * tp), one.shape[1]) for one in arrays]
-    kind = arrays[0].dtype
-    scratch = [pltpu.VMEM((4, tp, rows, width), kind) for rows, width in shapes]
-    scratch += [pltpu.VMEM((4, tp, rows, width), kind) for rows, width in shapes]
-    scratch += [pltpu.VMEM((tp, 2, rows // 2, width), kind) for rows, width in shapes]
-    scratch += [pltpu.VMEM((tp, 2, rows, width), kind) for rows, width in shapes]
-    scratch += [pltpu.VMEM((2, tp, rows, width), kind) for rows, width in shapes]
-    return pl.pallas_call(
-        functools.partial(scatter_kernel, tp, parts),
-        out_shape=[jax.ShapeDtypeStruct(shape, jnp.float32) for shape in shapes],
-        in_specs=[pl.BlockSpec(memory_space=pl.ANY)] * parts,
-        out_specs=[pl.BlockSpec(memory_space=pltpu.VMEM)] * parts,
-        scratch_shapes=scratch
-        + [
-            pltpu.SemaphoreType.DMA((4, tp, parts)),
-            pltpu.SemaphoreType.DMA((4, tp, parts)),
-            pltpu.SemaphoreType.DMA((4, tp, parts)),
-            pltpu.SemaphoreType.DMA((6, tp, parts)),
-            pltpu.SemaphoreType.DMA((6, tp, parts)),
-            pltpu.SemaphoreType.DMA((2, tp, parts)),
-            pltpu.SemaphoreType.DMA((2, tp, parts)),
-        ],
-        compiler_params=pltpu.CompilerParams(
-            collective_id=collective_id, has_side_effects=True, vmem_limit_bytes=48 << 20
-        ),
-        name="scatter_rows",
-    )(*arrays)
 
 
 def prologue_kernel(tp, halved, *refs):
@@ -1474,6 +1247,739 @@
     )(part, hidden, gain, grad_all, both, down, scale)
 
 
+TN = (((0,), (0,)), ((), ()))
+
+
+def outputs_kernel(tp, expert_width, shared_width, *refs):
+    y_ref, own_ref, x_ref, d_ref, h_ref, g_ref = refs[:6]
+    total_ref, rows_ref, ge_ref, gs_ref, de_ref, ds_ref = refs[6:12]
+    (
+        mine, other, diag_in, last_in, z_in, d_buf, h_buf, col_buf, ge_buf, gs_buf, de_buf, ds_buf,
+        l_sem, c_send, c_recv, p_send, p_recv, z_send, z_recv, a_sem, a_send, a_recv,
+        w_sem, col_sem, out_sem,
+    ) = refs[12:]
+    me, rank = place()
+    greet(me, rank, tp)
+    f32 = jnp.float32
+    bf16 = jnp.bfloat16
+    rows = total_ref.shape[0]
+    half = rows // 2
+    near = rank // 2
+    blocks = [3 * (1 - near), 2 - near, flipped(rank, 1), rank]
+    packs = [me, flipped(me, 2), flipped(me, 4), flipped(flipped(me, 2), 4)]
+    low, high = pl.ds(0, half), pl.ds(half, half)
+
+    def gather_z(block, right):
+        way = 0 if right else 1
+        spot = rows_ref.at[pl.ds(block * rows, rows)]
+        return pltpu.make_async_remote_copy(
+            src_ref=spot,
+            dst_ref=spot,
+            send_sem=a_send.at[way, block],
+            recv_sem=a_recv.at[way, block],
+            device_id=(me, rank + 1 if right else rank - 1),
+            device_id_type=MESH,
+        )
+
+    def gather_step(step):
+        @pl.when(rank >= step)
+        def _():
+            gather_z(rank - step, True).wait_recv()
+
+            @pl.when(rank < tp - 1)
+            def _():
+                gather_z(rank - step, True).start()
+
+        @pl.when(rank + step < tp)
+        def _():
+            gather_z(rank + step, False).wait_recv()
+
+            @pl.when(rank > 0)
+            def _():
+                gather_z(rank + step, False).start()
+
+    def region(pack, block):
+        return y_ref.at[pl.ds((pack * tp + block) * rows, rows)]
+
+    def local(k, j):
+        return pltpu.make_async_copy(region(packs[k], blocks[j]), mine.at[k, j], l_sem.at[k, j])
+
+    def core(k, j):
+        return pltpu.make_async_remote_copy(
+            src_ref=region(flipped(packs[k], 1), blocks[j]),
+            dst_ref=other.at[k, j],
+            send_sem=c_send.at[k, j],
+            recv_sem=c_recv.at[k, j],
+            device_id=(flipped(me, 1), rank),
+            device_id_type=MESH,
+        )
+
+    def across(bit, src, dst, slot, j):
+        return pltpu.make_async_remote_copy(
+            src_ref=src,
+            dst_ref=dst,
+            send_sem=p_send.at[slot, j],
+            recv_sem=p_recv.at[slot, j],
+            device_id=(flipped(me, bit), rank),
+            device_id_type=MESH,
+        )
+
+    def diag_x(j):
+        return across(2, mine.at[3, j, low], diag_in.at[j, 0], 0, j)
+
+    def diag_y(j):
+        return across(4, mine.at[3, j, high], diag_in.at[j, 1], 1, j)
+
+    def direct_x(j):
+        return across(2, mine.at[1, j, low], last_in.at[j, 0, low], 2, j)
+
+    def direct_y(j):
+        return across(4, mine.at[2, j, high], last_in.at[j, 1, high], 3, j)
+
+    def summed_x(j):
+        return across(2, mine.at[1, j, high], last_in.at[j, 0, high], 4, j)
+
+    def summed_y(j):
+        return across(4, mine.at[2, j, low], last_in.at[j, 1, low], 5, j)
+
+    def along_z(j, right):
+        way = 0 if right else 1
+        block = blocks[j]
+        return pltpu.make_async_remote_copy(
+            src_ref=mine.at[0, j],
+            dst_ref=z_in.at[way, block],
+            send_sem=z_send.at[way, block],
+            recv_sem=z_recv.at[way, block],
+            device_id=(me, rank + 1 if right else rank - 1),
+            device_id_type=MESH,
+        )
+
+    def add(ref, spot, one):
+        ref[spot] = (ref[spot].astype(f32) + one.astype(f32)).astype(ref.dtype)
+
+    def first(j):
+        for k in (3, 2, 1, 0):
+            core(k, j).wait_recv()
+            local(k, j).wait()
+            add(mine, (k, j), other[k, j])
+            if k == 3:
+                diag_x(j).start()
+                diag_y(j).start()
+            if k == 2:
+                direct_y(j).start()
+            if k == 1:
+                direct_x(j).start()
+
+    def second(j):
+        diag_x(j).wait_recv()
+        add(mine, (2, j, low), diag_in[j, 0])
+        summed_y(j).start()
+        diag_y(j).wait_recv()
+        add(mine, (1, j, high), diag_in[j, 1])
+        summed_x(j).start()
+
+    def third(j):
+        block = blocks[j]
+        direct_x(j).wait_recv()
+        direct_y(j).wait_recv()
+        summed_x(j).wait_recv()
+        summed_y(j).wait_recv()
+        total = mine[0, j].astype(f32) + last_in[j, 0].astype(f32) + last_in[j, 1].astype(f32)
+        if j < tp - 1:
+            mine[0, j] = total.astype(bf16)
+
+            @pl.when((block > rank) & (rank > 0))
+            def _():
+                along_z(j, True).wait_recv()
+                add(mine, (0, j), z_in[0, block])
+
+            @pl.when((block < rank) & (rank < tp - 1))
+            def _():
+                along_z(j, False).wait_recv()
+                add(mine, (0, j), z_in[1, block])
+
+            @pl.when(block > rank)
+            def _():
+                along_z(j, True).start()
+
+            @pl.when(block < rank)
+            def _():
+                along_z(j, False).start()
+        else:
+            total_ref[...] = total
+
+            @pl.when(rank > 0)
+            def _():
+                along_z(j, True).wait_recv()
+                total_ref[...] += z_in[0, block].astype(f32)
+
+            @pl.when(rank < tp - 1)
+            def _():
+                along_z(j, False).wait_recv()
+                total_ref[...] += z_in[1, block].astype(f32)
+
+    span = col_buf.shape[2]
+    steps = x_ref.shape[1] // span
+    units = SHARED + shared_width
+
+    def columns(n, slot, of_x):
+        ref = x_ref if of_x else g_ref
+        return pltpu.make_async_copy(
+            ref.at[:, pl.ds(pl.multiple_of(n * span, span), span)],
+            col_buf.at[slot],
+            col_sem.at[slot],
+        )
+
+    def up_stores(n, slot):
+        at = pl.ds(pl.multiple_of(n * span, span), span)
+        return (
+            pltpu.make_async_copy(ge_buf.at[slot], ge_ref.at[:, at], out_sem.at[0, slot]),
+            pltpu.make_async_copy(gs_buf.at[slot], gs_ref.at[:, at], out_sem.at[1, slot]),
+        )
+
+    def down_stores(n, slot):
+        at = pl.ds(pl.multiple_of(n * span, span), span)
+        return (
+            pltpu.make_async_copy(de_buf.at[slot], de_ref.at[:, at], out_sem.at[2, slot]),
+            pltpu.make_async_copy(ds_buf.at[slot], ds_ref.at[n], out_sem.at[3, slot]),
+        )
+
+    def up_step(n, carry):
+        slot = n % 2
+
+        @pl.when(n + 1 < steps)
+        def _():
+            columns(n + 1, 1 - slot, True).start()
+
+        @pl.when(n + 1 == steps)
+        def _():
+            columns(0, 1 - slot, False).start()
+
+        columns(n, slot, True).wait()
+
+        @pl.when(n >= 2)
+        def _():
+            for copy in up_stores(n - 2, slot):
+                copy.wait()
+
+        grads = lax.dot_general(col_buf[slot], d_buf[...], TN, preferred_element_type=f32)
+        for part in range(2):
+            base = part * UNIT
+            ge_buf[slot, part] = grads[:, base : base + expert_width]
+            gs_buf[slot, part] = grads[:, base + SHARED : base + units].astype(bf16)
+        for copy in up_stores(n, slot):
+            copy.start()
+        return carry
+
+    def down_step(n, carry):
+        slot = n % 2
+
+        @pl.when(n + 1 < steps)
+        def _():
+            columns(n + 1, 1 - slot, False).start()
+
+        columns(n, slot, False).wait()
+
+        @pl.when(n >= 2)
+        def _():
+            for copy in down_stores(n - 2, slot):
+                copy.wait()
+
+        grads = lax.dot_general(h_buf[...], col_buf[slot], TN, preferred_element_type=f32)
+        de_buf[slot] = grads[:expert_width]
+        ds_buf[slot] = grads[SHARED:units].astype(bf16)
+        for copy in down_stores(n, slot):
+            copy.start()
+        return carry
+
+    load_d = pltpu.make_async_copy(d_ref, d_buf, w_sem.at[0])
+    load_h = pltpu.make_async_copy(h_ref, h_buf, w_sem.at[1])
+    own = pltpu.make_async_copy(own_ref, rows_ref.at[pl.ds(rank * rows, rows)], a_sem)
+    own.start()
+    for j in range(tp):
+        for k in (3, 2, 1, 0):
+            core(k, j).start()
+            local(k, j).start()
+    load_d.start()
+    columns(0, 0, True).start()
+    load_h.start()
+    own.wait()
+
+    @pl.when(rank < tp - 1)
+    def _():
+        gather_z(rank, True).start()
+
+    @pl.when(rank > 0)
+    def _():
+        gather_z(rank, False).start()
+
+    first(0)
+    first(1)
+    load_d.wait()
+    lax.fori_loop(0, 2, up_step, 0)
+    second(0)
+    gather_step(1)
+    first(2)
+    lax.fori_loop(2, 4, up_step, 0)
+    second(1)
+    first(3)
+    lax.fori_loop(4, 6, up_step, 0)
+    gather_step(2)
+    third(0)
+    second(2)
+    lax.fori_loop(6, 8, up_step, 0)
+    gather_step(3)
+    third(1)
+    second(3)
+    load_h.wait()
+    lax.fori_loop(0, steps, down_step, 0)
+    third(2)
+    third(3)
+
+    for n in (steps - 2, steps - 1):
+        for copy in up_stores(n, n % 2) + down_stores(n, n % 2):
+            copy.wait()
+    for j in range(tp):
+        for k in range(4):
+            core(k, j).wait_send()
+        for copy in (diag_x, diag_y, direct_x, direct_y, summed_x, summed_y):
+            copy(j).wait_send()
+        block = blocks[j]
+        if j < tp - 1:
+
+            @pl.when(block > rank)
+            def _():
+                along_z(j, True).wait_send()
+
+            @pl.when(block < rank)
+            def _():
+                along_z(j, False).wait_send()
+
+    for block in range(tp):
+
+        @pl.when((block <= rank) & (rank < tp - 1))
+        def _():
+            gather_z(block, True).wait_send()
+
+        @pl.when((block >= rank) & (rank > 0))
+        def _():
+            gather_z(block, False).wait_send()
+
+
+def outputs(y, own, x, d, h, g, fsdp, tp, expert_width, shared_width, collective_id):
+    rows, width = own.shape
+    tokens = y.shape[0]
+    span = width // fsdp
+    bf16 = jnp.bfloat16
+    f32 = jnp.float32
+    dma = pltpu.SemaphoreType.DMA
+    anywhere = pl.BlockSpec(memory_space=pl.ANY)
+    return pl.pallas_call(
+        functools.partial(outputs_kernel, tp, expert_width, shared_width),
+        out_shape=[
+            jax.ShapeDtypeStruct((rows, width), f32),
+            jax.ShapeDtypeStruct((rows * tp, width), bf16),
+            jax.ShapeDtypeStruct((2, width, expert_width), f32),
+            jax.ShapeDtypeStruct((2, width, shared_width), bf16),
+            jax.ShapeDtypeStruct((expert_width, width), f32),
+            jax.ShapeDtypeStruct((fsdp, shared_width, span), bf16),
+        ],
+        in_specs=[anywhere] * 6,
+        out_specs=[pl.BlockSpec(memory_space=pltpu.VMEM)] + [anywhere] * 5,
+        scratch_shapes=[
+            pltpu.VMEM((4, tp, rows, width), bf16),
+            pltpu.VMEM((4, tp, rows, width), bf16),
+            pltpu.VMEM((tp, 2, rows // 2, width), bf16),
+            pltpu.VMEM((tp, 2, rows, width), bf16),
+            pltpu.VMEM((2, tp, rows, width), bf16),
+            pltpu.VMEM((tokens, 2 * UNIT), bf16),
+            pltpu.VMEM((tokens, UNIT), bf16),
+            pltpu.VMEM((2, tokens, span), bf16),
+            pltpu.VMEM((2, 2, span, expert_width), f32),
+            pltpu.VMEM((2, 2, span, shared_width), bf16),
+            pltpu.VMEM((2, expert_width, span), f32),
+            pltpu.VMEM((2, shared_width, span), bf16),
+            dma((4, tp)), dma((4, tp)), dma((4, tp)), dma((6, tp)), dma((6, tp)),
+            dma((2, tp)), dma((2, tp)), dma, dma((2, tp)), dma((2, tp)),
+            dma((2,)), dma((2,)), dma((4, 2)),
+        ],
+        compiler_params=pltpu.CompilerParams(
+            collective_id=collective_id, has_side_effects=True, vmem_limit_bytes=60 << 20
+        ),
+        name="outputs",
+    )(y, own, x, d, h, g)
+
+
+def epilogue_kernel(fsdp, tp, parts, *refs):
+    ins, refs = refs[:parts], refs[parts:]
+    gs_ref, ds_ref, dn_ref, hidden_ref, grad_ref, gain_ref, sums_ref = refs[:7]
+    refs = refs[7:]
+    outs, refs = refs[:parts], refs[parts:]
+    gs_out, ds_out, hidden_grad_ref, gains_ref = refs[:4]
+    refs = refs[4:]
+    mine, other, diag_in, last_in = (refs[i * parts : (i + 1) * parts] for i in range(4))
+    (
+        gs_in, ds_in, dn_buf, z_in, v_send, v_in, w_send, w_in,
+        l_sem, c_send, c_recv, p_send, p_recv, s_sem, s_send, s_recv,
+        f_sem, f_send, f_recv, v_ssem, v_rsem, w_ssem, w_rsem,
+    ) = refs[4 * parts :]
+    me, rank = place()
+    f32 = jnp.float32
+    bf16 = jnp.bfloat16
+    rows, width = hidden_ref.shape
+    near = rank // 2
+    blocks = [3 * (1 - near), 2 - near, flipped(rank, 1), rank]
+    packs = [me, flipped(me, 2), flipped(me, 4), flipped(flipped(me, 2), 4)]
+    every = range(parts)
+    chunks = outs[0].shape[0]
+    sizes = [ref.shape[1] for ref in outs]
+    low = [pl.ds(0, size // 2) for size in sizes]
+    high = [pl.ds(size // 2, size // 2) for size in sizes]
+
+    def plane(bits):
+        peer = me
+        for one in (1, 2, 4):
+            if bits & one:
+                peer = flipped(peer, one)
+        return peer
+
+    def line(bits):
+        peer = rank
+        for one in (1, 2):
+            if bits & one:
+                peer = flipped(peer, one)
+        return peer
+
+    barrier = pltpu.get_barrier_semaphore()
+    for bits in range(1, fsdp):
+        pl.semaphore_signal(
+            barrier, inc=1, device_id=(plane(bits), rank), device_id_type=MESH
+        )
+    for bits in range(1, tp):
+        pl.semaphore_signal(barrier, inc=1, device_id=(me, line(bits)), device_id_type=MESH)
+    pl.semaphore_wait(barrier, fsdp - 1 + tp - 1)
+
+    def add(ref, spot, one):
+        ref[spot] = (ref[spot].astype(f32) + one.astype(f32)).astype(ref.dtype)
+
+    def region(i, pack, j):
+        return ins[i].at[pl.ds((pack * chunks + j) * sizes[i], sizes[i])]
+
+    def local(k, j, i):
+        return pltpu.make_async_copy(region(i, packs[k], j), mine[i].at[k, j], l_sem.at[k, j, i])
+
+    def core(k, j, i):
+        return pltpu.make_async_remote_copy(
+            src_ref=region(i, flipped(packs[k], 1), j),
+            dst_ref=other[i].at[k, j],
+            send_sem=c_send.at[k, j, i],
+            recv_sem=c_recv.at[k, j, i],
+            device_id=(flipped(me, 1), rank),
+            device_id_type=MESH,
+        )
+
+    def across(bit, src, dst, slot, j, i):
+        return pltpu.make_async_remote_copy(
+            src_ref=src,
+            dst_ref=dst,
+            send_sem=p_send.at[slot, j, i],
+            recv_sem=p_recv.at[slot, j, i],
+            device_id=(flipped(me, bit), rank),
+            device_id_type=MESH,
+        )
+
+    def diag_x(j, i):
+        return across(2, mine[i].at[3, j, low[i]], diag_in[i].at[j, 0], 0, j, i)
+
+    def diag_y(j, i):
+        return across(4, mine[i].at[3, j, high[i]], diag_in[i].at[j, 1], 1, j, i)
+
+    def direct_x(j, i):
+        return across(2, mine[i].at[1, j, low[i]], last_in[i].at[j, 0, low[i]], 2, j, i)
+
+    def direct_y(j, i):
+        return across(4, mine[i].at[2, j, high[i]], last_in[i].at[j, 1, high[i]], 3, j, i)
+
+    def summed_x(j, i):
+        return across(2, mine[i].at[1, j, high[i]], last_in[i].at[j, 0, high[i]], 4, j, i)
+
+    def summed_y(j, i):
+        return across(4, mine[i].at[2, j, low[i]], last_in[i].at[j, 1, low[i]], 5, j, i)
+
+    def first(j):
+        for i in every:
+            for k in (3, 2, 1, 0):
+                core(k, j, i).wait_recv()
+                local(k, j, i).wait()
+                add(mine[i], (k, j), other[i][k, j])
+                if k == 3:
+                    diag_x(j, i).start()
+                    diag_y(j, i).start()
+                if k == 2:
+                    direct_y(j, i).start()
+                if k == 1:
+                    direct_x(j, i).start()
+
+    def second(j):
+        for i in every:
+            diag_x(j, i).wait_recv()
+            add(mine[i], (2, j, low[i]), diag_in[i][j, 0])
+            summed_y(j, i).start()
+            diag_y(j, i).wait_recv()
+            add(mine[i], (1, j, high[i]), diag_in[i][j, 1])
+            summed_x(j, i).start()
+
+    def third(j):
+        for i in every:
+            direct_x(j, i).wait_recv()
+            direct_y(j, i).wait_recv()
+            summed_x(j, i).wait_recv()
+            summed_y(j, i).wait_recv()
+            outs[i][j] = (
+                mine[i][0, j].astype(f32)
+                + last_in[i][j, 0].astype(f32)
+                + last_in[i][j, 1].astype(f32)
+            )
+
+    span = ds_ref.shape[2]
+
+    def shared_up(bits):
+        at = pl.ds(pl.multiple_of(plane(bits) * span, span), span)
+        return pltpu.make_async_remote_copy(
+            src_ref=gs_ref.at[:, at],
+            dst_ref=gs_in.at[me],
+            send_sem=s_send.at[0, bits],
+            recv_sem=s_recv.at[0, bits],
+            device_id=(plane(bits), rank),
+            device_id_type=MESH,
+        )
+
+    def shared_down(bits):
+        return pltpu.make_async_remote_copy(
+            src_ref=ds_ref.at[plane(bits)],
+            dst_ref=ds_in.at[me],
+            send_sem=s_send.at[1, bits],
+            recv_sem=s_recv.at[1, bits],
+            device_id=(plane(bits), rank),
+            device_id_type=MESH,
+        )
+
+    own_up = pltpu.make_async_copy(
+        gs_ref.at[:, pl.ds(pl.multiple_of(me * span, span), span)], gs_in.at[me], s_sem.at[0]
+    )
+    own_down = pltpu.make_async_copy(ds_ref.at[me], ds_in.at[me], s_sem.at[1])
+
+    def front_load(block):
+        return pltpu.make_async_copy(
+            dn_ref.at[pl.ds(block * rows, rows)], dn_buf.at[block], f_sem.at[block]
+        )
+
+    def front_z(j, right):
+        way = 0 if right else 1
+        block = blocks[j]
+        return pltpu.make_async_remote_copy(
+            src_ref=dn_buf.at[block],
+            dst_ref=z_in.at[way, block],
+            send_sem=f_send.at[way, block],
+            recv_sem=f_recv.at[way, block],
+            device_id=(me, rank + 1 if right else rank - 1),
+            device_id_type=MESH,
+        )
+
+    def front(j):
+        block = blocks[j]
+        front_load(block).wait()
+        if j < tp - 1:
+
+            @pl.when((block > rank) & (rank > 0))
+            def _():
+                front_z(j, True).wait_recv()
+                add(dn_buf, (block,), z_in[0, block])
+
+            @pl.when((block < rank) & (rank < tp - 1))
+            def _():
+                front_z(j, False).wait_recv()
+                add(dn_buf, (block,), z_in[1, block])
+
+            @pl.when(block > rank)
+            def _():
+                front_z(j, True).start()
+
+            @pl.when(block < rank)
+            def _():
+                front_z(j, False).start()
+        else:
+            hidden_grad_ref[...] = dn_buf[block].astype(f32)
+
+            @pl.when(rank > 0)
+            def _():
+                front_z(j, True).wait_recv()
+                hidden_grad_ref[...] += z_in[0, block].astype(f32)
+
+            @pl.when(rank < tp - 1)
+            def _():
+                front_z(j, False).wait_recv()
+                hidden_grad_ref[...] += z_in[1, block].astype(f32)
+
+    share = width // fsdp
+    part = share // tp
+
+    def gains_plane(bits):
+        return pltpu.make_async_remote_copy(
+            src_ref=v_send.at[plane(bits)],
+            dst_ref=v_in.at[me],
+            send_sem=v_ssem.at[bits],
+            recv_sem=v_rsem.at[bits],
+            device_id=(plane(bits), rank),
+            device_id_type=MESH,
+        )
+
+    def gains_line(bits):
+        return pltpu.make_async_remote_copy(
+            src_ref=w_send.at[line(bits)],
+            dst_ref=w_in.at[rank],
+            send_sem=w_ssem.at[bits],
+            recv_sem=w_rsem.at[bits],
+            device_id=(me, line(bits)),
+            device_id_type=MESH,
+        )
+
+    for block in blocks:
+        front_load(block).start()
+    for j in range(chunks):
+        for i in every:
+            for k in (3, 2, 1, 0):
+                core(k, j, i).start()
+                local(k, j, i).start()
+    front(0)
+    first(0)
+    for bits in (6, 7, 2, 3, 4, 5, 1):
+        shared_up(bits).start()
+        shared_down(bits).start()
+    own_up.start()
+    own_down.start()
+    first(1)
+    second(0)
+    front(1)
+    second(1)
+    front(2)
+    front(3)
+    d_normed = hidden_grad_ref[...]
+    hidden = hidden_ref[...].astype(f32)
+    inverse = lax.rsqrt(jnp.mean(hidden * hidden, axis=-1, keepdims=True) + epsilon)
+    hat = hidden * inverse
+    v_send[...] = jnp.zeros_like(v_send)
+    attn_gain = jnp.sum(d_normed * hat, axis=0, keepdims=True)
+    for owner in range(fsdp):
+        at = slice(owner * share, (owner + 1) * share)
+        v_send[owner, 0:1] = attn_gain[:, at]
+        v_send[owner, 1:3] = sums_ref[:, at]
+    for bits in range(1, fsdp):
+        gains_plane(bits).start()
+    d_hat = d_normed * gain_ref[...]
+    mean = jnp.mean(d_hat * hat, axis=-1, keepdims=True)
+    hidden_grad_ref[...] = grad_ref[...] + inverse * (d_hat - hat * mean)
+    third(0)
+    total = v_send[me]
+    for bits in range(1, fsdp):
+        gains_plane(bits).wait_recv()
+        total = total + v_in[plane(bits)]
+    w_send[...] = jnp.zeros_like(w_send)
+    for owner in range(tp):
+        w_send[owner, :, :part] = total[:, owner * part : (owner + 1) * part]
+    for bits in range(1, tp):
+        gains_line(bits).start()
+    third(1)
+    own_up.wait()
+    own_down.wait()
+    for bits in range(1, fsdp):
+        shared_up(bits).wait_recv()
+        shared_down(bits).wait_recv()
+    units = gs_in.shape[3]
+    for owner in range(fsdp):
+        at = slice(owner * units, (owner + 1) * units)
+        gs_out[:, :, at] = gs_in[owner].astype(f32)
+        ds_out[at] = ds_in[owner].astype(f32)
+    total = w_send[rank]
+    for bits in range(1, tp):
+        gains_line(bits).wait_recv()
+        total = total + w_in[line(bits)]
+    gains_ref[...] = total
+
+    for j in range(chunks):
+        for i in every:
+            for k in range(4):
+                core(k, j, i).wait_send()
+            for copy in (diag_x, diag_y, direct_x, direct_y, summed_x, summed_y):
+                copy(j, i).wait_send()
+    for bits in range(1, fsdp):
+        shared_up(bits).wait_send()
+        shared_down(bits).wait_send()
+        gains_plane(bits).wait_send()
+    for bits in range(1, tp):
+        gains_line(bits).wait_send()
+    for j in range(tp - 1):
+        block = blocks[j]
+
+        @pl.when(block > rank)
+        def _():
+            front_z(j, True).wait_send()
+
+        @pl.when(block < rank)
+        def _():
+            front_z(j, False).wait_send()
+
+
+def epilogue(arrays, shared_up, shared_down, dn, hidden, grad, gain, sums, fsdp, tp, collective_id):
+    chunks = 2
+    parts = len(arrays)
+    rows, width = hidden.shape
+    units = shared_up.shape[2]
+    span = shared_down.shape[2]
+    f32 = jnp.float32
+    shapes = [(one.shape[0] // (fsdp * chunks), one.shape[1], one.dtype) for one in arrays]
+    scratch = [pltpu.VMEM((4, chunks, size, w), kind) for size, w, kind in shapes]
+    scratch += [pltpu.VMEM((4, chunks, size, w), kind) for size, w, kind in shapes]
+    scratch += [pltpu.VMEM((chunks, 2, size // 2, w), kind) for size, w, kind in shapes]
+    scratch += [pltpu.VMEM((chunks, 2, size, w), kind) for size, w, kind in shapes]
+    dma = pltpu.SemaphoreType.DMA
+    anywhere = pl.BlockSpec(memory_space=pl.ANY)
+    vmem = pl.BlockSpec(memory_space=pltpu.VMEM)
+    out_shape = [jax.ShapeDtypeStruct((chunks, size, w), f32) for size, w, _ in shapes]
+    out_shape += [
+        jax.ShapeDtypeStruct((2, span, fsdp * units), f32),
+        jax.ShapeDtypeStruct((fsdp * units, span), f32),
+        jax.ShapeDtypeStruct((rows, width), f32),
+        jax.ShapeDtypeStruct((8, 128), f32),
+    ]
+    return pl.pallas_call(
+        functools.partial(epilogue_kernel, fsdp, tp, parts),
+        out_shape=out_shape,
+        in_specs=[anywhere] * (parts + 3) + [vmem] * 4,
+        out_specs=[vmem] * len(out_shape),
+        scratch_shapes=scratch
+        + [
+            pltpu.VMEM((fsdp, 2, span, units), shared_up.dtype),
+            pltpu.VMEM((fsdp, units, span), shared_down.dtype),
+            pltpu.VMEM((tp, rows, width), dn.dtype),
+            pltpu.VMEM((2, tp, rows, width), dn.dtype),
+            pltpu.VMEM((fsdp, 8, width // fsdp), f32),
+            pltpu.VMEM((fsdp, 8, width // fsdp), f32),
+            pltpu.VMEM((tp, 8, 128), f32),
+            pltpu.VMEM((tp, 8, 128), f32),
+            dma((4, chunks, parts)), dma((4, chunks, parts)), dma((4, chunks, parts)),
+            dma((6, chunks, parts)), dma((6, chunks, parts)),
+            dma((2,)), dma((2, fsdp)), dma((2, fsdp)),
+            dma((tp,)), dma((2, tp)), dma((2, tp)),
+            dma((fsdp,)), dma((fsdp,)), dma((tp,)), dma((tp,)),
+        ],
+        compiler_params=pltpu.CompilerParams(
+            collective_id=collective_id, has_side_effects=True, vmem_limit_bytes=48 << 20
+        ),
+        name="epilogue",
+    )(*arrays, shared_up, shared_down, dn, hidden, grad, gain, sums)
+
+
 def dense_plan(
     hidden_in,
     out_grad,
@@ -1593,33 +2099,11 @@
     )
     ffn_inverse = inverse_rms(middle)
     normed_two_own = (middle * ffn_inverse * ffn_gain).astype(bf16)
-    (total,) = scatter_sum([token_part], experts, lax.axis_size("tp"), 3)
-    hidden_out = (middle + total).astype(bf16)
     own_start = tp_rank * own_rows
     ids_own = lax.dynamic_slice_in_dim(expert_ids, own_start, own_rows)
     picked = ids_own[:, :, None] == jnp.arange(experts, dtype=jnp.int32)
     route_grad = jnp.sum(jnp.where(picked, extra_sum[:experts].T[:, None, :], 0.0), axis=-1)
     gate_grad = extra_sum[experts]
-    units = SHARED + shared_width
-    g_down = jnp.dot(hidden_all.T, grad_all, preferred_element_type=f32)
-    g_both = jnp.dot(normed_all.T, d_all, preferred_element_type=f32)
-    g_expert_down = g_down[:expert_width][None]
-    g_expert_gate_up = jnp.stack(
-        [g_both[:, :expert_width], g_both[:, UNIT : UNIT + expert_width]], axis=1
-    )[None]
-    g_shared_gate_up = lax.all_to_all(
-        jnp.stack(
-            [g_both[:, SHARED:units], g_both[:, UNIT + SHARED : UNIT + units]], axis=1
-        ).astype(bf16),
-        "fsdp",
-        split_axis=0,
-        concat_axis=2,
-        tiled=True,
-    ).astype(f32)
-    g_shared_down = lax.all_to_all(
-        g_down[SHARED:units].astype(bf16), "fsdp", split_axis=1, concat_axis=0, tiled=True
-    ).astype(f32)
-
     own_gate = jax.nn.sigmoid(jnp.sum(normed_two_own.astype(f32) * shared_gate_vec, axis=-1))
     logit_grad = gate_grad * own_gate * (1.0 - own_gate)
     d_normed_two = d_normed_two + logit_grad[:, None] * shared_gate_vec
@@ -1627,8 +2111,26 @@
     hat_two = middle * ffn_inverse
     g_ffn_gain = jnp.sum(d_normed_two * hat_two, axis=0)
     middle_grad = out_grad.astype(f32) + norm_backward(d_normed_two, hat_two, ffn_inverse, ffn_gain)
-    d_rows = spread(middle_grad.astype(bf16))
-    g_out = jnp.dot(heads_out.T, d_rows, preferred_element_type=f32)
+    total, d_rows, g_expert_up, g_shared_up, g_expert_down, g_shared_down = outputs(
+        token_part,
+        middle_grad.astype(bf16),
+        normed_all,
+        d_all,
+        hidden_all,
+        grad_all,
+        experts,
+        lax.axis_size("tp"),
+        expert_width,
+        shared_width,
+        2,
+    )
+    hidden_out = (middle + total).astype(bf16)
+    g_out = jnp.einsum(
+        "tk,tfn->fkn",
+        heads_out,
+        d_rows.reshape(length, experts, -1),
+        preferred_element_type=f32,
+    ).astype(bf16)
     d_heads = (
         jnp.dot(d_rows, out_full.T, preferred_element_type=f32)
         .astype(bf16)
@@ -1648,37 +2150,40 @@
         [unrotate(d_query, cos_table, sin_table), unrotate(d_keys, cos_table, sin_table), d_values],
         axis=1,
     )
-    g_bias = jnp.sum(d_qkv, axis=0)
+    g_bias = jnp.sum(d_qkv, axis=0).reshape(bias_rows, experts, bias_columns).transpose(1, 0, 2)
+    g_bias = jnp.pad(g_bias, ((0, 0), (0, 32 - bias_rows), (0, 128 - bias_columns)))
     d_qkv_b = d_qkv.astype(bf16).reshape(length, -1)
-    g_qkv = jnp.dot(normed_one.T, d_qkv_b, preferred_element_type=f32).reshape(model_width, 3, local_heads, head_dim)
-    d_normed_one = head_total(jnp.dot(d_qkv_b, qkv_flat.T, preferred_element_type=f32))
-    hat_one = hidden_float * attn_inverse
-    g_attn_gain = jnp.sum(d_normed_one * hat_one, axis=0)
-    hidden_grad = middle_grad + norm_backward(d_normed_one, hat_one, attn_inverse, attn_gain)
-    g_qkv, g_bias, g_out = (
-        lax.psum_scatter(g_qkv.astype(bf16), "fsdp", scatter_dimension=0, tiled=True).astype(f32),
-        lax.psum_scatter(g_bias.astype(bf16), "fsdp", scatter_dimension=2, tiled=True).astype(f32),
-        lax.psum_scatter(g_out.astype(bf16), "fsdp", scatter_dimension=1, tiled=True).astype(f32),
-    )
-    g_attn_gain, g_ffn_gain, g_gate_vec = (
-        lax.psum_scatter(g_attn_gain, every, scatter_dimension=0, tiled=True),
-        lax.psum_scatter(g_ffn_gain, every, scatter_dimension=0, tiled=True),
-        lax.psum_scatter(g_gate_vec, every, scatter_dimension=0, tiled=True),
-    )
+    g_qkv = jnp.dot(normed_one.T, d_qkv_b, preferred_element_type=f32).astype(bf16)
+    d_normed_one = jnp.dot(d_qkv_b, qkv_flat.T, preferred_element_type=f32).astype(bf16)
+    g_qkv, g_out, g_bias, g_shared_up, g_shared_down, hidden_grad, gains = epilogue(
+        [g_qkv, g_out.reshape(-1, g_out.shape[2]), g_bias.reshape(-1, 128)],
+        g_shared_up,
+        g_shared_down,
+        d_normed_one,
+        hidden_in,
+        middle_grad,
+        attn_gain[None],
+        jnp.stack([g_ffn_gain, g_gate_vec]),
+        experts,
+        lax.axis_size("tp"),
+        3,
+    )
+    share = model_width // (experts * lax.axis_size("tp"))
+    g_bias = g_bias.reshape(32, 128)[:bias_rows, :bias_columns]
     return (
         hidden_out,
         hidden_grad,
         route_grad,
-        g_attn_gain,
-        g_ffn_gain,
-        g_qkv,
-        g_bias,
-        g_out,
-        g_shared_gate_up,
+        gains[0, :share],
+        gains[1, :share],
+        g_qkv.reshape(-1, 3, local_heads, head_dim),
+        g_bias.reshape(qkv_bias.shape),
+        g_out.reshape(out_weight.shape),
+        g_shared_up.transpose(1, 0, 2),
         g_shared_down,
-        g_gate_vec,
-        g_expert_gate_up,
-        g_expert_down,
+        gains[2, :share],
+        g_expert_up.transpose(1, 0, 2)[None],
+        g_expert_down[None],
     )
 
 

time: 757 us -> 695 us (0.918)
  Pallas kernels: 389 us -> 499 us
  waiting for transfers between devices: 84.3 us -> 12.5 us
  matrix products: 83.4 us -> 40.6 us
  blocking collectives: 38.3 us -> 0 us
  starting transfers between devices: 23.4 us -> 9.68 us
  local copies, waits for them, and re-layouts: 81.5 us -> 93.3 us
  other arithmetic: 31.4 us -> 20.5 us
    pallas_call x1 -> x2, Pallas kernels: 99.9 us -> 207 us  [the longest x1 112 us: outputs(): pl.pallas_call(functools.partial(outputs_kernel, tp, expert_width, shared...]
    all_gather x1 -> x0, waiting for transfers between devices: 48.9 us -> none  [spread(): return lax.all_gather(rows, 'tp', axis=0, tiled=True)]
    dot_general x5 -> x3, matrix products: 64.3 us -> 18 us  [the longest x1 8.17 us: dense_plan(): jnp.dot(d_qkv_b, qkv_flat.T, preferred_element_type=f32).astype(bf16)]
    unnamed x1 -> x0, blocking collectives: 38.3 us -> none
    all_to_all x2 -> x0, waiting for transfers between devices: 22.2 us -> none  [the longest x1 15.1 us: dense_plan(): lax.all_to_all(jnp.stack([g_both[:, SHARED:units], g_both[:, UNIT + SHARE...]
    all_to_all x2 -> x0, starting transfers between devices: 8.82 us -> none  [the longest x1 4.6 us: dense_plan(): lax.all_to_all(jnp.stack([g_both[:, SHARED:units], g_both[:, UNIT + SHARE...]
    another operation x3 -> x0, local copies, waits for them, and re-layouts: 8.76 us -> none  [the longest x1 4.83 us: dense_plan(): jnp.stack([g_both[:, :expert_width], g_both[:, UNIT:UNIT + expert_width]]...]
    unnamed x107 -> x106, local copies, waits for them, and re-layouts: 27.5 us -> 34.6 us
  transfers between devices with their start and end apart: 10 -> 3, of which waited for: 5 -> 1; matrix products, arithmetic and copies ran while one was open for 22% -> 10% of each run, Pallas kernels for 9% -> 10%
where the time goes in v5:
time: 695 us; the launch traced here: 691 us
  Pallas kernels  499 us (72%)
  local copies, waits for them, and re-layouts  93.3 us (13%)
  matrix products  40.6 us (6%)
  other arithmetic  20.5 us (3%)
  between operations  15 us (2%)
  waiting for transfers between devices  12.5 us (2%)
  starting transfers between devices  9.68 us (1%)
    pallas_call x1, Pallas kernels, ffn(): pl.pallas_call(functools.partial(ffn_kernel, tp, expert_width, shared_wid...  223 us
    pallas_call x1, Pallas kernels, outputs(): pl.pallas_call(functools.partial(outputs_kernel, tp, expert_width, shared...  112 us
    pallas_call x1, Pallas kernels, epilogue(): pl.pallas_call(functools.partial(epilogue_kernel, fsdp, tp, parts), out_s...  94.8 us
    pallas_call x1, Pallas kernels, prologue(): pl.pallas_call(functools.partial(prologue_kernel, tp, halved), out_shape=...  69.5 us
    unnamed x106, local copies, waits for them, and re-layouts  34.6 us
  transfers between devices with their start and end apart: 3, of which 1 were waited for; matrix products, arithmetic and copies ran while one was open for 10% of the time, Pallas kernels for 10%

profile of v5, /device:TPU:0, one launch (start us, length us, event | category | flops | bytes accessed | tf_op | source)
XLA Modules:
  0.0 691.0 jit_solution(5020373172386144190)
XLA Ops:
  7.9 5.2 all-to-all-start.1
  18.5 4.0 copy.124
  22.5 4.7 copy.123
  27.7 69.5 %prologue.1 = (bf16[512,2048]{1,0:T(8,128)(2,1)S(1)}, bf16[2048,1536]{1,0:T(8,128)(2,1)S(1)}, bf16[4096,256]{1,0:T(8,128)(2,1)S(1)}, f32[64,512]{1,0:T(8,128)S(1)}, f32[128,128]{1,0:T(8,128)S(1)}) custom-call(bf16[128,2048]{1,0:T(8,128)(2,1)S(1)} %fusion.8.refs_0_, bf16[256,1536]{1,0:T(8,128)(2,1)S(1)} %reshape.219.refs_1_, bf16[512,256]{1,0:T(8,128)(2,1)S(1)} %copy-done.8, ...), custom_call_target="tpu_custom_call" | custom-call | tf_op jit(solution)/shard_map/prologue/pallas_call | solution.py:526
  98.5 3.8 copy-done.10
  102.4 3.9 copy.122
  106.3 7.9 %fusion.25 = f32[512,1536]{1,0:T(8,128)} fusion(bf16[512,2048]{1,0:T(8,128)(2,1)S(1)} %get-tuple-element.38, bf16[2048,1536]{1,0:T(8,128)(2,1)} %copy-done.10), kind=kOutput, calls=%fused_computation.89 | convolution fusion | flops 3221225472 | bytes 11534336 | tf_op jit(solution)/shard_map/dot_general | solution.py:2049
  114.2 4.9 reshape.221
  130.8 4.5 all-to-all-start
  135.9 4.0 slice_bitcast_fusion
  143.1 11.8 %all-to-all-done = bf16[256,2,1408]{0,1,2:T(2,128)(2,1)} async-done(((bf16[256,2,1408]{0,1,2:T(2,128)(2,1)}), bf16[256,2,1408]{0,1,2:T(2,128)(2,1)}, u32[]{:S(2)}, u32[]{:S(2)}) %all-to-all-start) | async-done | bytes 1441824 | tf_op jit(solution)/shard_map/all_to_all | solution.py:2011
  157.6 3.7 copy.126
  166.1 10.9 %concatenate.22.refs_4_ = bf16[2048,1280]{1,0:T(8,128)(2,1)} concatenate(bf16[2048,352]{1,0:T(8,128)(2,1)} %get-tuple-element.123, bf16[2048,32]{1,0:T(8,128)(2,1)S(1)} %broadcast_in_dim.103, bf16[2048,176]{1,0:T(8,128)(2,1)} %get-tuple-element.127, bf16[2048,1]{1,0:T(8,128)(2,1)} %broadcast_in_dim.114, bf16[2048,1]{1,0:T(8,128)(2,1)S(1)} %copy-done.32, bf16[2048,78]{1,0:T(8,128)(2,1)} %slice.80, ...), dimensions={1} | concatenate | bytes 10485760 | tf_op jit(solution)/shard_map/concatenate | solution.py:2070
  179.0 222.7 %ffn.1 = (f32[128,2048]{1,0:T(8,128)}, bf16[4096,2048]{1,0:T(8,128)(2,1)}, bf16[4096,1280]{1,0:T(8,128)(2,1)}, bf16[4096,640]{1,0:T(8,128)(2,1)}, bf16[4096,2048...) custom-call(bf16[512,2048]{1,0:T(8,128)(2,1)} %convolution_convert_fusion.2.refs_0_, ...), custom_call_target="tpu_custom_call" | custom-call | tf_op jit(solution)/shard_map/ffn/pallas_call | solution.py:1206
  409.6 112.4 %outputs.1 = (f32[128,2048]{1,0:T(8,128)}, bf16[512,2048]{1,0:T(8,128)(2,1)}, f32[2,2048,352]{2,1,0:T(8,128)}, bf16[2,2048,176]{2,1,0:T(8,128)(2,1)}, f32[352,2048]{1,0:T(8,128)}, /*index=5*/bf16[8,176,256]{2,1,0:T(8,128)(2,1)}) custom-call(bf16[4096,2048]{1,0:T(8,128)(2,1)} %get-tuple-element.44.refs_0_, bf16[128,2048]{1,0:T(8,128)(2,1)} %get-tuple-element.118.refs_1_, ...), custom_call_target="tpu_custom_call" | custom-call | tf_op jit(solution)/shard_map/outputs/pallas_call | solution.py:1577
  522.0 3.7 multiply_reduce_fusion.1
  535.4 4.1 copy.160
  542.1 8.2 %convolution_convert_fusion.1.refs_5_ = bf16[512,2048]{1,0:T(8,128)(2,1)} fusion(bf16[512,1536]{0,1:T(8,128)(2,1)} %bitcast.125, bf16[2048,1536]{1,0:T(8,128)(2,1)} %copy-done.10), kind=kOutput, calls=%fused_computation.8 | convolution fusion | flops 3222274048 | bytes 9961472 | tf_op jit(solution)/shard_map/dot_general | solution.py:2157
  550.2 5.5 convolution_convert_fusion.refs_0_
  556.8 4.3 convert_bitcast_fusion
  561.1 4.0 copy.143
  566.2 94.8 %epilogue.1 = (f32[2,128,1536]{2,1,0:T(8,128)}, f32[2,256,256]{2,1,0:T(8,128)S(1)}, f32[2,16,128]{2,1,0:T(8,128)S(1)}, f32[2,256,1408]{2,1,0:T(8,128)}, f32[1408...) custom-call(bf16[2048,1536]{1,0:T(8,128)(2,1)} %convolution_convert_fusion.refs_0_, ...), custom_call_target="tpu_custom_call" | custom-call | tf_op jit(solution)/shard_map/epilogue/pallas_call | solution.py:1955
  666.7 5.6 copy.145
  672.3 6.5 copy.146
  (167 shorter events, 65.6 us)
Async XLA Ops:
  7.2 11.0 %copy-start.37 = (bf16[256,3,4,128]{3,2,1,0:T(4,128)(2,1)S(1)}, bf16[256,3,4,128]{3,2,1,0:T(4,128)(2,1)}, u32[]{:S(2)}) copy-start(bf16[256,3,4,128]{3,2,1,0:T(4,128)(2,1)} %param.22) | copy-start | bytes 2359300
  7.2 11.3 %copy-start.34 = (bf16[256,2,1408]{2,1,0:T(2,128)(2,1)S(1)}, bf16[256,2,1408]{2,1,0:T(2,128)(2,1)}, u32[]{:S(2)}) copy-start(bf16[256,2,1408]{2,1,0:T(2,128)(2,1)} %param.25) | copy-start | bytes 4325380
  7.2 169.9 %all-gather.2.cloned.1.call-start = ((), (), s32[]{:S(2)}) async-start(), calls=%async_computation.2 | async-start | bytes 17301504 | tf_op jit(solution)/shard_map/all_gather | solution.py:2010
  7.9 122.9 %all-to-all-start.1 = ((bf16[8,176,256]{2,1,0:T(8,128)(2,1)}), bf16[8,176,256]{2,1,0:T(8,128)(2,1)}, u32[]{:S(2)}, u32[]{:S(2)}) async-start(bf16[8,176,256]{2,1,0:T(8,128)(2,1)} %bitcast.128), calls=%async_computation.1 | async-start | bytes 1441792 | tf_op jit(solution)/shard_map/all_to_all | solution.py:2012
  22.5 5.0 copy-start.9
  22.5 5.2 copy-start.8
  114.2 4.9 copy-start.41
  130.8 24.1 %all-to-all-start = ((bf16[256,2,1408]{0,1,2:T(2,128)(2,1)}), bf16[256,2,1408]{0,1,2:T(2,128)(2,1)}, u32[]{:S(2)}, u32[]{:S(2)}) async-start(bf16[256,2,1408]{0,1,2:T(2,128)(2,1)} %copy.124), calls=%async_computation | async-start | bytes 2883584 | tf_op jit(solution)/shard_map/all_to_all | solution.py:2011
  135.8 5.2 copy-start.35
  135.8 5.2 copy-start.42
  135.9 5.2 copy-start.43
  161.2 4.9 copy-start.32
  179.0 224.3 %copy-start.38 = (f32[2048]{0:T(1024)S(1)}, f32[2048]{0:T(1024)}, u32[]{:S(2)}) copy-start(f32[2048]{0:T(1024)} %param.27) | copy-start | bytes 24580
  179.0 224.3 %copy-start.39 = (f32[2048]{0:T(1024)S(1)}, f32[2048]{0:T(1024)}, u32[]{:S(2)}) copy-start(f32[2048]{0:T(1024)} %param.21) | copy-start | bytes 24580
  401.8 6.6 copy-start.11
  401.8 6.6 copy-start.24
  401.8 6.6 copy-start.30
  409.6 112.4 %copy-start.47 = (bf16[4,128,512]{2,1,0:T(8,128)(2,1)S(1)}, bf16[4,128,512]{2,1,0:T(8,128)(2,1)}, u32[]{:S(2)}) copy-start(bf16[4,128,512]{2,1,0:T(8,128)(2,1)} %copy-done.46) | copy-start | bytes 1572868
  542.1 8.2 %copy-start.33 = (bf16[512,3,4,128]{0,3,2,1:T(8,128)(2,1)S(1)}, bf16[512,3,4,128]{0,3,2,1:T(8,128)(2,1)}, u32[]{:S(2)}) copy-start(bf16[512,3,4,128]{0,3,2,1:T(8,128)(2,1)} %copy.140) | copy-start | bytes 4718596
  550.2 5.5 copy-start.12
  550.2 5.5 copy-start.36
  672.3 6.5 copy-start.44
  672.3 7.1 %copy-start.4 = (f32[128,2048]{1,0:T(8,128)S(1)}, f32[128,2048]{1,0:T(8,128)}, u32[]{:S(2)}) copy-start(f32[128,2048]{1,0:T(8,128)} %copy-done.3) | copy-start | bytes 3145732
  672.3 8.1 %copy-start.7 = (f32[2,256,256]{2,1,0:T(8,128)S(1)}, f32[2,256,256]{2,1,0:T(8,128)}, u32[]{:S(2)}) copy-start(f32[2,256,256]{2,1,0:T(8,128)} %copy-done.6) | copy-start | bytes 1572868
  (27 other events, 65.3 us)
Sparse Core Ops, SparseCore 0:
  11.0 140.6 all-gather.1

commit v6 on v5

--- a/solution.py
+++ b/solution.py
@@ -373,678 +373,560 @@
     pl.semaphore_wait(barrier, 3 + left + right)
 
 
-def prologue_kernel(tp, halved, *refs):
-    parts = len(halved)
-    own_ref, pieces = refs[0], refs[1 : 1 + parts]
-    rows_ref, fulls = refs[1 + parts], refs[2 + parts : 2 + 2 * parts]
-    l_sem, z_send, z_recv, p_send, p_recv = refs[2 + 2 * parts :]
-    me, rank = place()
-    greet(me, rank, tp)
-    rows = own_ref.shape[0]
-
-    def along_z(block, right):
-        way = 0 if right else 1
-        spot = rows_ref.at[pl.ds(block * rows, rows)]
-        return pltpu.make_async_remote_copy(
-            src_ref=spot,
-            dst_ref=spot,
-            send_sem=z_send.at[way, block],
-            recv_sem=z_recv.at[way, block],
-            device_id=(me, rank + 1 if right else rank - 1),
-            device_id_type=MESH,
-        )
-
-    def region(i, owner_bits, start=0, count=None):
-        owner = me
-        for one in (2, 4):
-            if owner_bits & one:
-                owner = flipped(owner, one)
-        size = pieces[i].shape[0]
-        count = size if count is None else count
-        return fulls[i].at[pl.ds(owner * size + start, count)]
-
-    def across(i, bit, owner_bits, slot, start=0, count=None):
-        spot = region(i, owner_bits, start, count)
-        return pltpu.make_async_remote_copy(
-            src_ref=pieces[i] if owner_bits == 0 else spot,
-            dst_ref=spot,
-            send_sem=p_send.at[slot, i],
-            recv_sem=p_recv.at[slot, i],
-            device_id=(flipped(me, bit), rank),
-            device_id_type=MESH,
-        )
-
-    def to_core(q, i):
-        return across(i, 1, 2 * q, q)
-
-    def own_x(i):
-        return across(i, 2, 0, 4)
-
-    def own_y(i):
-        return across(i, 4, 0, 5)
-
-    def x_to_y(i):
-        size = pieces[i].shape[0]
-        return across(i, 4, 2, 6, 0, size // 2 if halved[i] else size)
-
-    def y_to_x(i):
-        size = pieces[i].shape[0]
-        return across(i, 2, 4, 7, size // 2, size // 2)
-
-    def local(i):
-        return pltpu.make_async_copy(pieces[i], region(i, 0), l_sem.at[i])
-
-    def forward(i):
-        own_x(i).wait_recv()
-        x_to_y(i).start()
-        to_core(1, i).start()
-        own_y(i).wait_recv()
-        if halved[i]:
-            y_to_x(i).start()
-        to_core(2, i).start()
-
-    def finish(i):
-        x_to_y(i).wait_recv()
-        if halved[i]:
-            y_to_x(i).wait_recv()
-        to_core(3, i).start()
-
-    def z_step(step):
-        @pl.when(rank >= step)
-        def _():
-            along_z(rank - step, True).wait_recv()
-
-            @pl.when(rank < tp - 1)
-            def _():
-                along_z(rank - step, True).start()
-
-        @pl.when(rank + step < tp)
-        def _():
-            along_z(rank + step, False).wait_recv()
-
-            @pl.when(rank > 0)
-            def _():
-                along_z(rank + step, False).start()
-
-    for i in range(parts):
-        own_x(i).start()
-        own_y(i).start()
-        to_core(0, i).start()
-    mine = pltpu.make_async_copy(own_ref, rows_ref.at[pl.ds(rank * rows, rows)], l_sem.at[parts])
-    mine.start()
-    for i in range(parts):
-        local(i).start()
-    mine.wait()
-
-    @pl.when(rank < tp - 1)
-    def _():
-        along_z(rank, True).start()
-
-    @pl.when(rank > 0)
-    def _():
-        along_z(rank, False).start()
-
-    z_step(1)
-    forward(0)
-    z_step(2)
-    for i in range(1, parts):
-        forward(i)
-    finish(0)
-    z_step(3)
-    for i in range(1, parts):
-        finish(i)
-    for i in range(parts):
-        local(i).wait()
-        for q in range(4):
-            to_core(q, i).wait_recv()
-    for i in range(parts):
-        for q in range(4):
-            to_core(q, i).wait_send()
-        own_x(i).wait_send()
-        own_y(i).wait_send()
-        x_to_y(i).wait_send()
-        if halved[i]:
-            y_to_x(i).wait_send()
-    for block in range(tp):
-
-        @pl.when((block <= rank) & (rank < tp - 1))
-        def _():
-            along_z(block, True).wait_send()
-
-        @pl.when((block >= rank) & (rank > 0))
-        def _():
-            along_z(block, False).wait_send()
-
-
-def prologue(own, pieces, fsdp, tp, collective_id):
-    parts = len(pieces)
-    halved = [one.shape[0] >= 32 for one in pieces]
-    dma = pltpu.SemaphoreType.DMA
-    anywhere = pl.BlockSpec(memory_space=pl.ANY)
-    shapes = [(own.shape[0] * tp, own.shape[1])]
-    shapes += [(one.shape[0] * fsdp, one.shape[1]) for one in pieces]
-    return pl.pallas_call(
-        functools.partial(prologue_kernel, tp, halved),
-        out_shape=[
-            jax.ShapeDtypeStruct(shape, one.dtype) for shape, one in zip(shapes, [own] + pieces)
-        ],
-        in_specs=[anywhere] * (1 + parts),
-        out_specs=[anywhere] * (1 + parts),
-        scratch_shapes=[
-            dma((parts + 1,)),
-            dma((2, tp)),
-            dma((2, tp)),
-            dma((8, parts)),
-            dma((8, parts)),
-        ],
-        compiler_params=pltpu.CompilerParams(
-            collective_id=collective_id, has_side_effects=True, vmem_limit_bytes=16 << 20
-        ),
-        name="prologue",
-    )(own, *pieces)
-
-
 UNIT = 640
 SHARED = 384
 NT = (((1,), (1,)), ((), ()))
 
 
 def ffn_kernel(tp, expert_width, shared_width, *refs):
-    part_ref, hidden_ref, gain_ref, grad_ref, both_ref, down_ref, scale_ref = refs[:7]
-    middle_ref, all_ref, d_ref, hid_ref, y_ref, dsum_ref, esum_ref = refs[7:14]
+    part_ref, hidden_ref, gain_ref, vec_ref, scale_ref, grad_ref = refs[:6]
+    expert_up, shared_up, expert_down, shared_down = refs[6:10]
+    middle_ref, all_ref, grads_ref, d_ref, hid_ref, y_ref, dsum_ref, esum_ref = refs[10:18]
     (
-        n_buf, g_buf, x_buf, dh_buf, d_buf, stage, acc, diag_in, last_in, z_in,
-        stage_e, acc_e, other_e, diag_e, last_e, z_in_e,
-        local_sem, g_sem, x_sem, d_sem, h_sem, y_sem,
-        az_send, az_recv, ap_send, ap_recv,
+        x_all, g_buf, dh_buf, d_buf, stage, acc, diag_in, last_in, z_in, both_buf, down_buf,
+        eu_buf, su_buf, stage_e, acc_e, other_e, diag_e, last_e, z_in_e,
+        local_sem, w_sem, dn_sem, g_sem, x_sem, d_sem, h_sem, y_sem, f_sem, f_send, f_recv,
+        az_send, az_recv, ap_send, ap_recv, gp_send, gp_recv,
         c_send, c_recv, ce_send, ce_recv, p_send, p_recv, pe_send, pe_recv,
-        z_send, z_recv, ze_send, ze_recv, f_sem, f_send, f_recv,
-    ) = refs[14:]
+        z_send, z_recv, ze_send, ze_recv,
+    ) = refs[18:]
     me, rank = place()
     greet(me, rank, tp)
     f32 = jnp.float32
     bf16 = jnp.bfloat16
-    rows = hidden_ref.shape[0]
-    pack_rows = rows * tp
-    tile = pack_rows // 2
+    subs, rows, width = hidden_ref.shape
+    tile = tp * rows
+    pack_rows = subs * tile
+    packs = x_all.shape[0]
     near = rank // 2
-    tokens = all_ref.shape[0]
-
-    def region(pack, block, start=0, count=None):
-        count = rows if count is None else count
-        return all_ref.at[pl.ds(pack * pack_rows + block * rows + start, count)]
-
-    def gather_z(block, right):
-        way = 0 if right else 1
-        ref = region(me, block)
+    order = [rank]
+    for bit in (1, 2):
+        order = order + [flipped(one, bit) for one in order]
+    blocks = [3 * (1 - near), 2 - near, flipped(rank, 1), rank]
+    core_of, x_of, y_of = me % 2, (me // 2) % 2, me // 4
+
+    def pack_of(bits):
+        return (
+            4 * ((y_of + bits // 4) % 2)
+            + 2 * ((x_of + (bits // 2) % 2) % 2)
+            + (core_of + bits % 2) % 2
+        )
+
+    def add(ref, spot, one):
+        ref[spot] = (ref[spot].astype(f32) + one.astype(f32)).astype(ref.dtype)
+
+    def remote(src, dst, send, recv, bit):
         return pltpu.make_async_remote_copy(
-            src_ref=ref,
-            dst_ref=ref,
-            send_sem=az_send.at[way, block],
-            recv_sem=az_recv.at[way, block],
+            src_ref=src,
+            dst_ref=dst,
+            send_sem=send,
+            recv_sem=recv,
+            device_id=(flipped(me, bit), rank),
+            device_id_type=MESH,
+        )
+
+    def remote_z(src, dst, send, recv, right):
+        return pltpu.make_async_remote_copy(
+            src_ref=src,
+            dst_ref=dst,
+            send_sem=send,
+            recv_sem=recv,
             device_id=(me, rank + 1 if right else rank - 1),
             device_id_type=MESH,
         )
 
-    def gather(bit, pack_bits, block, slot, start=0, count=None):
-        pack = me
-        for one in (2, 4):
-            if pack_bits & one:
-                pack = flipped(pack, one)
-        ref = region(pack, block, start, count)
-        return pltpu.make_async_remote_copy(
-            src_ref=ref,
-            dst_ref=ref,
-            send_sem=ap_send.at[slot, block],
-            recv_sem=ap_recv.at[slot, block],
-            device_id=(flipped(me, bit), rank),
-            device_id_type=MESH,
-        )
-
-    def to_core(q, block):
-        return gather(1, 2 * q, block, q)
-
-    def own_x(block):
-        return gather(2, 0, block, 4)
-
-    def own_y(block):
-        return gather(4, 0, block, 5)
-
-    def x_to_y(block):
-        return gather(4, 2, block, 6, 0, rows // 2)
-
-    def y_to_x(block):
-        return gather(2, 4, block, 7, rows // 2, rows // 2)
-
-    def start_plane(block):
-        own_x(block).start()
-        own_y(block).start()
-        to_core(0, block).start()
-
-    def forward(block):
-        own_x(block).wait_recv()
-        x_to_y(block).start()
-        to_core(1, block).start()
-        own_y(block).wait_recv()
-        y_to_x(block).start()
-        to_core(2, block).start()
-
-    def finish(block):
-        x_to_y(block).wait_recv()
-        y_to_x(block).wait_recv()
-        to_core(3, block).start()
-
-    def z_step(step):
+    def gather_z(block, sub, right):
+        way = 0 if right else 1
+        ref = x_all.at[me, block, sub]
+        return remote_z(
+            ref, ref, az_send.at[way, block, sub], az_recv.at[way, block, sub], right
+        )
+
+    def gather(bit, pack_bits, block, sub, slot, start=0, count=None):
+        count = rows if count is None else count
+        ref = x_all.at[pack_of(pack_bits), block, sub, pl.ds(start, count)]
+        return remote(ref, ref, ap_send.at[slot, block, sub], ap_recv.at[slot, block, sub], bit)
+
+    def to_core(q, block, sub):
+        return gather(1, 2 * q, block, sub, q)
+
+    def own_x(block, sub):
+        return gather(2, 0, block, sub, 4)
+
+    def own_y(block, sub):
+        return gather(4, 0, block, sub, 5)
+
+    def x_to_y(block, sub):
+        return gather(4, 2, block, sub, 6, 0, rows // 2)
+
+    def y_to_x(block, sub):
+        return gather(2, 4, block, sub, 7, rows // 2, rows // 2)
+
+    def start_plane(block, sub):
+        own_x(block, sub).start()
+        own_y(block, sub).start()
+        to_core(0, block, sub).start()
+
+    def start_rows(sub):
+        @pl.when(rank < tp - 1)
+        def _():
+            gather_z(rank, sub, True).start()
+
+        @pl.when(rank > 0)
+        def _():
+            gather_z(rank, sub, False).start()
+
+        start_plane(rank, sub)
+
+    def forward(place_in, sub):
+        block = order[place_in]
+        own_x(block, sub).wait_recv()
+        x_to_y(block, sub).start()
+        to_core(1, block, sub).start()
+        own_y(block, sub).wait_recv()
+        y_to_x(block, sub).start()
+        to_core(2, block, sub).start()
+
+    def finish(place_in, sub):
+        block = order[place_in]
+        x_to_y(block, sub).wait_recv()
+        y_to_x(block, sub).wait_recv()
+        to_core(3, block, sub).start()
+
+    def z_step(step, sub):
         @pl.when(rank >= step)
         def _():
             block = rank - step
-            gather_z(block, True).wait_recv()
+            gather_z(block, sub, True).wait_recv()
 
             @pl.when(rank < tp - 1)
             def _():
-                gather_z(block, True).start()
-
-            start_plane(block)
+                gather_z(block, sub, True).start()
+
+            start_plane(block, sub)
 
         @pl.when(rank + step < tp)
         def _():
             block = rank + step
-            gather_z(block, False).wait_recv()
+            gather_z(block, sub, False).wait_recv()
 
             @pl.when(rank > 0)
             def _():
-                gather_z(block, False).start()
-
-            start_plane(block)
-
-    order = [rank]
-    for bit in (1, 2):
-        order = order + [flipped(one, bit) for one in order]
+                gather_z(block, sub, False).start()
+
+            start_plane(block, sub)
 
     def control(i):
         steps = {
-            0: [(forward, order[0])],
-            1: [(z_step, 2), (forward, order[1])],
-            2: [(z_step, 3)],
-            3: [(finish, order[0])],
-            4: [(finish, order[1])],
-            5: [(forward, order[2])],
-            7: [(forward, order[3])],
-            8: [(finish, order[2])],
-            11: [(finish, order[3])],
+            0: [(z_step, 1, 1), (finish, 1, 0)],
+            1: [(forward, 3, 0)],
+            2: [(forward, 0, 1), (finish, 2, 0)],
+            3: [(z_step, 2, 1)],
+            4: [(finish, 3, 0), (forward, 1, 1)],
+            5: [(z_step, 3, 1)],
+            6: [(finish, 0, 1)],
+            7: [(forward, 2, 1)],
+            8: [(finish, 1, 1)],
+            9: [(forward, 3, 1)],
+            10: [(finish, 2, 1)],
+            11: [(finish, 3, 1)],
         }
         for at, todo in steps.items():
 
             @pl.when(i == at)
             def _():
-                for act, what in todo:
-                    act(what)
-
-    def core(q, h):
-        return pltpu.make_async_remote_copy(
-            src_ref=stage.at[h],
-            dst_ref=acc.at[q, h],
-            send_sem=c_send.at[q, h],
-            recv_sem=c_recv.at[q, h],
-            device_id=(flipped(me, 1), rank),
-            device_id_type=MESH,
-        )
+                for act, what, sub in todo:
+                    act(what, sub)
+
+    def grad_region(pack, c, start=0, count=None):
+        count = tile if count is None else count
+        return grads_ref.at[pl.ds(pack * pack_rows + c * tile + start, count)]
+
+    def grads(bit, pack_bits, c, slot, start=0, count=None):
+        dst = grad_region(pack_of(pack_bits), c, start, count)
+        src = grad_ref.at[pl.ds(c * tile, tile)] if pack_bits == 0 else dst
+        return remote(src, dst, gp_send.at[slot, c], gp_recv.at[slot, c], bit)
+
+    def grad_core(q, c):
+        return grads(1, 2 * q, c, q)
+
+    def grad_x(c):
+        return grads(2, 0, c, 4)
+
+    def grad_y(c):
+        return grads(4, 0, c, 5)
+
+    def grad_x_to_y(c):
+        return grads(4, 2, c, 6, 0, tile // 2)
+
+    def grad_y_to_x(c):
+        return grads(2, 4, c, 7, tile // 2, tile // 2)
+
+    def grad_forward(c):
+        grad_x(c).wait_recv()
+        grad_x_to_y(c).start()
+        grad_core(1, c).start()
+        grad_y(c).wait_recv()
+        grad_y_to_x(c).start()
+        grad_core(2, c).start()
+
+    def grad_finish(c):
+        grad_x_to_y(c).wait_recv()
+        grad_y_to_x(c).wait_recv()
+        grad_core(3, c).start()
+
+    def core(q, s):
+        return remote(stage.at[s], acc.at[q, s], c_send.at[q, s], c_recv.at[q, s], 1)
 
     def core_e(q):
-        return pltpu.make_async_remote_copy(
-            src_ref=stage_e.at[q],
-            dst_ref=other_e.at[q],
-            send_sem=ce_send.at[q],
-            recv_sem=ce_recv.at[q],
-            device_id=(flipped(me, 1), rank),
-            device_id_type=MESH,
-        )
-
-    def across(bit, src, dst, slot, h):
-        return pltpu.make_async_remote_copy(
-            src_ref=src,
-            dst_ref=dst,
-            send_sem=p_send.at[slot, h],
-            recv_sem=p_recv.at[slot, h],
-            device_id=(flipped(me, bit), rank),
-            device_id_type=MESH,
-        )
-
-    def diag_x(h):
-        return across(2, acc.at[3, h, 0], diag_in.at[h, 0], 0, h)
-
-    def diag_y(h):
-        return across(4, acc.at[3, h, 1], diag_in.at[h, 1], 1, h)
-
-    def direct_x(h):
-        return across(2, acc.at[1, h, 0], last_in.at[h, 0, 0], 2, h)
-
-    def direct_y(h):
-        return across(4, acc.at[2, h, 1], last_in.at[h, 1, 1], 3, h)
-
-    def summed_x(h):
-        return across(2, acc.at[1, h, 1], last_in.at[h, 0, 1], 4, h)
-
-    def summed_y(h):
-        return across(4, acc.at[2, h, 0], last_in.at[h, 1, 0], 5, h)
-
-    def across_e(bit, src, dst, slot):
-        return pltpu.make_async_remote_copy(
-            src_ref=src,
-            dst_ref=dst,
-            send_sem=pe_send.at[slot],
-            recv_sem=pe_recv.at[slot],
-            device_id=(flipped(me, bit), rank),
-            device_id_type=MESH,
-        )
+        return remote(stage_e.at[q], other_e.at[q], ce_send.at[q], ce_recv.at[q], 1)
+
+    low, high = pl.ds(0, tp // 2), pl.ds(tp // 2, tp // 2)
+
+    def across(bit, src, dst, slot, s):
+        return remote(src, dst, p_send.at[slot, s], p_recv.at[slot, s], bit)
+
+    def diag_x(s):
+        return across(2, acc.at[3, s, low], diag_in.at[s, 0], 0, s)
+
+    def diag_y(s):
+        return across(4, acc.at[3, s, high], diag_in.at[s, 1], 1, s)
+
+    def direct_x(s):
+        return across(2, acc.at[1, s, low], last_in.at[s, 0, low], 2, s)
+
+    def direct_y(s):
+        return across(4, acc.at[2, s, high], last_in.at[s, 1, high], 3, s)
+
+    def summed_x(s):
+        return across(2, acc.at[1, s, high], last_in.at[s, 0, high], 4, s)
+
+    def summed_y(s):
+        return across(4, acc.at[2, s, low], last_in.at[s, 1, low], 5, s)
 
     def diag_lines():
-        return across_e(2, acc_e.at[3], diag_e, 0)
+        return remote(acc_e.at[3], diag_e, pe_send.at[0], pe_recv.at[0], 2)
 
     def direct_lines():
-        return across_e(2, acc_e.at[1], last_e.at[0], 1)
+        return remote(acc_e.at[1], last_e.at[0], pe_send.at[1], pe_recv.at[1], 2)
 
     def summed_lines():
-        return across_e(4, acc_e.at[2], last_e.at[1], 2)
-
-    blocks = [3 * (1 - near), 2 - near, flipped(rank, 1), rank]
-
-    def along_z(j, right):
+        return remote(acc_e.at[2], last_e.at[1], pe_send.at[2], pe_recv.at[2], 4)
+
+    def along_z(j, s, right):
         way = 0 if right else 1
         block = blocks[j]
-        return pltpu.make_async_remote_copy(
-            src_ref=acc.at[0, j // 2, block % 2],
-            dst_ref=z_in.at[way, block],
-            send_sem=z_send.at[way, block],
-            recv_sem=z_recv.at[way, block],
-            device_id=(me, rank + 1 if right else rank - 1),
-            device_id_type=MESH,
-        )
-
-    def along_z_e(j, right):
+        return remote_z(
+            acc.at[0, s, block],
+            z_in.at[way, block, s],
+            z_send.at[way, block, s],
+            z_recv.at[way, block, s],
+            right,
+        )
+
+    def lines_z(right):
+        way = 0 if right else 1
+        return remote_z(
+            acc_e.at[1 + way], z_in_e.at[way], ze_send.at[way], ze_recv.at[way], right
+        )
+
+    def second(s):
+        diag_x(s).wait_recv()
+        add(acc, (2, s, low), diag_in[s, 0])
+        summed_y(s).start()
+        diag_y(s).wait_recv()
+        add(acc, (1, s, high), diag_in[s, 1])
+        summed_x(s).start()
+
+    def third(j, s):
+        block = blocks[j]
+        if j == 0:
+            direct_x(s).wait_recv()
+            direct_y(s).wait_recv()
+            summed_x(s).wait_recv()
+            summed_y(s).wait_recv()
+        total = (
+            acc[0, s, block].astype(f32)
+            + last_in[s, 0, block].astype(f32)
+            + last_in[s, 1, block].astype(f32)
+        )
+        if j < tp - 1:
+            acc[0, s, block] = total.astype(bf16)
+
+            @pl.when((block > rank) & (rank > 0))
+            def _():
+                along_z(j, s, True).wait_recv()
+                add(acc, (0, s, block), z_in[0, block, s])
+
+            @pl.when((block < rank) & (rank < tp - 1))
+            def _():
+                along_z(j, s, False).wait_recv()
+                add(acc, (0, s, block), z_in[1, block, s])
+
+            @pl.when(block > rank)
+            def _():
+                along_z(j, s, True).start()
+
+            @pl.when(block < rank)
+            def _():
+                along_z(j, s, False).start()
+        else:
+            dsum_ref[s] = total
+
+            @pl.when(rank > 0)
+            def _():
+                along_z(j, s, True).wait_recv()
+                dsum_ref[s] += z_in[0, block, s].astype(f32)
+
+            @pl.when(rank < tp - 1)
+            def _():
+                along_z(j, s, False).wait_recv()
+                dsum_ref[s] += z_in[1, block, s].astype(f32)
+
+    def sum_lines():
+        direct_lines().wait_recv()
+        summed_lines().wait_recv()
+        direct_lines().wait_send()
+        summed_lines().wait_send()
+        own = acc_e[0] + last_e[0] + last_e[1]
+        esum_ref[...] = own
+        acc_e[1] = own
+        acc_e[2] = own
+
+        @pl.when(rank > 0)
+        def _():
+            lines_z(True).wait_recv()
+            esum_ref[...] += z_in_e[0]
+            acc_e[1] = own + z_in_e[0]
+
+        @pl.when(rank < tp - 1)
+        def _():
+            lines_z(True).start()
+            lines_z(False).wait_recv()
+            esum_ref[...] += z_in_e[1]
+            acc_e[2] = own + z_in_e[1]
+
+        @pl.when(rank > 0)
+        def _():
+            lines_z(False).start()
+
+    def front_load(block, s):
+        return pltpu.make_async_copy(
+            part_ref.at[block, s], stage.at[s, block], f_sem.at[block, s]
+        )
+
+    def front_z(j, s, right):
         way = 0 if right else 1
         block = blocks[j]
-        return pltpu.make_async_remote_copy(
-            src_ref=acc_e.at[0, block],
-            dst_ref=z_in_e.at[way, block],
-            send_sem=ze_send.at[way, block],
-            recv_sem=ze_recv.at[way, block],
-            device_id=(me, rank + 1 if right else rank - 1),
-            device_id_type=MESH,
-        )
-
-    def add(ref, spot, one):
-        ref[spot] = (ref[spot].astype(f32) + one.astype(f32)).astype(ref.dtype)
-
-    def second(h):
-        diag_x(h).wait_recv()
-        add(acc, (2, h, 0), diag_in[h, 0])
-        summed_y(h).start()
-        diag_y(h).wait_recv()
-        add(acc, (1, h, 1), diag_in[h, 1])
-        summed_x(h).start()
-
-    def third(j):
-        h = j // 2
+        return remote_z(
+            stage.at[s, block],
+            z_in.at[way, block, s],
+            f_send.at[way, block, s],
+            f_recv.at[way, block, s],
+            right,
+        )
+
+    def front(j, s):
         block = blocks[j]
-        part = block % 2
-        if j % 2 == 0:
-            direct_x(h).wait_recv()
-            direct_y(h).wait_recv()
-            summed_x(h).wait_recv()
-            summed_y(h).wait_recv()
-        if j == 0:
-            direct_lines().wait_recv()
-            summed_lines().wait_recv()
-        total = (
-            acc[0, h, part].astype(f32)
-            + last_in[h, 0, part].astype(f32)
-            + last_in[h, 1, part].astype(f32)
-        )
-        lines = acc_e[0, block] + last_e[0, block] + last_e[1, block]
+        front_load(block, s).wait()
         if j < tp - 1:
-            acc[0, h, part] = total.astype(bf16)
-            acc_e[0, block] = lines
 
             @pl.when((block > rank) & (rank > 0))
             def _():
-                along_z(j, True).wait_recv()
-                along_z_e(j, True).wait_recv()
-                add(acc, (0, h, part), z_in[0, block])
-                add(acc_e, (0, block), z_in_e[0, block])
+                front_z(j, s, True).wait_recv()
+                add(stage, (s, block), z_in[0, block, s])
 
             @pl.when((block < rank) & (rank < tp - 1))
             def _():
-                along_z(j, False).wait_recv()
-                along_z_e(j, False).wait_recv()
-                add(acc, (0, h, part), z_in[1, block])
-                add(acc_e, (0, block), z_in_e[1, block])
+                front_z(j, s, False).wait_recv()
+                add(stage, (s, block), z_in[1, block, s])
 
             @pl.when(block > rank)
             def _():
-                along_z(j, True).start()
-                along_z_e(j, True).start()
+                front_z(j, s, True).start()
 
             @pl.when(block < rank)
             def _():
-                along_z(j, False).start()
-                along_z_e(j, False).start()
+                front_z(j, s, False).start()
         else:
-            dsum_ref[...] = total
-            esum_ref[...] = lines
+            middle_ref[s] = hidden_ref[s].astype(f32) + stage[s, block].astype(f32)
 
             @pl.when(rank > 0)
             def _():
-                along_z(j, True).wait_recv()
-                along_z_e(j, True).wait_recv()
-                dsum_ref[...] += z_in[0, block].astype(f32)
-                esum_ref[...] += z_in_e[0, block]
+                front_z(j, s, True).wait_recv()
+                middle_ref[s] += z_in[0, block, s].astype(f32)
 
             @pl.when(rank < tp - 1)
             def _():
-                along_z(j, False).wait_recv()
-                along_z_e(j, False).wait_recv()
-                dsum_ref[...] += z_in[1, block].astype(f32)
-                esum_ref[...] += z_in_e[1, block]
-
-    def front_load(block):
-        return pltpu.make_async_copy(
-            part_ref.at[pl.ds(block * rows, rows)],
-            x_buf.at[block // 2, pl.ds(block % 2 * rows, rows)],
-            f_sem.at[block],
-        )
-
-    def front_z(j, right):
-        way = 0 if right else 1
-        block = blocks[j]
-        return pltpu.make_async_remote_copy(
-            src_ref=x_buf.at[block // 2, pl.ds(block % 2 * rows, rows)],
-            dst_ref=z_in.at[way, block],
-            send_sem=f_send.at[way, block],
-            recv_sem=f_recv.at[way, block],
-            device_id=(me, rank + 1 if right else rank - 1),
-            device_id_type=MESH,
-        )
-
-    def front(j):
-        block = blocks[j]
-        spot = (block // 2, pl.ds(pl.multiple_of(block % 2 * rows, rows), rows))
-        front_load(block).wait()
-        if j < tp - 1:
-
-            @pl.when((block > rank) & (rank > 0))
-            def _():
-                front_z(j, True).wait_recv()
-                add(x_buf, spot, z_in[0, block])
-
-            @pl.when((block < rank) & (rank < tp - 1))
-            def _():
-                front_z(j, False).wait_recv()
-                add(x_buf, spot, z_in[1, block])
-
-            @pl.when(block > rank)
-            def _():
-                front_z(j, True).start()
-
-            @pl.when(block < rank)
-            def _():
-                front_z(j, False).start()
-        else:
-            middle_ref[...] = hidden_ref[...].astype(f32) + x_buf[spot].astype(f32)
-
-            @pl.when(rank > 0)
-            def _():
-                front_z(j, True).wait_recv()
-                middle_ref[...] += z_in[0, block].astype(f32)
-
-            @pl.when(rank < tp - 1)
-            def _():
-                front_z(j, False).wait_recv()
-                middle_ref[...] += z_in[1, block].astype(f32)
-
-            middle = middle_ref[...]
+                front_z(j, s, False).wait_recv()
+                middle_ref[s] += z_in[1, block, s].astype(f32)
+
+            middle = middle_ref[s]
             mean = jnp.mean(middle * middle, axis=-1, keepdims=True)
             normed = middle * lax.rsqrt(mean + epsilon) * gain_ref[...]
-            n_buf[...] = normed.astype(bf16)
-
-    def grad_load(n, slot):
-        return pltpu.make_async_copy(
-            grad_ref.at[pl.ds(n * pack_rows, pack_rows)], g_buf.at[slot], g_sem.at[slot]
-        )
-
-    def hidden_grads(first, last):
+            x_all[me, rank, s] = normed.astype(bf16)
+            start_rows(s)
+
+    cut = eu_buf.shape[1]
+    cuts = width // cut
+    units = SHARED + shared_width
+
+    def weight_loads(part, n, slot):
+        at = pl.ds(pl.multiple_of(n * cut, cut), cut)
+        return (
+            pltpu.make_async_copy(expert_up.at[part, at], eu_buf.at[slot], w_sem.at[0, slot]),
+            pltpu.make_async_copy(shared_up.at[part, at], su_buf.at[slot], w_sem.at[1, slot]),
+        )
+
+    def lay_out(part):
+        base = part * UNIT
+
         def body(n, carry):
             slot = n % 2
 
-            @pl.when(n + 1 < tokens // pack_rows)
-            def _():
-                grad_load(n + 1, 1 - slot).start()
-
-            grad_load(n, slot).wait()
-            dh_buf[pl.ds(n * pack_rows, pack_rows), :] = lax.dot_general(
-                g_buf[slot], down_ref[...], NT, preferred_element_type=f32
+            @pl.when(n + 1 < cuts)
+            def _():
+                for copy in weight_loads(part, n + 1, 1 - slot):
+                    copy.start()
+
+            for copy in weight_loads(part, n, slot):
+                copy.wait()
+            at = pl.ds(pl.multiple_of(n * cut, cut), cut)
+            both_buf[at, base : base + UNIT] = jnp.zeros((cut, UNIT), bf16)
+            both_buf[at, base : base + expert_width] = eu_buf[slot]
+            both_buf[at, base + SHARED : base + units] = su_buf[slot]
+            return carry
+
+        for copy in weight_loads(part, 0, 0):
+            copy.start()
+        lax.fori_loop(0, cuts, body, 0)
+
+    down_loads = (
+        pltpu.make_async_copy(expert_down, down_buf.at[pl.ds(0, expert_width)], dn_sem.at[0]),
+        pltpu.make_async_copy(shared_down, down_buf.at[pl.ds(SHARED, shared_width)], dn_sem.at[1]),
+    )
+
+    def hidden_grads(count, task, own=False):
+        def load(n, slot):
+            pack_bits, c = task(n)
+            src = grad_ref.at[pl.ds(c * tile, tile)] if own else grad_region(pack_of(pack_bits), c)
+            return pltpu.make_async_copy(src, g_buf.at[slot], g_sem.at[slot])
+
+        def body(n, carry):
+            slot = n % 2
+
+            @pl.when(n + 1 < count)
+            def _():
+                load(n + 1, 1 - slot).start()
+
+            load(n, slot).wait()
+            pack_bits, c = task(n)
+            d_hidden = lax.dot_general(
+                g_buf[slot], down_buf[...], NT, preferred_element_type=f32
             ).astype(bf16)
+            dh_buf[pack_of(pack_bits), pl.ds(2 * c, 2)] = d_hidden.reshape(2, subs, rows, UNIT)
             return carry
 
-        lax.fori_loop(first, last, body, 0)
-
-    core_of, x_of, y_of = me % 2, (me // 2) % 2, me // 4
+        load(0, 0).start()
+        lax.fori_loop(0, count, body, 0)
+        if own:
+            for c in range(2):
+                own_store(c).start()
+            for c in range(2):
+                own_store(c).wait()
+
+    def own_store(c):
+        return pltpu.make_async_copy(g_buf.at[c], grad_region(me, c), local_sem.at[c])
 
     def tile_of(i):
-        t = i // 2
+        s = i // 8
+        q = order_of(s, i // 2 % 4)
         o = i % 2
-        s = t // 6
-        q = (1 - s) * (t % 3) + 3 * s
-        h = (1 - s) * (1 - t // 3) + s * (t - 6)
-        pack = (
-            4 * ((y_of + q // 2) % 2) + 2 * ((x_of + q % 2) % 2) + (core_of + 1 - o) % 2
-        )
-        half = h * near + (1 - h) * (1 - near)
-        return q, o, h, pack, half
-
-    def tile_rows(pack, half):
-        return pl.ds(pl.multiple_of(pack * pack_rows + half * tile, tile), tile)
-
-    def row_load(i):
-        q, o, h, pack, half = tile_of(i)
-        return pltpu.make_async_copy(
-            all_ref.at[tile_rows(pack, half)], x_buf.at[i % 2], x_sem.at[i % 2]
-        )
-
-    def prefetch(i):
-        q, o, h, pack, half = tile_of(i)
+        return q, o, s, pack_of(2 * q + 1 - o)
+
+    def order_of(s, r):
+        return r + s * (r // 2) * (1 - 2 * (r % 2))
+
+    def d_store(i):
+        q, o, s, pack = tile_of(i)
+        return pltpu.make_async_copy(d_buf.at[i % 2], d_ref.at[pack, :, s], d_sem.at[i % 2])
+
+    def x_store(i):
+        q, o, s, pack = tile_of(i)
+        return pltpu.make_async_copy(x_all.at[pack, :, s], all_ref.at[pack, :, s], x_sem.at[i % 2])
+
+    def one_tile(i, carry):
+        q, o, s, pack = tile_of(i)
+        slot = i % 2
 
         @pl.when(o == 0)
         def _():
-            for part in range(2):
-                block = 2 * half + part
-                ref = region(pack, block)
-                pltpu.make_async_remote_copy(
-                    src_ref=ref,
-                    dst_ref=ref,
-                    send_sem=ap_send.at[q, block],
-                    recv_sem=ap_recv.at[q, block],
-                    device_id=(flipped(me, 1), rank),
-                    device_id_type=MESH,
+            for block in range(tp):
+                ref = x_all.at[pack, block, s]
+                remote(
+                    ref, ref, ap_send.at[q, block, s], ap_recv.at[q, block, s], 1
                 ).wait_recv()
-
-        row_load(i).start()
-
-    def d_store(i):
-        q, o, h, pack, half = tile_of(i)
-        return pltpu.make_async_copy(
-            d_buf.at[i % 2], d_ref.at[tile_rows(pack, half)], d_sem.at[i % 2]
-        )
-
-    units = SHARED + shared_width
-
-    def one_tile(i, carry):
-        q, o, h, pack, half = tile_of(i)
-        slot = i % 2
-        at = tile_rows(pack, half)
-        row_load(i).wait()
 
         @pl.when(i >= 2)
         def _():
             d_store(i - 2).wait()
-
-        pre = jnp.dot(x_buf[slot], both_ref[...], preferred_element_type=f32)
+            x_store(i - 2).wait()
+
+        x_store(i).start()
+        x = x_all[pack, :, s].reshape(tile, width)
+        pre = jnp.dot(x, both_buf[...], preferred_element_type=f32)
         gate, upper = pre[:, :UNIT], pre[:, UNIT:]
         lane = lax.broadcasted_iota(jnp.int32, (1, UNIT), 1)
-        logit = gate[:, units : units + 1] + gate[:, units + 1 : units + 2]
+        logit = jnp.sum(x.astype(f32) * vec_ref[...], axis=-1, keepdims=True)
         gate_prob = 1.0 / (1.0 + jnp.exp(-logit))
-        scale = jnp.where(
-            lane < expert_width, scale_ref[at, :1], jnp.where(lane < units, gate_prob, 0.0)
-        )
+        own_scale = jnp.broadcast_to(scale_ref[pack, s], (128, tile)).T[:, :1]
+        scale = jnp.where(lane < SHARED, own_scale, gate_prob)
         sigmoid = 1.0 / (1.0 + jnp.exp(-gate))
         act = gate * sigmoid
         slope = sigmoid * (1.0 + gate * (1.0 - sigmoid))
         hidden = act * upper
-        d_hidden = dh_buf[at, :].astype(f32)
+        d_hidden = dh_buf[pack, :, s].reshape(tile, UNIT).astype(f32)
         line = lax.broadcasted_iota(jnp.int32, (16, UNIT), 0)
         unit = lax.broadcasted_iota(jnp.int32, (16, UNIT), 1)
-        of_expert = (line == me) & (unit < expert_width)
+        of_expert = (line == me) & (unit < SHARED)
         of_shared = (line == 8) & (unit >= SHARED)
         pick = jnp.where(of_expert | of_shared, 1.0, 0.0).astype(bf16)
         lines = lax.dot_general(
             pick, (d_hidden * hidden).astype(bf16), NT, preferred_element_type=f32
         )
-        dh_buf[at, :] = (hidden * scale).astype(bf16)
+        dh_buf[pack, :, s] = (hidden * scale).astype(bf16).reshape(tp, rows, UNIT)
         d_scaled = d_hidden * scale
-        d_buf[slot, :, :UNIT] = (d_scaled * upper * slope).astype(bf16)
-        d_buf[slot, :, UNIT:] = (d_scaled * act).astype(bf16)
+        d_gate = (d_scaled * upper * slope).astype(bf16)
+        d_upper = (d_scaled * act).astype(bf16)
+        d_buf[slot, :, :, :UNIT] = d_gate.reshape(tp, rows, UNIT)
+        d_buf[slot, :, :, UNIT:] = d_upper.reshape(tp, rows, UNIT)
         control(i)
-
-        @pl.when(i < 15)
-        def _():
-            prefetch(i + 1)
-
-        d_rows = lax.dot_general(d_buf[slot], both_ref[...], NT, preferred_element_type=f32)
+        d_both = d_buf[slot].reshape(tile, 2 * UNIT)
+        d_rows = lax.dot_general(d_both, both_buf[...], NT, preferred_element_type=f32)
+        d_rows = d_rows.reshape(tp, rows, width)
         d_store(i).start()
 
         @pl.when(o == 0)
         def _():
-            @pl.when(q > 0)
-            def _():
-                core(q - 1, h).wait_send()
-
-            for part in range(2):
-                stage[h, part] = d_rows[part * rows : (part + 1) * rows].astype(bf16)
-                stage_e[q, 2 * half + part] = lines[:, part * rows : (part + 1) * rows]
-            core(q, h).start()
-
-            @pl.when(((h == 0) & (q < 3)) | ((h == 1) & (q == 3)))
+            @pl.when(i % 8 >= 2)
+            def _():
+                core(order_of(s, i // 2 % 4 - 1), s).wait_send()
+
+            stage[s] = d_rows.astype(bf16)
+            stage_e[q, s] = lines
+            core(q, s).start()
+
+            @pl.when(s == 1)
             def _():
                 core_e(q).start()
 
         @pl.when(o == 1)
         def _():
-            core(q, h).wait_recv()
-            for part in range(2):
-                add(acc, (q, h, part), d_rows[part * rows : (part + 1) * rows])
-                acc_e[q, 2 * half + part] = lines[:, part * rows : (part + 1) * rows]
-
-            @pl.when(((h == 0) & (q < 3)) | ((h == 1) & (q == 3)))
+            core(q, s).wait_recv()
+            add(acc, (q, s), d_rows)
+            acc_e[q, s] = lines
+
+            @pl.when(s == 1)
             def _():
                 core_e(q).wait_recv()
                 acc_e[q] = acc_e[q] + other_e[q]
@@ -1059,22 +941,26 @@
 
             @pl.when(q == 1)
             def _():
-                direct_x(h).start()
+                direct_x(s).start()
 
             @pl.when(q == 2)
             def _():
-                direct_y(h).start()
+                direct_y(s).start()
 
             @pl.when(q == 3)
             def _():
-                diag_x(h).start()
-                diag_y(h).start()
+                diag_x(s).start()
+                diag_y(s).start()
+
+            @pl.when(i == 11)
+            def _():
+                second(0)
 
         return carry
 
     def y_store(n, slot):
         return pltpu.make_async_copy(
-            g_buf.at[slot], y_ref.at[pl.ds(n * pack_rows, pack_rows)], y_sem.at[slot]
+            g_buf.at[slot], y_ref.at[pl.ds(n * tile, tile)], y_sem.at[slot]
         )
 
     def outputs(first, last):
@@ -1085,169 +971,214 @@
             def _():
                 y_store(n - 2, slot).wait()
 
-            g_buf[slot] = jnp.dot(
-                dh_buf[pl.ds(n * pack_rows, pack_rows), :],
-                down_ref[...],
-                preferred_element_type=f32,
-            ).astype(bf16)
+            hidden = dh_buf[n // 2, pl.ds(n % 2 * 2, 2)].reshape(tile, UNIT)
+            g_buf[slot] = jnp.dot(hidden, down_buf[...], preferred_element_type=f32).astype(bf16)
             y_store(n, slot).start()
             return carry
 
         lax.fori_loop(first, last, body, 0)
 
-    grad_load(0, 0).start()
-    packs = tokens // pack_rows
-    for block in blocks:
-        front_load(block).start()
-    front(0)
-    hidden_grads(0, 3)
-    front(1)
-    hidden_grads(3, 6)
-    front(2)
-    hidden_grads(6, packs)
-    front(3)
-    mine = pltpu.make_async_copy(n_buf, region(me, rank), local_sem)
-    mine.start()
-    mine.wait()
-
-    @pl.when(rank < tp - 1)
-    def _():
-        gather_z(rank, True).start()
-
-    @pl.when(rank > 0)
-    def _():
-        gather_z(rank, False).start()
-
-    start_plane(rank)
-    for j in range(tp - 1):
-        block = blocks[j]
-
-        @pl.when(block > rank)
-        def _():
-            front_z(j, True).wait_send()
-
-        @pl.when(block < rank)
-        def _():
-            front_z(j, False).wait_send()
-
-    z_step(1)
-    prefetch(0)
+    for c in range(2):
+        grad_x(c).start()
+        grad_y(c).start()
+        grad_core(0, c).start()
+    for s in range(subs):
+        for block in blocks:
+            front_load(block, s).start()
+    down_buf[...] = jnp.zeros_like(down_buf)
+    for copy in down_loads:
+        copy.start()
+    front(0, 0)
+    lay_out(0)
+    front(1, 0)
+    lay_out(1)
+    front(0, 1)
+    front(2, 0)
+    for copy in down_loads:
+        copy.wait()
+    front(3, 0)
+    hidden_grads(2, lambda n: (0 * n, n), own=True)
+    for c in range(2):
+        grad_core(0, c).wait_recv()
+    hidden_grads(2, lambda n: (0 * n + 1, n))
+    grad_forward(0)
+    front(1, 1)
+    z_step(1, 0)
+    for q in (1, 2):
+        grad_core(q, 0).wait_recv()
+    hidden_grads(4, lambda n: (2 + n, 0 * n))
+    front(2, 1)
+    z_step(2, 0)
+    front(3, 1)
+    z_step(3, 0)
+    grad_forward(1)
+    for q in (1, 2):
+        grad_core(q, 1).wait_recv()
+    hidden_grads(4, lambda n: (2 + n, 0 * n + 1))
+    for s in range(subs):
+        for j in range(tp - 1):
+            block = blocks[j]
+
+            @pl.when(block > rank)
+            def _():
+                front_z(j, s, True).wait_send()
+
+            @pl.when(block < rank)
+            def _():
+                front_z(j, s, False).wait_send()
+
+    forward(0, 0)
+    grad_finish(0)
+    forward(1, 0)
+    grad_finish(1)
+    for c in range(2):
+        grad_core(3, c).wait_recv()
+    hidden_grads(4, lambda n: (6 + n // 2, n % 2))
+    finish(0, 0)
+    forward(2, 0)
     lax.fori_loop(0, 16, one_tile, 0)
     hidden_store = pltpu.make_async_copy(dh_buf, hid_ref, h_sem)
     hidden_store.start()
-    outputs(0, 4)
-    second(0)
-    outputs(4, 6)
     diag_lines().wait_recv()
     acc_e[2] = acc_e[2] + diag_e[...]
     summed_lines().start()
+    outputs(0, 2)
+    third(0, 0)
+    outputs(2, 4)
     second(1)
-    outputs(6, packs)
-    third(0)
-    third(1)
-    third(2)
-    third(3)
+    third(1, 0)
+    outputs(4, 6)
+    third(2, 0)
+    outputs(6, 8)
+    third(3, 0)
+    sum_lines()
+    outputs(8, 16)
+    for j in range(tp):
+        third(j, 1)
 
     hidden_store.wait()
-    for n in (packs - 2, packs - 1):
+    for n in (14, 15):
         y_store(n, n % 2).wait()
-    for i in (14, 15):
-        d_store(i).wait()
+        d_store(n).wait()
+        x_store(n).wait()
     core(3, 0).wait_send()
-    core(3, 1).wait_send()
+    core(2, 1).wait_send()
+    diag_lines().wait_send()
     for q in range(4):
         core_e(q).wait_send()
-    for copy in (diag_lines, direct_lines, summed_lines):
-        copy().wait_send()
-    for h in range(2):
+    for c in range(2):
+        for q in range(4):
+            grad_core(q, c).wait_send()
+        for copy in (grad_x, grad_y, grad_x_to_y, grad_y_to_x):
+            copy(c).wait_send()
+    for s in range(subs):
         for copy in (diag_x, diag_y, direct_x, direct_y, summed_x, summed_y):
-            copy(h).wait_send()
-    for block in order:
-        for q in range(4):
-            to_core(q, block).wait_send()
-        for copy in (own_x, own_y, x_to_y, y_to_x):
-            copy(block).wait_send()
-    for j in range(tp - 1):
-        block = blocks[j]
-
-        @pl.when(block > rank)
-        def _():
-            along_z(j, True).wait_send()
-            along_z_e(j, True).wait_send()
-
-        @pl.when(block < rank)
-        def _():
-            along_z(j, False).wait_send()
-            along_z_e(j, False).wait_send()
-
-    for block in range(tp):
-
-        @pl.when((block <= rank) & (rank < tp - 1))
-        def _():
-            gather_z(block, True).wait_send()
-
-        @pl.when((block >= rank) & (rank > 0))
-        def _():
-            gather_z(block, False).wait_send()
+            copy(s).wait_send()
+        for block in range(tp):
+            for q in range(4):
+                to_core(q, block, s).wait_send()
+            for copy in (own_x, own_y, x_to_y, y_to_x):
+                copy(block, s).wait_send()
+
+            @pl.when((block <= rank) & (rank < tp - 1))
+            def _():
+                gather_z(block, s, True).wait_send()
+
+            @pl.when((block >= rank) & (rank > 0))
+            def _():
+                gather_z(block, s, False).wait_send()
+
+        for j in range(tp - 1):
+            block = blocks[j]
+
+            @pl.when(block > rank)
+            def _():
+                along_z(j, s, True).wait_send()
+
+            @pl.when(block < rank)
+            def _():
+                along_z(j, s, False).wait_send()
+
+    @pl.when(rank < tp - 1)
+    def _():
+        lines_z(True).wait_send()
+
+    @pl.when(rank > 0)
+    def _():
+        lines_z(False).wait_send()
 
 
 def ffn(
-    part, hidden, gain, grad_all, both, down, scale, fsdp, tp, expert_width, shared_width, collective_id
+    part, hidden, gain, vec, scale, grad, expert_up, shared_up, expert_down, shared_down,
+    fsdp, tp, collective_id,
 ):
-    rows, width = hidden.shape
-    tokens = rows * fsdp * tp
-    pack_rows = rows * tp
-    tile = pack_rows // 2
+    own, width = hidden.shape
+    subs = 2
+    rows = own // subs
+    tile = tp * rows
+    tokens = fsdp * tp * own
+    expert_width, shared_width = expert_down.shape[0], shared_down.shape[0]
     bf16 = jnp.bfloat16
     f32 = jnp.float32
     dma = pltpu.SemaphoreType.DMA
     anywhere = pl.BlockSpec(memory_space=pl.ANY)
     vmem = pl.BlockSpec(memory_space=pltpu.VMEM)
+    all_rows = (fsdp, tp, subs, rows)
+    lines = (subs, 16, tile)
     return pl.pallas_call(
         functools.partial(ffn_kernel, tp, expert_width, shared_width),
         out_shape=[
-            jax.ShapeDtypeStruct((rows, width), f32),
+            jax.ShapeDtypeStruct((subs, rows, width), f32),
+            jax.ShapeDtypeStruct(all_rows + (width,), bf16),
             jax.ShapeDtypeStruct((tokens, width), bf16),
-            jax.ShapeDtypeStruct((tokens, 2 * UNIT), bf16),
-            jax.ShapeDtypeStruct((tokens, UNIT), bf16),
+            jax.ShapeDtypeStruct(all_rows + (2 * UNIT,), bf16),
+            jax.ShapeDtypeStruct(all_rows + (UNIT,), bf16),
             jax.ShapeDtypeStruct((tokens, width), bf16),
-            jax.ShapeDtypeStruct((rows, width), f32),
-            jax.ShapeDtypeStruct((16, rows), f32),
+            jax.ShapeDtypeStruct((subs, rows, width), f32),
+            jax.ShapeDtypeStruct(lines, f32),
         ],
-        in_specs=[anywhere, vmem, vmem, anywhere, vmem, vmem, vmem],
-        out_specs=[vmem, anywhere, anywhere, anywhere, anywhere, vmem, vmem],
+        in_specs=[anywhere] + [vmem] * 4 + [anywhere] * 5,
+        out_specs=[vmem] + [anywhere] * 5 + [vmem] * 2,
         scratch_shapes=[
-            pltpu.VMEM((rows, width), bf16),
-            pltpu.VMEM((2, pack_rows, width), bf16),
+            pltpu.VMEM(all_rows + (width,), bf16),
             pltpu.VMEM((2, tile, width), bf16),
-            pltpu.VMEM((tokens, UNIT), bf16),
-            pltpu.VMEM((2, tile, 2 * UNIT), bf16),
-            pltpu.VMEM((2, 2, rows, width), bf16),
-            pltpu.VMEM((4, 2, 2, rows, width), bf16),
-            pltpu.VMEM((2, 2, rows, width), bf16),
-            pltpu.VMEM((2, 2, 2, rows, width), bf16),
-            pltpu.VMEM((2, tp, rows, width), bf16),
-            pltpu.VMEM((4, tp, 16, rows), f32),
-            pltpu.VMEM((4, tp, 16, rows), f32),
-            pltpu.VMEM((4, tp, 16, rows), f32),
-            pltpu.VMEM((tp, 16, rows), f32),
-            pltpu.VMEM((2, tp, 16, rows), f32),
-            pltpu.VMEM((2, tp, 16, rows), f32),
-            dma, dma((2,)), dma((2,)), dma((2,)), dma, dma((2,)),
-            dma((2, tp)), dma((2, tp)), dma((8, tp)), dma((8, tp)),
-            dma((4, 2)), dma((4, 2)), dma((4,)), dma((4,)),
-            dma((6, 2)), dma((6, 2)), dma((3,)), dma((3,)),
-            dma((2, tp)), dma((2, tp)), dma((2, tp)), dma((2, tp)),
-            dma((tp,)), dma((2, tp)), dma((2, tp)),
+            pltpu.VMEM(all_rows + (UNIT,), bf16),
+            pltpu.VMEM((2, tp, rows, 2 * UNIT), bf16),
+            pltpu.VMEM((subs, tp, rows, width), bf16),
+            pltpu.VMEM((4, subs, tp, rows, width), bf16),
+            pltpu.VMEM((subs, 2, tp // 2, rows, width), bf16),
+            pltpu.VMEM((subs, 2, tp, rows, width), bf16),
+            pltpu.VMEM((2, tp, subs, rows, width), bf16),
+            pltpu.VMEM((width, 2 * UNIT), bf16),
+            pltpu.VMEM((UNIT, width), bf16),
+            pltpu.VMEM((2, width // 8, expert_width), bf16),
+            pltpu.VMEM((2, width // 8, shared_width), bf16),
+            pltpu.VMEM((4,) + lines, f32),
+            pltpu.VMEM((4,) + lines, f32),
+            pltpu.VMEM((4,) + lines, f32),
+            pltpu.VMEM(lines, f32),
+            pltpu.VMEM((2,) + lines, f32),
+            pltpu.VMEM((2,) + lines, f32),
+            dma((2,)), dma((2, 2)), dma((2,)), dma((2,)), dma((2,)), dma((2,)), dma, dma((2,)),
+            dma((tp, subs)), dma((2, tp, subs)), dma((2, tp, subs)),
+            dma((2, tp, subs)), dma((2, tp, subs)), dma((8, tp, subs)), dma((8, tp, subs)),
+            dma((8, 2)), dma((8, 2)),
+            dma((4, subs)), dma((4, subs)), dma((4,)), dma((4,)),
+            dma((6, subs)), dma((6, subs)), dma((3,)), dma((3,)),
+            dma((2, tp, subs)), dma((2, tp, subs)), dma((2,)), dma((2,)),
         ],
         compiler_params=pltpu.CompilerParams(
-            collective_id=collective_id, has_side_effects=True, vmem_limit_bytes=61 << 20
+            collective_id=collective_id, has_side_effects=True, vmem_limit_bytes=63 << 20
         ),
         name="ffn",
-    )(part, hidden, gain, grad_all, both, down, scale)
+    )(
+        part.reshape(tp, subs, rows, width), hidden.reshape(subs, rows, width), gain, vec,
+        scale, grad, expert_up, shared_up, expert_down, shared_down,
+    )
 
 
 TN = (((0,), (0,)), ((), ()))
+SUB = 2
 
 
 def outputs_kernel(tp, expert_width, shared_width, *refs):
@@ -1263,9 +1194,11 @@
     f32 = jnp.float32
     bf16 = jnp.bfloat16
     rows = total_ref.shape[0]
-    half = rows // 2
+    cut = rows // SUB
+    half = cut // 2
     near = rank // 2
     blocks = [3 * (1 - near), 2 - near, flipped(rank, 1), rank]
+    pieces = range(tp * SUB)
     packs = [me, flipped(me, 2), flipped(me, 4), flipped(flipped(me, 2), 4)]
     low, high = pl.ds(0, half), pl.ds(half, half)
 
@@ -1298,15 +1231,18 @@
             def _():
                 gather_z(rank + step, False).start()
 
-    def region(pack, block):
-        return y_ref.at[pl.ds((pack * tp + block) * rows, rows)]
+    def spot_of(j):
+        return blocks[j // SUB] * SUB + j % SUB
+
+    def region(pack, j):
+        return y_ref.at[pl.ds((pack * tp * SUB + spot_of(j)) * cut, cut)]
 
     def local(k, j):
-        return pltpu.make_async_copy(region(packs[k], blocks[j]), mine.at[k, j], l_sem.at[k, j])
+        return pltpu.make_async_copy(region(packs[k], j), mine.at[k, j], l_sem.at[k, j])
 
     def core(k, j):
         return pltpu.make_async_remote_copy(
-            src_ref=region(flipped(packs[k], 1), blocks[j]),
+            src_ref=region(flipped(packs[k], 1), j),
             dst_ref=other.at[k, j],
             send_sem=c_send.at[k, j],
             recv_sem=c_recv.at[k, j],
@@ -1344,12 +1280,12 @@
 
     def along_z(j, right):
         way = 0 if right else 1
-        block = blocks[j]
+        spot = spot_of(j)
         return pltpu.make_async_remote_copy(
             src_ref=mine.at[0, j],
-            dst_ref=z_in.at[way, block],
-            send_sem=z_send.at[way, block],
-            recv_sem=z_recv.at[way, block],
+            dst_ref=z_in.at[way, spot],
+            send_sem=z_send.at[way, spot],
+            recv_sem=z_recv.at[way, spot],
             device_id=(me, rank + 1 if right else rank - 1),
             device_id_type=MESH,
         )
@@ -1379,24 +1315,25 @@
         summed_x(j).start()
 
     def third(j):
-        block = blocks[j]
+        block = blocks[j // SUB]
+        spot = spot_of(j)
         direct_x(j).wait_recv()
         direct_y(j).wait_recv()
         summed_x(j).wait_recv()
         summed_y(j).wait_recv()
         total = mine[0, j].astype(f32) + last_in[j, 0].astype(f32) + last_in[j, 1].astype(f32)
-        if j < tp - 1:
+        if j < (tp - 1) * SUB:
             mine[0, j] = total.astype(bf16)
 
             @pl.when((block > rank) & (rank > 0))
             def _():
                 along_z(j, True).wait_recv()
-                add(mine, (0, j), z_in[0, block])
+                add(mine, (0, j), z_in[0, spot])
 
             @pl.when((block < rank) & (rank < tp - 1))
             def _():
                 along_z(j, False).wait_recv()
-                add(mine, (0, j), z_in[1, block])
+                add(mine, (0, j), z_in[1, spot])
 
             @pl.when(block > rank)
             def _():
@@ -1406,17 +1343,18 @@
             def _():
                 along_z(j, False).start()
         else:
-            total_ref[...] = total
+            own_rows = pl.ds(j % SUB * cut, cut)
+            total_ref[own_rows] = total
 
             @pl.when(rank > 0)
             def _():
                 along_z(j, True).wait_recv()
-                total_ref[...] += z_in[0, block].astype(f32)
+                total_ref[own_rows] += z_in[0, spot].astype(f32)
 
             @pl.when(rank < tp - 1)
             def _():
                 along_z(j, False).wait_recv()
-                total_ref[...] += z_in[1, block].astype(f32)
+                total_ref[own_rows] += z_in[1, spot].astype(f32)
 
     span = col_buf.shape[2]
     steps = x_ref.shape[1] // span
@@ -1496,7 +1434,7 @@
     load_h = pltpu.make_async_copy(h_ref, h_buf, w_sem.at[1])
     own = pltpu.make_async_copy(own_ref, rows_ref.at[pl.ds(rank * rows, rows)], a_sem)
     own.start()
-    for j in range(tp):
+    for j in pieces:
         for k in (3, 2, 1, 0):
             core(k, j).start()
             local(k, j).start()
@@ -1516,36 +1454,33 @@
     first(0)
     first(1)
     load_d.wait()
-    lax.fori_loop(0, 2, up_step, 0)
-    second(0)
-    gather_step(1)
-    first(2)
-    lax.fori_loop(2, 4, up_step, 0)
-    second(1)
-    first(3)
-    lax.fori_loop(4, 6, up_step, 0)
-    gather_step(2)
-    third(0)
-    second(2)
-    lax.fori_loop(6, 8, up_step, 0)
-    gather_step(3)
-    third(1)
-    second(3)
     load_h.wait()
-    lax.fori_loop(0, steps, down_step, 0)
-    third(2)
-    third(3)
+    for j in pieces:
+        if j < len(pieces) // 2:
+            lax.fori_loop(2 * j, 2 * j + 2, up_step, 0)
+        else:
+            later = j - len(pieces) // 2
+            lax.fori_loop(2 * later, 2 * later + 2, down_step, 0)
+        second(j)
+        if j + 2 < len(pieces):
+            first(j + 2)
+        if j in (1, 3, 5):
+            gather_step((j + 1) // 2)
+        if j >= 2:
+            third(j - 2)
+    third(len(pieces) - 2)
+    third(len(pieces) - 1)
 
     for n in (steps - 2, steps - 1):
         for copy in up_stores(n, n % 2) + down_stores(n, n % 2):
             copy.wait()
-    for j in range(tp):
+    for j in pieces:
         for k in range(4):
             core(k, j).wait_send()
         for copy in (diag_x, diag_y, direct_x, direct_y, summed_x, summed_y):
             copy(j).wait_send()
-        block = blocks[j]
-        if j < tp - 1:
+        block = blocks[j // SUB]
+        if j < (tp - 1) * SUB:
 
             @pl.when(block > rank)
             def _():
@@ -1570,6 +1505,7 @@
     rows, width = own.shape
     tokens = y.shape[0]
     span = width // fsdp
+    cut = rows // SUB
     bf16 = jnp.bfloat16
     f32 = jnp.float32
     dma = pltpu.SemaphoreType.DMA
@@ -1584,14 +1520,14 @@
             jax.ShapeDtypeStruct((expert_width, width), f32),
             jax.ShapeDtypeStruct((fsdp, shared_width, span), bf16),
         ],
-        in_specs=[anywhere] * 6,
+        in_specs=[anywhere, pl.BlockSpec(memory_space=pltpu.VMEM)] + [anywhere] * 4,
         out_specs=[pl.BlockSpec(memory_space=pltpu.VMEM)] + [anywhere] * 5,
         scratch_shapes=[
-            pltpu.VMEM((4, tp, rows, width), bf16),
-            pltpu.VMEM((4, tp, rows, width), bf16),
-            pltpu.VMEM((tp, 2, rows // 2, width), bf16),
-            pltpu.VMEM((tp, 2, rows, width), bf16),
-            pltpu.VMEM((2, tp, rows, width), bf16),
+            pltpu.VMEM((4, tp * SUB, cut, width), bf16),
+            pltpu.VMEM((4, tp * SUB, cut, width), bf16),
+            pltpu.VMEM((tp * SUB, 2, cut // 2, width), bf16),
+            pltpu.VMEM((tp * SUB, 2, cut, width), bf16),
+            pltpu.VMEM((2, tp * SUB, cut, width), bf16),
             pltpu.VMEM((tokens, 2 * UNIT), bf16),
             pltpu.VMEM((tokens, UNIT), bf16),
             pltpu.VMEM((2, tokens, span), bf16),
@@ -1599,8 +1535,9 @@
             pltpu.VMEM((2, 2, span, shared_width), bf16),
             pltpu.VMEM((2, expert_width, span), f32),
             pltpu.VMEM((2, shared_width, span), bf16),
-            dma((4, tp)), dma((4, tp)), dma((4, tp)), dma((6, tp)), dma((6, tp)),
-            dma((2, tp)), dma((2, tp)), dma, dma((2, tp)), dma((2, tp)),
+            dma((4, tp * SUB)), dma((4, tp * SUB)), dma((4, tp * SUB)),
+            dma((6, tp * SUB)), dma((6, tp * SUB)),
+            dma((2, tp * SUB)), dma((2, tp * SUB)), dma, dma((2, tp)), dma((2, tp)),
             dma((2,)), dma((2,)), dma((4, 2)),
         ],
         compiler_params=pltpu.CompilerParams(
@@ -1851,16 +1788,31 @@
             for k in (3, 2, 1, 0):
                 core(k, j, i).start()
                 local(k, j, i).start()
-    front(0)
-    first(0)
-    for bits in (6, 7, 2, 3, 4, 5, 1):
+    ends = (rank == 0) | (rank == tp - 1)
+
+    @pl.when(ends)
+    def _():
+        front(0)
+        front(1)
+
+    for bits in (6, 7, 2, 4, 3, 5, 1):
         shared_up(bits).start()
         shared_down(bits).start()
     own_up.start()
     own_down.start()
+    first(0)
     first(1)
+
+    @pl.when(jnp.logical_not(ends))
+    def _():
+        front(0)
+
     second(0)
-    front(1)
+
+    @pl.when(jnp.logical_not(ends))
+    def _():
+        front(1)
+
     second(1)
     front(2)
     front(3)
@@ -1979,6 +1931,368 @@
         name="epilogue",
     )(*arrays, shared_up, shared_down, dn, hidden, grad, gain, sums)
 
+def plane_peer(me, bits):
+    for one in (1, 2, 4):
+        if bits & one:
+            me = flipped(me, one)
+    return me
+
+
+def attend_kernel(tp, heads, halved, *refs):
+    parts = len(halved)
+    hidden_ref, gain_ref, grad_ref, seg_row_ref, seg_col_ref, cos_ref, sin_ref = refs[:7]
+    up_ref, down_ref = refs[7:9]
+    pieces, refs = refs[9 : 9 + parts], refs[9 + parts :]
+    rows_out, grads_ref, q_ref, k_ref, v_ref, lt_ref, heads_ref, part_ref = refs[:8]
+    up_out, down_out = refs[8:10]
+    fulls_out, refs = refs[10 : 10 + parts], refs[10 + parts :]
+    rows_ref, fulls, refs = refs[0], refs[1 : 1 + parts], refs[1 + parts :]
+    (
+        up_buf, down_buf, l_sem, e_sem, z_send, z_recv, g_send, g_recv, p_send, p_recv, s_sem, s_send, s_recv,
+    ) = refs
+    me, rank = place()
+    f32 = jnp.float32
+    bf16 = jnp.bfloat16
+    rows, width = hidden_ref.shape
+    length = rows * tp
+
+    barrier = pltpu.get_barrier_semaphore()
+    for bits in range(1, 8):
+        pl.semaphore_signal(
+            barrier, inc=1, device_id=(plane_peer(me, bits), rank), device_id_type=MESH
+        )
+
+    @pl.when(rank > 0)
+    def _():
+        pl.semaphore_signal(barrier, inc=1, device_id=(me, rank - 1), device_id_type=MESH)
+
+    @pl.when(rank < tp - 1)
+    def _():
+        pl.semaphore_signal(barrier, inc=1, device_id=(me, rank + 1), device_id_type=MESH)
+
+    left = (rank + tp - 1) // tp
+    right = (2 * (tp - 1) - rank) // tp
+    pl.semaphore_wait(barrier, 7 + left + right)
+
+    def along_z(ref, sends, recvs, block, to_right):
+        way = 0 if to_right else 1
+        spot = ref.at[pl.ds(block * rows, rows)]
+        return pltpu.make_async_remote_copy(
+            src_ref=spot,
+            dst_ref=spot,
+            send_sem=sends.at[way, block],
+            recv_sem=recvs.at[way, block],
+            device_id=(me, rank + 1 if to_right else rank - 1),
+            device_id_type=MESH,
+        )
+
+    def row_z(block, to_right):
+        return along_z(rows_ref, z_send, z_recv, block, to_right)
+
+    def grad_z(block, to_right):
+        return along_z(grads_ref, g_send, g_recv, block, to_right)
+
+    def z_start(copy):
+        @pl.when(rank < tp - 1)
+        def _():
+            copy(rank, True).start()
+
+        @pl.when(rank > 0)
+        def _():
+            copy(rank, False).start()
+
+    def z_step(copy, step):
+        @pl.when(rank >= step)
+        def _():
+            copy(rank - step, True).wait_recv()
+
+            @pl.when(rank < tp - 1)
+            def _():
+                copy(rank - step, True).start()
+
+        @pl.when(rank + step < tp)
+        def _():
+            copy(rank + step, False).wait_recv()
+
+            @pl.when(rank > 0)
+            def _():
+                copy(rank + step, False).start()
+
+    def z_end(copy):
+        for block in range(tp):
+
+            @pl.when((block <= rank) & (rank < tp - 1))
+            def _():
+                copy(block, True).wait_send()
+
+            @pl.when((block >= rank) & (rank > 0))
+            def _():
+                copy(block, False).wait_send()
+
+    def region(i, owner_bits, start=0, count=None):
+        size = pieces[i].shape[0]
+        count = size if count is None else count
+        return fulls[i].at[pl.ds(plane_peer(me, owner_bits) * size + start, count)]
+
+    def across(i, bit, owner_bits, slot, start=0, count=None):
+        spot = region(i, owner_bits, start, count)
+        return pltpu.make_async_remote_copy(
+            src_ref=pieces[i] if owner_bits == 0 else spot,
+            dst_ref=spot,
+            send_sem=p_send.at[slot, i],
+            recv_sem=p_recv.at[slot, i],
+            device_id=(flipped(me, bit), rank),
+            device_id_type=MESH,
+        )
+
+    def to_core(q, i):
+        return across(i, 1, 2 * q, q)
+
+    def own_x(i):
+        return across(i, 2, 0, 4)
+
+    def own_y(i):
+        return across(i, 4, 0, 5)
+
+    def x_to_y(i):
+        size = pieces[i].shape[0]
+        return across(i, 4, 2, 6, 0, size // 2 if halved[i] else size)
+
+    def y_to_x(i):
+        size = pieces[i].shape[0]
+        return across(i, 2, 4, 7, size // 2, size // 2)
+
+    def local(i):
+        return pltpu.make_async_copy(pieces[i], region(i, 0), l_sem.at[i])
+
+    def export(i):
+        return pltpu.make_async_copy(fulls[i], fulls_out[i], e_sem.at[i])
+
+    def forward(i):
+        own_x(i).wait_recv()
+        x_to_y(i).start()
+        to_core(1, i).start()
+        own_y(i).wait_recv()
+        if halved[i]:
+            y_to_x(i).start()
+        to_core(2, i).start()
+
+    def finish(i):
+        x_to_y(i).wait_recv()
+        if halved[i]:
+            y_to_x(i).wait_recv()
+        to_core(3, i).start()
+
+    def arrived(i):
+        local(i).wait()
+        for q in range(4):
+            to_core(q, i).wait_recv()
+        export(i).start()
+
+    up_rows = up_ref.shape[2]
+    span = down_ref.shape[2]
+
+    def shared_up(bits):
+        return pltpu.make_async_remote_copy(
+            src_ref=up_ref.at[plane_peer(me, bits)],
+            dst_ref=up_out.at[:, pl.ds(pl.multiple_of(me * up_rows, up_rows), up_rows)],
+            send_sem=s_send.at[0, bits],
+            recv_sem=s_recv.at[0, bits],
+            device_id=(plane_peer(me, bits), rank),
+            device_id_type=MESH,
+        )
+
+    def shared_down(bits):
+        return pltpu.make_async_remote_copy(
+            src_ref=down_ref.at[plane_peer(me, bits)],
+            dst_ref=down_out.at[:, pl.ds(pl.multiple_of(me * span, span), span)],
+            send_sem=s_send.at[1, bits],
+            recv_sem=s_recv.at[1, bits],
+            device_id=(plane_peer(me, bits), rank),
+            device_id_type=MESH,
+        )
+
+    own_loads = (
+        pltpu.make_async_copy(up_ref.at[me], up_buf, s_sem.at[0]),
+        pltpu.make_async_copy(down_ref.at[me], down_buf, s_sem.at[1]),
+    )
+    own_stores = (
+        pltpu.make_async_copy(
+            up_buf,
+            up_out.at[:, pl.ds(pl.multiple_of(me * up_rows, up_rows), up_rows)],
+            s_sem.at[0],
+        ),
+        pltpu.make_async_copy(
+            down_buf, down_out.at[:, pl.ds(pl.multiple_of(me * span, span), span)], s_sem.at[1]
+        ),
+    )
+
+    def project(which):
+        at = slice(which * heads * 128, (which + 1) * heads * 128)
+        return jnp.dot(rows_ref[...], fulls[0][:, at], preferred_element_type=f32)
+
+    def bias(which, head):
+        line = which * heads + head
+        size = pieces[3].shape[0]
+        share = 128 // 8
+        return jnp.concatenate(
+            [fulls[3][owner * size + line : owner * size + line + 1, :share] for owner in range(8)],
+            axis=1,
+        )
+
+    def rotated(columns):
+        return columns * cos_ref[...] + pltpu.roll(columns, 64, 1) * sin_ref[...]
+
+    def make_heads():
+        for which, ref in ((0, q_ref), (1, k_ref), (2, v_ref)):
+            all_heads = project(which)
+            for head in range(heads):
+                at = slice(head * 128, (head + 1) * 128)
+                one = all_heads[:, at] + bias(which, head)
+                if which < 2:
+                    one = rotated(one)
+                ref[:, at] = one.astype(bf16)
+
+    def attend(head):
+        at = slice(head * 128, (head + 1) * 128)
+        scores = lax.dot_general(q_ref[:, at], k_ref[:, at], NT, preferred_element_type=f32)
+        line = lax.broadcasted_iota(jnp.int32, (length, length), 0)
+        column = lax.broadcasted_iota(jnp.int32, (length, length), 1)
+        allowed = (line >= column) & (seg_col_ref[...] == seg_row_ref[...])
+        scores = jnp.where(allowed, scores * 128 ** (-0.5), -1e30)
+        peak = jnp.max(scores, axis=-1, keepdims=True)
+        log_total = peak + jnp.log(jnp.sum(jnp.exp(scores - peak), axis=-1, keepdims=True))
+        probs = jnp.exp(scores - log_total).astype(bf16)
+        lane = lax.broadcasted_iota(jnp.int32, (length, 128), 1)
+        before = jnp.zeros((length, 128), f32) if head == 0 else lt_ref[...]
+        lt_ref[...] = jnp.where(lane == head, log_total, before)
+        heads_ref[:, at] = jnp.dot(probs, v_ref[:, at], preferred_element_type=f32).astype(bf16)
+
+    def project_out():
+        size = pieces[1].shape[0]
+        share = width // 8
+        for owner in range(8):
+            part_ref[:, owner * share : (owner + 1) * share] = jnp.dot(
+                heads_ref[...],
+                fulls[1][owner * size : (owner + 1) * size, :],
+                preferred_element_type=f32,
+            ).astype(bf16)
+
+    for i in range(parts):
+        own_x(i).start()
+        own_y(i).start()
+        to_core(0, i).start()
+    hidden = hidden_ref[...].astype(f32)
+    inverse = lax.rsqrt(jnp.mean(hidden * hidden, axis=-1, keepdims=True) + epsilon)
+    own_rows = pl.ds(pl.multiple_of(rank * rows, rows), rows)
+    rows_ref[own_rows, :] = (hidden * inverse * gain_ref[...]).astype(bf16)
+    z_start(row_z)
+    own_grad = pltpu.make_async_copy(grad_ref, grads_ref.at[own_rows], l_sem.at[parts])
+    own_grad.start()
+    for i in range(parts):
+        local(i).start()
+    for copy in own_loads:
+        copy.start()
+    z_step(row_z, 1)
+    forward(0)
+    for load, store in zip(own_loads, own_stores):
+        load.wait()
+        store.start()
+    z_step(row_z, 2)
+    own_grad.wait()
+    z_start(grad_z)
+    for i in range(1, parts):
+        forward(i)
+    for bits in (6, 7, 2, 4, 3, 5, 1):
+        shared_up(bits).start()
+        shared_down(bits).start()
+    finish(0)
+    z_step(row_z, 3)
+    rows_export = pltpu.make_async_copy(rows_ref, rows_out, e_sem.at[parts])
+    rows_export.start()
+    for i in range(1, parts):
+        finish(i)
+    z_step(grad_z, 1)
+    for i in range(parts):
+        arrived(i)
+    make_heads()
+    z_step(grad_z, 2)
+    for head in range(heads):
+        attend(head)
+    project_out()
+    z_step(grad_z, 3)
+
+    rows_export.wait()
+    for store in own_stores:
+        store.wait()
+    for i in range(parts):
+        export(i).wait()
+        for q in range(4):
+            to_core(q, i).wait_send()
+        own_x(i).wait_send()
+        own_y(i).wait_send()
+        x_to_y(i).wait_send()
+        if halved[i]:
+            y_to_x(i).wait_send()
+    for bits in range(1, 8):
+        for copy in (shared_up, shared_down):
+            copy(bits).wait_recv()
+            copy(bits).wait_send()
+    z_end(row_z)
+    z_end(grad_z)
+
+
+def attend_pack(
+    hidden, gain, grad, segments, cos, sin, shared_up, shared_down, pieces, fsdp, tp, heads, number
+):
+    rows, width = hidden.shape
+    length = rows * tp
+    parts = len(pieces)
+    halved = [one.shape[0] >= 32 for one in pieces]
+    bf16 = jnp.bfloat16
+    f32 = jnp.float32
+    dma = pltpu.SemaphoreType.DMA
+    anywhere = pl.BlockSpec(memory_space=pl.ANY)
+    vmem = pl.BlockSpec(memory_space=pltpu.VMEM)
+    fulls = [(one.shape[0] * fsdp, one.shape[1]) for one in pieces]
+    of_heads = jax.ShapeDtypeStruct((length, heads * 128), bf16)
+    return pl.pallas_call(
+        functools.partial(attend_kernel, tp, heads, halved),
+        out_shape=[
+            jax.ShapeDtypeStruct((length, width), bf16),
+            jax.ShapeDtypeStruct((length, width), bf16),
+            of_heads,
+            of_heads,
+            of_heads,
+            jax.ShapeDtypeStruct((length, 128), f32),
+            of_heads,
+            jax.ShapeDtypeStruct((length, width), bf16),
+            jax.ShapeDtypeStruct(
+                (2, shared_up.shape[2] * fsdp, shared_up.shape[3]), shared_up.dtype
+            ),
+            jax.ShapeDtypeStruct((shared_down.shape[1], width), shared_down.dtype),
+        ]
+        + [jax.ShapeDtypeStruct(shape, one.dtype) for shape, one in zip(fulls, pieces)],
+        in_specs=[vmem] * 7 + [anywhere] * (2 + parts),
+        out_specs=[anywhere, anywhere] + [vmem] * 6 + [anywhere] * (2 + parts),
+        scratch_shapes=[pltpu.VMEM((length, width), bf16)]
+        + [pltpu.VMEM(shape, one.dtype) for shape, one in zip(fulls, pieces)]
+        + [
+            pltpu.VMEM(shared_up.shape[1:], shared_up.dtype),
+            pltpu.VMEM(shared_down.shape[1:], shared_down.dtype),
+            dma((parts + 1,)), dma((parts + 1,)),
+            dma((2, tp)), dma((2, tp)), dma((2, tp)), dma((2, tp)),
+            dma((8, parts)), dma((8, parts)), dma((2,)), dma((2, 8)), dma((2, 8)),
+        ],
+        compiler_params=pltpu.CompilerParams(
+            collective_id=number, has_side_effects=True, vmem_limit_bytes=48 << 20
+        ),
+        name="attend",
+    )(
+        hidden, gain, grad, segments.reshape(1, -1), segments.reshape(-1, 1), cos, sin,
+        shared_up, shared_down, *pieces,
+    )
+
 
 def dense_plan(
     hidden_in,
@@ -2003,17 +2317,15 @@
     packs = experts
     length = segment_ids.shape[1]
     own_rows = hidden_in.shape[0]
+    own_units = shared_gate_up.shape[0]
     model_width = hidden_in.shape[1]
     bf16 = jnp.bfloat16
     f32 = jnp.float32
 
-    grad_all = lax.all_gather(out_grad, every, axis=0, tiled=True)
-    shared_up = lax.all_to_all(shared_gate_up, "fsdp", split_axis=2, concat_axis=0, tiled=True)
-    shared_dn = lax.all_to_all(shared_down, "fsdp", split_axis=0, concat_axis=1, tiled=True)
     expert_up = expert_gate_up[0]
     expert_dn = expert_down[0]
     expert_width = expert_up.shape[2]
-    shared_width = shared_up.shape[2]
+    shared_width = shared_gate_up.shape[2] // experts
 
     chosen = expert_ids[:, :, None] == jnp.arange(experts, dtype=jnp.int32)
     table = jnp.sum(jnp.where(chosen, route_weights[:, :, None], 0.0), axis=1)
@@ -2031,72 +2343,74 @@
     bias_piece = jnp.pad(
         qkv_bias.reshape(bias_rows, bias_columns), ((0, 16 - bias_rows), (0, 128 - bias_columns))
     )
-    normed_one, qkv_flat, out_pieces, tables, bias_pieces = prologue(
-        (hidden_float * attn_inverse * attn_gain).astype(bf16),
-        [qkv_weight.reshape(-1, 3 * local_heads * head_dim), out_weight, table.T, bias_piece],
+    heads_width = local_heads * head_dim
+    up_pieces = shared_gate_up.reshape(own_units, 2, experts, shared_width).transpose(2, 1, 0, 3)
+    cos_two = jnp.concatenate([cos_table[:, 0], cos_table[:, 0]], axis=1)
+    sin_two = jnp.concatenate([-sin_table[:, 0], sin_table[:, 0]], axis=1)
+    (
+        normed_one,
+        grad_pack,
+        query,
+        keys,
+        values,
+        log_total,
+        heads_out,
+        projected,
+        shared_up,
+        shared_dn,
+        qkv_flat,
+        out_pieces,
+        tables,
+        bias_pieces,
+    ) = attend_pack(
+        hidden_in,
+        attn_gain[None],
+        out_grad,
+        segments,
+        cos_two,
+        sin_two,
+        up_pieces,
+        shared_down.reshape(experts, shared_width, -1),
+        [qkv_weight.reshape(-1, 3 * heads_width), out_weight, table.T, bias_piece],
         experts,
         lax.axis_size("tp"),
+        local_heads,
         4,
     )
-    out_full = out_pieces.reshape(experts, local_heads * head_dim, -1)
-    out_full = out_full.transpose(1, 0, 2).reshape(local_heads * head_dim, model_width)
+    query, keys, values = (
+        one.reshape(length, local_heads, head_dim) for one in (query, keys, values)
+    )
+    log_total = log_total[:, :local_heads].T[:, :, None]
+    out_full = out_pieces.reshape(experts, heads_width, -1)
+    out_full = out_full.transpose(1, 0, 2).reshape(heads_width, model_width)
     expert_scale = lax.dynamic_index_in_dim(
         tables.reshape(packs, experts, length), lax.axis_index("fsdp"), axis=1, keepdims=False
     ).reshape(-1)
-    bias_full = bias_pieces.reshape(experts, 16, 128)[:, :bias_rows, :bias_columns]
-    bias_full = bias_full.transpose(1, 0, 2).reshape(3, local_heads, head_dim)
-    qkv = (
-        jnp.dot(normed_one, qkv_flat, preferred_element_type=f32).reshape(
-            length, 3, local_heads, head_dim
-        )
-        + bias_full
-    )
-    query = rotate(qkv[:, 0], cos_table, sin_table).astype(bf16)
-    keys = rotate(qkv[:, 1], cos_table, sin_table).astype(bf16)
-    values = qkv[:, 2].astype(bf16)
-    scores = masked_scores(query, keys, allowed, score_scale)
-    row_peak = jnp.max(scores, axis=-1, keepdims=True)
-    log_total = row_peak + jnp.log(jnp.sum(jnp.exp(scores - row_peak), axis=-1, keepdims=True))
-    probs_b = jnp.exp(scores - log_total).astype(bf16)
-    heads_out = (
-        jnp.einsum("hqk,khd->qhd", probs_b, values, preferred_element_type=f32)
-        .astype(bf16)
-        .reshape(length, -1)
-    )
-    vec_high = shared_gate_vec.astype(bf16)
-    vec_low = (shared_gate_vec - vec_high.astype(f32)).astype(bf16)
-    gap = jnp.zeros((model_width, SHARED - expert_width), bf16)
-    rest = jnp.zeros((model_width, UNIT - SHARED - shared_width), bf16)
-    both_w = jnp.concatenate(
-        [
-            expert_up[:, 0],
-            gap,
-            shared_up[:, 0],
-            vec_high[:, None],
-            vec_low[:, None],
-            rest[:, 2:],
-            expert_up[:, 1],
-            gap,
-            shared_up[:, 1],
-            rest,
-        ],
-        axis=1,
-    )
-    down_w = jnp.concatenate([expert_dn, gap.T, shared_dn, rest.T], axis=0)
-    middle, normed_all, d_all, hidden_all, token_part, d_normed_two, extra_sum = ffn(
-        jnp.dot(heads_out, out_full, preferred_element_type=f32).astype(bf16),
+    scales = expert_scale.reshape(packs, lax.axis_size("tp"), 2, own_rows // 2)
+    scales = scales.transpose(0, 2, 1, 3).reshape(packs, 2, 1, length // 2)
+    middle, normed_all, grad_all, d_all, hidden_all, token_part, d_normed_two, lines = ffn(
+        projected,
         hidden_in,
         ffn_gain[None],
-        grad_all,
-        both_w,
-        down_w,
-        jnp.broadcast_to(expert_scale[:, None], (expert_scale.shape[0], 128)),
+        shared_gate_vec[None],
+        scales,
+        grad_pack,
+        expert_up.transpose(1, 0, 2),
+        shared_up,
+        expert_dn,
+        shared_dn,
         experts,
         lax.axis_size("tp"),
-        expert_width,
-        shared_width,
         1,
     )
+    tokens = token_part.shape[0]
+    middle = middle.reshape(own_rows, model_width)
+    normed_all = normed_all.reshape(tokens, model_width)
+    d_all = d_all.reshape(tokens, -1)
+    hidden_all = hidden_all.reshape(tokens, -1)
+    d_normed_two = d_normed_two.reshape(own_rows, model_width)
+    lines = lax.dynamic_slice_in_dim(lines, tp_rank * (own_rows // 2), own_rows // 2, axis=2)
+    extra_sum = lines.transpose(1, 0, 2).reshape(16, own_rows)
     ffn_inverse = inverse_rms(middle)
     normed_two_own = (middle * ffn_inverse * ffn_gain).astype(bf16)
     own_start = tp_rank * own_rows
@@ -2125,12 +2439,7 @@
         2,
     )
     hidden_out = (middle + total).astype(bf16)
-    g_out = jnp.einsum(
-        "tk,tfn->fkn",
-        heads_out,
-        d_rows.reshape(length, experts, -1),
-        preferred_element_type=f32,
-    ).astype(bf16)
+    g_out = jnp.dot(d_rows.T, heads_out, preferred_element_type=f32).astype(bf16)
     d_heads = (
         jnp.dot(d_rows, out_full.T, preferred_element_type=f32)
         .astype(bf16)
@@ -2156,7 +2465,7 @@
     g_qkv = jnp.dot(normed_one.T, d_qkv_b, preferred_element_type=f32).astype(bf16)
     d_normed_one = jnp.dot(d_qkv_b, qkv_flat.T, preferred_element_type=f32).astype(bf16)
     g_qkv, g_out, g_bias, g_shared_up, g_shared_down, hidden_grad, gains = epilogue(
-        [g_qkv, g_out.reshape(-1, g_out.shape[2]), g_bias.reshape(-1, 128)],
+        [g_qkv, g_out, g_bias.reshape(-1, 128)],
         g_shared_up,
         g_shared_down,
         d_normed_one,
@@ -2178,7 +2487,7 @@
         gains[1, :share],
         g_qkv.reshape(-1, 3, local_heads, head_dim),
         g_bias.reshape(qkv_bias.shape),
-        g_out.reshape(out_weight.shape),
+        g_out.reshape(out_weight.shape[::-1]).T,
         g_shared_up.transpose(1, 0, 2),
         g_shared_down,
         gains[2, :share],

time: 695 us -> 638 us (0.918)
  Pallas kernels: 499 us -> 541 us
  local copies, waits for them, and re-layouts: 93.3 us -> 53.4 us
  between operations: 15 us -> 1.56 us
  waiting for transfers between devices: 12.5 us -> 0 us
  starting transfers between devices: 9.68 us -> 0 us
  matrix products: 40.6 us -> 32 us
  other arithmetic: 20.5 us -> 12.7 us
    pallas_call x1, Pallas kernels: 223 us -> 295 us  [ffn(): pl.pallas_call(functools.partial(ffn_kernel, tp, expert_width, shared_wid...]
    pallas_call x1, Pallas kernels: 112 us -> 79.3 us  [outputs(): pl.pallas_call(functools.partial(outputs_kernel, tp, expert_width, shared...]
    concatenate x3 -> x0, local copies, waits for them, and re-layouts: 12.3 us -> none  [the longest x1 10.9 us: dense_plan(): jnp.concatenate([expert_up[:, 0], gap, shared_up[:, 0], vec_high[:, None]...]
    all_to_all x2 -> x0, waiting for transfers between devices: 11.8 us -> none  [the longest x1 11.8 us: dense_plan(): lax.all_to_all(shared_gate_up, 'fsdp', split_axis=2, concat_axis=0, tiled...]
    dot_general x4 -> x1, matrix products: 16.1 us -> 4.35 us  [dense_plan(): jnp.dot(d_rows.T, heads_out, preferred_element_type=f32).astype(bf16)]
    pallas_call x1, Pallas kernels: 69.5 us -> 80.7 us  [attend_pack(): pl.pallas_call(functools.partial(attend_kernel, tp, heads, halved), out_s...]
    all_to_all x2 -> x0, starting transfers between devices: 9.64 us -> none  [the longest x1 5.18 us: dense_plan(): lax.all_to_all(shared_down, 'fsdp', split_axis=0, concat_axis=1, tiled=True)]
    pallas_call x1, Pallas kernels: 94.8 us -> 85.8 us  [epilogue(): pl.pallas_call(functools.partial(epilogue_kernel, fsdp, tp, parts), out_s...]
  transfers between devices with their start and end apart: 3 -> 0, of which waited for: 1 -> 0; matrix products, arithmetic and copies ran while one was open for 10% -> 0% of each run, Pallas kernels for 10% -> 0%
where the time goes in v6:
time: 638 us; the launch traced here: 640 us
  Pallas kernels  541 us (85%)
  local copies, waits for them, and re-layouts  53.4 us (8%)
  matrix products  32 us (5%)
  other arithmetic  12.7 us (2%)
    pallas_call x1, Pallas kernels, ffn(): pl.pallas_call(functools.partial(ffn_kernel, tp, expert_width, shared_wid...  295 us
    pallas_call x1, Pallas kernels, epilogue(): pl.pallas_call(functools.partial(epilogue_kernel, fsdp, tp, parts), out_s...  85.8 us
    pallas_call x1, Pallas kernels, attend_pack(): pl.pallas_call(functools.partial(attend_kernel, tp, heads, halved), out_s...  80.7 us
    pallas_call x1, Pallas kernels, outputs(): pl.pallas_call(functools.partial(outputs_kernel, tp, expert_width, shared...  79.3 us
    unnamed x113, local copies, waits for them, and re-layouts  31.6 us

profile of v6, /device:TPU:0, one launch (start us, length us, event | category | flops | bytes accessed | tf_op | source)
XLA Modules:
  0.0 640.4 jit_solution(12934693876550260385)
XLA Ops:
  2.6 3.3 copy.94
  6.0 3.8 copy.95
  9.8 2.3 reshape.316.refs_9_
  12.4 80.7 %attend.1 = (bf16[512,2048]{1,0:T(8,128)(2,1)}, bf16[512,2048]{1,0:T(8,128)(2,1)}, bf16[512,512]{1,0:T(8,128)(2,1)S(1)}, bf16[512,512]{1,0:T(8,128)(2,1)S(1)}, b...) custom-call(bf16[128,2048]{1,0:T(8,128)(2,1)S(1)} %copy-done, ...), custom_call_target="tpu_custom_call" | custom-call | tf_op jit(solution)/shard_map/attend/pallas_call | solution.py:2259
  97.9 4.6 copy.99
  102.5 295.0 %ffn.1 = (f32[2,64,2048]{2,1,0:T(8,128)}, bf16[8,4,2,64,2048]{4,3,2,1,0:T(8,128)(2,1)}, bf16[4096,2048]{1,0:T(8,128)(2,1)}, bf16[8,4,2,64,1280]{4,3,2,1,0:T(8,12...) custom-call(bf16[4,2,64,2048]{3,2,1,0:T(8,128)(2,1)} %bitcast.140, ...), custom_call_target="tpu_custom_call" | custom-call | tf_op jit(solution)/shard_map/ffn/pallas_call | solution.py:1128
  401.7 2.6 fusion.30
  404.2 79.3 %outputs.1 = (f32[128,2048]{1,0:T(8,128)}, bf16[512,2048]{1,0:T(8,128)(2,1)}, f32[2,2048,352]{2,1,0:T(8,128)}, bf16[2,2048,176]{2,1,0:T(8,128)(2,1)}, f32[352,2048]{1,0:T(8,128)}, /*index=5*/bf16[8,176,256]{2,1,0:T(8,128)(2,1)}) custom-call(bf16[4096,2048]{1,0:T(8,128)(2,1)} %get-tuple-element.53.refs_0_, bf16[128,2048]{1,0:T(8,128)(2,1)} %get-tuple-element.136.refs_1_, ...), custom_call_target="tpu_custom_call" | custom-call | tf_op jit(solution)/shard_map/outputs/pallas_call | solution.py:1513
  484.7 3.9 copy.103
  488.6 4.7 multiply_reduce_fusion.1
  494.5 3.9 fusion.32
  498.8 4.1 multiply_convert_fusion
  504.4 1.8 fusion.13
  507.4 1.6 multiply_add_fusion.2
  509.2 2.0 copy-done.28
  513.3 4.7 convolution_convert_fusion.1.refs_5_
  518.4 4.4 convolution_convert_fusion.2.refs_1_
  522.7 5.7 convolution_convert_fusion.refs_0_
  528.5 85.8 %epilogue.1 = (f32[2,128,1536]{2,1,0:T(8,128)}, f32[2,128,512]{2,1,0:T(8,128)S(1)}, f32[2,16,128]{2,1,0:T(8,128)S(1)}, f32[2,256,1408]{2,1,0:T(8,128)}, f32[1408...) custom-call(bf16[2048,1536]{1,0:T(8,128)(2,1)} %convolution_convert_fusion.refs_0_, ...), custom_call_target="tpu_custom_call" | custom-call | tf_op jit(solution)/shard_map/epilogue/pallas_call | solution.py:1907
  614.3 5.8 copy.114
  620.2 2.8 reshape.335
  625.9 6.5 %copy.115 = f32[1,2048,2,352]{1,3,2,0:T(8,128)} copy(f32[1,2048,2,352]{3,1,2,0:T(8,128)} %bitcast.129) | data formatting | bytes 11534336
  632.3 2.1 fusion.21
  638.6 1.6 copy.132
  (159 shorter events, 26.1 us)
Async XLA Ops:
  5.9 6.2 copy-start.18
  5.9 6.4 copy-start.42
  5.9 6.4 copy-start.46
  5.9 6.4 %copy-start.47 = (f32[3,4,16]{2,1,0:T(4,128)S(1)}, f32[3,4,16]{2,1,0:T(4,128)}, u32[]{:S(2)}) copy-start(f32[3,4,16]{2,1,0:T(4,128)} %param.23) | copy-start | bytes 2308
  5.9 6.4 %copy-start = (bf16[128,2048]{1,0:T(8,128)(2,1)S(1)}, bf16[128,2048]{1,0:T(8,128)(2,1)}, u32[]{:S(2)}) copy-start(bf16[128,2048]{1,0:T(8,128)(2,1)} %refs_6_.1) | copy-start | bytes 1572868
  5.9 6.4 %copy-start.2 = (bf16[128,2048]{1,0:T(8,128)(2,1)S(1)}, bf16[128,2048]{1,0:T(8,128)(2,1)}, u32[]{:S(2)}) copy-start(bf16[128,2048]{1,0:T(8,128)(2,1)} %refs_2_.1) | copy-start | bytes 1572868
  5.9 6.4 %copy-start.5 = (bf16[1408,256]{1,0:T(8,128)(2,1)S(1)}, bf16[1408,256]{1,0:T(8,128)(2,1)}, u32[]{:S(2)}) copy-start(bf16[1408,256]{1,0:T(8,128)(2,1)} %param.26) | copy-start | bytes 2162692
  5.9 6.4 %copy-start.15 = (bf16[512,256]{1,0:T(8,128)(2,1)S(1)}, bf16[512,256]{1,0:T(8,128)(2,1)}, u32[]{:S(2)}) copy-start(bf16[512,256]{1,0:T(8,128)(2,1)} %refs_10_.1) | copy-start | bytes 786436
  6.0 6.4 %copy-start.16 = (f32[2048]{0:T(1024)S(1)}, f32[2048]{0:T(1024)}, u32[]{:S(2)}) copy-start(f32[2048]{0:T(1024)} %param.20) | copy-start | bytes 24580
  102.5 296.6 %copy-start.39 = (f32[2048]{0:T(1024)S(1)}, f32[2048]{0:T(1024)}, u32[]{:S(2)}) copy-start(f32[2048]{0:T(1024)} %param.21) | copy-start | bytes 24580
  102.5 296.6 %copy-start.40 = (f32[2048]{0:T(1024)S(1)}, f32[2048]{0:T(1024)}, u32[]{:S(2)}) copy-start(f32[2048]{0:T(1024)} %param.27) | copy-start | bytes 24580
  404.2 79.3 %copy-start.8 = (bf16[512,512]{1,0:T(8,128)(2,1)S(1)}, bf16[512,512]{1,0:T(8,128)(2,1)}, u32[]{:S(2)}) copy-start(bf16[512,512]{1,0:T(8,128)(2,1)} %copy-done.7) | copy-start | bytes 1572868
  488.6 4.7 copy-start.12
  488.6 5.7 copy-start.10
  512.9 5.0 copy-start.34
  518.3 4.4 copy-start.35
  518.3 4.4 copy-start.48
  522.7 5.7 copy-start.1
  522.7 5.7 copy-start.4
  522.7 5.7 copy-start.17
  614.3 5.8 copy-start.13
  614.3 5.8 copy-start.19
  614.3 5.8 copy-start.21
  625.9 6.5 %copy-start.25 = (f32[2,64,2048]{2,1,0:T(8,128)S(1)}, f32[2,64,2048]{2,1,0:T(8,128)}, u32[]{:S(2)}) copy-start(f32[2,64,2048]{2,1,0:T(8,128)} %get-tuple-element.52) | copy-start | bytes 3145732
  (29 other events, 69.8 us)

commit v7 on v6

--- a/solution.py
+++ b/solution.py
@@ -1547,18 +1547,20 @@
     )(y, own, x, d, h, g)
 
 
-def epilogue_kernel(fsdp, tp, parts, *refs):
-    ins, refs = refs[:parts], refs[parts:]
-    gs_ref, ds_ref, dn_ref, hidden_ref, grad_ref, gain_ref, sums_ref = refs[:7]
-    refs = refs[7:]
+def backward_kernel(fsdp, tp, heads, *refs):
+    parts = 3
+    d_ref, ho_ref, q_ref, k_ref, v_ref, lt_ref, cos_ref, sin_ref = refs[:8]
+    seg_row_ref, seg_col_ref, normed_ref, qkv_ref, out_ref = refs[8:13]
+    gs_ref, ds_ref, hidden_ref, grad_ref, gain_ref, sums_ref = refs[13:19]
+    refs = refs[19:]
     outs, refs = refs[:parts], refs[parts:]
     gs_out, ds_out, hidden_grad_ref, gains_ref = refs[:4]
     refs = refs[4:]
     mine, other, diag_in, last_in = (refs[i * parts : (i + 1) * parts] for i in range(4))
     (
-        gs_in, ds_in, dn_buf, z_in, v_send, v_in, w_send, w_in,
-        l_sem, c_send, c_recv, p_send, p_recv, s_sem, s_send, s_recv,
-        f_sem, f_send, f_recv, v_ssem, v_rsem, w_ssem, w_rsem,
+        dh_buf, dqkv_buf, gs_in, ds_in, dn_buf, z_in, v_send, v_in, w_send, w_in,
+        c_send, c_recv, p_send, p_recv, s_sem, s_send, s_recv,
+        f_send, f_recv, v_ssem, v_rsem, w_ssem, w_rsem,
     ) = refs[4 * parts :]
     me, rank = place()
     f32 = jnp.float32
@@ -1599,15 +1601,18 @@
     def add(ref, spot, one):
         ref[spot] = (ref[spot].astype(f32) + one.astype(f32)).astype(ref.dtype)
 
-    def region(i, pack, j):
-        return ins[i].at[pl.ds((pack * chunks + j) * sizes[i], sizes[i])]
-
-    def local(k, j, i):
-        return pltpu.make_async_copy(region(i, packs[k], j), mine[i].at[k, j], l_sem.at[k, j, i])
+    core_of, x_of, y_of = me % 2, (me // 2) % 2, me // 4
+
+    def pack_of(bits):
+        return (
+            4 * ((y_of + bits // 4) % 2)
+            + 2 * ((x_of + (bits // 2) % 2) % 2)
+            + (core_of + bits % 2) % 2
+        )
 
     def core(k, j, i):
         return pltpu.make_async_remote_copy(
-            src_ref=region(i, flipped(packs[k], 1), j),
+            src_ref=mine[i].at[pack_of(2 * k + 1), j],
             dst_ref=other[i].at[k, j],
             send_sem=c_send.at[k, j, i],
             recv_sem=c_recv.at[k, j, i],
@@ -1626,44 +1631,60 @@
         )
 
     def diag_x(j, i):
-        return across(2, mine[i].at[3, j, low[i]], diag_in[i].at[j, 0], 0, j, i)
+        return across(2, mine[i].at[packs[3], j, low[i]], diag_in[i].at[j, 0], 0, j, i)
 
     def diag_y(j, i):
-        return across(4, mine[i].at[3, j, high[i]], diag_in[i].at[j, 1], 1, j, i)
+        return across(4, mine[i].at[packs[3], j, high[i]], diag_in[i].at[j, 1], 1, j, i)
 
     def direct_x(j, i):
-        return across(2, mine[i].at[1, j, low[i]], last_in[i].at[j, 0, low[i]], 2, j, i)
+        return across(2, mine[i].at[packs[1], j, low[i]], last_in[i].at[j, 0, low[i]], 2, j, i)
 
     def direct_y(j, i):
-        return across(4, mine[i].at[2, j, high[i]], last_in[i].at[j, 1, high[i]], 3, j, i)
+        return across(4, mine[i].at[packs[2], j, high[i]], last_in[i].at[j, 1, high[i]], 3, j, i)
 
     def summed_x(j, i):
-        return across(2, mine[i].at[1, j, high[i]], last_in[i].at[j, 0, high[i]], 4, j, i)
+        return across(2, mine[i].at[packs[1], j, high[i]], last_in[i].at[j, 0, high[i]], 4, j, i)
 
     def summed_y(j, i):
-        return across(4, mine[i].at[2, j, low[i]], last_in[i].at[j, 1, low[i]], 5, j, i)
-
-    def first(j):
-        for i in every:
-            for k in (3, 2, 1, 0):
+        return across(4, mine[i].at[packs[2], j, low[i]], last_in[i].at[j, 1, low[i]], 5, j, i)
+
+    def send_piece(bits, i):
+        k = bits // 2
+
+        @pl.when(bits % 2 == 1)
+        def _():
+            for j in range(chunks):
+                core(k, j, i).start()
+
+        @pl.when(bits % 2 == 0)
+        def _():
+            for j in range(chunks):
                 core(k, j, i).wait_recv()
-                local(k, j, i).wait()
-                add(mine[i], (k, j), other[i][k, j])
-                if k == 3:
+                add(mine[i], (pack_of(bits), j), other[i][k, j])
+
+            @pl.when(k == 3)
+            def _():
+                for j in range(chunks):
                     diag_x(j, i).start()
                     diag_y(j, i).start()
-                if k == 2:
+
+            @pl.when(k == 2)
+            def _():
+                for j in range(chunks):
                     direct_y(j, i).start()
-                if k == 1:
+
+            @pl.when(k == 1)
+            def _():
+                for j in range(chunks):
                     direct_x(j, i).start()
 
     def second(j):
         for i in every:
             diag_x(j, i).wait_recv()
-            add(mine[i], (2, j, low[i]), diag_in[i][j, 0])
+            add(mine[i], (packs[2], j, low[i]), diag_in[i][j, 0])
             summed_y(j, i).start()
             diag_y(j, i).wait_recv()
-            add(mine[i], (1, j, high[i]), diag_in[i][j, 1])
+            add(mine[i], (packs[1], j, high[i]), diag_in[i][j, 1])
             summed_x(j, i).start()
 
     def third(j):
@@ -1673,7 +1694,7 @@
             summed_x(j, i).wait_recv()
             summed_y(j, i).wait_recv()
             outs[i][j] = (
-                mine[i][0, j].astype(f32)
+                mine[i][me, j].astype(f32)
                 + last_in[i][j, 0].astype(f32)
                 + last_in[i][j, 1].astype(f32)
             )
@@ -1705,11 +1726,6 @@
         gs_ref.at[:, pl.ds(pl.multiple_of(me * span, span), span)], gs_in.at[me], s_sem.at[0]
     )
     own_down = pltpu.make_async_copy(ds_ref.at[me], ds_in.at[me], s_sem.at[1])
-
-    def front_load(block):
-        return pltpu.make_async_copy(
-            dn_ref.at[pl.ds(block * rows, rows)], dn_buf.at[block], f_sem.at[block]
-        )
 
     def front_z(j, right):
         way = 0 if right else 1
@@ -1725,7 +1741,6 @@
 
     def front(j):
         block = blocks[j]
-        front_load(block).wait()
         if j < tp - 1:
 
             @pl.when((block > rank) & (rank > 0))
@@ -1781,27 +1796,95 @@
             device_id_type=MESH,
         )
 
-    for block in blocks:
-        front_load(block).start()
-    for j in range(chunks):
-        for i in every:
-            for k in (3, 2, 1, 0):
-                core(k, j, i).start()
-                local(k, j, i).start()
+    length = d_ref.shape[0]
+    cut = width // fsdp
+    size = heads * 128
+    scale = 128 ** (-0.5)
+
+    def out_piece(n, carry):
+        bits = fsdp - 1 - n
+        pack = pack_of(bits)
+        at = pl.ds(pl.multiple_of(pack * cut, cut), cut)
+        piece = lax.dot_general(d_ref[:, at], ho_ref[...], TN, preferred_element_type=f32)
+        mine[1][pack] = piece.astype(bf16).reshape(chunks, cut // chunks, size)
+        send_piece(bits, 1)
+        return carry
+
+    def qkv_piece(n, carry):
+        bits = fsdp - 1 - n
+        pack = pack_of(bits)
+        at = pl.ds(pl.multiple_of(pack * cut, cut), cut)
+        piece = lax.dot_general(normed_ref[:, at], dqkv_buf[...], TN, preferred_element_type=f32)
+        mine[0][pack] = piece.astype(bf16).reshape(chunks, cut // chunks, 3 * size)
+        send_piece(bits, 0)
+        return carry
+
+    def head_grads():
+        total = jnp.zeros((length, size), f32)
+        for owner in range(fsdp):
+            total = total + lax.dot_general(
+                d_ref[:, owner * cut : (owner + 1) * cut],
+                out_ref[owner * size : (owner + 1) * size, :],
+                NT,
+                preferred_element_type=f32,
+            )
+        dh_buf[...] = total.astype(bf16)
+
+    def unrotated(columns):
+        return columns * cos_ref[...] - pltpu.roll(columns, 64, 1) * sin_ref[...]
+
+    def attend_back(head):
+        at = slice(head * 128, (head + 1) * 128)
+        query, keys, values = q_ref[:, at], k_ref[:, at], v_ref[:, at]
+        d_head = dh_buf[:, at]
+        scores = lax.dot_general(query, keys, NT, preferred_element_type=f32) * scale
+        line = lax.broadcasted_iota(jnp.int32, (length, length), 0)
+        column = lax.broadcasted_iota(jnp.int32, (length, length), 1)
+        allowed = (line >= column) & (seg_col_ref[...] == seg_row_ref[...])
+        probs = jnp.exp(jnp.where(allowed, scores, -1e30) - lt_ref[:, head : head + 1])
+        d_values = lax.dot_general(probs.astype(bf16), d_head, TN, preferred_element_type=f32)
+        d_probs = lax.dot_general(d_head, values, NT, preferred_element_type=f32)
+        delta = jnp.sum(
+            d_head.astype(f32) * ho_ref[:, at].astype(f32), axis=-1, keepdims=True
+        )
+        d_scores = (probs * (d_probs - delta)).astype(bf16)
+        d_query = jnp.dot(d_scores, keys, preferred_element_type=f32) * scale
+        d_keys = lax.dot_general(d_scores, query, TN, preferred_element_type=f32) * scale
+        for which, grad in enumerate((unrotated(d_query), unrotated(d_keys), d_values)):
+            base = which * size + head * 128
+            dqkv_buf[:, base : base + 128] = grad.astype(bf16)
+            here = which * heads + head
+            mine[2][0, 0, here : here + 1] = jnp.sum(grad, axis=0, keepdims=True)
+
+    def row_grads(half):
+        at = pl.ds(pl.multiple_of(half * 2 * rows, 2 * rows), 2 * rows)
+        grads = lax.dot_general(dqkv_buf[at, :], qkv_ref[...], NT, preferred_element_type=f32)
+        dn_buf[pl.ds(2 * half, 2)] = grads.astype(bf16).reshape(2, rows, width)
+
     ends = (rank == 0) | (rank == tp - 1)
-
-    @pl.when(ends)
-    def _():
-        front(0)
-        front(1)
-
     for bits in (6, 7, 2, 4, 3, 5, 1):
         shared_up(bits).start()
         shared_down(bits).start()
     own_up.start()
     own_down.start()
-    first(0)
-    first(1)
+    lax.fori_loop(0, fsdp, out_piece, 0)
+    head_grads()
+    mine[2][...] = jnp.zeros_like(mine[2])
+    for head in range(heads):
+        attend_back(head)
+    row_grads(1 - near)
+
+    @pl.when(ends)
+    def _():
+        front(0)
+        front(1)
+
+    row_grads(near)
+    for owner in range(1, fsdp):
+        mine[2][owner] = mine[2][0]
+    lax.fori_loop(0, fsdp, qkv_piece, 0)
+    for n in range(fsdp):
+        send_piece(jnp.int32(fsdp - 1 - n), 2)
 
     @pl.when(jnp.logical_not(ends))
     def _():
@@ -1882,22 +1965,27 @@
             front_z(j, False).wait_send()
 
 
-def epilogue(arrays, shared_up, shared_down, dn, hidden, grad, gain, sums, fsdp, tp, collective_id):
+def backward(
+    d_rows, heads_out, query, keys, values, log_total, cos, sin, segments, normed, qkv, out,
+    shared_up, shared_down, hidden, grad, gain, sums, fsdp, tp, heads, number,
+):
     chunks = 2
-    parts = len(arrays)
     rows, width = hidden.shape
+    length = rows * tp
     units = shared_up.shape[2]
     span = shared_down.shape[2]
+    size = heads * 128
+    bf16 = jnp.bfloat16
     f32 = jnp.float32
-    shapes = [(one.shape[0] // (fsdp * chunks), one.shape[1], one.dtype) for one in arrays]
-    scratch = [pltpu.VMEM((4, chunks, size, w), kind) for size, w, kind in shapes]
-    scratch += [pltpu.VMEM((4, chunks, size, w), kind) for size, w, kind in shapes]
-    scratch += [pltpu.VMEM((chunks, 2, size // 2, w), kind) for size, w, kind in shapes]
-    scratch += [pltpu.VMEM((chunks, 2, size, w), kind) for size, w, kind in shapes]
+    shapes = [(width // (fsdp * chunks), 3 * size, bf16), (span // chunks, size, bf16), (16, 128, f32)]
+    scratch = [pltpu.VMEM((fsdp, chunks, count, w), kind) for count, w, kind in shapes]
+    scratch += [pltpu.VMEM((4, chunks, count, w), kind) for count, w, kind in shapes]
+    scratch += [pltpu.VMEM((chunks, 2, count // 2, w), kind) for count, w, kind in shapes]
+    scratch += [pltpu.VMEM((chunks, 2, count, w), kind) for count, w, kind in shapes]
     dma = pltpu.SemaphoreType.DMA
     anywhere = pl.BlockSpec(memory_space=pl.ANY)
     vmem = pl.BlockSpec(memory_space=pltpu.VMEM)
-    out_shape = [jax.ShapeDtypeStruct((chunks, size, w), f32) for size, w, _ in shapes]
+    out_shape = [jax.ShapeDtypeStruct((chunks, count, w), f32) for count, w, _ in shapes]
     out_shape += [
         jax.ShapeDtypeStruct((2, span, fsdp * units), f32),
         jax.ShapeDtypeStruct((fsdp * units, span), f32),
@@ -1905,31 +1993,37 @@
         jax.ShapeDtypeStruct((8, 128), f32),
     ]
     return pl.pallas_call(
-        functools.partial(epilogue_kernel, fsdp, tp, parts),
+        functools.partial(backward_kernel, fsdp, tp, heads),
         out_shape=out_shape,
-        in_specs=[anywhere] * (parts + 3) + [vmem] * 4,
+        in_specs=[vmem] * 13 + [anywhere] * 2 + [vmem] * 4,
         out_specs=[vmem] * len(out_shape),
         scratch_shapes=scratch
         + [
+            pltpu.VMEM((length, size), bf16),
+            pltpu.VMEM((length, 3 * size), bf16),
             pltpu.VMEM((fsdp, 2, span, units), shared_up.dtype),
             pltpu.VMEM((fsdp, units, span), shared_down.dtype),
-            pltpu.VMEM((tp, rows, width), dn.dtype),
-            pltpu.VMEM((2, tp, rows, width), dn.dtype),
+            pltpu.VMEM((tp, rows, width), bf16),
+            pltpu.VMEM((2, tp, rows, width), bf16),
             pltpu.VMEM((fsdp, 8, width // fsdp), f32),
             pltpu.VMEM((fsdp, 8, width // fsdp), f32),
             pltpu.VMEM((tp, 8, 128), f32),
             pltpu.VMEM((tp, 8, 128), f32),
-            dma((4, chunks, parts)), dma((4, chunks, parts)), dma((4, chunks, parts)),
-            dma((6, chunks, parts)), dma((6, chunks, parts)),
+            dma((4, chunks, 3)), dma((4, chunks, 3)),
+            dma((6, chunks, 3)), dma((6, chunks, 3)),
             dma((2,)), dma((2, fsdp)), dma((2, fsdp)),
-            dma((tp,)), dma((2, tp)), dma((2, tp)),
+            dma((2, tp)), dma((2, tp)),
             dma((fsdp,)), dma((fsdp,)), dma((tp,)), dma((tp,)),
         ],
         compiler_params=pltpu.CompilerParams(
-            collective_id=collective_id, has_side_effects=True, vmem_limit_bytes=48 << 20
+            collective_id=number, has_side_effects=True, vmem_limit_bytes=61 << 20
         ),
-        name="epilogue",
-    )(*arrays, shared_up, shared_down, dn, hidden, grad, gain, sums)
+        name="backward",
+    )(
+        d_rows, heads_out, query, keys, values, log_total, cos, sin, segments.reshape(1, -1),
+        segments.reshape(-1, 1), normed, qkv, out, shared_up, shared_down, hidden, grad, gain, sums,
+    )
+
 
 def plane_peer(me, bits):
     for one in (1, 2, 4):
@@ -2331,11 +2425,8 @@
     table = jnp.sum(jnp.where(chosen, route_weights[:, :, None], 0.0), axis=1)
     local_heads = qkv_weight.shape[2]
     head_dim = qkv_weight.shape[3]
-    score_scale = head_dim ** (-0.5)
     cos_table, sin_table = rope_tables(length, head_dim)
-    positions = jnp.arange(length, dtype=jnp.int32)
     segments = segment_ids[0]
-    allowed = (positions[:, None] >= positions[None, :]) & (segments[:, None] == segments[None, :])
     hidden_float = hidden_in.astype(f32)
     attn_inverse = inverse_rms(hidden_float)
     bias_rows = 3 * local_heads
@@ -2377,12 +2468,6 @@
         local_heads,
         4,
     )
-    query, keys, values = (
-        one.reshape(length, local_heads, head_dim) for one in (query, keys, values)
-    )
-    log_total = log_total[:, :local_heads].T[:, :, None]
-    out_full = out_pieces.reshape(experts, heads_width, -1)
-    out_full = out_full.transpose(1, 0, 2).reshape(heads_width, model_width)
     expert_scale = lax.dynamic_index_in_dim(
         tables.reshape(packs, experts, length), lax.axis_index("fsdp"), axis=1, keepdims=False
     ).reshape(-1)
@@ -2439,46 +2524,34 @@
         2,
     )
     hidden_out = (middle + total).astype(bf16)
-    g_out = jnp.dot(d_rows.T, heads_out, preferred_element_type=f32).astype(bf16)
-    d_heads = (
-        jnp.dot(d_rows, out_full.T, preferred_element_type=f32)
-        .astype(bf16)
-        .reshape(length, local_heads, head_dim)
-    )
-    heads_three = heads_out.reshape(length, local_heads, head_dim)
-    scores_again = masked_scores(query, keys, allowed, score_scale)
-    probs_full = jnp.exp(scores_again - log_total)
-    probs_again = probs_full.astype(bf16)
-    d_values = jnp.einsum("hqk,qhd->khd", probs_again, d_heads, preferred_element_type=f32)
-    d_probs = jnp.einsum("qhd,khd->hqk", d_heads, values, preferred_element_type=f32)
-    delta = jnp.sum(d_heads.astype(f32) * heads_three.astype(f32), axis=-1)
-    d_scores = (probs_full * (d_probs - delta.T[:, :, None])).astype(bf16)
-    d_query = jnp.einsum("hqk,khd->qhd", d_scores, keys, preferred_element_type=f32) * score_scale
-    d_keys = jnp.einsum("hqk,qhd->khd", d_scores, query, preferred_element_type=f32) * score_scale
-    d_qkv = jnp.stack(
-        [unrotate(d_query, cos_table, sin_table), unrotate(d_keys, cos_table, sin_table), d_values],
-        axis=1,
-    )
-    g_bias = jnp.sum(d_qkv, axis=0).reshape(bias_rows, experts, bias_columns).transpose(1, 0, 2)
-    g_bias = jnp.pad(g_bias, ((0, 0), (0, 32 - bias_rows), (0, 128 - bias_columns)))
-    d_qkv_b = d_qkv.astype(bf16).reshape(length, -1)
-    g_qkv = jnp.dot(normed_one.T, d_qkv_b, preferred_element_type=f32).astype(bf16)
-    d_normed_one = jnp.dot(d_qkv_b, qkv_flat.T, preferred_element_type=f32).astype(bf16)
-    g_qkv, g_out, g_bias, g_shared_up, g_shared_down, hidden_grad, gains = epilogue(
-        [g_qkv, g_out, g_bias.reshape(-1, 128)],
+    g_qkv, g_out, g_bias, g_shared_up, g_shared_down, hidden_grad, gains = backward(
+        d_rows,
+        heads_out,
+        query,
+        keys,
+        values,
+        log_total,
+        cos_two,
+        sin_two,
+        segments,
+        normed_one,
+        qkv_flat,
+        out_pieces,
         g_shared_up,
         g_shared_down,
-        d_normed_one,
         hidden_in,
         middle_grad,
         attn_gain[None],
         jnp.stack([g_ffn_gain, g_gate_vec]),
         experts,
         lax.axis_size("tp"),
+        local_heads,
         3,
     )
     share = model_width // (experts * lax.axis_size("tp"))
-    g_bias = g_bias.reshape(32, 128)[:bias_rows, :bias_columns]
+    g_bias = lax.dynamic_slice_in_dim(
+        g_bias.reshape(32, 128)[:bias_rows], lax.axis_index("fsdp") * bias_columns, bias_columns, 1
+    )
     return (
         hidden_out,
         hidden_grad,

time: 638 us -> 588 us (0.922)
  matrix products: 32 us -> 0 us
  local copies, waits for them, and re-layouts: 53.4 us -> 41.7 us
  Pallas kernels: 541 us -> 532 us
    dot_general x9 -> x0, matrix products: 32 us -> none  [the longest x1 5.73 us: dense_plan(): jnp.dot(normed_one.T, d_qkv_b, preferred_element_type=f32).astype(bf16)]
    pallas_call x1, Pallas kernels: 295 us -> 281 us  [ffn(): pl.pallas_call(functools.partial(ffn_kernel, tp, expert_width, shared_wid...]
    unnamed x113 -> x66, local copies, waits for them, and re-layouts: 31.6 us -> 28.8 us
where the time goes in v7:
time: 588 us; the launch traced here: 584 us
  Pallas kernels  532 us (90%)
  local copies, waits for them, and re-layouts  41.7 us (7%)
  other arithmetic  9.28 us (2%)
    pallas_call x1, Pallas kernels, ffn(): pl.pallas_call(functools.partial(ffn_kernel, tp, expert_width, shared_wid...  281 us
    pallas_call x1, Pallas kernels, backward(): pl.pallas_call(functools.partial(backward_kernel, fsdp, tp, heads), out_s...  89.3 us
    pallas_call x1, Pallas kernels, outputs(): pl.pallas_call(functools.partial(outputs_kernel, tp, expert_width, shared...  81.3 us
    pallas_call x1, Pallas kernels, attend_pack(): pl.pallas_call(functools.partial(attend_kernel, tp, heads, halved), out_s...  80.5 us
    unnamed x66, local copies, waits for them, and re-layouts  28.8 us

profile of v7, /device:TPU:0, one launch (start us, length us, event | category | flops | bytes accessed | tf_op | source)
XLA Modules:
  0.0 584.3 jit_solution(8522999769157977602)
XLA Ops:
  2.9 0.8 copy.52.refs_4_.refs_9_
  3.7 1.0 fusion.10
  4.9 1.2 reshape.207.refs_9_
  6.1 3.7 copy.50
  9.8 2.4 copy.51
  12.2 4.7 copy.55
  17.0 0.9 copy-done.13
  17.9 80.5 %attend.1 = (bf16[512,2048]{1,0:T(8,128)(2,1)}, bf16[512,2048]{1,0:T(8,128)(2,1)}, bf16[512,512]{1,0:T(8,128)(2,1)S(1)}, bf16[512,512]{1,0:T(8,128)(2,1)S(1)}, b...) custom-call(bf16[128,2048]{1,0:T(8,128)(2,1)S(1)} %copy-done, ...), custom_call_target="tpu_custom_call" | custom-call | tf_op jit(solution)/shard_map/attend/pallas_call | solution.py:2353
  98.4 0.8 copy-done.7
  104.0 281.0 %ffn.1 = (f32[2,64,2048]{2,1,0:T(8,128)}, bf16[8,4,2,64,2048]{4,3,2,1,0:T(8,128)(2,1)}, bf16[4096,2048]{1,0:T(8,128)(2,1)}, bf16[8,4,2,64,1280]{4,3,2,1,0:T(8,12...) custom-call(bf16[4,2,64,2048]{3,2,1,0:T(8,128)(2,1)} %bitcast.78, ...), custom_call_target="tpu_custom_call" | custom-call | tf_op jit(solution)/shard_map/ffn/pallas_call | solution.py:1128
  385.1 1.5 multiply_reduce_fusion.2
  386.7 1.5 fusion
  390.5 1.6 fusion.11
  392.1 81.3 %outputs.1 = (f32[128,2048]{1,0:T(8,128)}, bf16[512,2048]{1,0:T(8,128)(2,1)}, f32[2,2048,352]{2,1,0:T(8,128)}, bf16[2,2048,176]{2,1,0:T(8,128)(2,1)}, f32[352,2048]{1,0:T(8,128)}, /*index=5*/bf16[8,176,256]{2,1,0:T(8,128)(2,1)}) custom-call(bf16[4096,2048]{1,0:T(8,128)(2,1)} %get-tuple-element.53.refs_0_, bf16[128,2048]{1,0:T(8,128)(2,1)} %get-tuple-element.123.refs_1_, ...), custom_call_target="tpu_custom_call" | custom-call | tf_op jit(solution)/shard_map/outputs/pallas_call | solution.py:1513
  473.4 89.3 %backward.1 = (f32[2,128,1536]{2,1,0:T(8,128)}, f32[2,128,512]{2,1,0:T(8,128)}, f32[2,16,128]{2,1,0:T(8,128)}, f32[2,256,1408]{2,1,0:T(8,128)}, f32[1408,256]{1,...) custom-call(bf16[512,2048]{1,0:T(8,128)(2,1)} %get-tuple-element.61.refs_0_, bf16[512,512]{1,0:T(8,128)(2,1)} %copy-done.11, ...), custom_call_target="tpu_custom_call" | custom-call | tf_op jit(solution)/shard_map/backward/pallas_call | solution.py:1995
  562.7 0.9 fusion.7
  563.6 1.3 slice_bitcast_fusion
  565.6 1.0 copy.58
  566.6 2.8 reshape.218
  569.4 3.8 copy.59
  573.2 6.5 %copy.60 = f32[1,2048,2,352]{1,3,2,0:T(8,128)} copy(f32[1,2048,2,352]{3,1,2,0:T(8,128)} %bitcast.73) | data formatting | bytes 11534336
  579.8 1.0 copy.65
  580.7 1.1 copy.66
  582.5 1.6 copy.67
  (86 shorter events, 10.8 us)
Async XLA Ops:
  0.6 4.3 copy-start.23
  3.7 13.2 %copy-start.3 = (s32[512,1]{1,0:T(8,128)}, s32[512,1]{1,0:T(8,128)S(1)}, u32[]{:S(2)}) copy-start(s32[512,1]{1,0:T(8,128)S(1)} %copy.52.refs_4_.refs_9_) | copy-start | bytes 6148
  4.9 12.0 %copy-start.1 = (f32[512,128]{1,0:T(8,128)}, f32[512,128]{1,0:T(8,128)S(1)}, u32[]{:S(2)}) copy-start(f32[512,128]{1,0:T(8,128)S(1)} %get-tuple-element.135.refs_5_.refs_6_) | copy-start | bytes 786436
  4.9 12.0 %copy-start.2 = (f32[512,128]{1,0:T(8,128)}, f32[512,128]{1,0:T(8,128)S(1)}, u32[]{:S(2)}) copy-start(f32[512,128]{1,0:T(8,128)S(1)} %get-tuple-element.136.refs_6_.refs_7_) | copy-start | bytes 786436
  12.2 4.7 copy-start
  12.2 4.8 copy-start.4
  12.2 4.8 copy-start.6
  12.2 4.8 copy-start.14
  12.2 4.8 copy-start.15
  17.0 1.0 copy-start.13
  98.4 0.9 copy-start.7
  104.0 282.7 %copy-start.25 = (f32[2048]{0:T(1024)S(1)}, f32[2048]{0:T(1024)}, u32[]{:S(2)}) copy-start(f32[2048]{0:T(1024)} %param.21) | copy-start | bytes 24580
  104.0 282.7 %copy-start.26 = (f32[2048]{0:T(1024)S(1)}, f32[2048]{0:T(1024)}, u32[]{:S(2)}) copy-start(f32[2048]{0:T(1024)} %param.27) | copy-start | bytes 24580
  385.0 3.2 copy-start.27
  385.0 4.2 copy-start.16
  385.1 4.2 copy-start.17
  385.1 5.4 copy-start.5
  473.4 89.3 %copy-start.22 = (f32[128,2048]{1,0:T(8,128)S(1)}, f32[128,2048]{1,0:T(8,128)}, u32[]{:S(2)}) copy-start(f32[128,2048]{1,0:T(8,128)} %get-tuple-element.60) | copy-start | bytes 3145732
  562.7 2.3 copy-start.28
  562.7 2.9 copy-start.24
  565.6 3.8 copy-start.19
  573.2 6.5 %copy-start.21 = (f32[128,2048]{1,0:T(8,128)S(1)}, f32[128,2048]{1,0:T(8,128)}, u32[]{:S(2)}) copy-start(f32[128,2048]{1,0:T(8,128)} %get-tuple-element.151) | copy-start | bytes 3145732
  573.2 7.5 %copy-start.20 = (f32[1408,256]{1,0:T(8,128)S(1)}, f32[1408,256]{1,0:T(8,128)}, u32[]{:S(2)}) copy-start(f32[1408,256]{1,0:T(8,128)} %get-tuple-element.159) | copy-start | bytes 4325380
  579.8 2.7 copy-start.18
  (5 other events, 3.9 us)

commit v8 on v7

--- a/solution.py
+++ b/solution.py
@@ -373,25 +373,52 @@
     pl.semaphore_wait(barrier, 3 + left + right)
 
 
+def plane_peer(me, bits):
+    for one in (1, 2, 4):
+        if bits & one:
+            me = flipped(me, one)
+    return me
+
+
+def greet_plane(me, rank, tp):
+    barrier = pltpu.get_barrier_semaphore()
+    for bits in range(1, 8):
+        pl.semaphore_signal(
+            barrier, inc=1, device_id=(plane_peer(me, bits), rank), device_id_type=MESH
+        )
+
+    @pl.when(rank > 0)
+    def _():
+        pl.semaphore_signal(barrier, inc=1, device_id=(me, rank - 1), device_id_type=MESH)
+
+    @pl.when(rank < tp - 1)
+    def _():
+        pl.semaphore_signal(barrier, inc=1, device_id=(me, rank + 1), device_id_type=MESH)
+
+    left = (rank + tp - 1) // tp
+    right = (2 * (tp - 1) - rank) // tp
+    pl.semaphore_wait(barrier, 7 + left + right)
+
+
 UNIT = 640
 SHARED = 384
 NT = (((1,), (1,)), ((), ()))
 
 
 def ffn_kernel(tp, expert_width, shared_width, *refs):
-    part_ref, hidden_ref, gain_ref, vec_ref, scale_ref, grad_ref = refs[:6]
-    expert_up, shared_up, expert_down, shared_down = refs[6:10]
-    middle_ref, all_ref, grads_ref, d_ref, hid_ref, y_ref, dsum_ref, esum_ref = refs[10:18]
+    part_ref, hidden_ref, gain_ref, vec_ref, scale_ref, grads_ref = refs[:6]
+    expert_up, up_ref, expert_down, down_ref = refs[6:10]
+    middle_ref, all_ref, up_in, d_ref, hid_ref, y_ref, dsum_ref, esum_ref = refs[10:18]
     (
         x_all, g_buf, dh_buf, d_buf, stage, acc, diag_in, last_in, z_in, both_buf, down_buf,
         eu_buf, su_buf, stage_e, acc_e, other_e, diag_e, last_e, z_in_e,
-        local_sem, w_sem, dn_sem, g_sem, x_sem, d_sem, h_sem, y_sem, f_sem, f_send, f_recv,
-        az_send, az_recv, ap_send, ap_recv, gp_send, gp_recv,
+        w_sem, dn_sem, g_sem, x_sem, d_sem, h_sem, y_sem, f_sem, f_send, f_recv,
+        az_send, az_recv, ap_send, ap_recv, s_send, s_recv,
         c_send, c_recv, ce_send, ce_recv, p_send, p_recv, pe_send, pe_recv,
         z_send, z_recv, ze_send, ze_recv,
     ) = refs[18:]
     me, rank = place()
-    greet(me, rank, tp)
+    greet_plane(me, rank, tp)
     f32 = jnp.float32
     bf16 = jnp.bfloat16
     subs, rows, width = hidden_ref.shape
@@ -518,7 +545,6 @@
 
     def control(i):
         steps = {
-            0: [(z_step, 1, 1), (finish, 1, 0)],
             1: [(forward, 3, 0)],
             2: [(forward, 0, 1), (finish, 2, 0)],
             3: [(z_step, 2, 1)],
@@ -538,42 +564,33 @@
                 for act, what, sub in todo:
                     act(what, sub)
 
-    def grad_region(pack, c, start=0, count=None):
-        count = tile if count is None else count
-        return grads_ref.at[pl.ds(pack * pack_rows + c * tile + start, count)]
-
-    def grads(bit, pack_bits, c, slot, start=0, count=None):
-        dst = grad_region(pack_of(pack_bits), c, start, count)
-        src = grad_ref.at[pl.ds(c * tile, tile)] if pack_bits == 0 else dst
-        return remote(src, dst, gp_send.at[slot, c], gp_recv.at[slot, c], bit)
-
-    def grad_core(q, c):
-        return grads(1, 2 * q, c, q)
-
-    def grad_x(c):
-        return grads(2, 0, c, 4)
-
-    def grad_y(c):
-        return grads(4, 0, c, 5)
-
-    def grad_x_to_y(c):
-        return grads(4, 2, c, 6, 0, tile // 2)
-
-    def grad_y_to_x(c):
-        return grads(2, 4, c, 7, tile // 2, tile // 2)
-
-    def grad_forward(c):
-        grad_x(c).wait_recv()
-        grad_x_to_y(c).start()
-        grad_core(1, c).start()
-        grad_y(c).wait_recv()
-        grad_y_to_x(c).start()
-        grad_core(2, c).start()
-
-    def grad_finish(c):
-        grad_x_to_y(c).wait_recv()
-        grad_y_to_x(c).wait_recv()
-        grad_core(3, c).start()
+    up_rows = up_ref.shape[2]
+    span = down_ref.shape[2]
+
+    def up_to(bits):
+        return pltpu.make_async_remote_copy(
+            src_ref=up_ref.at[plane_peer(me, bits)],
+            dst_ref=up_in.at[:, pl.ds(pl.multiple_of(me * up_rows, up_rows), up_rows)],
+            send_sem=s_send.at[0, bits],
+            recv_sem=s_recv.at[0, bits],
+            device_id=(plane_peer(me, bits), rank),
+            device_id_type=MESH,
+        )
+
+    def down_spot():
+        return down_buf.at[
+            pl.ds(SHARED, shared_width), pl.ds(pl.multiple_of(me * span, span), span)
+        ]
+
+    def down_to(bits):
+        return pltpu.make_async_remote_copy(
+            src_ref=down_ref.at[plane_peer(me, bits)],
+            dst_ref=down_spot(),
+            send_sem=s_send.at[1, bits],
+            recv_sem=s_recv.at[1, bits],
+            device_id=(plane_peer(me, bits), rank),
+            device_id_type=MESH,
+        )
 
     def core(q, s):
         return remote(stage.at[s], acc.at[q, s], c_send.at[q, s], c_recv.at[q, s], 1)
@@ -775,8 +792,21 @@
         at = pl.ds(pl.multiple_of(n * cut, cut), cut)
         return (
             pltpu.make_async_copy(expert_up.at[part, at], eu_buf.at[slot], w_sem.at[0, slot]),
-            pltpu.make_async_copy(shared_up.at[part, at], su_buf.at[slot], w_sem.at[1, slot]),
-        )
+            pltpu.make_async_copy(up_in.at[part, at], su_buf.at[slot], w_sem.at[1, slot]),
+        )
+
+    def start_loads(part, n, slot):
+        of_expert, of_shared = weight_loads(part, n, slot)
+        of_expert.start()
+
+        @pl.when(n == me)
+        def _():
+            own = up_ref.at[me, part]
+            pltpu.make_async_copy(own, su_buf.at[slot], w_sem.at[1, slot]).start()
+
+        @pl.when(n != me)
+        def _():
+            of_shared.start()
 
     def lay_out(part):
         base = part * UNIT
@@ -786,8 +816,7 @@
 
             @pl.when(n + 1 < cuts)
             def _():
-                for copy in weight_loads(part, n + 1, 1 - slot):
-                    copy.start()
+                start_loads(part, n + 1, 1 - slot)
 
             for copy in weight_loads(part, n, slot):
                 copy.wait()
@@ -797,46 +826,34 @@
             both_buf[at, base + SHARED : base + units] = su_buf[slot]
             return carry
 
-        for copy in weight_loads(part, 0, 0):
-            copy.start()
+        start_loads(part, 0, 0)
         lax.fori_loop(0, cuts, body, 0)
 
     down_loads = (
         pltpu.make_async_copy(expert_down, down_buf.at[pl.ds(0, expert_width)], dn_sem.at[0]),
-        pltpu.make_async_copy(shared_down, down_buf.at[pl.ds(SHARED, shared_width)], dn_sem.at[1]),
-    )
-
-    def hidden_grads(count, task, own=False):
-        def load(n, slot):
-            pack_bits, c = task(n)
-            src = grad_ref.at[pl.ds(c * tile, tile)] if own else grad_region(pack_of(pack_bits), c)
-            return pltpu.make_async_copy(src, g_buf.at[slot], g_sem.at[slot])
-
+        pltpu.make_async_copy(down_ref.at[me], down_spot(), dn_sem.at[1]),
+    )
+
+    def grad_load(n, slot):
+        at = pl.ds(n * tile, tile)
+        return pltpu.make_async_copy(grads_ref.at[at], g_buf.at[slot], g_sem.at[slot])
+
+    def hidden_grads(first, last):
         def body(n, carry):
             slot = n % 2
 
-            @pl.when(n + 1 < count)
-            def _():
-                load(n + 1, 1 - slot).start()
-
-            load(n, slot).wait()
-            pack_bits, c = task(n)
+            @pl.when(n + 1 < 2 * packs)
+            def _():
+                grad_load(n + 1, 1 - slot).start()
+
+            grad_load(n, slot).wait()
             d_hidden = lax.dot_general(
                 g_buf[slot], down_buf[...], NT, preferred_element_type=f32
             ).astype(bf16)
-            dh_buf[pack_of(pack_bits), pl.ds(2 * c, 2)] = d_hidden.reshape(2, subs, rows, UNIT)
+            dh_buf[n // 2, pl.ds(n % 2 * 2, 2)] = d_hidden.reshape(2, subs, rows, UNIT)
             return carry
 
-        load(0, 0).start()
-        lax.fori_loop(0, count, body, 0)
-        if own:
-            for c in range(2):
-                own_store(c).start()
-            for c in range(2):
-                own_store(c).wait()
-
-    def own_store(c):
-        return pltpu.make_async_copy(g_buf.at[c], grad_region(me, c), local_sem.at[c])
+        lax.fori_loop(first, last, body, 0)
 
     def tile_of(i):
         s = i // 8
@@ -952,9 +969,13 @@
                 diag_x(s).start()
                 diag_y(s).start()
 
-            @pl.when(i == 11)
+            @pl.when(i == 9)
             def _():
                 second(0)
+
+            @pl.when(i == 15)
+            def _():
+                third(0, 0)
 
         return carry
 
@@ -978,43 +999,76 @@
 
         lax.fori_loop(first, last, body, 0)
 
-    for c in range(2):
-        grad_x(c).start()
-        grad_y(c).start()
-        grad_core(0, c).start()
+    for bits in (6, 7, 2, 4, 3, 5, 1):
+        down_to(bits).start()
+    for bits in (6, 7, 2, 4, 3, 5, 1):
+        up_to(bits).start()
+    grad_load(0, 0).start()
     for s in range(subs):
         for block in blocks:
             front_load(block, s).start()
-    down_buf[...] = jnp.zeros_like(down_buf)
+    down_buf[expert_width:SHARED, :] = jnp.zeros((SHARED - expert_width, width), bf16)
+    down_buf[units:, :] = jnp.zeros((UNIT - units, width), bf16)
     for copy in down_loads:
         copy.start()
+    ends = (rank == 0) | (rank == tp - 1)
+    inner = (rank > 0) & (rank < tp - 1)
     front(0, 0)
-    lay_out(0)
     front(1, 0)
-    lay_out(1)
-    front(0, 1)
     front(2, 0)
+
+    @pl.when(ends)
+    def _():
+        front(0, 1)
+
     for copy in down_loads:
         copy.wait()
+    for bits in range(1, 8):
+        down_to(bits).wait_recv()
+
+    @pl.when(ends)
+    def _():
+        hidden_grads(0, 6)
+
     front(3, 0)
-    hidden_grads(2, lambda n: (0 * n, n), own=True)
-    for c in range(2):
-        grad_core(0, c).wait_recv()
-    hidden_grads(2, lambda n: (0 * n + 1, n))
-    grad_forward(0)
-    front(1, 1)
+
+    @pl.when(ends)
+    def _():
+        front(1, 1)
+        front(2, 1)
+
+    @pl.when(inner)
+    def _():
+        front(0, 1)
+
     z_step(1, 0)
-    for q in (1, 2):
-        grad_core(q, 0).wait_recv()
-    hidden_grads(4, lambda n: (2 + n, 0 * n))
-    front(2, 1)
+    forward(0, 0)
+
+    @pl.when(inner)
+    def _():
+        hidden_grads(0, 4)
+
     z_step(2, 0)
+
+    @pl.when(inner)
+    def _():
+        front(1, 1)
+        hidden_grads(4, 6)
+        front(2, 1)
+
+    for bits in range(1, 8):
+        up_to(bits).wait_recv()
+    lay_out(0)
+    z_step(3, 0)
+    forward(1, 0)
+    finish(0, 0)
     front(3, 1)
-    z_step(3, 0)
-    grad_forward(1)
-    for q in (1, 2):
-        grad_core(q, 1).wait_recv()
-    hidden_grads(4, lambda n: (2 + n, 0 * n + 1))
+    lay_out(1)
+    forward(2, 0)
+    z_step(1, 1)
+    hidden_grads(6, 11)
+    finish(1, 0)
+    hidden_grads(11, 2 * packs)
     for s in range(subs):
         for j in range(tp - 1):
             block = blocks[j]
@@ -1027,15 +1081,6 @@
             def _():
                 front_z(j, s, False).wait_send()
 
-    forward(0, 0)
-    grad_finish(0)
-    forward(1, 0)
-    grad_finish(1)
-    for c in range(2):
-        grad_core(3, c).wait_recv()
-    hidden_grads(4, lambda n: (6 + n // 2, n % 2))
-    finish(0, 0)
-    forward(2, 0)
     lax.fori_loop(0, 16, one_tile, 0)
     hidden_store = pltpu.make_async_copy(dh_buf, hid_ref, h_sem)
     hidden_store.start()
@@ -1043,19 +1088,22 @@
     acc_e[2] = acc_e[2] + diag_e[...]
     summed_lines().start()
     outputs(0, 2)
-    third(0, 0)
-    outputs(2, 4)
     second(1)
     third(1, 0)
+    outputs(2, 4)
+    third(2, 0)
     outputs(4, 6)
-    third(2, 0)
-    outputs(6, 8)
     third(3, 0)
     sum_lines()
-    outputs(8, 16)
-    for j in range(tp):
-        third(j, 1)
-
+    outputs(6, 8)
+    third(0, 1)
+    outputs(8, 10)
+    third(1, 1)
+    outputs(10, 12)
+    third(2, 1)
+    outputs(12, 14)
+    third(3, 1)
+    outputs(14, 16)
     hidden_store.wait()
     for n in (14, 15):
         y_store(n, n % 2).wait()
@@ -1066,11 +1114,9 @@
     diag_lines().wait_send()
     for q in range(4):
         core_e(q).wait_send()
-    for c in range(2):
-        for q in range(4):
-            grad_core(q, c).wait_send()
-        for copy in (grad_x, grad_y, grad_x_to_y, grad_y_to_x):
-            copy(c).wait_send()
+    for bits in range(1, 8):
+        up_to(bits).wait_send()
+        down_to(bits).wait_send()
     for s in range(subs):
         for copy in (diag_x, diag_y, direct_x, direct_y, summed_x, summed_y):
             copy(s).wait_send()
@@ -1109,7 +1155,7 @@
 
 
 def ffn(
-    part, hidden, gain, vec, scale, grad, expert_up, shared_up, expert_down, shared_down,
+    part, hidden, gain, vec, scale, grads, expert_up, shared_up, expert_down, shared_down,
     fsdp, tp, collective_id,
 ):
     own, width = hidden.shape
@@ -1117,7 +1163,7 @@
     rows = own // subs
     tile = tp * rows
     tokens = fsdp * tp * own
-    expert_width, shared_width = expert_down.shape[0], shared_down.shape[0]
+    expert_width, shared_width = expert_down.shape[0], shared_down.shape[1]
     bf16 = jnp.bfloat16
     f32 = jnp.float32
     dma = pltpu.SemaphoreType.DMA
@@ -1130,7 +1176,7 @@
         out_shape=[
             jax.ShapeDtypeStruct((subs, rows, width), f32),
             jax.ShapeDtypeStruct(all_rows + (width,), bf16),
-            jax.ShapeDtypeStruct((tokens, width), bf16),
+            jax.ShapeDtypeStruct((2, width, shared_width), bf16),
             jax.ShapeDtypeStruct(all_rows + (2 * UNIT,), bf16),
             jax.ShapeDtypeStruct(all_rows + (UNIT,), bf16),
             jax.ShapeDtypeStruct((tokens, width), bf16),
@@ -1159,10 +1205,10 @@
             pltpu.VMEM(lines, f32),
             pltpu.VMEM((2,) + lines, f32),
             pltpu.VMEM((2,) + lines, f32),
-            dma((2,)), dma((2, 2)), dma((2,)), dma((2,)), dma((2,)), dma((2,)), dma, dma((2,)),
+            dma((2, 2)), dma((2,)), dma((2,)), dma((2,)), dma((2,)), dma, dma((2,)),
             dma((tp, subs)), dma((2, tp, subs)), dma((2, tp, subs)),
             dma((2, tp, subs)), dma((2, tp, subs)), dma((8, tp, subs)), dma((8, tp, subs)),
-            dma((8, 2)), dma((8, 2)),
+            dma((2, fsdp)), dma((2, fsdp)),
             dma((4, subs)), dma((4, subs)), dma((4,)), dma((4,)),
             dma((6, subs)), dma((6, subs)), dma((3,)), dma((3,)),
             dma((2, tp, subs)), dma((2, tp, subs)), dma((2,)), dma((2,)),
@@ -1173,7 +1219,7 @@
         name="ffn",
     )(
         part.reshape(tp, subs, rows, width), hidden.reshape(subs, rows, width), gain, vec,
-        scale, grad, expert_up, shared_up, expert_down, shared_down,
+        scale, grads, expert_up, shared_up, expert_down, shared_down,
     )
 
 
@@ -1862,7 +1908,7 @@
         dn_buf[pl.ds(2 * half, 2)] = grads.astype(bf16).reshape(2, rows, width)
 
     ends = (rank == 0) | (rank == tp - 1)
-    for bits in (6, 7, 2, 4, 3, 5, 1):
+    for bits in (6, 7, 2, 4):
         shared_up(bits).start()
         shared_down(bits).start()
     own_up.start()
@@ -1897,6 +1943,9 @@
         front(1)
 
     second(1)
+    for bits in (3, 5, 1):
+        shared_up(bits).start()
+        shared_down(bits).start()
     front(2)
     front(3)
     d_normed = hidden_grad_ref[...]
@@ -2025,24 +2074,15 @@
     )
 
 
-def plane_peer(me, bits):
-    for one in (1, 2, 4):
-        if bits & one:
-            me = flipped(me, one)
-    return me
-
-
 def attend_kernel(tp, heads, halved, *refs):
     parts = len(halved)
     hidden_ref, gain_ref, grad_ref, seg_row_ref, seg_col_ref, cos_ref, sin_ref = refs[:7]
-    up_ref, down_ref = refs[7:9]
-    pieces, refs = refs[9 : 9 + parts], refs[9 + parts :]
+    pieces, refs = refs[7 : 7 + parts], refs[7 + parts :]
     rows_out, grads_ref, q_ref, k_ref, v_ref, lt_ref, heads_ref, part_ref = refs[:8]
-    up_out, down_out = refs[8:10]
-    fulls_out, refs = refs[10 : 10 + parts], refs[10 + parts :]
+    fulls_out, refs = refs[8 : 8 + parts], refs[8 + parts :]
     rows_ref, fulls, refs = refs[0], refs[1 : 1 + parts], refs[1 + parts :]
     (
-        up_buf, down_buf, l_sem, e_sem, z_send, z_recv, g_send, g_recv, p_send, p_recv, s_sem, s_send, s_recv,
+        l_sem, e_sem, z_send, z_recv, g_send, g_recv, p_send, p_recv, gp_send, gp_recv,
     ) = refs
     me, rank = place()
     f32 = jnp.float32
@@ -2050,27 +2090,10 @@
     rows, width = hidden_ref.shape
     length = rows * tp
 
-    barrier = pltpu.get_barrier_semaphore()
-    for bits in range(1, 8):
-        pl.semaphore_signal(
-            barrier, inc=1, device_id=(plane_peer(me, bits), rank), device_id_type=MESH
-        )
-
-    @pl.when(rank > 0)
-    def _():
-        pl.semaphore_signal(barrier, inc=1, device_id=(me, rank - 1), device_id_type=MESH)
-
-    @pl.when(rank < tp - 1)
-    def _():
-        pl.semaphore_signal(barrier, inc=1, device_id=(me, rank + 1), device_id_type=MESH)
-
-    left = (rank + tp - 1) // tp
-    right = (2 * (tp - 1) - rank) // tp
-    pl.semaphore_wait(barrier, 7 + left + right)
-
-    def along_z(ref, sends, recvs, block, to_right):
+    greet(me, rank, tp)
+
+    def along_z(spot, sends, recvs, block, to_right):
         way = 0 if to_right else 1
-        spot = ref.at[pl.ds(block * rows, rows)]
         return pltpu.make_async_remote_copy(
             src_ref=spot,
             dst_ref=spot,
@@ -2081,10 +2104,11 @@
         )
 
     def row_z(block, to_right):
-        return along_z(rows_ref, z_send, z_recv, block, to_right)
+        spot = rows_ref.at[pl.ds(block * rows, rows)]
+        return along_z(spot, z_send, z_recv, block, to_right)
 
     def grad_z(block, to_right):
-        return along_z(grads_ref, g_send, g_recv, block, to_right)
+        return along_z(grad_region(me, block), g_send, g_recv, block, to_right)
 
     def z_start(copy):
         @pl.when(rank < tp - 1)
@@ -2095,7 +2119,7 @@
         def _():
             copy(rank, False).start()
 
-    def z_step(copy, step):
+    def z_step(copy, step, then=None):
         @pl.when(rank >= step)
         def _():
             copy(rank - step, True).wait_recv()
@@ -2104,6 +2128,9 @@
             def _():
                 copy(rank - step, True).start()
 
+            if then is not None:
+                then(rank - step)
+
         @pl.when(rank + step < tp)
         def _():
             copy(rank + step, False).wait_recv()
@@ -2111,6 +2138,9 @@
             @pl.when(rank > 0)
             def _():
                 copy(rank + step, False).start()
+
+            if then is not None:
+                then(rank + step)
 
     def z_end(copy):
         for block in range(tp):
@@ -2183,43 +2213,57 @@
             to_core(q, i).wait_recv()
         export(i).start()
 
-    up_rows = up_ref.shape[2]
-    span = down_ref.shape[2]
-
-    def shared_up(bits):
+    order = [rank]
+    for bit in (1, 2):
+        order = order + [flipped(one, bit) for one in order]
+
+    def grad_region(pack, block, start=0, count=None):
+        count = rows if count is None else count
+        return grads_ref.at[pl.ds(pack * length + block * rows + start, count)]
+
+    def grad_across(bit, pack_bits, block, slot, start=0, count=None):
+        spot = grad_region(plane_peer(me, pack_bits), block, start, count)
         return pltpu.make_async_remote_copy(
-            src_ref=up_ref.at[plane_peer(me, bits)],
-            dst_ref=up_out.at[:, pl.ds(pl.multiple_of(me * up_rows, up_rows), up_rows)],
-            send_sem=s_send.at[0, bits],
-            recv_sem=s_recv.at[0, bits],
-            device_id=(plane_peer(me, bits), rank),
+            src_ref=spot,
+            dst_ref=spot,
+            send_sem=gp_send.at[slot, block],
+            recv_sem=gp_recv.at[slot, block],
+            device_id=(flipped(me, bit), rank),
             device_id_type=MESH,
         )
 
-    def shared_down(bits):
-        return pltpu.make_async_remote_copy(
-            src_ref=down_ref.at[plane_peer(me, bits)],
-            dst_ref=down_out.at[:, pl.ds(pl.multiple_of(me * span, span), span)],
-            send_sem=s_send.at[1, bits],
-            recv_sem=s_recv.at[1, bits],
-            device_id=(plane_peer(me, bits), rank),
-            device_id_type=MESH,
-        )
-
-    own_loads = (
-        pltpu.make_async_copy(up_ref.at[me], up_buf, s_sem.at[0]),
-        pltpu.make_async_copy(down_ref.at[me], down_buf, s_sem.at[1]),
-    )
-    own_stores = (
-        pltpu.make_async_copy(
-            up_buf,
-            up_out.at[:, pl.ds(pl.multiple_of(me * up_rows, up_rows), up_rows)],
-            s_sem.at[0],
-        ),
-        pltpu.make_async_copy(
-            down_buf, down_out.at[:, pl.ds(pl.multiple_of(me * span, span), span)], s_sem.at[1]
-        ),
-    )
+    def grad_core(q, block):
+        return grad_across(1, 2 * q, block, q)
+
+    def grad_x(block):
+        return grad_across(2, 0, block, 4)
+
+    def grad_y(block):
+        return grad_across(4, 0, block, 5)
+
+    def grad_x_to_y(block):
+        return grad_across(4, 2, block, 6, 0, rows // 2)
+
+    def grad_y_to_x(block):
+        return grad_across(2, 4, block, 7, rows // 2, rows // 2)
+
+    def grad_plane(block):
+        grad_x(block).start()
+        grad_y(block).start()
+        grad_core(0, block).start()
+
+    def grad_forward(block):
+        grad_x(block).wait_recv()
+        grad_x_to_y(block).start()
+        grad_core(1, block).start()
+        grad_y(block).wait_recv()
+        grad_y_to_x(block).start()
+        grad_core(2, block).start()
+
+    def grad_finish(block):
+        grad_x_to_y(block).wait_recv()
+        grad_y_to_x(block).wait_recv()
+        grad_core(3, block).start()
 
     def project(which):
         at = slice(which * heads * 128, (which + 1) * heads * 128)
@@ -2281,44 +2325,48 @@
     own_rows = pl.ds(pl.multiple_of(rank * rows, rows), rows)
     rows_ref[own_rows, :] = (hidden * inverse * gain_ref[...]).astype(bf16)
     z_start(row_z)
-    own_grad = pltpu.make_async_copy(grad_ref, grads_ref.at[own_rows], l_sem.at[parts])
+    own_grad = pltpu.make_async_copy(grad_ref, grad_region(me, rank), l_sem.at[parts])
     own_grad.start()
     for i in range(parts):
         local(i).start()
-    for copy in own_loads:
-        copy.start()
+    own_grad.wait()
+    grad_plane(rank)
     z_step(row_z, 1)
     forward(0)
-    for load, store in zip(own_loads, own_stores):
-        load.wait()
-        store.start()
     z_step(row_z, 2)
-    own_grad.wait()
     z_start(grad_z)
     for i in range(1, parts):
         forward(i)
-    for bits in (6, 7, 2, 4, 3, 5, 1):
-        shared_up(bits).start()
-        shared_down(bits).start()
     finish(0)
     z_step(row_z, 3)
     rows_export = pltpu.make_async_copy(rows_ref, rows_out, e_sem.at[parts])
     rows_export.start()
     for i in range(1, parts):
         finish(i)
-    z_step(grad_z, 1)
+    grad_forward(order[0])
+    z_step(grad_z, 1, grad_plane)
     for i in range(parts):
         arrived(i)
     make_heads()
-    z_step(grad_z, 2)
-    for head in range(heads):
+    grad_finish(order[0])
+    z_step(grad_z, 2, grad_plane)
+    attend(0)
+    attend(1)
+    grad_forward(order[1])
+    z_step(grad_z, 3, grad_plane)
+    for head in range(2, heads):
         attend(head)
+    grad_finish(order[1])
+    grad_forward(order[2])
     project_out()
-    z_step(grad_z, 3)
+    grad_finish(order[2])
+    grad_forward(order[3])
+    grad_finish(order[3])
+    for block in order:
+        for q in range(4):
+            grad_core(q, block).wait_recv()
 
     rows_export.wait()
-    for store in own_stores:
-        store.wait()
     for i in range(parts):
         export(i).wait()
         for q in range(4):
@@ -2328,17 +2376,16 @@
         x_to_y(i).wait_send()
         if halved[i]:
             y_to_x(i).wait_send()
-    for bits in range(1, 8):
-        for copy in (shared_up, shared_down):
-            copy(bits).wait_recv()
-            copy(bits).wait_send()
+    for block in order:
+        for q in range(4):
+            grad_core(q, block).wait_send()
+        for copy in (grad_x, grad_y, grad_x_to_y, grad_y_to_x):
+            copy(block).wait_send()
     z_end(row_z)
     z_end(grad_z)
 
 
-def attend_pack(
-    hidden, gain, grad, segments, cos, sin, shared_up, shared_down, pieces, fsdp, tp, heads, number
-):
+def attend_pack(hidden, gain, grad, segments, cos, sin, pieces, fsdp, tp, heads, number):
     rows, width = hidden.shape
     length = rows * tp
     parts = len(pieces)
@@ -2354,29 +2401,23 @@
         functools.partial(attend_kernel, tp, heads, halved),
         out_shape=[
             jax.ShapeDtypeStruct((length, width), bf16),
-            jax.ShapeDtypeStruct((length, width), bf16),
+            jax.ShapeDtypeStruct((length * fsdp, width), bf16),
             of_heads,
             of_heads,
             of_heads,
             jax.ShapeDtypeStruct((length, 128), f32),
             of_heads,
             jax.ShapeDtypeStruct((length, width), bf16),
-            jax.ShapeDtypeStruct(
-                (2, shared_up.shape[2] * fsdp, shared_up.shape[3]), shared_up.dtype
-            ),
-            jax.ShapeDtypeStruct((shared_down.shape[1], width), shared_down.dtype),
         ]
         + [jax.ShapeDtypeStruct(shape, one.dtype) for shape, one in zip(fulls, pieces)],
-        in_specs=[vmem] * 7 + [anywhere] * (2 + parts),
-        out_specs=[anywhere, anywhere] + [vmem] * 6 + [anywhere] * (2 + parts),
+        in_specs=[vmem] * 7 + [anywhere] * parts,
+        out_specs=[anywhere, anywhere] + [vmem] * 6 + [anywhere] * parts,
         scratch_shapes=[pltpu.VMEM((length, width), bf16)]
         + [pltpu.VMEM(shape, one.dtype) for shape, one in zip(fulls, pieces)]
         + [
-            pltpu.VMEM(shared_up.shape[1:], shared_up.dtype),
-            pltpu.VMEM(shared_down.shape[1:], shared_down.dtype),
             dma((parts + 1,)), dma((parts + 1,)),
             dma((2, tp)), dma((2, tp)), dma((2, tp)), dma((2, tp)),
-            dma((8, parts)), dma((8, parts)), dma((2,)), dma((2, 8)), dma((2, 8)),
+            dma((8, parts)), dma((8, parts)), dma((8, tp)), dma((8, tp)),
         ],
         compiler_params=pltpu.CompilerParams(
             collective_id=number, has_side_effects=True, vmem_limit_bytes=48 << 20
@@ -2384,7 +2425,7 @@
         name="attend",
     )(
         hidden, gain, grad, segments.reshape(1, -1), segments.reshape(-1, 1), cos, sin,
-        shared_up, shared_down, *pieces,
+        *pieces,
     )
 
 
@@ -2440,15 +2481,13 @@
     sin_two = jnp.concatenate([-sin_table[:, 0], sin_table[:, 0]], axis=1)
     (
         normed_one,
-        grad_pack,
+        grad_all,
         query,
         keys,
         values,
         log_total,
         heads_out,
         projected,
-        shared_up,
-        shared_dn,
         qkv_flat,
         out_pieces,
         tables,
@@ -2460,8 +2499,6 @@
         segments,
         cos_two,
         sin_two,
-        up_pieces,
-        shared_down.reshape(experts, shared_width, -1),
         [qkv_weight.reshape(-1, 3 * heads_width), out_weight, table.T, bias_piece],
         experts,
         lax.axis_size("tp"),
@@ -2473,17 +2510,17 @@
     ).reshape(-1)
     scales = expert_scale.reshape(packs, lax.axis_size("tp"), 2, own_rows // 2)
     scales = scales.transpose(0, 2, 1, 3).reshape(packs, 2, 1, length // 2)
-    middle, normed_all, grad_all, d_all, hidden_all, token_part, d_normed_two, lines = ffn(
+    middle, normed_all, _, d_all, hidden_all, token_part, d_normed_two, lines = ffn(
         projected,
         hidden_in,
         ffn_gain[None],
         shared_gate_vec[None],
         scales,
-        grad_pack,
+        grad_all,
         expert_up.transpose(1, 0, 2),
-        shared_up,
+        up_pieces,
         expert_dn,
-        shared_dn,
+        shared_down.reshape(experts, shared_width, -1),
         experts,
         lax.axis_size("tp"),
         1,

time: 588 us -> 575 us (0.978); the launches traced: 584 us -> 565 us
  Pallas kernels: 532 us -> 511 us
    pallas_call x1, Pallas kernels: 281 us -> 232 us  [ffn(): pl.pallas_call(functools.partial(ffn_kernel, tp, expert_width, shared_wid...]
    pallas_call x1, Pallas kernels: 80.5 us -> 114 us  [attend_pack(): pl.pallas_call(functools.partial(attend_kernel, tp, heads, halved), out_s...]
    unnamed x66 -> x58, local copies, waits for them, and re-layouts: 28.8 us -> 27.9 us
where the time goes in v8:
time: 575 us; the launch traced here: 565 us
  Pallas kernels  511 us (89%)
  local copies, waits for them, and re-layouts  41.3 us (7%)
  other arithmetic  10.6 us (2%)
    pallas_call x1, Pallas kernels, ffn(): pl.pallas_call(functools.partial(ffn_kernel, tp, expert_width, shared_wid...  232 us
    pallas_call x1, Pallas kernels, attend_pack(): pl.pallas_call(functools.partial(attend_kernel, tp, heads, halved), out_s...  114 us
    pallas_call x1, Pallas kernels, backward(): pl.pallas_call(functools.partial(backward_kernel, fsdp, tp, heads), out_s...  84.3 us
    pallas_call x1, Pallas kernels, outputs(): pl.pallas_call(functools.partial(outputs_kernel, tp, expert_width, shared...  81.5 us
    unnamed x58, local copies, waits for them, and re-layouts  27.9 us

profile of v8, /device:TPU:0, one launch (start us, length us, event | category | flops | bytes accessed | tf_op | source)
XLA Modules:
  0.0 564.7 jit_solution(3822365530218857903)
XLA Ops:
  2.9 0.8 copy.50.refs_4_.refs_9_
  3.7 1.0 fusion.10
  5.3 3.7 copy.54
  9.0 2.4 copy.55
  11.3 4.7 copy.53
  16.1 0.9 copy-done.11
  17.0 113.9 %attend.1 = (bf16[512,2048]{1,0:T(8,128)(2,1)}, bf16[4096,2048]{1,0:T(8,128)(2,1)}, bf16[512,512]{1,0:T(8,128)(2,1)S(1)}, bf16[512,512]{1,0:T(8,128)(2,1)S(1)}, ...) custom-call(bf16[128,2048]{1,0:T(8,128)(2,1)S(1)} %copy-done, ...), custom_call_target="tpu_custom_call" | custom-call | tf_op jit(solution)/shard_map/attend/pallas_call | solution.py:2400
  135.6 231.7 %ffn.1 = (f32[2,64,2048]{2,1,0:T(8,128)}, bf16[8,4,2,64,2048]{4,3,2,1,0:T(8,128)(2,1)}, bf16[2,2048,176]{2,1,0:T(8,128)(2,1)}, bf16[8,4,2,64,1280]{4,3,2,1,0:T(8...) custom-call(bf16[4,2,64,2048]{3,2,1,0:T(8,128)(2,1)} %bitcast.77, ...), custom_call_target="tpu_custom_call" | custom-call | tf_op jit(solution)/shard_map/ffn/pallas_call | solution.py:1174
  367.4 1.5 multiply_reduce_fusion.2
  369.0 1.5 fusion
  370.6 0.8 dynamic-slice_bitcast_fusion
  372.3 1.9 multiply_reduce_fusion
  374.8 1.6 fusion.11
  376.4 81.5 %outputs.1 = (f32[128,2048]{1,0:T(8,128)}, bf16[512,2048]{1,0:T(8,128)(2,1)}, f32[2,2048,352]{2,1,0:T(8,128)}, bf16[2,2048,176]{2,1,0:T(8,128)(2,1)}, f32[352,2048]{1,0:T(8,128)}, /*index=5*/bf16[8,176,256]{2,1,0:T(8,128)(2,1)}) custom-call(bf16[4096,2048]{1,0:T(8,128)(2,1)} %get-tuple-element.48.refs_0_, bf16[128,2048]{1,0:T(8,128)(2,1)} %get-tuple-element.117.refs_1_, ...), custom_call_target="tpu_custom_call" | custom-call | tf_op jit(solution)/shard_map/outputs/pallas_call | solution.py:1559
  457.9 84.3 %backward.1 = (f32[2,128,1536]{2,1,0:T(8,128)}, f32[2,128,512]{2,1,0:T(8,128)}, f32[2,16,128]{2,1,0:T(8,128)}, f32[2,256,1408]{2,1,0:T(8,128)}, f32[1408,256]{1,...) custom-call(bf16[512,2048]{1,0:T(8,128)(2,1)} %get-tuple-element.55.refs_0_, bf16[512,512]{1,0:T(8,128)(2,1)} %copy-done.9, ...), custom_call_target="tpu_custom_call" | custom-call | tf_op jit(solution)/shard_map/backward/pallas_call | solution.py:2044
  542.2 0.9 fusion.7
  543.2 1.4 slice_bitcast_fusion
  545.9 1.0 copy.58
  546.9 2.7 reshape.218
  549.6 3.8 copy.59
  553.4 6.5 %copy.60 = f32[1,2048,2,352]{1,3,2,0:T(8,128)} copy(f32[1,2048,2,352]{3,1,2,0:T(8,128)} %bitcast.72) | data formatting | bytes 11534336
  560.0 1.0 copy.65
  560.9 1.1 copy.66
  562.7 1.6 copy.67
  (78 shorter events, 11.2 us)
Async XLA Ops:
  0.6 4.3 copy-start.21
  3.7 12.3 %copy-start.3 = (s32[512,1]{1,0:T(8,128)}, s32[512,1]{1,0:T(8,128)S(1)}, u32[]{:S(2)}) copy-start(s32[512,1]{1,0:T(8,128)S(1)} %copy.50.refs_4_.refs_9_) | copy-start | bytes 6148
  4.9 11.1 %copy-start.1 = (f32[512,128]{1,0:T(8,128)}, f32[512,128]{1,0:T(8,128)S(1)}, u32[]{:S(2)}) copy-start(f32[512,128]{1,0:T(8,128)S(1)} %get-tuple-element.129.refs_5_.refs_6_) | copy-start | bytes 786436
  4.9 11.1 %copy-start.2 = (f32[512,128]{1,0:T(8,128)}, f32[512,128]{1,0:T(8,128)S(1)}, u32[]{:S(2)}) copy-start(f32[512,128]{1,0:T(8,128)S(1)} %get-tuple-element.130.refs_6_.refs_7_) | copy-start | bytes 786436
  11.3 4.7 copy-start
  11.3 4.7 copy-start.4
  11.3 4.7 copy-start.12
  11.3 4.7 copy-start.13
  16.1 1.0 copy-start.11
  130.9 0.8 copy-start.6
  131.7 0.8 copy-start.7
  132.5 0.8 copy-start.8
  133.3 0.8 copy-start.9
  135.6 233.4 %copy-start.23 = (f32[2048]{0:T(1024)S(1)}, f32[2048]{0:T(1024)}, u32[]{:S(2)}) copy-start(f32[2048]{0:T(1024)} %param.21) | copy-start | bytes 24580
  135.6 233.4 %copy-start.24 = (f32[2048]{0:T(1024)S(1)}, f32[2048]{0:T(1024)}, u32[]{:S(2)}) copy-start(f32[2048]{0:T(1024)} %param.27) | copy-start | bytes 24580
  367.4 4.9 copy-start.14
  367.4 7.4 %copy-start.5 = (bf16[128,2048]{1,0:T(8,128)(2,1)S(1)}, bf16[128,2048]{1,0:T(8,128)(2,1)}, u32[]{:S(2)}) copy-start(bf16[128,2048]{1,0:T(8,128)(2,1)} %refs_2_.1) | copy-start | bytes 1572868
  367.4 7.4 %copy-start.15 = (f32[2,64,2048]{2,1,0:T(8,128)S(1)}, f32[2,64,2048]{2,1,0:T(8,128)}, u32[]{:S(2)}) copy-start(f32[2,64,2048]{2,1,0:T(8,128)} %get-tuple-element.49) | copy-start | bytes 3145732
  457.9 84.3 %copy-start.20 = (f32[128,2048]{1,0:T(8,128)S(1)}, f32[128,2048]{1,0:T(8,128)}, u32[]{:S(2)}) copy-start(f32[128,2048]{1,0:T(8,128)} %get-tuple-element.54) | copy-start | bytes 3145732
  542.2 3.7 copy-start.22
  543.2 6.5 %copy-start.17 = (f32[2,256,1408]{2,1,0:T(8,128)S(1)}, f32[2,256,1408]{2,1,0:T(8,128)}, u32[]{:S(2)}) copy-start(f32[2,256,1408]{2,1,0:T(8,128)} %get-tuple-element.71) | copy-start | bytes 8650756
  553.4 6.5 %copy-start.19 = (f32[128,2048]{1,0:T(8,128)S(1)}, f32[128,2048]{1,0:T(8,128)}, u32[]{:S(2)}) copy-start(f32[128,2048]{1,0:T(8,128)} %get-tuple-element.145) | copy-start | bytes 3145732
  553.4 7.5 %copy-start.18 = (f32[1408,256]{1,0:T(8,128)S(1)}, f32[1408,256]{1,0:T(8,128)}, u32[]{:S(2)}) copy-start(f32[1408,256]{1,0:T(8,128)} %get-tuple-element.153) | copy-start | bytes 4325380
  560.0 2.7 copy-start.16
  (1 other events, 0.7 us)

commit v9 on v8

--- a/solution.py
+++ b/solution.py
@@ -1228,13 +1228,14 @@
 
 
 def outputs_kernel(tp, expert_width, shared_width, *refs):
-    y_ref, own_ref, x_ref, d_ref, h_ref, g_ref = refs[:6]
-    total_ref, rows_ref, ge_ref, gs_ref, de_ref, ds_ref = refs[6:12]
+    y_ref, x_ref, d_ref, h_ref, g_ref = refs[:5]
+    middle_ref, dsum_ref, gate_ref, og_ref, gain_ref, vec_ref = refs[5:11]
+    hidden_ref, grad_ref, sums_ref, rows_ref, ge_ref, gs_ref, de_ref, ds_ref = refs[11:19]
     (
-        mine, other, diag_in, last_in, z_in, d_buf, h_buf, col_buf, ge_buf, gs_buf, de_buf, ds_buf,
+        total_ref, own_ref, mine, other, diag_in, last_in, z_in, d_buf, h_buf, col_buf, ge_buf, gs_buf, de_buf, ds_buf,
         l_sem, c_send, c_recv, p_send, p_recv, z_send, z_recv, a_sem, a_send, a_recv,
         w_sem, col_sem, out_sem,
-    ) = refs[12:]
+    ) = refs[19:]
     me, rank = place()
     greet(me, rank, tp)
     f32 = jnp.float32
@@ -1476,10 +1477,27 @@
             copy.start()
         return carry
 
+    def norm_back():
+        middle = middle_ref[...]
+        gain, vec = gain_ref[...], vec_ref[...]
+        inverse = lax.rsqrt(jnp.mean(middle * middle, axis=-1, keepdims=True) + epsilon)
+        hat = middle * inverse
+        normed = (hat * gain).astype(bf16).astype(f32)
+        logit = jnp.sum(normed * vec, axis=-1, keepdims=True)
+        gate_prob = 1.0 / (1.0 + jnp.exp(-logit))
+        logit_grad = gate_ref[...] * gate_prob * (1.0 - gate_prob)
+        d_normed = dsum_ref[...] + logit_grad * vec
+        sums_ref[0:1] = jnp.sum(d_normed * hat, axis=0, keepdims=True)
+        sums_ref[1:2] = jnp.sum(normed * logit_grad, axis=0, keepdims=True)
+        d_hat = d_normed * gain
+        mean = jnp.mean(d_hat * hat, axis=-1, keepdims=True)
+        grad = og_ref[...].astype(f32) + inverse * (d_hat - hat * mean)
+        grad_ref[...] = grad
+        own_ref[...] = grad.astype(bf16)
+
     load_d = pltpu.make_async_copy(d_ref, d_buf, w_sem.at[0])
     load_h = pltpu.make_async_copy(h_ref, h_buf, w_sem.at[1])
     own = pltpu.make_async_copy(own_ref, rows_ref.at[pl.ds(rank * rows, rows)], a_sem)
-    own.start()
     for j in pieces:
         for k in (3, 2, 1, 0):
             core(k, j).start()
@@ -1487,6 +1505,8 @@
     load_d.start()
     columns(0, 0, True).start()
     load_h.start()
+    norm_back()
+    own.start()
     own.wait()
 
     @pl.when(rank < tp - 1)
@@ -1516,6 +1536,7 @@
             third(j - 2)
     third(len(pieces) - 2)
     third(len(pieces) - 1)
+    hidden_ref[...] = (middle_ref[...] + total_ref[...]).astype(bf16)
 
     for n in (steps - 2, steps - 1):
         for copy in up_stores(n, n % 2) + down_stores(n, n % 2):
@@ -1547,8 +1568,11 @@
             gather_z(block, False).wait_send()
 
 
-def outputs(y, own, x, d, h, g, fsdp, tp, expert_width, shared_width, collective_id):
-    rows, width = own.shape
+def outputs(
+    y, x, d, h, g, middle, d_normed, gate_grad, out_grad, gain, vec,
+    fsdp, tp, expert_width, shared_width, collective_id,
+):
+    rows, width = middle.shape
     tokens = y.shape[0]
     span = width // fsdp
     cut = rows // SUB
@@ -1559,16 +1583,20 @@
     return pl.pallas_call(
         functools.partial(outputs_kernel, tp, expert_width, shared_width),
         out_shape=[
+            jax.ShapeDtypeStruct((rows, width), bf16),
             jax.ShapeDtypeStruct((rows, width), f32),
+            jax.ShapeDtypeStruct((2, width), f32),
             jax.ShapeDtypeStruct((rows * tp, width), bf16),
             jax.ShapeDtypeStruct((2, width, expert_width), f32),
             jax.ShapeDtypeStruct((2, width, shared_width), bf16),
             jax.ShapeDtypeStruct((expert_width, width), f32),
             jax.ShapeDtypeStruct((fsdp, shared_width, span), bf16),
         ],
-        in_specs=[anywhere, pl.BlockSpec(memory_space=pltpu.VMEM)] + [anywhere] * 4,
-        out_specs=[pl.BlockSpec(memory_space=pltpu.VMEM)] + [anywhere] * 5,
+        in_specs=[anywhere] * 5 + [pl.BlockSpec(memory_space=pltpu.VMEM)] * 6,
+        out_specs=[pl.BlockSpec(memory_space=pltpu.VMEM)] * 3 + [anywhere] * 5,
         scratch_shapes=[
+            pltpu.VMEM((rows, width), f32),
+            pltpu.VMEM((rows, width), bf16),
             pltpu.VMEM((4, tp * SUB, cut, width), bf16),
             pltpu.VMEM((4, tp * SUB, cut, width), bf16),
             pltpu.VMEM((tp * SUB, 2, cut // 2, width), bf16),
@@ -1590,13 +1618,13 @@
             collective_id=collective_id, has_side_effects=True, vmem_limit_bytes=60 << 20
         ),
         name="outputs",
-    )(y, own, x, d, h, g)
+    )(y, x, d, h, g, middle, d_normed, gate_grad, out_grad, gain, vec)
 
 
 def backward_kernel(fsdp, tp, heads, *refs):
     parts = 3
     d_ref, ho_ref, q_ref, k_ref, v_ref, lt_ref, cos_ref, sin_ref = refs[:8]
-    seg_row_ref, seg_col_ref, normed_ref, qkv_ref, out_ref = refs[8:13]
+    seg_row_ref, seg_col_ref, normed_in, qkv_in, out_in = refs[8:13]
     gs_ref, ds_ref, hidden_ref, grad_ref, gain_ref, sums_ref = refs[13:19]
     refs = refs[19:]
     outs, refs = refs[:parts], refs[parts:]
@@ -1604,7 +1632,7 @@
     refs = refs[4:]
     mine, other, diag_in, last_in = (refs[i * parts : (i + 1) * parts] for i in range(4))
     (
-        dh_buf, dqkv_buf, gs_in, ds_in, dn_buf, z_in, v_send, v_in, w_send, w_in,
+        normed_ref, qkv_ref, out_ref, in_sem, dh_buf, dqkv_buf, gs_in, ds_in, dn_buf, z_in, v_send, v_in, w_send, w_in,
         c_send, c_recv, p_send, p_recv, s_sem, s_send, s_recv,
         f_send, f_recv, v_ssem, v_rsem, w_ssem, w_rsem,
     ) = refs[4 * parts :]
@@ -1913,11 +1941,21 @@
         shared_down(bits).start()
     own_up.start()
     own_down.start()
+    loads = [
+        pltpu.make_async_copy(src, dst, in_sem.at[i])
+        for i, (src, dst) in enumerate(
+            ((out_in, out_ref), (qkv_in, qkv_ref), (normed_in, normed_ref))
+        )
+    ]
+    for load in loads:
+        load.start()
     lax.fori_loop(0, fsdp, out_piece, 0)
+    loads[0].wait()
     head_grads()
     mine[2][...] = jnp.zeros_like(mine[2])
     for head in range(heads):
         attend_back(head)
+    loads[1].wait()
     row_grads(1 - near)
 
     @pl.when(ends)
@@ -1928,6 +1966,7 @@
     row_grads(near)
     for owner in range(1, fsdp):
         mine[2][owner] = mine[2][0]
+    loads[2].wait()
     lax.fori_loop(0, fsdp, qkv_piece, 0)
     for n in range(fsdp):
         send_piece(jnp.int32(fsdp - 1 - n), 2)
@@ -2044,10 +2083,14 @@
     return pl.pallas_call(
         functools.partial(backward_kernel, fsdp, tp, heads),
         out_shape=out_shape,
-        in_specs=[vmem] * 13 + [anywhere] * 2 + [vmem] * 4,
+        in_specs=[vmem] * 10 + [anywhere] * 5 + [vmem] * 4,
         out_specs=[vmem] * len(out_shape),
         scratch_shapes=scratch
         + [
+            pltpu.VMEM(normed.shape, bf16),
+            pltpu.VMEM(qkv.shape, bf16),
+            pltpu.VMEM(out.shape, bf16),
+            dma((3,)),
             pltpu.VMEM((length, size), bf16),
             pltpu.VMEM((length, 3 * size), bf16),
             pltpu.VMEM((fsdp, 2, span, units), shared_up.dtype),
@@ -2533,34 +2576,38 @@
     d_normed_two = d_normed_two.reshape(own_rows, model_width)
     lines = lax.dynamic_slice_in_dim(lines, tp_rank * (own_rows // 2), own_rows // 2, axis=2)
     extra_sum = lines.transpose(1, 0, 2).reshape(16, own_rows)
-    ffn_inverse = inverse_rms(middle)
-    normed_two_own = (middle * ffn_inverse * ffn_gain).astype(bf16)
     own_start = tp_rank * own_rows
     ids_own = lax.dynamic_slice_in_dim(expert_ids, own_start, own_rows)
     picked = ids_own[:, :, None] == jnp.arange(experts, dtype=jnp.int32)
     route_grad = jnp.sum(jnp.where(picked, extra_sum[:experts].T[:, None, :], 0.0), axis=-1)
     gate_grad = extra_sum[experts]
-    own_gate = jax.nn.sigmoid(jnp.sum(normed_two_own.astype(f32) * shared_gate_vec, axis=-1))
-    logit_grad = gate_grad * own_gate * (1.0 - own_gate)
-    d_normed_two = d_normed_two + logit_grad[:, None] * shared_gate_vec
-    g_gate_vec = jnp.sum(normed_two_own.astype(f32) * logit_grad[:, None], axis=0)
-    hat_two = middle * ffn_inverse
-    g_ffn_gain = jnp.sum(d_normed_two * hat_two, axis=0)
-    middle_grad = out_grad.astype(f32) + norm_backward(d_normed_two, hat_two, ffn_inverse, ffn_gain)
-    total, d_rows, g_expert_up, g_shared_up, g_expert_down, g_shared_down = outputs(
+    (
+        hidden_out,
+        middle_grad,
+        norm_sums,
+        d_rows,
+        g_expert_up,
+        g_shared_up,
+        g_expert_down,
+        g_shared_down,
+    ) = outputs(
         token_part,
-        middle_grad.astype(bf16),
         normed_all,
         d_all,
         hidden_all,
         grad_all,
+        middle,
+        d_normed_two,
+        gate_grad[:, None],
+        out_grad,
+        ffn_gain[None],
+        shared_gate_vec[None],
         experts,
         lax.axis_size("tp"),
         expert_width,
         shared_width,
         2,
     )
-    hidden_out = (middle + total).astype(bf16)
     g_qkv, g_out, g_bias, g_shared_up, g_shared_down, hidden_grad, gains = backward(
         d_rows,
         heads_out,
@@ -2579,7 +2626,7 @@
         hidden_in,
         middle_grad,
         attn_gain[None],
-        jnp.stack([g_ffn_gain, g_gate_vec]),
+        norm_sums,
         experts,
         lax.axis_size("tp"),
         local_heads,

time: 575 us -> 571 us (level)
  other arithmetic: 10.6 us -> 2.53 us
  Pallas kernels: 511 us -> 519 us
    pallas_call x1, Pallas kernels: 232 us -> 240 us  [ffn(): pl.pallas_call(functools.partial(ffn_kernel, tp, expert_width, shared_wid...]
    unnamed x58 -> x47, local copies, waits for them, and re-layouts: 27.9 us -> 28 us
where the time goes in v9:
time: 571 us; the launch traced here: 566 us
  Pallas kernels  519 us (91%)
  local copies, waits for them, and re-layouts  42.9 us (8%)
    pallas_call x1, Pallas kernels, ffn(): pl.pallas_call(functools.partial(ffn_kernel, tp, expert_width, shared_wid...  240 us
    pallas_call x1, Pallas kernels, attend_pack(): pl.pallas_call(functools.partial(attend_kernel, tp, heads, halved), out_s...  114 us
    pallas_call x1, Pallas kernels, outputs(): pl.pallas_call(functools.partial(outputs_kernel, tp, expert_width, shared...  84.3 us
    pallas_call x1, Pallas kernels, backward(): pl.pallas_call(functools.partial(backward_kernel, fsdp, tp, heads), out_s...  81.2 us
    unnamed x47, local copies, waits for them, and re-layouts  28 us

profile of v9, /device:TPU:0, one launch (start us, length us, event | category | flops | bytes accessed | tf_op | source)
XLA Modules:
  0.0 566.0 jit_solution(756371287081865280)
XLA Ops:
  2.9 0.8 copy.52.refs_4_.refs_9_
  3.7 1.0 fusion.2
  5.3 3.7 copy.56
  9.0 2.4 copy.57
  11.3 4.7 copy.55
  16.1 0.9 copy-done.10
  17.0 113.9 %attend.1 = (bf16[512,2048]{1,0:T(8,128)(2,1)}, bf16[4096,2048]{1,0:T(8,128)(2,1)}, bf16[512,512]{1,0:T(8,128)(2,1)S(1)}, bf16[512,512]{1,0:T(8,128)(2,1)S(1)}, ...) custom-call(bf16[128,2048]{1,0:T(8,128)(2,1)S(1)} %copy-done, ...), custom_call_target="tpu_custom_call" | custom-call | tf_op jit(solution)/shard_map/attend/pallas_call | solution.py:2443
  130.9 0.8 copy-done.5
  131.7 0.8 copy-done.6
  132.5 0.8 copy-done.7
  133.3 0.8 copy-done.8
  135.6 240.0 %ffn.1 = (f32[2,64,2048]{2,1,0:T(8,128)}, bf16[8,4,2,64,2048]{4,3,2,1,0:T(8,128)(2,1)}, bf16[2,2048,176]{2,1,0:T(8,128)(2,1)}, bf16[8,4,2,64,1280]{4,3,2,1,0:T(8...) custom-call(bf16[4,2,64,2048]{3,2,1,0:T(8,128)(2,1)} %bitcast.55, ...), custom_call_target="tpu_custom_call" | custom-call | tf_op jit(solution)/shard_map/ffn/pallas_call | solution.py:1174
  375.6 0.8 dynamic-slice_bitcast_fusion
  377.9 84.3 %outputs.1 = (bf16[128,2048]{1,0:T(8,128)(2,1)}, f32[128,2048]{1,0:T(8,128)}, f32[2,2048]{1,0:T(2,128)}, bf16[512,2048]{1,0:T(8,128)(2,1)}, f32[2,2048,352]{2,1,...) custom-call(bf16[4096,2048]{1,0:T(8,128)(2,1)} %get-tuple-element.49.refs_0_, ...), custom_call_target="tpu_custom_call" | custom-call | tf_op jit(solution)/shard_map/outputs/pallas_call | solution.py:1583
  462.2 81.2 %backward.1 = (f32[2,128,1536]{2,1,0:T(8,128)}, f32[2,128,512]{2,1,0:T(8,128)}, f32[2,16,128]{2,1,0:T(8,128)}, f32[2,256,1408]{2,1,0:T(8,128)}, f32[1408,256]{1,...) custom-call(bf16[512,2048]{1,0:T(8,128)(2,1)} %get-tuple-element.57.refs_0_, bf16[512,512]{1,0:T(8,128)(2,1)} %copy-done.8, ...), custom_call_target="tpu_custom_call" | custom-call | tf_op jit(solution)/shard_map/backward/pallas_call | solution.py:2083
  543.4 1.4 slice_bitcast_fusion
  546.2 2.0 copy.61
  548.2 2.7 reshape.104
  551.0 3.8 copy.62
  554.8 6.5 %copy.63 = f32[1,2048,2,352]{1,3,2,0:T(8,128)} copy(f32[1,2048,2,352]{3,1,2,0:T(8,128)} %bitcast.50) | data formatting | bytes 11534336
  561.3 0.8 copy.69
  562.1 1.0 copy.70
  563.1 1.1 copy.71
  564.2 1.6 copy.72
  (54 shorter events, 7.1 us)
Async XLA Ops:
  0.6 4.3 copy-start.17
  3.7 12.3 %copy-start.3 = (s32[512,1]{1,0:T(8,128)}, s32[512,1]{1,0:T(8,128)S(1)}, u32[]{:S(2)}) copy-start(s32[512,1]{1,0:T(8,128)S(1)} %copy.52.refs_4_.refs_9_) | copy-start | bytes 6148
  4.9 11.1 %copy-start.1 = (f32[512,128]{1,0:T(8,128)}, f32[512,128]{1,0:T(8,128)S(1)}, u32[]{:S(2)}) copy-start(f32[512,128]{1,0:T(8,128)S(1)} %get-tuple-element.124.refs_5_.refs_6_) | copy-start | bytes 786436
  4.9 11.1 %copy-start.2 = (f32[512,128]{1,0:T(8,128)}, f32[512,128]{1,0:T(8,128)S(1)}, u32[]{:S(2)}) copy-start(f32[512,128]{1,0:T(8,128)S(1)} %get-tuple-element.125.refs_6_.refs_7_) | copy-start | bytes 786436
  11.3 4.7 copy-start
  11.3 4.7 copy-start.4
  11.3 4.7 copy-start.11
  11.3 4.7 copy-start.12
  16.1 1.0 copy-start.10
  130.9 0.8 copy-start.5
  131.7 0.8 copy-start.6
  132.5 0.8 copy-start.7
  133.3 0.8 copy-start.8
  134.1 0.7 copy-start.9
  543.4 7.5 %copy-start.14 = (f32[2,256,1408]{2,1,0:T(8,128)S(1)}, f32[2,256,1408]{2,1,0:T(8,128)}, u32[]{:S(2)}) copy-start(f32[2,256,1408]{2,1,0:T(8,128)} %get-tuple-element.75) | copy-start | bytes 8650756
  554.8 6.5 %copy-start.18 = (bf16[128,2048]{1,0:T(8,128)(2,1)S(1)}, bf16[128,2048]{1,0:T(8,128)(2,1)}, u32[]{:S(2)}) copy-start(bf16[128,2048]{1,0:T(8,128)(2,1)} %get-tuple-element.139) | copy-start | bytes 1572868
  554.8 7.3 %copy-start.16 = (f32[128,2048]{1,0:T(8,128)S(1)}, f32[128,2048]{1,0:T(8,128)}, u32[]{:S(2)}) copy-start(f32[128,2048]{1,0:T(8,128)} %get-tuple-element.140) | copy-start | bytes 3145732
  554.8 8.3 %copy-start.15 = (f32[1408,256]{1,0:T(8,128)S(1)}, f32[1408,256]{1,0:T(8,128)}, u32[]{:S(2)}) copy-start(f32[1408,256]{1,0:T(8,128)} %get-tuple-element.148) | copy-start | bytes 4325380
  561.3 2.9 copy-start.13

commit v10 on v9

--- a/solution.py
+++ b/solution.py
@@ -1519,6 +1519,7 @@
 
     first(0)
     first(1)
+    first(2)
     load_d.wait()
     load_h.wait()
     for j in pieces:
@@ -1528,8 +1529,8 @@
             later = j - len(pieces) // 2
             lax.fori_loop(2 * later, 2 * later + 2, down_step, 0)
         second(j)
-        if j + 2 < len(pieces):
-            first(j + 2)
+        if j + 3 < len(pieces):
+            first(j + 3)
         if j in (1, 3, 5):
             gather_step((j + 1) // 2)
         if j >= 2:

time: 571 us -> 572 us (level)
  no operation moved by 1% of the time
where the time goes in v10:
time: 572 us; the launch traced here: 566 us
  Pallas kernels  520 us (91%)
  local copies, waits for them, and re-layouts  42.9 us (8%)
    pallas_call x1, Pallas kernels, ffn(): pl.pallas_call(functools.partial(ffn_kernel, tp, expert_width, shared_wid...  240 us
    pallas_call x1, Pallas kernels, attend_pack(): pl.pallas_call(functools.partial(attend_kernel, tp, heads, halved), out_s...  114 us
    pallas_call x1, Pallas kernels, outputs(): pl.pallas_call(functools.partial(outputs_kernel, tp, expert_width, shared...  84.3 us
    pallas_call x1, Pallas kernels, backward(): pl.pallas_call(functools.partial(backward_kernel, fsdp, tp, heads), out_s...  81.2 us
    unnamed x47, local copies, waits for them, and re-layouts  28 us

profile of v10, /device:TPU:0, one launch (start us, length us, event | category | flops | bytes accessed | tf_op | source)
XLA Modules:
  0.0 566.2 jit_solution(11455173944721186032)
XLA Ops:
  2.9 0.8 copy.52.refs_4_.refs_9_
  3.7 1.0 fusion.2
  5.3 3.7 copy.56
  9.0 2.4 copy.57
  11.3 4.7 copy.55
  16.1 0.9 copy-done.10
  17.0 113.9 %attend.1 = (bf16[512,2048]{1,0:T(8,128)(2,1)}, bf16[4096,2048]{1,0:T(8,128)(2,1)}, bf16[512,512]{1,0:T(8,128)(2,1)S(1)}, bf16[512,512]{1,0:T(8,128)(2,1)S(1)}, ...) custom-call(bf16[128,2048]{1,0:T(8,128)(2,1)S(1)} %copy-done, ...), custom_call_target="tpu_custom_call" | custom-call | tf_op jit(solution)/shard_map/attend/pallas_call | solution.py:2444
  130.9 0.8 copy-done.5
  131.7 0.8 copy-done.6
  132.5 0.8 copy-done.7
  133.3 0.8 copy-done.8
  135.6 240.2 %ffn.1 = (f32[2,64,2048]{2,1,0:T(8,128)}, bf16[8,4,2,64,2048]{4,3,2,1,0:T(8,128)(2,1)}, bf16[2,2048,176]{2,1,0:T(8,128)(2,1)}, bf16[8,4,2,64,1280]{4,3,2,1,0:T(8...) custom-call(bf16[4,2,64,2048]{3,2,1,0:T(8,128)(2,1)} %bitcast.55, ...), custom_call_target="tpu_custom_call" | custom-call | tf_op jit(solution)/shard_map/ffn/pallas_call | solution.py:1174
  375.8 0.8 dynamic-slice_bitcast_fusion
  378.1 84.3 %outputs.1 = (bf16[128,2048]{1,0:T(8,128)(2,1)}, f32[128,2048]{1,0:T(8,128)}, f32[2,2048]{1,0:T(2,128)}, bf16[512,2048]{1,0:T(8,128)(2,1)}, f32[2,2048,352]{2,1,...) custom-call(bf16[4096,2048]{1,0:T(8,128)(2,1)} %get-tuple-element.49.refs_0_, ...), custom_call_target="tpu_custom_call" | custom-call | tf_op jit(solution)/shard_map/outputs/pallas_call | solution.py:1584
  462.4 81.2 %backward.1 = (f32[2,128,1536]{2,1,0:T(8,128)}, f32[2,128,512]{2,1,0:T(8,128)}, f32[2,16,128]{2,1,0:T(8,128)}, f32[2,256,1408]{2,1,0:T(8,128)}, f32[1408,256]{1,...) custom-call(bf16[512,2048]{1,0:T(8,128)(2,1)} %get-tuple-element.57.refs_0_, bf16[512,512]{1,0:T(8,128)(2,1)} %copy-done.8, ...), custom_call_target="tpu_custom_call" | custom-call | tf_op jit(solution)/shard_map/backward/pallas_call | solution.py:2084
  543.6 1.4 slice_bitcast_fusion
  546.4 2.0 copy.61
  548.4 2.7 reshape.104
  551.1 3.8 copy.62
  555.0 6.5 %copy.63 = f32[1,2048,2,352]{1,3,2,0:T(8,128)} copy(f32[1,2048,2,352]{3,1,2,0:T(8,128)} %bitcast.50) | data formatting | bytes 11534336
  561.5 0.8 copy.69
  562.3 1.0 copy.70
  563.3 1.1 copy.71
  564.4 1.6 copy.72
  (54 shorter events, 7.1 us)
Async XLA Ops:
  0.6 4.3 copy-start.17
  3.7 12.3 %copy-start.3 = (s32[512,1]{1,0:T(8,128)}, s32[512,1]{1,0:T(8,128)S(1)}, u32[]{:S(2)}) copy-start(s32[512,1]{1,0:T(8,128)S(1)} %copy.52.refs_4_.refs_9_) | copy-start | bytes 6148
  4.9 11.1 %copy-start.1 = (f32[512,128]{1,0:T(8,128)}, f32[512,128]{1,0:T(8,128)S(1)}, u32[]{:S(2)}) copy-start(f32[512,128]{1,0:T(8,128)S(1)} %get-tuple-element.124.refs_5_.refs_6_) | copy-start | bytes 786436
  4.9 11.1 %copy-start.2 = (f32[512,128]{1,0:T(8,128)}, f32[512,128]{1,0:T(8,128)S(1)}, u32[]{:S(2)}) copy-start(f32[512,128]{1,0:T(8,128)S(1)} %get-tuple-element.125.refs_6_.refs_7_) | copy-start | bytes 786436
  11.3 4.7 copy-start
  11.3 4.7 copy-start.4
  11.3 4.7 copy-start.11
  11.3 4.7 copy-start.12
  16.1 1.0 copy-start.10
  130.9 0.8 copy-start.5
  131.7 0.8 copy-start.6
  132.5 0.8 copy-start.7
  133.3 0.8 copy-start.8
  134.1 0.7 copy-start.9
  543.6 7.5 %copy-start.14 = (f32[2,256,1408]{2,1,0:T(8,128)S(1)}, f32[2,256,1408]{2,1,0:T(8,128)}, u32[]{:S(2)}) copy-start(f32[2,256,1408]{2,1,0:T(8,128)} %get-tuple-element.75) | copy-start | bytes 8650756
  554.9 6.5 %copy-start.18 = (bf16[128,2048]{1,0:T(8,128)(2,1)S(1)}, bf16[128,2048]{1,0:T(8,128)(2,1)}, u32[]{:S(2)}) copy-start(bf16[128,2048]{1,0:T(8,128)(2,1)} %get-tuple-element.139) | copy-start | bytes 1572868
  554.9 7.3 %copy-start.16 = (f32[128,2048]{1,0:T(8,128)S(1)}, f32[128,2048]{1,0:T(8,128)}, u32[]{:S(2)}) copy-start(f32[128,2048]{1,0:T(8,128)} %get-tuple-element.140) | copy-start | bytes 3145732
  555.0 8.3 %copy-start.15 = (f32[1408,256]{1,0:T(8,128)S(1)}, f32[1408,256]{1,0:T(8,128)}, u32[]{:S(2)}) copy-start(f32[1408,256]{1,0:T(8,128)} %get-tuple-element.148) | copy-start | bytes 4325380
  561.5 2.9 copy-start.13
